TPU v7x, 32 devices: a whole 2x2x4 slice. The times are simulated.
32 devices in a mesh: dp: 16 (over z, y, x), tensor: 2 (over core).
Axes of the slice: x: 2, y: 2, z: 4, core: 2. Of those that a mesh axis runs over, the one named last changes fastest.
Arguments:
- tokens: bfloat16 [6144, 2048], P(('dp', 'tensor')), may hold values from -6 to 6
- segments: int32 [6144], P('dp'), may hold values from 0 to 31, never falling along the last dimension, each value on 1 to 384 neighbouring positions
- decay: float32 [8], P('tensor'), may hold values from 0.0005 to 0.03
- norm1_gain: float32 [2048], replicated, may hold values from 0.5 to 1.5
- w_query: bfloat16 [2048, 2048], P('dp', 'tensor'), may hold values from -0.110485435 to 0.110485435
- w_key: bfloat16 [2048, 2048], P('dp', 'tensor'), may hold values from -0.15467961 to 0.15467961
- w_value: bfloat16 [2048, 4096], P('dp', 'tensor'), may hold values from -0.125 to 0.125
- w_swish: bfloat16 [2048, 4096], P('dp', 'tensor'), may hold values from -0.125 to 0.125
- w_out: bfloat16 [4096, 2048], P('tensor', 'dp'), may hold values from -0.09375 to 0.09375
- norm2_gain: float32 [2048], replicated, may hold values from 0.5 to 1.5
- w_up: bfloat16 [2048, 4096], P('dp', 'tensor'), may hold values from -0.125 to 0.125
- w_gate: bfloat16 [2048, 4096], P('dp', 'tensor'), may hold values from -0.125 to 0.125
- w_down: bfloat16 [4096, 2048], P('tensor', 'dp'), may hold values from -0.09375 to 0.09375
- cotangent: bfloat16 [6144, 2048], P(('dp', 'tensor')), may hold values from -6 to 6
Outputs:
- mixed: bfloat16 [6144, 2048], P(('dp', 'tensor'))
- grad_tokens: float32 [6144, 2048], P(('dp', 'tensor'))
- grad_norm1: float32 [2048], replicated
- grad_query: float32 [2048, 2048], P('dp', 'tensor')
- grad_key: float32 [2048, 2048], P('dp', 'tensor')
- grad_value: float32 [2048, 4096], P('dp', 'tensor')
- grad_swish: float32 [2048, 4096], P('dp', 'tensor')
- grad_out: float32 [4096, 2048], P('tensor', 'dp')
- grad_norm2: float32 [2048], replicated
- grad_up: float32 [2048, 4096], P('dp', 'tensor')
- grad_gate: float32 [2048, 4096], P('dp', 'tensor')
- grad_down: float32 [4096, 2048], P('tensor', 'dp')
Inputs may be any that keep to these rules, and one draw needn't show every extreme that they name: `segments`: segment numbers never fall along the tokens; a document has 1 to 384 tokens, and one has exactly 384.
All inputs are finite; a program needn't handle non-finite values.
Results may differ from a plain program's by a relative error of at most 0.015.
Values may be sent and summed in bfloat16 or wider, within the bound.
No kernel may reach another device: no remote copies, remote signals or barrier semaphores. Data moves between devices by JAX's collectives and lax.ppermute only.
A program may use at most 320 MiB of HBM per device.

v0:
```python
import jax
import jax.numpy as jnp
from jax import lax
from jax.sharding import PartitionSpec as P

epsilon = 1e-05


def normalize(values):
    centred = values - jnp.mean(values, axis=-1, keepdims=True)
    variance = jnp.mean(centred * centred, axis=-1, keepdims=True)
    return centred * lax.rsqrt(variance + epsilon)


def layer_norm(rows, gain):
    return normalize(rows) * gain


def product(left, right):
    return jnp.dot(left, right, preferred_element_type=jnp.float32)


def left_product(left, right):
    return lax.dot_general(
        left, right, (((0,), (0,)), ((), ())), preferred_element_type=jnp.float32
    )


def right_product(left, right):
    return lax.dot_general(
        left, right, (((1,), (1,)), ((), ())), preferred_element_type=jnp.float32
    )


def gate_piece(swish_in, retained):
    shaped = jax.nn.silu(swish_in).reshape(retained.shape) * normalize(retained)
    return shaped.reshape(swish_in.shape)


def gelu_piece(gate_rows, up_rows):
    return jax.nn.gelu(gate_rows) * up_rows


def local(
    tokens,
    segments,
    decay,
    norm1_gain,
    w_query,
    w_key,
    w_value,
    w_swish,
    w_out,
    norm2_gain,
    w_up,
    w_gate,
    w_down,
    cotangent,
):
    full_query, full_key, full_value, full_swish, full_out = (
        lax.all_gather(w_query, "dp", axis=0, tiled=True),
        lax.all_gather(w_key, "dp", axis=0, tiled=True),
        lax.all_gather(w_value, "dp", axis=0, tiled=True),
        lax.all_gather(w_swish, "dp", axis=0, tiled=True),
        lax.all_gather(w_out, "dp", axis=1, tiled=True),
    )
    full_up, full_gate, full_down = (
        lax.all_gather(w_up, "dp", axis=0, tiled=True),
        lax.all_gather(w_gate, "dp", axis=0, tiled=True),
        lax.all_gather(w_down, "dp", axis=1, tiled=True),
    )
    bf16 = jnp.bfloat16
    heads_local = decay.shape[0]
    key_size = full_query.shape[1] // heads_local
    value_size = full_value.shape[1] // heads_local
    rows_local = tokens.astype(jnp.float32)
    normed_local = layer_norm(rows_local, norm1_gain).astype(bf16)
    normed = lax.all_gather(normed_local, "tensor", axis=0, tiled=True)
    length = normed.shape[0]
    query_rows = product(normed, full_query).astype(bf16).reshape(length, heads_local, key_size)
    key_rows = product(normed, full_key).astype(bf16).reshape(length, heads_local, key_size)
    values = product(normed, full_value).astype(bf16).reshape(length, heads_local, value_size)
    swish_in = product(normed, full_swish)
    position = jnp.arange(length, dtype=jnp.int32)
    offset = position[:, None] - position[None, :]
    allowed = (offset >= 0) & (segments[:, None] == segments[None, :])
    distance = jnp.maximum(offset, 0).astype(jnp.float32)
    decay_mask = jnp.where(allowed[None], jnp.exp(-decay[:, None, None] * distance[None]), 0.0)
    unmasked_scores = jnp.einsum(
        "pqk,aqk->qpa", query_rows, key_rows, preferred_element_type=jnp.float32
    )
    scores = (unmasked_scores * decay_mask).astype(bf16)
    retained = jnp.einsum("hnm,mhe->nhe", scores, values, preferred_element_type=jnp.float32)
    gated = gate_piece(swish_in, retained).astype(bf16)
    branch_local = lax.psum_scatter(
        product(gated, full_out), "tensor", scatter_dimension=0, tiled=True
    )
    middle = rows_local + branch_local
    normed_two_local = layer_norm(middle, norm2_gain).astype(bf16)
    normed_two = lax.all_gather(normed_two_local, "tensor", axis=0, tiled=True)
    up_rows = product(normed_two, full_up)
    gate_rows = product(normed_two, full_gate)
    hidden = gelu_piece(gate_rows, up_rows).astype(bf16)
    feed_local = lax.psum_scatter(
        product(hidden, full_down), "tensor", scatter_dimension=0, tiled=True
    )
    mixed = (middle + feed_local).astype(bf16)
    grad_rows = lax.all_gather(cotangent, "tensor", axis=0, tiled=True)
    grad_down = left_product(hidden, grad_rows)
    grad_hidden = right_product(grad_rows, full_down)
    gelu_value, gelu_pull = jax.vjp(gelu_piece, gate_rows, up_rows)
    grad_gate_rows, grad_up_rows = gelu_pull(grad_hidden)
    grad_gate_rows = grad_gate_rows.astype(bf16)
    grad_up_rows = grad_up_rows.astype(bf16)
    grad_up = left_product(normed_two, grad_up_rows)
    grad_gate = left_product(normed_two, grad_gate_rows)
    back_two = right_product(grad_up_rows, full_up) + right_product(grad_gate_rows, full_gate)
    back_two_local = lax.psum_scatter(back_two, "tensor", scatter_dimension=0, tiled=True)
    norm_two_value, norm_two_pull = jax.vjp(layer_norm, middle, norm2_gain)
    grad_mid_norm, grad_norm2_local = norm_two_pull(back_two_local)
    grad_middle = cotangent.astype(jnp.float32) + grad_mid_norm
    grad_branch = lax.all_gather(grad_middle.astype(bf16), "tensor", axis=0, tiled=True)
    grad_out = left_product(gated, grad_branch)
    grad_gated = right_product(grad_branch, full_out)
    gate_value, gate_pull = jax.vjp(gate_piece, swish_in, retained)
    grad_swish_in, grad_retained = gate_pull(grad_gated)
    grad_swish_in = grad_swish_in.astype(bf16)
    grad_retained = grad_retained.astype(bf16)
    grad_scores = jnp.einsum(
        "nhe,mhe->hnm", grad_retained, values, preferred_element_type=jnp.float32
    )
    grad_values = jnp.einsum(
        "hnm,nhe->mhe", scores, grad_retained, preferred_element_type=jnp.float32
    ).astype(bf16)
    grad_raw_scores = (grad_scores * decay_mask).astype(bf16)
    grad_queries = jnp.einsum(
        "gyo,ogl->ygl", grad_raw_scores, key_rows, preferred_element_type=jnp.float32
    ).astype(bf16)
    grad_keys = jnp.einsum(
        "axv,xaw->vaw", grad_raw_scores, query_rows, preferred_element_type=jnp.float32
    ).astype(bf16)
    grad_queries = grad_queries.reshape(length, heads_local * key_size)
    grad_keys = grad_keys.reshape(length, heads_local * key_size)
    grad_values = grad_values.reshape(length, heads_local * value_size)
    grad_query = left_product(normed, grad_queries)
    grad_key = left_product(normed, grad_keys)
    grad_value = left_product(normed, grad_values)
    grad_swish = left_product(normed, grad_swish_in)
    back_one = right_product(grad_queries, full_query) + right_product(grad_keys, full_key)
    back_one = (
        back_one + right_product(grad_values, full_value) + right_product(grad_swish_in, full_swish)
    )
    back_one_local = lax.psum_scatter(back_one, "tensor", scatter_dimension=0, tiled=True)
    first_norm_output, norm_one_pull = jax.vjp(layer_norm, rows_local, norm1_gain)
    grad_tok_norm, grad_norm1_local = norm_one_pull(back_one_local)
    grad_tokens = grad_middle + grad_tok_norm
    grad_norm1, grad_norm2 = lax.psum((grad_norm1_local, grad_norm2_local), ("dp", "tensor"))
    grad_query, grad_key, grad_value, grad_swish, grad_out, grad_up, grad_gate, grad_down = (
        lax.psum_scatter(grad_query, "dp", scatter_dimension=0, tiled=True),
        lax.psum_scatter(grad_key, "dp", scatter_dimension=0, tiled=True),
        lax.psum_scatter(grad_value, "dp", scatter_dimension=0, tiled=True),
        lax.psum_scatter(grad_swish, "dp", scatter_dimension=0, tiled=True),
        lax.psum_scatter(grad_out, "dp", scatter_dimension=1, tiled=True),
        lax.psum_scatter(grad_up, "dp", scatter_dimension=0, tiled=True),
        lax.psum_scatter(grad_gate, "dp", scatter_dimension=0, tiled=True),
        lax.psum_scatter(grad_down, "dp", scatter_dimension=1, tiled=True),
    )
    return (
        mixed,
        grad_tokens,
        grad_norm1,
        grad_query,
        grad_key,
        grad_value,
        grad_swish,
        grad_out,
        grad_norm2,
        grad_up,
        grad_gate,
        grad_down,
    )


def solution(mesh):
    placed = (
        P(("dp", "tensor"), None),
        P("dp"),
        P("tensor"),
        P(),
        P("dp", "tensor"),
        P("dp", "tensor"),
        P("dp", "tensor"),
        P("dp", "tensor"),
        P("tensor", "dp"),
        P(),
        P("dp", "tensor"),
        P("dp", "tensor"),
        P("tensor", "dp"),
        P(("dp", "tensor"), None),
    )
    return jax.shard_map(
        local,
        mesh=mesh,
        in_specs=placed,
        out_specs=(
            P(("dp", "tensor"), None),
            P(("dp", "tensor"), None),
            P(),
            P("dp", "tensor"),
            P("dp", "tensor"),
            P("dp", "tensor"),
            P("dp", "tensor"),
            P("tensor", "dp"),
            P(),
            P("dp", "tensor"),
            P("dp", "tensor"),
            P("tensor", "dp"),
        ),
        check_vma=False,
    )
```

profile of v0, /device:TPU:0, one launch (start us, length us, event | category | flops | bytes accessed | tf_op | source)
XLA Modules:
  0.0 3599.1 jit_solution(15614466216740350265)
XLA Ops:
  16.9 8.4 all-gather.13.cloned.1.call-done
  25.3 80.1 %all-gather.21.cloned.1.call-done = bf16[2048,1024]{1,0:T(8,128)(2,1)} async-done(((bf16[128,1024]{1,0:T(8,128)(2,1)}), bf16[2048,1024]{1,0:T(8,128)(2,1)}) %all-gather.21.cloned.1.call-update) | async-done | bytes 4194320 | tf_op jit(solution)/shard_map/all_gather | solution.py:62
  105.3 4.5 convolution_convert_fusion.4
  110.2 72.7 %all-gather.19.cloned.1.call-done = bf16[2048,1024]{1,0:T(8,128)(2,1)} async-done(((bf16[128,1024]{1,0:T(8,128)(2,1)}), bf16[2048,1024]{1,0:T(8,128)(2,1)}) %all-gather.19.cloned.1.call-update) | async-done | bytes 4194320 | tf_op jit(solution)/shard_map/all_gather | solution.py:61
  182.8 4.9 convolution_convert_fusion.5
  192.5 104.5 %all-gather.15.cloned.1.call-done = bf16[2048,2048]{1,0:T(8,128)(2,1)} async-done(((bf16[128,2048]{1,0:T(8,128)(2,1)}), bf16[2048,2048]{1,0:T(8,128)(2,1)}) %all-gather.15.cloned.1.call-update) | async-done | bytes 8388624 | tf_op jit(solution)/shard_map/all_gather | solution.py:64
  296.9 9.0 fusion.10
  305.9 3.6 copy.40
  309.5 101.1 %all-gather.17.cloned.1.call-done = bf16[2048,2048]{1,0:T(8,128)(2,1)} async-done(((bf16[128,2048]{1,0:T(8,128)(2,1)}), bf16[2048,2048]{1,0:T(8,128)(2,1)}) %all-gather.17.cloned.1.call-update) | async-done | bytes 8388624 | tf_op jit(solution)/shard_map/all_gather | solution.py:63
  410.6 6.9 convolution_convert_fusion
  422.5 131.2 %all-gather.23.cloned.1.call-done = bf16[2048,2048]{1,0:T(8,128)(2,1)} async-done(((bf16[2048,128]{1,0:T(8,128)(2,1)}), bf16[2048,2048]{1,0:T(8,128)(2,1)}) %all-gather.23.cloned.1.call-update) | async-done | bytes 8388624 | tf_op jit(solution)/shard_map/all_gather | solution.py:65
  553.7 9.0 fusion.36
  564.8 7.1 reduce-scatter.13.cloned.1.call-done
  577.1 7.4 all-gather.33.cloned.1.call-done
  584.6 146.6 %all-gather.31.cloned.1.call-done = bf16[2048,2048]{1,0:T(8,128)(2,1)} async-done(((bf16[2048,128]{1,0:T(8,128)(2,1)}), bf16[2048,2048]{1,0:T(8,128)(2,1)}) %all-gather.31.cloned.1.call-update) | async-done | bytes 8388624 | tf_op jit(solution)/shard_map/all_gather | solution.py:70
  731.2 9.0 fusion.39
  740.2 105.0 %all-gather.29.cloned.1.call-done = bf16[2048,2048]{1,0:T(8,128)(2,1)} async-done(((bf16[128,2048]{1,0:T(8,128)(2,1)}), bf16[2048,2048]{1,0:T(8,128)(2,1)}) %all-gather.29.cloned.1.call-update) | async-done | bytes 8388624 | tf_op jit(solution)/shard_map/all_gather | solution.py:68
  845.3 10.2 all-gather.25.cloned.1.call-done
  855.5 9.0 fusion.37
  864.4 108.1 %all-gather.27.cloned.1.call-done = bf16[2048,2048]{1,0:T(8,128)(2,1)} async-done(((bf16[128,2048]{1,0:T(8,128)(2,1)}), bf16[2048,2048]{1,0:T(8,128)(2,1)}) %all-gather.27.cloned.1.call-update) | async-done | bytes 8388624 | tf_op jit(solution)/shard_map/all_gather | solution.py:69
  972.5 12.6 fusion.6
  985.1 5.7 fusion.40
  990.8 6.3 convolution_add_fusion
  997.2 9.0 fusion.38
  1008.8 11.8 reduce-scatter.15.cloned.1.call-done
  1020.6 3.8 fusion.34
  1027.0 10.9 all-gather.35.cloned.1.call-done
  1037.9 9.6 multiply_reduce_fusion
  1059.7 4.3 fusion.9
  1064.1 9.1 fusion.43
  1080.3 7.5 add_add_fusion.1
  1089.1 5.6 fusion.45
  1094.9 5.7 fusion.44
  1102.0 9.8 fusion.50
  1111.9 9.7 fusion.49
  1123.0 9.6 fusion.51
  1134.0 9.5 fusion.48
  1145.0 8.3 fusion.47
  1154.6 8.3 fusion.46
  1166.8 44.0 %all-reduce = (f32[2048]{0:T(1024)}, f32[2048]{0:T(1024)}) all-reduce(f32[2048]{0:T(1024)S(1)} %get-tuple-element.14, f32[2048]{0:T(1024)S(1)} %get-tuple-element.12), channel_id=1, replica_groups=mesh['dp'=16,'tensor'=2] {'dp','tensor'}, use_global_device_ids=true, to_apply=%region_17.18 | all-reduce | flops 4096 | bytes 32768 | tf_op jit(solution)/shard_map/psum | solution.py:157
  1214.1 69.0 %reduce-scatter.23.cloned.1.call-done = f32[128,1024]{1,0:T(8,128)} async-done(((f32[2048,1024]{1,0:T(8,128)}), f32[128,1024]{1,0:T(8,128)}) %reduce-scatter.23.cloned.1.call-update) | async-done | bytes 524304 | tf_op jit(solution)/shard_map/reduce_scatter | solution.py:160
  1283.1 183.0 %reduce-scatter.21.cloned.1.call-done = f32[128,1024]{1,0:T(8,128)} async-done(((f32[2048,1024]{1,0:T(8,128)}), f32[128,1024]{1,0:T(8,128)}) %reduce-scatter.21.cloned.1.call-update) | async-done | bytes 524304 | tf_op jit(solution)/shard_map/reduce_scatter | solution.py:159
  1466.1 351.7 %reduce-scatter.33.cloned.1.call-done = f32[128,2048]{1,0:T(8,128)} async-done(((f32[2048,2048]{1,0:T(8,128)}), f32[128,2048]{1,0:T(8,128)}) %reduce-scatter.33.cloned.1.call-update) | async-done | bytes 1048592 | tf_op jit(solution)/shard_map/reduce_scatter | solution.py:165
  1817.8 354.7 %reduce-scatter.31.cloned.1.call-done = f32[128,2048]{1,0:T(8,128)} async-done(((f32[2048,2048]{1,0:T(8,128)}), f32[128,2048]{1,0:T(8,128)}) %reduce-scatter.31.cloned.1.call-update) | async-done | bytes 1048592 | tf_op jit(solution)/shard_map/reduce_scatter | solution.py:164
  2172.6 354.9 %reduce-scatter.35.cloned.1.call-done = f32[2048,128]{1,0:T(8,128)} async-done(((f32[2048,2048]{1,0:T(8,128)}), f32[2048,128]{1,0:T(8,128)}) %reduce-scatter.35.cloned.1.call-update) | async-done | bytes 1048592 | tf_op jit(solution)/shard_map/reduce_scatter | solution.py:166
  2527.5 354.9 %reduce-scatter.29.cloned.1.call-done = f32[2048,128]{1,0:T(8,128)} async-done(((f32[2048,2048]{1,0:T(8,128)}), f32[2048,128]{1,0:T(8,128)}) %reduce-scatter.29.cloned.1.call-update) | async-done | bytes 1048592 | tf_op jit(solution)/shard_map/reduce_scatter | solution.py:163
  2882.4 354.9 %reduce-scatter.27.cloned.1.call-done = f32[128,2048]{1,0:T(8,128)} async-done(((f32[2048,2048]{1,0:T(8,128)}), f32[128,2048]{1,0:T(8,128)}) %reduce-scatter.27.cloned.1.call-update) | async-done | bytes 1048592 | tf_op jit(solution)/shard_map/reduce_scatter | solution.py:162
  3237.3 354.8 %reduce-scatter.25.cloned.1.call-done = f32[128,2048]{1,0:T(8,128)} async-done(((f32[2048,2048]{1,0:T(8,128)}), f32[128,2048]{1,0:T(8,128)}) %reduce-scatter.25.cloned.1.call-update) | async-done | bytes 1048592 | tf_op jit(solution)/shard_map/reduce_scatter | solution.py:161
  (189 shorter events, 66.9 us)
Async XLA Ops:
  7.2 4.1 copy-start.5
  7.2 4.1 copy-start.32
  7.2 18.1 all-gather.13.cloned.1.call-start
  12.6 3.3 copy-start.46
  12.6 4.2 copy-start.41
  12.6 92.7 %all-gather.21.cloned.1.call-start = ((), (), s32[]{:S(2)}) async-start(), calls=%async_computation.16 | async-start | bytes 4456448 | tf_op jit(solution)/shard_map/all_gather | solution.py:62
  13.4 169.5 %all-gather.19.cloned.1.call-start = ((), (), s32[]{:S(2)}) async-start(), calls=%async_computation.15 | async-start | bytes 4456448 | tf_op jit(solution)/shard_map/all_gather | solution.py:61
  14.1 282.8 %all-gather.15.cloned.1.call-start = ((), (), s32[]{:S(2)}) async-start(), calls=%async_computation.13 | async-start | bytes 8912896 | tf_op jit(solution)/shard_map/all_gather | solution.py:64
  14.7 395.9 %all-gather.17.cloned.1.call-start = ((), (), s32[]{:S(2)}) async-start(), calls=%async_computation.14 | async-start | bytes 8912896 | tf_op jit(solution)/shard_map/all_gather | solution.py:63
  15.3 538.5 %all-gather.23.cloned.1.call-start = ((), (), s32[]{:S(2)}) async-start(), calls=%async_computation.17 | async-start | bytes 8912896 | tf_op jit(solution)/shard_map/all_gather | solution.py:65
  15.9 556.1 %reduce-scatter.13.cloned.1.call-start = ((), (), s32[]{:S(2)}) async-start(), calls=%async_computation.18 | async-start | bytes 4718592 | tf_op jit(solution)/shard_map/reduce_scatter | solution.py:95
  109.8 73.0 %copy-start.2 = (bf16[384,2048]{1,0:T(8,128)(2,1)S(1)}, bf16[384,2048]{1,0:T(8,128)(2,1)}, u32[]{:S(2)}) copy-start(bf16[384,2048]{1,0:T(8,128)(2,1)} %all-gather.13.cloned.1.call-done) | copy-start | bytes 4718596
  110.2 79.0 %copy-start.22 = (bf16[384,1024]{0,1:T(8,128)(2,1)}, bf16[384,1024]{0,1:T(8,128)(2,1)S(1)}, u32[]{:S(2)}) copy-start(bf16[384,1024]{0,1:T(8,128)(2,1)S(1)} %copy.42) | copy-start | bytes 2359300
  189.2 3.3 copy-start.24
  410.6 6.9 copy-start.18
  562.7 21.9 all-gather.33.cloned.1.call-start
  563.5 167.7 %all-gather.31.cloned.1.call-start = ((), (), s32[]{:S(2)}) async-start(), calls=%async_computation.22 | async-start | bytes 8912896 | tf_op jit(solution)/shard_map/all_gather | solution.py:70
  564.2 281.1 %all-gather.29.cloned.1.call-start = ((), (), s32[]{:S(2)}) async-start(), calls=%async_computation.21 | async-start | bytes 8912896 | tf_op jit(solution)/shard_map/all_gather | solution.py:68
  564.8 290.7 %all-gather.25.cloned.1.call-start = ((), (), s32[]{:S(2)}) async-start(), calls=%async_computation.19 | async-start | bytes 2359296 | tf_op jit(solution)/shard_map/all_gather | solution.py:100
  576.3 396.3 %all-gather.27.cloned.1.call-start = ((), (), s32[]{:S(2)}) async-start(), calls=%async_computation.20 | async-start | bytes 8912896 | tf_op jit(solution)/shard_map/all_gather | solution.py:69
  576.8 429.6 %reduce-scatter.17.cloned.1.call-start = ((), (), s32[]{:S(2)}) async-start(), calls=%async_computation.25 | async-start | bytes 4718592 | tf_op jit(solution)/shard_map/reduce_scatter | solution.py:118
  972.5 12.6 copy-start.42
  985.1 5.7 copy-start.27
  985.1 5.7 copy-start.28
  985.1 5.7 copy-start.43
  997.2 23.5 reduce-scatter.15.cloned.1.call-start
  1006.2 31.7 all-gather.35.cloned.1.call-start
  1020.6 5.0 copy-start.12
  1026.8 136.3 %reduce-scatter.19.cloned.1.call-start = ((), (), s32[]{:S(2)}) async-start(), calls=%async_computation.27 | async-start | bytes 4718592 | tf_op jit(solution)/shard_map/reduce_scatter | solution.py:153
  1037.9 9.6 copy-start.1
  1051.6 3.9 copy-start.23
  1059.7 4.3 copy-start.14
  1064.0 16.2 copy-start.16
  1064.0 9.1 copy-start.20
  1064.0 9.1 copy-start.45
  1073.1 3.5 copy-start.21
  1073.1 3.5 copy-start.44
  1073.1 7.1 slice-start
  1076.7 3.6 slice-start.1
  1087.8 195.4 %reduce-scatter.23.cloned.1.call-start = ((), (), s32[]{:S(2)}) async-start(), calls=%async_computation.29 | async-start | bytes 8912896 | tf_op jit(solution)/shard_map/reduce_scatter | solution.py:160
  1094.8 371.3 %reduce-scatter.21.cloned.1.call-start = ((), (), s32[]{:S(2)}) async-start(), calls=%async_computation.28 | async-start | bytes 8912896 | tf_op jit(solution)/shard_map/reduce_scatter | solution.py:159
  1100.6 717.2 %reduce-scatter.33.cloned.1.call-start = ((), (), s32[]{:S(2)}) async-start(), calls=%async_computation.34 | async-start | bytes 17825792 | tf_op jit(solution)/shard_map/reduce_scatter | solution.py:165
  1111.8 1060.8 %reduce-scatter.31.cloned.1.call-start = ((), (), s32[]{:S(2)}) async-start(), calls=%async_computation.33 | async-start | bytes 17825792 | tf_op jit(solution)/shard_map/reduce_scatter | solution.py:164
  1121.6 1405.9 %reduce-scatter.35.cloned.1.call-start = ((), (), s32[]{:S(2)}) async-start(), calls=%async_computation.35 | async-start | bytes 17825792 | tf_op jit(solution)/shard_map/reduce_scatter | solution.py:166
  1132.6 1749.8 %reduce-scatter.29.cloned.1.call-start = ((), (), s32[]{:S(2)}) async-start(), calls=%async_computation.32 | async-start | bytes 17825792 | tf_op jit(solution)/shard_map/reduce_scatter | solution.py:163
  1143.6 2093.7 %reduce-scatter.27.cloned.1.call-start = ((), (), s32[]{:S(2)}) async-start(), calls=%async_computation.31 | async-start | bytes 17825792 | tf_op jit(solution)/shard_map/reduce_scatter | solution.py:162
  1153.3 2438.8 %reduce-scatter.25.cloned.1.call-start = ((), (), s32[]{:S(2)}) async-start(), calls=%async_computation.30 | async-start | bytes 17825792 | tf_op jit(solution)/shard_map/reduce_scatter | solution.py:161
  1166.1 44.8 %copy-start.13 = (bf16[192,2048]{1,0:T(8,128)(2,1)S(1)}, bf16[192,2048]{1,0:T(8,128)(2,1)}, u32[]{:S(2)}) copy-start(bf16[192,2048]{1,0:T(8,128)(2,1)} %param.27) | copy-start | bytes 2359300
  (25 other events, 42.4 us)
Sparse Core Ops, SparseCore 0:
  12.8 12.4 all-gather.12
  28.1 77.2 all-gather.20
  108.1 74.6 all-gather.18
  185.5 111.4 all-gather.14
  299.5 111.0 all-gather.16
  413.2 140.5 all-gather.22
  562.8 9.0 reduce-scatter.12
  573.6 10.9 all-gather.32
  587.7 143.5 all-gather.30
  734.2 111.0 all-gather.28
  847.5 7.9 all-gather.24
  858.5 113.9 all-gather.26
  997.3 9.0 reduce-scatter.16
  1008.5 12.0 reduce-scatter.14
  1026.9 10.9 all-gather.34
  1087.9 12.0 reduce-scatter.18
  1102.7 180.3 reduce-scatter.22
  1285.9 180.2 reduce-scatter.20
  1469.0 348.7 reduce-scatter.32
  1820.5 351.9 reduce-scatter.30
  2175.5 351.9 reduce-scatter.34
  2530.3 351.9 reduce-scatter.28
  2885.3 351.9 reduce-scatter.26
  3240.0 351.9 reduce-scatter.24
where the time goes:
time: 3610 us; the launch traced here: 3600 us
  waiting for transfers between devices  3290 us (91%)
  matrix products  197 us (5%)
  blocking collectives  44 us (1%)
    reduce_scatter x1, waiting for transfers between devices, local(): lax.psum_scatter(grad_swish, 'dp', scatter_dimension=0, tiled=True)  355 us
    reduce_scatter x1, waiting for transfers between devices, local(): lax.psum_scatter(grad_down, 'dp', scatter_dimension=1, tiled=True)  355 us
    reduce_scatter x1, waiting for transfers between devices, local(): lax.psum_scatter(grad_out, 'dp', scatter_dimension=1, tiled=True)  355 us
    reduce_scatter x1, waiting for transfers between devices, local(): lax.psum_scatter(grad_value, 'dp', scatter_dimension=0, tiled=True)  355 us
    reduce_scatter x1, waiting for transfers between devices, local(): lax.psum_scatter(grad_up, 'dp', scatter_dimension=0, tiled=True)  355 us
    reduce_scatter x1, waiting for transfers between devices, local(): lax.psum_scatter(grad_gate, 'dp', scatter_dimension=0, tiled=True)  352 us
    reduce_scatter x1, waiting for transfers between devices, local(): lax.psum_scatter(grad_query, 'dp', scatter_dimension=0, tiled=True)  183 us
    all_gather x1, waiting for transfers between devices, local(): lax.all_gather(w_down, 'dp', axis=1, tiled=True)  147 us
  transfers between devices with their start and end apart: 24, of which 23 were waited for; matrix products, arithmetic and copies ran while one was open for 4% of the time, Pallas kernels for 0%

commit v1 on v0

v1 whole, which is shorter than its diff:
```python
import jax
import jax.numpy as jnp
from jax import lax
from jax.sharding import Mesh, PartitionSpec as P

epsilon = 1e-05
bf16 = jnp.bfloat16
f32 = jnp.float32
SPREAD = ("zh", "zl", "y", "x")
GROUP = ("zl", "x")


def normalize(values):
    centred = values - jnp.mean(values, axis=-1, keepdims=True)
    variance = jnp.mean(centred * centred, axis=-1, keepdims=True)
    return centred * lax.rsqrt(variance + epsilon)


def layer_norm(rows, gain):
    return normalize(rows) * gain


def product(left, right):
    return jnp.dot(left, right, preferred_element_type=f32)


def left_product(left, right):
    return lax.dot_general(left, right, (((0,), (0,)), ((), ())), preferred_element_type=f32)


def right_product(left, right):
    return lax.dot_general(left, right, (((1,), (1,)), ((), ())), preferred_element_type=f32)


def gate_piece(swish_in, retained):
    shaped = jax.nn.silu(swish_in).reshape(retained.shape) * normalize(retained)
    return shaped.reshape(swish_in.shape)


def gelu_piece(gate_rows, up_rows):
    return jax.nn.gelu(gate_rows) * up_rows


def swap(a, axis):
    return lax.ppermute(a, axis, [(0, 1), (1, 0)])


def both(own, axis, dim):
    if lax.axis_size(axis) != 2:
        return lax.all_gather(own, axis, axis=dim)
    return ordered(own, swap(own, axis), axis, dim)


def ordered(own, other, axis, dim):
    first = lax.axis_index(axis) == 0
    return jnp.stack([jnp.where(first, own, other), jnp.where(first, other, own)], dim)


def gather_weight(piece):
    piece = piece.reshape((2, 2) + piece.shape[1:])
    if lax.axis_size("zh") == 2:
        far = swap(piece, "zh")
        near_y = swap(piece, "y")
        far_y = swap(far, "y")
        own = ordered(piece, near_y, "y", 1)
        other = ordered(far, far_y, "y", 1)
        whole = ordered(own, other, "zh", 0)
    else:
        whole = both(lax.all_gather(piece, "zh"), "y", 2)
    return whole


def gather_rows_split(w):
    rows, cols = w.shape
    n = cols // 4
    parts = w.reshape(rows, 4, n).transpose(1, 0, 2)
    piece = lax.all_to_all(parts, GROUP, 0, 0, tiled=True)
    return gather_weight(piece).reshape(-1, n)


def gather_columns_split(w):
    rows, cols = w.shape
    n = rows // 4
    piece = lax.all_to_all(w.reshape(4, n, cols), GROUP, 0, 0, tiled=True)
    whole = gather_weight(piece)
    return whole.transpose(4, 0, 1, 2, 3, 5).reshape(n, -1)


def take(a, index, dim):
    return lax.dynamic_index_in_dim(a, index, dim, keepdims=False)


def scatter_weight(g):
    y = lax.axis_index("y")
    got = swap(take(g, 1 - y, 2), "y")
    g = (take(g, y, 2).astype(f32) + got.astype(f32)).astype(bf16)
    if lax.axis_size("zh") == 2:
        zh = lax.axis_index("zh")
        got = swap(take(g, 1 - zh, 0), "zh")
        g = (take(g, zh, 0).astype(f32) + got.astype(f32)).astype(bf16)
    else:
        g = lax.psum_scatter(g, "zh", scatter_dimension=0)
    g = g.reshape((4,) + g.shape[2:])
    return lax.all_to_all(g, GROUP, 0, 0, tiled=True)


def mesh_sizes():
    return tuple(lax.axis_size(a) for a in SPREAD)


def scatter_rows_split(g):
    n = g.shape[1]
    parts = scatter_weight(g.astype(bf16).reshape(mesh_sizes() + (-1, n)))
    return parts.transpose(1, 0, 2).reshape(-1, 4 * n).astype(f32)


def scatter_columns_split(g):
    n = g.shape[0]
    g = g.astype(bf16).reshape((n,) + mesh_sizes() + (-1,)).transpose(1, 2, 3, 4, 0, 5)
    parts = scatter_weight(g)
    return parts.reshape(4 * n, -1).astype(f32)


def gather_tokens(a):
    half = a.shape[1] // 2
    ax = swap(a, "x")
    az = swap(a, "zl")
    ad = jnp.concatenate([swap(az[:, :half], "x"), swap(ax[:, half:], "zl")], 1)
    pieces = [a, ax, az, ad]
    return jnp.stack([jnp.stack([p, swap(p, "tensor")]) for p in pieces])


def scatter_tokens(p):
    half = p.shape[3] // 2
    p = p.astype(bf16)
    s = []
    for r in (3, 2, 1, 0):
        s.append(p[r, 0].astype(f32) + swap(p[r, 1], "tensor").astype(f32))
    diag, zmate, xmate, own = s
    diag = diag.astype(bf16)
    through_x = swap(diag[:, :half], "x").astype(f32)
    through_z = swap(diag[:, half:], "zl").astype(f32)
    zmate = jnp.concatenate([zmate[:, :half] + through_x, zmate[:, half:]], 1).astype(bf16)
    xmate = jnp.concatenate([xmate[:, :half], xmate[:, half:] + through_z], 1).astype(bf16)
    return own + swap(xmate, "x").astype(f32) + swap(zmate, "zl").astype(f32)


def sum_everywhere(a):
    for axis in ("tensor",) + SPREAD:
        if lax.axis_size(axis) == 2:
            a = a + swap(a, axis)
        else:
            a = lax.psum(a, axis)
    return a


def local(
    tokens,
    segments,
    decay,
    norm1_gain,
    w_query,
    w_key,
    w_value,
    w_swish,
    w_out,
    norm2_gain,
    w_up,
    w_gate,
    w_down,
    cotangent,
):
    quarter = 2 * lax.axis_index("zl") + lax.axis_index("x")
    core = lax.axis_index("tensor")
    length = segments.shape[0]
    rows_each = tokens.shape[0]
    key_size = w_query.shape[1] // 4
    value_size = w_value.shape[1] // 4
    rate = take(decay, quarter, 0)

    rows_q, rows_v = w_query.shape[0], w_value.shape[0]
    w_qk = jnp.concatenate(
        [w_query.reshape(rows_q, 4, key_size), w_key.reshape(rows_q, 4, key_size)], 2
    ).reshape(rows_q, 8 * key_size)
    full_qk = gather_rows_split(w_qk)
    full_value = gather_rows_split(w_value)
    full_swish = gather_rows_split(w_swish)
    full_out = gather_columns_split(w_out)
    full_up = gather_rows_split(w_up)
    full_gate = gather_rows_split(w_gate)
    full_down = gather_columns_split(w_down)

    seg_x = jnp.stack([segments, swap(segments, "x")])
    segs = jnp.concatenate([seg_x, swap(seg_x, "zl")])
    segs = jnp.where(core == 0, segs, jnp.roll(segs, length // 2, 1))
    position = (jnp.arange(length, dtype=jnp.int32) + core * rows_each) % length

    rows_local = tokens.astype(f32)
    normed_local = layer_norm(rows_local, norm1_gain).astype(bf16)
    model = normed_local.shape[1]
    normed = gather_tokens(normed_local).reshape(-1, model)
    count = normed.shape[0]

    qk = product(normed, full_qk).astype(bf16)
    query_rows = qk[:, :key_size].reshape(4, length, key_size)
    key_rows = qk[:, key_size:].reshape(4, length, key_size)
    values = product(normed, full_value).astype(bf16).reshape(4, length, value_size)
    swish_in = product(normed, full_swish).reshape(4, length, value_size)
    offset = position[:, None] - position[None, :]
    allowed = (offset >= 0)[None] & (segs[:, :, None] == segs[:, None, :])
    distance = jnp.maximum(offset, 0).astype(f32)
    decay_mask = jnp.where(allowed, jnp.exp(-rate * distance)[None], 0.0)
    unmasked_scores = jnp.einsum("snd,smd->snm", query_rows, key_rows, preferred_element_type=f32)
    scores = (unmasked_scores * decay_mask).astype(bf16)
    retained = jnp.einsum("snm,sme->sne", scores, values, preferred_element_type=f32)
    gated = gate_piece(swish_in, retained).astype(bf16).reshape(count, value_size)
    branch = product(gated, full_out).reshape(4, 2, rows_each, model)
    middle = rows_local + scatter_tokens(branch)
    normed_two_local = layer_norm(middle, norm2_gain).astype(bf16)
    normed_two = gather_tokens(normed_two_local).reshape(count, model)
    grad_rows = gather_tokens(cotangent).reshape(count, model)
    up_rows = product(normed_two, full_up)
    gate_rows = product(normed_two, full_gate)
    grad_hidden = right_product(grad_rows, full_down)
    hidden = gelu_piece(gate_rows, up_rows).astype(bf16)
    _, gelu_pull = jax.vjp(gelu_piece, gate_rows, up_rows)
    grad_gate_rows, grad_up_rows = gelu_pull(grad_hidden)
    grad_gate_rows = grad_gate_rows.astype(bf16)
    grad_up_rows = grad_up_rows.astype(bf16)
    back_two = right_product(grad_up_rows, full_up) + right_product(grad_gate_rows, full_gate)
    back_two_local = scatter_tokens(back_two.reshape(4, 2, rows_each, model))
    _, norm_two_pull = jax.vjp(layer_norm, middle, norm2_gain)
    grad_mid_norm, grad_norm2_local = norm_two_pull(back_two_local)
    grad_middle = cotangent.astype(f32) + grad_mid_norm
    grad_branch = gather_tokens(grad_middle.astype(bf16)).reshape(count, model)

    feed = product(hidden, full_down).reshape(4, 2, rows_each, model)
    mixed = (middle + scatter_tokens(feed)).astype(bf16)
    grad_down = scatter_columns_split(left_product(hidden, grad_rows))
    grad_up = scatter_rows_split(left_product(normed_two, grad_up_rows))
    grad_gate = scatter_rows_split(left_product(normed_two, grad_gate_rows))

    grad_gated = right_product(grad_branch, full_out).reshape(4, length, value_size)
    _, gate_pull = jax.vjp(gate_piece, swish_in, retained)
    grad_swish_in, grad_retained = gate_pull(grad_gated)
    grad_swish_in = grad_swish_in.astype(bf16).reshape(count, value_size)
    grad_retained = grad_retained.astype(bf16)
    grad_scores = jnp.einsum("sne,sme->snm", grad_retained, values, preferred_element_type=f32)
    grad_values = jnp.einsum("snm,sne->sme", scores, grad_retained, preferred_element_type=f32)
    grad_values = grad_values.astype(bf16).reshape(count, value_size)
    grad_raw = (grad_scores * decay_mask).astype(bf16)
    grad_queries = jnp.einsum("snm,smd->snd", grad_raw, key_rows, preferred_element_type=f32)
    grad_keys = jnp.einsum("snm,snd->smd", grad_raw, query_rows, preferred_element_type=f32)
    grad_qk = jnp.concatenate([grad_queries, grad_keys], 2).astype(bf16)
    grad_qk = grad_qk.reshape(count, 2 * key_size)
    back_one = right_product(grad_qk, full_qk)
    back_one = back_one + right_product(grad_values, full_value)
    back_one = back_one + right_product(grad_swish_in, full_swish)
    back_one_local = scatter_tokens(back_one.reshape(4, 2, rows_each, model))

    grad_out = scatter_columns_split(left_product(gated, grad_branch))
    grad_swish = scatter_rows_split(left_product(normed, grad_swish_in))
    grad_value = scatter_rows_split(left_product(normed, grad_values))
    grad_qk = scatter_rows_split(left_product(normed, grad_qk))
    grad_qk = grad_qk.reshape(rows_q, 4, 2, key_size)
    grad_query = grad_qk[:, :, 0].reshape(rows_q, 4 * key_size)
    grad_key = grad_qk[:, :, 1].reshape(rows_q, 4 * key_size)

    _, norm_one_pull = jax.vjp(layer_norm, rows_local, norm1_gain)
    grad_tok_norm, grad_norm1_local = norm_one_pull(back_one_local)
    grad_tokens = grad_middle + grad_tok_norm
    grad_norm1 = sum_everywhere(grad_norm1_local)
    grad_norm2 = sum_everywhere(grad_norm2_local)
    return (
        mixed,
        grad_tokens,
        grad_norm1,
        grad_query,
        grad_key,
        grad_value,
        grad_swish,
        grad_out,
        grad_norm2,
        grad_up,
        grad_gate,
        grad_down,
    )


def solution(mesh):
    dp, tensor = mesh.shape["dp"], mesh.shape["tensor"]
    grid = Mesh(mesh.devices.reshape(dp // 8, 2, 2, 2, tensor), SPREAD + ("tensor",))
    rows = P(SPREAD + ("tensor",), None)
    rows_split = P(SPREAD, "tensor")
    columns_split = P("tensor", SPREAD)
    return jax.shard_map(
        local,
        mesh=grid,
        in_specs=(
            rows,
            P(SPREAD),
            P("tensor"),
            P(),
            rows_split,
            rows_split,
            rows_split,
            rows_split,
            columns_split,
            P(),
            rows_split,
            rows_split,
            columns_split,
            rows,
        ),
        out_specs=(
            rows,
            rows,
            P(),
            rows_split,
            rows_split,
            rows_split,
            rows_split,
            columns_split,
            P(),
            rows_split,
            rows_split,
            columns_split,
        ),
        check_vma=False,
    )
```

time: 3610 us -> 956 us (0.26)
  waiting for transfers between devices: 3290 us -> 413 us
  starting transfers between devices: 1.97 us -> 158 us
  other arithmetic: 30.6 us -> 140 us
  local copies, waits for them, and re-layouts: 21.7 us -> 107 us
  matrix products: 197 us -> 125 us
  blocking collectives: 44 us -> 0 us
    reduce_scatter x12 -> x0, waiting for transfers between devices: 2400 us -> none  [the longest x1 355 us: local(): lax.psum_scatter(grad_swish, 'dp', scatter_dimension=0, tiled=True)]
    all_gather x12 -> x0, waiting for transfers between devices: 886 us -> none  [the longest x1 147 us: local(): lax.all_gather(w_down, 'dp', axis=1, tiled=True)]
    ppermute x0 -> x111, waiting for transfers between devices: none -> 361 us  [swap(): return lax.ppermute(a, axis, [(0, 1), (1, 0)])]
    ppermute x0 -> x111, starting transfers between devices: none -> 99.7 us  [swap(): return lax.ppermute(a, axis, [(0, 1), (1, 0)])]
    all_to_all x0 -> x14, starting transfers between devices: none -> 58.7 us  [the longest x7 29.5 us: scatter_weight(): return lax.all_to_all(g, GROUP, 0, 0, tiled=True)]
    another operation x0 -> x50, other arithmetic: none -> 54.1 us  [the longest x22 29.9 us: gather_tokens(): return jnp.stack([jnp.stack([p, swap(p, 'tensor')]) for p in pieces])]
    all_to_all x0 -> x14, waiting for transfers between devices: none -> 51.6 us  [the longest x7 29.8 us: scatter_weight(): return lax.all_to_all(g, GROUP, 0, 0, tiled=True)]
    psum x1 -> x0, blocking collectives: 44 us -> none  [local(): lax.psum((grad_norm1_local, grad_norm2_local), ('dp', 'tensor'))]
  transfers between devices with their start and end apart: 24 -> 125, of which waited for: 23 -> 46; matrix products, arithmetic and copies ran while one was open for 4% -> 33% of each run, Pallas kernels for 0% -> 0%
where the time goes in v1:
time: 956 us; the launch traced here: 948 us
  waiting for transfers between devices  413 us (43%)
  starting transfers between devices  158 us (17%)
  other arithmetic  140 us (15%)
  matrix products  125 us (13%)
  local copies, waits for them, and re-layouts  107 us (11%)
    ppermute x111, waiting for transfers between devices, swap(): return lax.ppermute(a, axis, [(0, 1), (1, 0)])  361 us
    ppermute x111, starting transfers between devices, swap(): return lax.ppermute(a, axis, [(0, 1), (1, 0)])  99.7 us
    dot_general x7, matrix products, right_product(): lax.dot_general(left, right, (((1,), (1,)), ((), ())), preferred_element_...  47.3 us
    dot_general x7, matrix products, left_product(): lax.dot_general(left, right, (((0,), (0,)), ((), ())), preferred_element_...  39.5 us
    dot_general x7, matrix products, product(): return jnp.dot(left, right, preferred_element_type=f32)  31 us
    unnamed x248, local copies, waits for them, and re-layouts  31 us
    another operation x22, other arithmetic, gather_tokens(): return jnp.stack([jnp.stack([p, swap(p, 'tensor')]) for p in pieces])  29.9 us
    all_to_all x7, waiting for transfers between devices, scatter_weight(): return lax.all_to_all(g, GROUP, 0, 0, tiled=True)  29.8 us
  transfers between devices with their start and end apart: 125, of which 46 were waited for; matrix products, arithmetic and copies ran while one was open for 33% of the time, Pallas kernels for 0%

profile of v1, /device:TPU:0, one launch (start us, length us, event | category | flops | bytes accessed | tf_op | source)
XLA Modules:
  0.0 947.6 jit_solution(18182223509353142866)
XLA Ops:
  2.6 5.4 all-to-all-start.1
  8.8 7.7 all-to-all-done.1
  21.7 7.3 all-to-all-done.4
  33.8 6.8 all-to-all-done.2
  51.2 16.4 %collective-permute-done.14 = s32[384]{0:T(512)S(1)} collective-permute-done((s32[384]{0:T(512)S(1)}, s32[384]{0:T(512)S(1)}, u32[]{:S(2)}, u32[]{:S(2)}) %collective-permute-start.14) | collective-permute-done | bytes 1568 | tf_op jit(solution)/shard_map/ppermute | solution.py:45
  73.6 13.7 %collective-permute-done.15 = s32[2,384]{1,0:T(2,128)S(1)} collective-permute-done((s32[2,384]{1,0:T(2,128)S(1)}, s32[2,384]{1,0:T(2,128)S(1)}, u32[]{:S(2)}, u32[]{:S(2)}) %collective-permute-start.15) | collective-permute-done | bytes 3104 | tf_op jit(solution)/shard_map/ppermute | solution.py:45
  141.6 11.2 %collective-permute-done.44 = bf16[2,2,512,128]{3,1,0,2:T(2,128)(2,1)} collective-permute-done((bf16[2,2,512,128]{3,1,0,2:T(2,128)(2,1)S(1)}, bf16[2,2,512,128]{3,1,0,2:T(2,128)(2,1)}, u32[]{:S(2)}, u32[]{:S(2)}) %collective-permute-start.44) | collective-permute-done | bytes 524320 | tf_op jit(solution)/shard_map/ppermute | solution.py:45
  167.4 7.9 collective-permute-done.16
  176.6 10.0 %collective-permute-done.41 = bf16[2,2,128,512]{3,2,1,0:T(8,128)(2,1)} collective-permute-done((bf16[2,2,128,512]{3,2,1,0:T(8,128)(2,1)}, bf16[2,2,128,512]{3,2,1,0:T(8,128)(2,1)}, u32[]{:S(2)}, u32[]{:S(2)}) %collective-permute-start.41) | collective-permute-done | bytes 524320 | tf_op jit(solution)/shard_map/ppermute | solution.py:45
  187.8 5.8 collective-permute-done.8
  208.6 28.2 %collective-permute-done.17 = bf16[2,2,128,512]{3,2,1,0:T(8,128)(2,1)S(1)} collective-permute-done((bf16[2,2,128,512]{3,2,1,0:T(8,128)(2,1)}, bf16[2,2,128,512]{3,2,1,0:T(8,128)(2,1)S(1)}, u32[]{:S(2)}, u32[]{:S(2)}) %collective-permute-start.17) | collective-permute-done | bytes 524320 | tf_op jit(solution)/shard_map/ppermute | solution.py:45
  244.8 36.9 %collective-permute-done.20 = bf16[2,2,512,128]{3,1,0,2:T(2,128)(2,1)S(1)} collective-permute-done((bf16[2,2,512,128]{3,1,0,2:T(2,128)(2,1)S(1)}, bf16[2,2,512,128]{3,1,0,2:T(2,128)(2,1)S(1)}, u32[]{:S(2)}, u32[]{:S(2)}) %collective-permute-start.20) | collective-permute-done | bytes 524320 | tf_op jit(solution)/shard_map/ppermute | solution.py:45
  285.0 9.2 collective-permute-done.21
  305.7 9.0 collective-permute-done.45
  319.6 10.0 %collective-permute-done.10 = bf16[2,2,128,512]{3,2,1,0:T(8,128)(2,1)S(1)} collective-permute-done((bf16[2,2,128,512]{3,2,1,0:T(8,128)(2,1)S(1)}, bf16[2,2,128,512]{3,2,1,0:T(8,128)(2,1)S(1)}, u32[]{:S(2)}, u32[]{:S(2)}) %collective-permute-start.10) | collective-permute-done | bytes 524320 | tf_op jit(solution)/shard_map/ppermute | solution.py:45
  359.0 5.5 multiply_convert_fusion.2
  380.0 6.0 collective-permute-start.25
  405.3 8.7 collective-permute-done.28
  418.0 11.4 %collective-permute-done.26 = bf16[192,2048]{1,0:T(8,128)(2,1)S(1)} collective-permute-done((bf16[192,2048]{1,0:T(8,128)(2,1)S(1)}, bf16[192,2048]{1,0:T(8,128)(2,1)S(1)}, u32[]{:S(2)}, u32[]{:S(2)}) %collective-permute-start.26) | collective-permute-done | bytes 786464 | tf_op jit(solution)/shard_map/ppermute | solution.py:45
  438.4 15.5 %collective-permute-done.33 = bf16[192,2048]{1,0:T(8,128)(2,1)S(1)} collective-permute-done((bf16[192,2048]{1,0:T(8,128)(2,1)S(1)}, bf16[192,2048]{1,0:T(8,128)(2,1)S(1)}, u32[]{:S(2)}, u32[]{:S(2)}) %collective-permute-start.33) | collective-permute-done | bytes 786464 | tf_op jit(solution)/shard_map/ppermute | solution.py:45
  457.0 7.4 collective-permute-done.35
  472.5 6.8 fusion.22
  479.3 4.9 convolution_convert_fusion.4
  484.2 6.3 fusion.123
  490.5 4.7 convolution_convert_fusion.2
  503.3 6.6 convolution_convert_fusion.3
  512.6 6.6 add_convert_fusion.1
  532.3 17.2 %collective-permute-done.107 = bf16[2,2,2,128,512]{4,3,2,1,0:T(8,128)(2,1)} collective-permute-done((bf16[2,2,2,128,512]{4,3,2,1,0:T(8,128)(2,1)}, bf16[2,2,2,128,512]{4,3,2,1,0:T(8,128)(2,1)}, u32[]{:S(2)}, u32[]{:S(2)}) %collective-permute-start.107) | collective-permute-done | bytes 1048608 | tf_op jit(solution)/shard_map/ppermute | solution.py:45
  556.4 5.2 collective-permute-done.69
  563.1 6.9 collective-permute-done.53
  572.6 14.3 %collective-permute-done.67 = bf16[192,2048]{1,0:T(8,128)(2,1)S(1)} collective-permute-done((bf16[192,2048]{1,0:T(8,128)(2,1)S(1)}, bf16[192,2048]{1,0:T(8,128)(2,1)S(1)}, u32[]{:S(2)}, u32[]{:S(2)}) %collective-permute-start.67) | collective-permute-done | bytes 786464 | tf_op jit(solution)/shard_map/ppermute | solution.py:45
  592.2 9.8 %collective-permute-done.51 = bf16[192,2048]{1,0:T(8,128)(2,1)S(1)} collective-permute-done((bf16[192,2048]{1,0:T(8,128)(2,1)S(1)}, bf16[192,2048]{1,0:T(8,128)(2,1)S(1)}, u32[]{:S(2)}, u32[]{:S(2)}) %collective-permute-start.51) | collective-permute-done | bytes 786464 | tf_op jit(solution)/shard_map/ppermute | solution.py:45
  613.0 21.0 %collective-permute-done.101 = f32[2048]{0:T(1024)S(1)} collective-permute-done((f32[2048]{0:T(1024)S(1)}, f32[2048]{0:T(1024)S(1)}, u32[]{:S(2)}, u32[]{:S(2)}) %collective-permute-start.101) | collective-permute-done | bytes 8224 | tf_op jit(solution)/shard_map/ppermute | solution.py:45
  635.7 6.7 collective-permute-done.102
  648.7 4.4 all-to-all-start.13
  659.4 5.1 collective-permute-done.106
  670.6 7.8 collective-permute-done.77
  699.6 4.7 convolution_convert_fusion.7
  704.3 6.6 fusion.124
  712.3 4.6 convolution_convert_fusion.5
  721.9 6.8 convolution_convert_fusion.6
  731.8 6.5 fusion.69
  738.3 13.4 %add_convert_fusion = bf16[1536,2048]{1,0:T(8,128)(2,1)} fusion(f32[1536,2048]{1,0:T(8,128)} %fusion.69, f32[1536,2048]{1,0:T(8,128)} %fusion.124, bf16[1536,512]{1,0:T(8,128)(2,1)} %bitcast.517, bf16[2048,512]{1,0:T(8,128)(2,1)S(1)} %bitcast.511), kind=kOutput, calls=%fused_computation | convolution fusion | flops 3230662656 | bytes 35127296 | tf_op jit(solution)/shard_map/dot_general | solution.py:32
  755.5 7.1 convolution_convert_fusion.8
  779.2 13.9 %collective-permute-done.94 = bf16[2,2,2,128,512]{4,3,2,1,0:T(8,128)(2,1)} collective-permute-done((bf16[2,2,2,128,512]{4,3,2,1,0:T(8,128)(2,1)}, bf16[2,2,2,128,512]{4,3,2,1,0:T(8,128)(2,1)}, u32[]{:S(2)}, u32[]{:S(2)}) %collective-permute-start.94) | collective-permute-done | bytes 1048608 | tf_op jit(solution)/shard_map/ppermute | solution.py:45
  811.6 23.3 %collective-permute-done.97 = bf16[2,2,128,512]{3,2,1,0:T(8,128)(2,1)} collective-permute-done((bf16[2,2,128,512]{3,2,1,0:T(8,128)(2,1)}, bf16[2,2,128,512]{3,2,1,0:T(8,128)(2,1)}, u32[]{:S(2)}, u32[]{:S(2)}) %collective-permute-start.97) | collective-permute-done | bytes 524320 | tf_op jit(solution)/shard_map/ppermute | solution.py:45
  853.0 28.3 %all-to-all-done.9 = bf16[4,128,512]{2,1,0:T(8,128)(2,1)} async-done(((bf16[4,128,512]{2,1,0:T(8,128)(2,1)}), bf16[4,128,512]{2,1,0:T(8,128)(2,1)}, u32[]{:S(2)}, u32[]{:S(2)}) %all-to-all-start.9) | async-done | bytes 524320 | tf_op jit(solution)/shard_map/all_to_all | solution.py:104
  888.9 4.8 collective-permute-done.93
  (683 shorter events, 449.2 us)
Async XLA Ops:
  45.4 43.3 %collective-permute-start.3 = (bf16[192,2048]{1,0:T(8,128)(2,1)}, bf16[192,2048]{1,0:T(8,128)(2,1)}, u32[]{:S(2)}, u32[]{:S(2)}) collective-permute-start(bf16[192,2048]{1,0:T(8,128)(2,1)} %fusion.44), channel_id=1, source_target_pairs={{0,8},{8,0},{1,9},{9,1},{2,10},{10,2},{3,11},{11,3},{4,12},{12,4},... | collective-permute-start | bytes 2359304 | tf_op jit(solution)/shard_map/ppermute | solution.py:45
  47.3 50.2 %collective-permute-start.1 = (bf16[192,2048]{1,0:T(8,128)(2,1)}, bf16[192,2048]{1,0:T(8,128)(2,1)}, u32[]{:S(2)}, u32[]{:S(2)}) collective-permute-start(bf16[192,2048]{1,0:T(8,128)(2,1)} %fusion.44), channel_id=1, source_target_pairs={{0,2},{2,0},{1,3},{3,1},{4,6},{6,4},{5,7},{7,5},{8,10},{10,8},{9,1... | collective-permute-start | bytes 2359304 | tf_op jit(solution)/shard_map/ppermute | solution.py:45
  48.8 57.4 %collective-permute-start = (bf16[192,2048]{1,0:T(8,128)(2,1)}, bf16[192,2048]{1,0:T(8,128)(2,1)}, u32[]{:S(2)}, u32[]{:S(2)}) collective-permute-start(bf16[192,2048]{1,0:T(8,128)(2,1)} %fusion.44), channel_id=1, source_target_pairs={{0,1},{1,0},{2,3},{3,2},{4,5},{5,4},{6,7},{7,6},{8,9},{9,8},{10,11... | collective-permute-start | bytes 2359304 | tf_op jit(solution)/shard_map/ppermute | solution.py:45
  49.4 50.5 %collective-permute-start.58 = (bf16[192,2048]{1,0:T(8,128)(2,1)S(1)}, bf16[192,2048]{1,0:T(8,128)(2,1)}, u32[]{:S(2)}, u32[]{:S(2)}) collective-permute-start(bf16[192,2048]{1,0:T(8,128)(2,1)S(1)} %copy-done.10), channel_id=1, source_target_pairs={{0,8},{8,0},{1,9},{9,1},{2,10},{10,2},{3,11},{11,3},{4,12},{12,4},... | collective-permute-start | bytes 2359304 | tf_op jit(solution)/shard_map/ppermute | solution.py:45
  69.0 33.0 %all-to-all-start.6 = ((bf16[4,512,128]{2,1,0:T(8,128)(2,1)}), bf16[4,512,128]{2,1,0:T(8,128)(2,1)S(1)}, u32[]{:S(2)}, u32[]{:S(2)}) async-start(bf16[4,512,128]{2,1,0:T(8,128)(2,1)} %bitcast.610), calls=%async_computation.6 | async-start | bytes 1048576 | tf_op jit(solution)/shard_map/all_to_all | solution.py:84
  99.8 29.4 %collective-permute-start.6 = (bf16[192,1024]{1,0:T(8,128)(2,1)}, bf16[192,1024]{1,0:T(8,128)(2,1)}, u32[]{:S(2)}, u32[]{:S(2)}) collective-permute-start(bf16[192,1024]{1,0:T(8,128)(2,1)} %slice.291), channel_id=1, source_target_pairs={{0,8},{8,0},{1,9},{9,1},{2,10},{10,2},{3,11},{11,3},{4,12},{12,4},... | collective-permute-start | bytes 1179656 | tf_op jit(solution)/shard_map/ppermute | solution.py:45
  102.0 32.8 %all-to-all-start.5 = ((bf16[4,128,512]{2,1,0:T(8,128)(2,1)}), bf16[4,128,512]{2,1,0:T(8,128)(2,1)}, u32[]{:S(2)}, u32[]{:S(2)}) async-start(bf16[4,128,512]{2,1,0:T(8,128)(2,1)} %bitcast.568), calls=%async_computation.5 | async-start | bytes 1048576 | tf_op jit(solution)/shard_map/all_to_all | solution.py:77
  119.0 180.9 %collective-permute-start.12 = (bf16[2,2,128,512]{3,2,1,0:T(8,128)(2,1)}, bf16[2,2,128,512]{3,2,1,0:T(8,128)(2,1)}, u32[]{:S(2)}, u32[]{:S(2)}) collective-permute-start(bf16[2,2,128,512]{3,2,1,0:T(8,128)(2,1)} %bitcast.26), channel_id=1, source_target_pairs={{0,16},{16,0},{1,17},{17,1},{2,18},{18,2},{3,19},{19,3},{4,20},{20... | collective-permute-start | bytes 1572872 | tf_op jit(solution)/shard_map/ppermute | solution.py:45
  126.4 31.2 %collective-permute-start.11 = (bf16[2,2,128,512]{3,2,1,0:T(8,128)(2,1)}, bf16[2,2,128,512]{3,2,1,0:T(8,128)(2,1)}, u32[]{:S(2)}, u32[]{:S(2)}) collective-permute-start(bf16[2,2,128,512]{3,2,1,0:T(8,128)(2,1)} %bitcast.26), channel_id=1, source_target_pairs={{0,4},{4,0},{1,5},{5,1},{2,6},{6,2},{3,7},{7,3},{8,12},{12,8},{9,1... | collective-permute-start | bytes 1572872 | tf_op jit(solution)/shard_map/ppermute | solution.py:45
  131.5 72.8 %collective-permute-start.39 = (bf16[2,2,128,512]{3,2,1,0:T(8,128)(2,1)}, bf16[2,2,128,512]{3,2,1,0:T(8,128)(2,1)}, u32[]{:S(2)}, u32[]{:S(2)}) collective-permute-start(bf16[2,2,128,512]{3,2,1,0:T(8,128)(2,1)} %bitcast.80), channel_id=1, source_target_pairs={{0,16},{16,0},{1,17},{17,1},{2,18},{18,2},{3,19},{19,3},{4,20},{20... | collective-permute-start | bytes 1572872 | tf_op jit(solution)/shard_map/ppermute | solution.py:45
  164.1 29.6 %collective-permute-start.8 = (bf16[2,2,128,512]{3,2,1,0:T(8,128)(2,1)}, bf16[2,2,128,512]{3,2,1,0:T(8,128)(2,1)S(1)}, u32[]{:S(2)}, u32[]{:S(2)}) collective-permute-start(bf16[2,2,128,512]{3,2,1,0:T(8,128)(2,1)} %bitcast.13), channel_id=1, source_target_pairs={{0,4},{4,0},{1,5},{5,1},{2,6},{6,2},{3,7},{7,3},{8,12},{12,8},{9,1... | collective-permute-start | bytes 1572872 | tf_op jit(solution)/shard_map/ppermute | solution.py:45
  194.8 42.0 %collective-permute-start.59 = (bf16[192,2048]{1,0:T(8,128)(2,1)}, bf16[192,2048]{1,0:T(8,128)(2,1)S(1)}, u32[]{:S(2)}, u32[]{:S(2)}) collective-permute-start(bf16[192,2048]{1,0:T(8,128)(2,1)} %collective-permute-done.58), channel_id=1, source_target_pairs={{0,1},{1,0},{2,3},{3,2},{4,5},{5,4},{6,7},{7,6},{8,9},{9,8},{10,11... | collective-permute-start | bytes 2359304 | tf_op jit(solution)/shard_map/ppermute | solution.py:45
  198.4 38.3 %collective-permute-start.17 = (bf16[2,2,128,512]{3,2,1,0:T(8,128)(2,1)}, bf16[2,2,128,512]{3,2,1,0:T(8,128)(2,1)S(1)}, u32[]{:S(2)}, u32[]{:S(2)}) collective-permute-start(bf16[2,2,128,512]{3,2,1,0:T(8,128)(2,1)} %bitcast.39), channel_id=1, source_target_pairs={{0,16},{16,0},{1,17},{17,1},{2,18},{18,2},{3,19},{19,3},{4,20},{20... | collective-permute-start | bytes 1572872 | tf_op jit(solution)/shard_map/ppermute | solution.py:45
  204.2 80.8 %collective-permute-start.42 = (bf16[2,2,128,512]{3,2,1,0:T(8,128)(2,1)}, bf16[2,2,128,512]{3,2,1,0:T(8,128)(2,1)S(1)}, u32[]{:S(2)}, u32[]{:S(2)}) collective-permute-start(bf16[2,2,128,512]{3,2,1,0:T(8,128)(2,1)} %bitcast.87), channel_id=1, source_target_pairs={{0,16},{16,0},{1,17},{17,1},{2,18},{18,2},{3,19},{19,3},{4,20},{20... | collective-permute-start | bytes 1572872 | tf_op jit(solution)/shard_map/ppermute | solution.py:45
  204.3 36.5 %collective-permute-start.40 = (bf16[2,2,128,512]{3,2,1,0:T(8,128)(2,1)}, bf16[2,2,128,512]{3,2,1,0:T(8,128)(2,1)S(1)}, u32[]{:S(2)}, u32[]{:S(2)}) collective-permute-start(bf16[2,2,128,512]{3,2,1,0:T(8,128)(2,1)} %collective-permute-done.39), channel_id=1, source_target_pairs={{0,4},{4,0},{1,5},{5,1},{2,6},{6,2},{3,7},{7,3},{8,12},{12,8},{9,1... | collective-permute-start | bytes 1572872 | tf_op jit(solution)/shard_map/ppermute | solution.py:45
  236.7 44.9 %collective-permute-start.20 = (bf16[2,2,512,128]{3,1,0,2:T(2,128)(2,1)S(1)}, bf16[2,2,512,128]{3,1,0,2:T(2,128)(2,1)S(1)}, u32[]{:S(2)}, u32[]{:S(2)}) collective-permute-start(bf16[2,2,512,128]{3,1,0,2:T(2,128)(2,1)S(1)} %bitcast.547), channel_id=1, source_target_pairs={{0,16},{16,0},{1,17},{17,1},{2,18},{18,2},{3,19},{19,3},{4,20},{20... | collective-permute-start | bytes 1572872 | tf_op jit(solution)/shard_map/ppermute | solution.py:45
  236.8 44.9 %collective-permute-start.18 = (bf16[2,2,128,512]{3,2,1,0:T(8,128)(2,1)S(1)}, bf16[2,2,128,512]{3,2,1,0:T(8,128)(2,1)S(1)}, u32[]{:S(2)}, u32[]{:S(2)}) collective-permute-start(bf16[2,2,128,512]{3,2,1,0:T(8,128)(2,1)S(1)} %collective-permute-done.17), channel_id=1, source_target_pairs={{0,4},{4,0},{1,5},{5,1},{2,6},{6,2},{3,7},{7,3},{8,12},{12,8},{9,1... | collective-permute-start | bytes 1572872 | tf_op jit(solution)/shard_map/ppermute | solution.py:45
  240.8 63.3 %collective-permute-start.9 = (bf16[2,2,128,512]{3,2,1,0:T(8,128)(2,1)}, bf16[2,2,128,512]{3,2,1,0:T(8,128)(2,1)S(1)}, u32[]{:S(2)}, u32[]{:S(2)}) collective-permute-start(bf16[2,2,128,512]{3,2,1,0:T(8,128)(2,1)} %bitcast.13), channel_id=1, source_target_pairs={{0,16},{16,0},{1,17},{17,1},{2,18},{18,2},{3,19},{19,3},{4,20},{20... | collective-permute-start | bytes 1572872 | tf_op jit(solution)/shard_map/ppermute | solution.py:45
  281.7 33.1 %collective-permute-start.45 = (bf16[2,2,512,128]{3,1,0,2:T(2,128)(2,1)S(1)}, bf16[2,2,512,128]{3,1,0,2:T(2,128)(2,1)}, u32[]{:S(2)}, u32[]{:S(2)}) collective-permute-start(bf16[2,2,512,128]{3,1,0,2:T(2,128)(2,1)S(1)} %bitcast.544), channel_id=1, source_target_pairs={{0,16},{16,0},{1,17},{17,1},{2,18},{18,2},{3,19},{19,3},{4,20},{20... | collective-permute-start | bytes 1572872 | tf_op jit(solution)/shard_map/ppermute | solution.py:45
  285.0 54.6 %collective-permute-start.7 = (bf16[192,2048]{1,0:T(8,128)(2,1)}, bf16[192,2048]{1,0:T(8,128)(2,1)}, u32[]{:S(2)}, u32[]{:S(2)}) collective-permute-start(bf16[192,2048]{1,0:T(8,128)(2,1)} %constant_dynamic-update-slice_fusion), channel_id=1, source_target_pairs={{0,1},{1,0},{2,3},{3,2},{4,5},{5,4},{6,7},{7,6},{8,9},{9,8},{10,11... | collective-permute-start | bytes 2359304 | tf_op jit(solution)/shard_map/ppermute | solution.py:45
  299.9 114.3 %collective-permute-start.62 = (bf16[192,2048]{1,0:T(8,128)(2,1)}, bf16[192,2048]{1,0:T(8,128)(2,1)}, u32[]{:S(2)}, u32[]{:S(2)}) collective-permute-start(bf16[192,2048]{1,0:T(8,128)(2,1)} %constant_dynamic-update-slice_fusion.4), channel_id=1, source_target_pairs={{0,1},{1,0},{2,3},{3,2},{4,5},{5,4},{6,7},{7,6},{8,9},{9,8},{10,11... | collective-permute-start | bytes 2359304 | tf_op jit(solution)/shard_map/ppermute | solution.py:45
  304.2 33.6 %collective-permute-start.13 = (bf16[2,2,128,512]{3,2,1,0:T(8,128)(2,1)}, bf16[2,2,128,512]{3,2,1,0:T(8,128)(2,1)}, u32[]{:S(2)}, u32[]{:S(2)}) collective-permute-start(bf16[2,2,128,512]{3,2,1,0:T(8,128)(2,1)} %collective-permute-done.12), channel_id=1, source_target_pairs={{0,4},{4,0},{1,5},{5,1},{2,6},{6,2},{3,7},{7,3},{8,12},{12,8},{9,1... | collective-permute-start | bytes 1572872 | tf_op jit(solution)/shard_map/ppermute | solution.py:45
  316.3 54.2 %collective-permute-start.46 = (bf16[2,2,512,128]{3,1,0,2:T(2,128)(2,1)}, bf16[2,2,512,128]{3,1,0,2:T(2,128)(2,1)}, u32[]{:S(2)}, u32[]{:S(2)}) collective-permute-start(bf16[2,2,512,128]{3,1,0,2:T(2,128)(2,1)} %collective-permute-done.45), channel_id=1, source_target_pairs={{0,4},{4,0},{1,5},{5,1},{2,6},{6,2},{3,7},{7,3},{8,12},{12,8},{9,1... | collective-permute-start | bytes 1572872 | tf_op jit(solution)/shard_map/ppermute | solution.py:45
  433.6 32.2 %collective-permute-start.30 = (bf16[192,2048]{1,0:T(8,128)(2,1)S(1)}, bf16[192,2048]{1,0:T(8,128)(2,1)S(1)}, u32[]{:S(2)}, u32[]{:S(2)}) collective-permute-start(bf16[192,2048]{1,0:T(8,128)(2,1)S(1)} %multiply_convert_fusion.3), channel_id=1, source_target_pairs={{0,1},{1,0},{2,3},{3,2},{4,5},{5,4},{6,7},{7,6},{8,9},{9,8},{10,11... | collective-permute-start | bytes 2359304 | tf_op jit(solution)/shard_map/ppermute | solution.py:45
  501.7 50.0 %collective-permute-start.109 = (bf16[2,2,2,512,128]{4,2,1,0,3:T(2,128)(2,1)S(1)}, bf16[2,2,2,512,128]{4,2,1,0,3:T(2,128)(2,1)}, u32[]{:S(2)}, u32[]{:S(2)}) collective-permute-start(bf16[2,2,2,512,128]{4,2,1,0,3:T(2,128)(2,1)S(1)} %dynamic-slice_bitcast_fusion), channel_id=1, source_target_pairs={{0,4},{4,0},{1,5},{5,1},{2,6},{6,2},{3,7},{7,3},{8,12},{12,8},{9,1... | collective-permute-start | bytes 3145736 | tf_op jit(solution)/shard_map/ppermute | solution.py:45
  511.6 37.9 %collective-permute-start.107 = (bf16[2,2,2,128,512]{4,3,2,1,0:T(8,128)(2,1)}, bf16[2,2,2,128,512]{4,3,2,1,0:T(8,128)(2,1)}, u32[]{:S(2)}, u32[]{:S(2)}) collective-permute-start(bf16[2,2,2,128,512]{4,3,2,1,0:T(8,128)(2,1)} %dynamic-slice_bitcast_fusion.1), channel_id=1, source_target_pairs={{0,4},{4,0},{1,5},{5,1},{2,6},{6,2},{3,7},{7,3},{8,12},{12,8},{9,1... | collective-permute-start | bytes 3145736 | tf_op jit(solution)/shard_map/ppermute | solution.py:45
  528.3 42.4 %collective-permute-start.63 = (bf16[192,2048]{1,0:T(8,128)(2,1)S(1)}, bf16[192,2048]{1,0:T(8,128)(2,1)S(1)}, u32[]{:S(2)}, u32[]{:S(2)}) collective-permute-start(bf16[192,2048]{1,0:T(8,128)(2,1)S(1)} %get-tuple-element.68), channel_id=1, source_target_pairs={{0,1},{1,0},{2,3},{3,2},{4,5},{5,4},{6,7},{7,6},{8,9},{9,8},{10,11... | collective-permute-start | bytes 2359304 | tf_op jit(solution)/shard_map/ppermute | solution.py:45
  529.4 59.8 %collective-permute-start.47 = (bf16[192,2048]{1,0:T(8,128)(2,1)S(1)}, bf16[192,2048]{1,0:T(8,128)(2,1)S(1)}, u32[]{:S(2)}, u32[]{:S(2)}) collective-permute-start(bf16[192,2048]{1,0:T(8,128)(2,1)S(1)} %get-tuple-element.78), channel_id=1, source_target_pairs={{0,1},{1,0},{2,3},{3,2},{4,5},{5,4},{6,7},{7,6},{8,9},{9,8},{10,11... | collective-permute-start | bytes 2359304 | tf_op jit(solution)/shard_map/ppermute | solution.py:45
  570.0 32.0 %collective-permute-start.51 = (bf16[192,2048]{1,0:T(8,128)(2,1)S(1)}, bf16[192,2048]{1,0:T(8,128)(2,1)S(1)}, u32[]{:S(2)}, u32[]{:S(2)}) collective-permute-start(bf16[192,2048]{1,0:T(8,128)(2,1)S(1)} %pad_maximum_fusion.36), channel_id=1, source_target_pairs={{0,2},{2,0},{1,3},{3,1},{4,6},{6,4},{5,7},{7,5},{8,10},{10,8},{9,1... | collective-permute-start | bytes 2359304 | tf_op jit(solution)/shard_map/ppermute | solution.py:45
  570.7 32.1 %collective-permute-start.54 = (bf16[192,2048]{1,0:T(8,128)(2,1)S(1)}, bf16[192,2048]{1,0:T(8,128)(2,1)S(1)}, u32[]{:S(2)}, u32[]{:S(2)}) collective-permute-start(bf16[192,2048]{1,0:T(8,128)(2,1)S(1)} %pad_maximum_fusion.37), channel_id=1, source_target_pairs={{0,8},{8,0},{1,9},{9,1},{2,10},{10,2},{3,11},{11,3},{4,12},{12,4},... | collective-permute-start | bytes 2359304 | tf_op jit(solution)/shard_map/ppermute | solution.py:45
  588.4 54.0 %collective-permute-start.110 = (bf16[2,2,512,128]{3,1,0,2:T(2,128)(2,1)S(1)}, bf16[2,2,512,128]{3,1,0,2:T(2,128)(2,1)}, u32[]{:S(2)}, u32[]{:S(2)}) collective-permute-start(bf16[2,2,512,128]{3,1,0,2:T(2,128)(2,1)S(1)} %dynamic-slice_bitcast_fusion.7), channel_id=1, source_target_pairs={{0,16},{16,0},{1,17},{17,1},{2,18},{18,2},{3,19},{19,3},{4,20},{20... | collective-permute-start | bytes 1572872 | tf_op jit(solution)/shard_map/ppermute | solution.py:45
  589.2 68.2 %collective-permute-start.108 = (bf16[2,2,128,512]{3,2,1,0:T(8,128)(2,1)}, bf16[2,2,128,512]{3,2,1,0:T(8,128)(2,1)}, u32[]{:S(2)}, u32[]{:S(2)}) collective-permute-start(bf16[2,2,128,512]{3,2,1,0:T(8,128)(2,1)} %dynamic-slice_bitcast_fusion.8), channel_id=1, source_target_pairs={{0,16},{16,0},{1,17},{17,1},{2,18},{18,2},{3,19},{19,3},{4,20},{20... | collective-permute-start | bytes 1572872 | tf_op jit(solution)/shard_map/ppermute | solution.py:45
  606.5 49.8 %collective-permute-start.72 = (bf16[192,2048]{1,0:T(8,128)(2,1)}, bf16[192,2048]{1,0:T(8,128)(2,1)}, u32[]{:S(2)}, u32[]{:S(2)}) collective-permute-start(bf16[192,2048]{1,0:T(8,128)(2,1)} %fusion.70), channel_id=1, source_target_pairs={{0,2},{2,0},{1,3},{3,1},{4,6},{6,4},{5,7},{7,5},{8,10},{10,8},{9,1... | collective-permute-start | bytes 2359304 | tf_op jit(solution)/shard_map/ppermute | solution.py:45
  608.6 44.6 %collective-permute-start.74 = (bf16[192,2048]{1,0:T(8,128)(2,1)}, bf16[192,2048]{1,0:T(8,128)(2,1)}, u32[]{:S(2)}, u32[]{:S(2)}) collective-permute-start(bf16[192,2048]{1,0:T(8,128)(2,1)} %fusion.70), channel_id=1, source_target_pairs={{0,8},{8,0},{1,9},{9,1},{2,10},{10,2},{3,11},{11,3},{4,12},{12,4},... | collective-permute-start | bytes 2359304 | tf_op jit(solution)/shard_map/ppermute | solution.py:45
  646.1 32.6 %collective-permute-start.71 = (bf16[192,2048]{1,0:T(8,128)(2,1)}, bf16[192,2048]{1,0:T(8,128)(2,1)}, u32[]{:S(2)}, u32[]{:S(2)}) collective-permute-start(bf16[192,2048]{1,0:T(8,128)(2,1)} %fusion.70), channel_id=1, source_target_pairs={{0,1},{1,0},{2,3},{3,2},{4,5},{5,4},{6,7},{7,6},{8,9},{9,8},{10,11... | collective-permute-start | bytes 2359304 | tf_op jit(solution)/shard_map/ppermute | solution.py:45
  648.7 126.4 %all-to-all-start.13 = ((bf16[4,512,128]{2,1,0:T(8,128)(2,1)}), bf16[4,512,128]{2,1,0:T(8,128)(2,1)}, u32[]{:S(2)}, u32[]{:S(2)}) async-start(bf16[4,512,128]{2,1,0:T(8,128)(2,1)} %copy.155), calls=%async_computation.13 | async-start | bytes 1048576 | tf_op jit(solution)/shard_map/all_to_all | solution.py:104
  721.9 115.3 %collective-permute-start.98 = (bf16[2,2,2,512,128]{4,2,1,0,3:T(2,128)(2,1)}, bf16[2,2,2,512,128]{4,2,1,0,3:T(2,128)(2,1)}, u32[]{:S(2)}, u32[]{:S(2)}) collective-permute-start(bf16[2,2,2,512,128]{4,2,1,0,3:T(2,128)(2,1)} %dynamic-slice_bitcast_fusion.3), channel_id=1, source_target_pairs={{0,4},{4,0},{1,5},{5,1},{2,6},{6,2},{3,7},{7,3},{8,12},{12,8},{9,1... | collective-permute-start | bytes 3145736 | tf_op jit(solution)/shard_map/ppermute | solution.py:45
  729.8 41.8 %collective-permute-start.96 = (bf16[2,2,2,128,512]{4,3,2,1,0:T(8,128)(2,1)}, bf16[2,2,2,128,512]{4,3,2,1,0:T(8,128)(2,1)}, u32[]{:S(2)}, u32[]{:S(2)}) collective-permute-start(bf16[2,2,2,128,512]{4,3,2,1,0:T(8,128)(2,1)} %dynamic-slice_bitcast_fusion.4), channel_id=1, source_target_pairs={{0,4},{4,0},{1,5},{5,1},{2,6},{6,2},{3,7},{7,3},{8,12},{12,8},{9,1... | collective-permute-start | bytes 3145736 | tf_op jit(solution)/shard_map/ppermute | solution.py:45
  766.6 78.7 %collective-permute-start.92 = (bf16[2,2,2,128,512]{4,3,2,1,0:T(8,128)(2,1)}, bf16[2,2,2,128,512]{4,3,2,1,0:T(8,128)(2,1)}, u32[]{:S(2)}, u32[]{:S(2)}) collective-permute-start(bf16[2,2,2,128,512]{4,3,2,1,0:T(8,128)(2,1)} %dynamic-slice_bitcast_fusion.6), channel_id=1, source_target_pairs={{0,4},{4,0},{1,5},{5,1},{2,6},{6,2},{3,7},{7,3},{8,12},{12,8},{9,1... | collective-permute-start | bytes 3145736 | tf_op jit(solution)/shard_map/ppermute | solution.py:45
  766.9 118.5 %collective-permute-start.79 = (bf16[192,2048]{1,0:T(8,128)(2,1)}, bf16[192,2048]{1,0:T(8,128)(2,1)}, u32[]{:S(2)}, u32[]{:S(2)}) collective-permute-start(bf16[192,2048]{1,0:T(8,128)(2,1)} %get-tuple-element.61), channel_id=1, source_target_pairs={{0,1},{1,0},{2,3},{3,2},{4,5},{5,4},{6,7},{7,6},{8,9},{9,8},{10,11... | collective-permute-start | bytes 2359304 | tf_op jit(solution)/shard_map/ppermute | solution.py:45
  799.3 35.6 %collective-permute-start.97 = (bf16[2,2,128,512]{3,2,1,0:T(8,128)(2,1)}, bf16[2,2,128,512]{3,2,1,0:T(8,128)(2,1)}, u32[]{:S(2)}, u32[]{:S(2)}) collective-permute-start(bf16[2,2,128,512]{3,2,1,0:T(8,128)(2,1)} %dynamic-slice_bitcast_fusion.11), channel_id=1, source_target_pairs={{0,16},{16,0},{1,17},{17,1},{2,18},{18,2},{3,19},{19,3},{4,20},{20... | collective-permute-start | bytes 1572872 | tf_op jit(solution)/shard_map/ppermute | solution.py:45
  801.1 36.1 %all-to-all-start.11 = ((bf16[4,128,512]{2,1,0:T(8,128)(2,1)}), bf16[4,128,512]{2,1,0:T(8,128)(2,1)}, u32[]{:S(2)}, u32[]{:S(2)}) async-start(bf16[4,128,512]{2,1,0:T(8,128)(2,1)} %bitcast.566), calls=%async_computation.11 | async-start | bytes 1048576 | tf_op jit(solution)/shard_map/all_to_all | solution.py:104
  805.3 45.2 %collective-permute-start.95 = (bf16[2,2,128,512]{3,2,1,0:T(8,128)(2,1)}, bf16[2,2,128,512]{3,2,1,0:T(8,128)(2,1)}, u32[]{:S(2)}, u32[]{:S(2)}) collective-permute-start(bf16[2,2,128,512]{3,2,1,0:T(8,128)(2,1)} %dynamic-slice_bitcast_fusion.12), channel_id=1, source_target_pairs={{0,16},{16,0},{1,17},{17,1},{2,18},{18,2},{3,19},{19,3},{4,20},{20... | collective-permute-start | bytes 1572872 | tf_op jit(solution)/shard_map/ppermute | solution.py:45
  834.9 50.5 %collective-permute-start.83 = (bf16[192,2048]{1,0:T(8,128)(2,1)}, bf16[192,2048]{1,0:T(8,128)(2,1)}, u32[]{:S(2)}, u32[]{:S(2)}) collective-permute-start(bf16[192,2048]{1,0:T(8,128)(2,1)} %pad_maximum_fusion.40), channel_id=1, source_target_pairs={{0,2},{2,0},{1,3},{3,1},{4,6},{6,4},{5,7},{7,5},{8,10},{10,8},{9,1... | collective-permute-start | bytes 2359304 | tf_op jit(solution)/shard_map/ppermute | solution.py:45
  837.2 48.2 %collective-permute-start.86 = (bf16[192,2048]{1,0:T(8,128)(2,1)}, bf16[192,2048]{1,0:T(8,128)(2,1)}, u32[]{:S(2)}, u32[]{:S(2)}) collective-permute-start(bf16[192,2048]{1,0:T(8,128)(2,1)} %pad_maximum_fusion.41), channel_id=1, source_target_pairs={{0,8},{8,0},{1,9},{9,1},{2,10},{10,2},{3,11},{11,3},{4,12},{12,4},... | collective-permute-start | bytes 2359304 | tf_op jit(solution)/shard_map/ppermute | solution.py:45
  837.2 44.0 %all-to-all-start.9 = ((bf16[4,128,512]{2,1,0:T(8,128)(2,1)}), bf16[4,128,512]{2,1,0:T(8,128)(2,1)}, u32[]{:S(2)}, u32[]{:S(2)}) async-start(bf16[4,128,512]{2,1,0:T(8,128)(2,1)} %bitcast.570), calls=%async_computation.9 | async-start | bytes 1048576 | tf_op jit(solution)/shard_map/all_to_all | solution.py:104
  845.3 75.4 %collective-permute-start.99 = (bf16[2,2,512,128]{3,1,0,2:T(2,128)(2,1)}, bf16[2,2,512,128]{3,1,0,2:T(2,128)(2,1)}, u32[]{:S(2)}, u32[]{:S(2)}) collective-permute-start(bf16[2,2,512,128]{3,1,0,2:T(2,128)(2,1)} %dynamic-slice_bitcast_fusion.10), channel_id=1, source_target_pairs={{0,16},{16,0},{1,17},{17,1},{2,18},{18,2},{3,19},{19,3},{4,20},{20... | collective-permute-start | bytes 1572872 | tf_op jit(solution)/shard_map/ppermute | solution.py:45
  850.6 43.1 %collective-permute-start.93 = (bf16[2,2,128,512]{3,2,1,0:T(8,128)(2,1)}, bf16[2,2,128,512]{3,2,1,0:T(8,128)(2,1)}, u32[]{:S(2)}, u32[]{:S(2)}) collective-permute-start(bf16[2,2,128,512]{3,2,1,0:T(8,128)(2,1)} %dynamic-slice_bitcast_fusion.13), channel_id=1, source_target_pairs={{0,16},{16,0},{1,17},{17,1},{2,18},{18,2},{3,19},{19,3},{4,20},{20... | collective-permute-start | bytes 1572872 | tf_op jit(solution)/shard_map/ppermute | solution.py:45
  (196 other events, 2468.3 us)

commit v2 on v1

v2 whole, which is shorter than its diff:
```python
import functools
import jax
import jax.numpy as jnp
from jax import lax
from jax.experimental import pallas as pl
from jax.experimental.pallas import tpu as pltpu
from jax.sharding import Mesh, PartitionSpec as P

epsilon = 1e-05
bf16 = jnp.bfloat16
f32 = jnp.float32
SPREAD = ("zh", "zl", "y", "x")
GROUP = ("zl", "x")


def normalize(values):
    centred = values - jnp.mean(values, axis=-1, keepdims=True)
    variance = jnp.mean(centred * centred, axis=-1, keepdims=True)
    return centred * lax.rsqrt(variance + epsilon)


def layer_norm(rows, gain):
    return normalize(rows) * gain


def dot(left, right, dims):
    return lax.dot_general(left, right, (dims, ((), ())), preferred_element_type=f32)


NN = ((1,), (0,))
NT = ((1,), (1,))
TN = ((0,), (0,))


def swap(a, axis, label="move"):
    with jax.named_scope(label):
        return lax.ppermute(a, axis, [(0, 1), (1, 0)])


def after(value, *others):
    return lax.optimization_barrier((value,) + others)[0]


def ordered(own, other, axis, dim):
    first = lax.axis_index(axis) == 0
    return jnp.stack([jnp.where(first, own, other), jnp.where(first, other, own)], dim)


def by_quarter(w):
    rows, cols = w.shape
    return w.reshape(rows, 4, cols // 4).transpose(1, 0, 2)


def group_exchange(parts):
    return lax.all_to_all(parts, GROUP, 0, 0, tiled=True)


def far_half(piece, label):
    if lax.axis_size("zh") == 2:
        return swap(piece, "zh", label)
    return lax.all_gather(piece, "zh")


def whole_weight(piece, near_y, far, far_y, column, width):
    if lax.axis_size("zh") == 2:
        return [(piece, column), (near_y, column), (far, 0), (far_y, 0)], width
    shape = far.shape[:1] + (2, 2) + far.shape[2:]
    whole = ordered(far.reshape(shape), far_y.reshape(shape), "y", 2)
    return [(whole.reshape(16, -1, width), 0)], width


def take(a, index, dim):
    return lax.dynamic_index_in_dim(a, index, dim, keepdims=False)


def add(a, b):
    return (a.astype(f32) + b.astype(f32)).astype(bf16)


def scatter_y(keep, got):
    n = got.shape[-1]
    if lax.axis_size("zh") == 2:
        return add(keep[:2], got[:2]), add(keep[2:], got[2:])
    flip = lambda g: jnp.flip(g.reshape(2, 2, 1, -1, n), 0)
    g = jnp.concatenate([flip(keep), flip(got)], 2).reshape(lax.axis_size("zh"), 2, 2, 2, -1, n)
    y = lax.axis_index("y")
    return add(take(g, y, 2), swap(take(g, 1 - y, 2), "y")), None


def send_y(send):
    return swap(send, "y", "y_grad") if lax.axis_size("zh") == 2 else send


def scatter_zh(send, keep, label):
    if lax.axis_size("zh") == 2:
        g = add(keep, swap(send, "zh", label))
    else:
        g = lax.psum_scatter(send, "zh", scatter_dimension=0)
    return g.reshape(4, -1, g.shape[-1])


class Clock:
    def __init__(self):
        self.now = ()

    def done(self, *values):
        self.now = values

    def at(self, value):
        return after(value, *self.now)


class Gather:
    def __init__(self, clock, a, label):
        self.a, self.label, self.half = clock.at(a), label, a.shape[0] // 2
        self.x = swap(self.a, "x", label + "_x")
        self.z = swap(self.a, "zl", label + "_z")
        self.first = (self.x, self.z)

    def finish(self, clock):
        half, label = self.half, self.label
        ax, az = clock.at(self.x), clock.at(self.z)
        top = swap(az[:half], "x", label + "_dx")
        bottom = swap(ax[half:], "zl", label + "_dz")
        out = []
        for p in ((self.a,), (ax,), (az,), (top, bottom)):
            out += list(p) + [swap(q, "tensor", label + "_c") for q in p]
        return out


class Scatter:
    def __init__(self, send_rest, send_diag, keep, label):
        self.label, self.keep = label, keep
        self.diag = add(keep[3], swap(send_diag, "tensor", label + "_cd"))
        self.rest = swap(send_rest, "tensor", label + "_cr")

    def relay(self, clock):
        half = self.diag.shape[0] // 2
        diag = clock.at(self.diag)
        self.through_x = swap(diag[:half], "x", self.label + "_dx")
        self.through_z = swap(diag[half:], "zl", self.label + "_dz")
        self.second = (self.through_x, self.through_z, self.rest)

    def send(self, clock):
        through_x, through_z, rest = (clock.at(v).astype(f32) for v in self.second)
        half = through_x.shape[0]
        self.own, xmate, zmate = (self.keep[r].astype(f32) + rest[r] for r in range(3))
        zmate = jnp.concatenate([zmate[:half] + through_x, zmate[half:]]).astype(bf16)
        xmate = jnp.concatenate([xmate[:half], xmate[half:] + through_z]).astype(bf16)
        self.x = swap(xmate, "x", self.label + "_x")
        self.z = swap(zmate, "zl", self.label + "_z")
        self.last = (self.x, self.z)

    def finish(self):
        return self.own + self.x.astype(f32) + self.z.astype(f32)


VMEM_LIMIT = 60 * 2**20
PIECES = (
    (0, 0, 0, 1),
    (0, 1, 0, 1),
    (1, 2, 0, 1),
    (1, 3, 0, 1),
    (2, 4, 0, 1),
    (2, 5, 0, 1),
    (3, 6, 0, 2),
    (3, 6, 1, 2),
    (3, 7, 0, 2),
    (3, 7, 1, 2),
)
ANY = pl.BlockSpec(memory_space=pl.ANY)
SMEM = pl.BlockSpec(memory_space=pltpu.SMEM)


class Loader:
    def __init__(self, sems):
        self.sems, self.used = sems, 0

    def copy(self, src, dst):
        self.used += 1
        return pltpu.make_async_copy(src, dst, self.sems.at[self.used - 1])

    def tokens(self, refs, held):
        rows = held.shape[1]
        chips = [[], [], [], []]
        for ref, (chip, slot, part, parts) in zip(refs, PIECES):
            size = rows // parts
            chips[chip].append(self.copy(ref, held.at[slot, pl.ds(part * size, size)]))
        return chips

    def weight(self, refs, columns, held, coord):
        if len(refs) == 1:
            return [self.copy(refs[0], held)]
        copies, n = [], held.shape[2]
        for i, (ref, column) in enumerate(zip(refs, columns)):
            zh, y = coord[0] ^ (i // 2), coord[1] ^ (i % 2)
            for zl in range(2):
                row = ((zh * 2 + zl) * 2 + y) * 2
                block = ref.at[pl.ds(2 * zl, 2), :, pl.ds(column, n)]
                copies.append(self.copy(block, held.at[pl.ds(row, 2)]))
        return copies


def start(*copies):
    for c in copies:
        c.start()


def wait(*copies):
    for c in copies:
        c.wait()


def at_chip(r, chips):
    for i, copies in enumerate(chips):
        pl.when(r == i)(functools.partial(wait, *copies))


def rows_of(held, r):
    pair = held[pl.ds(2 * r, 2)]
    return pair.reshape(2 * pair.shape[1], pair.shape[2])


def flat(w):
    value = w[...]
    return value.reshape(value.shape[0] * value.shape[1], value.shape[2])


def by_chip(shape):
    return pl.BlockSpec((1,) + shape, lambda r: (r,) + (0,) * len(shape))


def chip_kernel(body, operands, specs, outs, out_specs, scratch, copies, flops):
    moved = sum(a.size * a.dtype.itemsize for a in operands) + sum(
        o.size * jnp.dtype(o.dtype).itemsize for o in outs
    )
    return pl.pallas_call(
        body,
        grid=(4,),
        in_specs=specs,
        out_specs=out_specs,
        out_shape=outs,
        scratch_shapes=scratch + [pltpu.SemaphoreType.DMA((copies,))],
        compiler_params=pltpu.CompilerParams(
            dimension_semantics=("arbitrary",), vmem_limit_bytes=VMEM_LIMIT
        ),
        cost_estimate=pl.CostEstimate(flops=flops, bytes_accessed=moved, transcendentals=0),
    )(*operands)


def held_tokens(pieces):
    return pltpu.VMEM((8,) + pieces[0].shape, bf16)


def held_weight(w):
    rows = sum(p.shape[0] * p.shape[1] for p, _ in w[0])
    return pltpu.VMEM((16, rows // 16, w[1]), bf16)


def arrays(*weights):
    return [p for w in weights for p, _ in w[0]]


def columns_of(w):
    return tuple(c for _, c in w[0])


def struct(shape, dtype):
    return jax.ShapeDtypeStruct(shape, dtype)


def column_loop(total, step, f):
    for j in range(0, total, step):
        f(j, step)


def partial_rows(grads, held, r, keep, store):
    rows = keep.shape[1]
    depth = held.shape[0] * held.shape[1]
    blocks = 4
    for j in range(0, held.shape[0], blocks):
        w = held[j : j + blocks].reshape(blocks * held.shape[1], held.shape[2])
        c = j * held.shape[1]
        out = dot(grads, w, NT).astype(bf16)
        keep[0, :, c : c + blocks * held.shape[1]] = out[:rows]
        store[r, :, c : c + blocks * held.shape[1]] = out[rows:]


def send_copies(load, store, rest, diag):
    return [load.copy(store.at[i], rest.at[i]) for i in range(3)] + [load.copy(store.at[3], diag)]


def at_chip_start(r, copies):
    for i, c in enumerate(copies):
        pl.when(r == i)(c.start)

    @pl.when(r == 3)
    def _():
        wait(*copies)


def partial_outs(rows, model):
    outs = [
        struct((3, rows, model), bf16),
        struct((rows, model), bf16),
        struct((4, rows, model), bf16),
    ]
    return outs, [ANY, ANY, by_chip((rows, model))]


def attend_body(c_qk, c_v, coord, mask, *refs):
    acts, refs = refs[:10], refs[10:]
    wqk, refs = refs[: len(c_qk)], refs[len(c_qk) :]
    wv, refs = refs[: len(c_v)], refs[len(c_v) :]
    q_out, k_out, v_out, score_out, hat_out, scale_out, held, held_qk, held_v, sems = refs
    load, r = Loader(sems), pl.program_id(0)
    w1 = load.weight(wqk, c_qk, held_qk, coord)
    chips = load.tokens(acts, held)
    w2 = load.weight(wv, c_v, held_v, coord)

    @pl.when(r == 0)
    def _():
        start(*w1, *chips[0], *w2, *chips[1], *chips[2], *chips[3])
        wait(*w1)

    at_chip(r, chips)
    x = rows_of(held, r)
    qk = dot(x, flat(held_qk), NN).astype(bf16)
    size = qk.shape[1] // 2
    q, k = qk[:, :size], qk[:, size:]
    q_out[0], k_out[0] = q, k
    scores = (dot(q, k, NT) * mask[0]).astype(bf16)
    score_out[0] = scores

    @pl.when(r == 0)
    def _():
        wait(*w2)

    v = dot(x, flat(held_v), NN).astype(bf16)
    v_out[0] = v
    hat_out[0] = dot(scores, v, NN)
    rows, step = hat_out.shape[1], 32

    def chunk(i, carry):
        at = pl.ds(pl.multiple_of(i * step, step), step)
        part = hat_out[0, at, :]
        part = part - jnp.mean(part, axis=-1, keepdims=True)
        scale = lax.rsqrt(jnp.mean(part * part, axis=-1, keepdims=True) + epsilon)
        hat_out[0, at, :] = part * scale
        scale_out[0, at, :] = jnp.broadcast_to(scale, (step, 128))
        return carry

    lax.fori_loop(0, rows // step, chunk, 0)


def attend(coord, mask, acts, wqk, wv, key_size):
    length, n = mask.shape[1], wv[1]
    model = acts[0].shape[1]
    outs = [
        struct((4, length, key_size), bf16),
        struct((4, length, key_size), bf16),
        struct((4, length, n), bf16),
        struct((4, length, length), bf16),
        struct((4, length, n), f32),
        struct((4, length, 128), f32),
    ]
    return chip_kernel(
        functools.partial(attend_body, columns_of(wqk), columns_of(wv)),
        [coord, mask, *acts, *arrays(wqk, wv)],
        [SMEM, by_chip((length, length))] + [ANY] * (10 + len(arrays(wqk, wv))),
        outs,
        [by_chip(o.shape[1:]) for o in outs],
        [held_tokens(acts), held_weight(wqk), held_weight(wv)],
        30,
        16 * length * model * n,
    )


def branch_body(c_s, c_o, coord, hat, *refs):
    acts, refs = refs[:10], refs[10:]
    ws, refs = refs[: len(c_s)], refs[len(c_s) :]
    wo, refs = refs[: len(c_o)], refs[len(c_o) :]
    s_out, gated_out, rest, diag, keep, held, held_s, held_o, store, sems = refs
    load, r = Loader(sems), pl.program_id(0)
    w1 = load.weight(ws, c_s, held_s, coord)
    chips = load.tokens(acts, held)
    w2 = load.weight(wo, c_o, held_o, coord)
    sends = send_copies(load, store, rest, diag)

    @pl.when(r == 0)
    def _():
        start(*w1, *chips[0], *w2, *chips[1], *chips[2], *chips[3])
        wait(*w1)

    at_chip(r, chips)
    s_out[0] = dot(rows_of(held, r), flat(held_s), NN)
    rows, step = s_out.shape[1], 32

    def chunk(i, carry):
        at = pl.ds(pl.multiple_of(i * step, step), step)
        s = s_out[0, at, :]
        gated_out[0, at, :] = (s / (1.0 + jnp.exp(-s)) * hat[0, at, :]).astype(bf16)
        return carry

    lax.fori_loop(0, rows // step, chunk, 0)

    @pl.when(r == 0)
    def _():
        wait(*w2)

    partial_rows(gated_out[0], held_o, r, keep, store)
    at_chip_start(r, sends)


def branch(coord, hat, acts, ws, wo):
    length, n = hat.shape[1:]
    rows, model = acts[0].shape
    outs, out_specs = partial_outs(rows, model)
    outs = [struct((4, length, n), f32), struct((4, length, n), bf16)] + outs
    return chip_kernel(
        functools.partial(branch_body, columns_of(ws), columns_of(wo)),
        [coord, hat, *acts, *arrays(ws, wo)],
        [SMEM, by_chip((length, n))] + [ANY] * (10 + len(arrays(ws, wo))),
        outs,
        [by_chip((length, n)), by_chip((length, n))] + out_specs,
        [held_tokens(acts), held_weight(ws), held_weight(wo), pltpu.VMEM((4, rows, model), bf16)],
        40,
        16 * length * model * n,
    )


def feed_body(c_ug, c_d, coord, *refs):
    acts, cots, refs = refs[:10], refs[10:20], refs[20:]
    wug, refs = refs[: len(c_ug)], refs[len(c_ug) :]
    wd, refs = refs[: len(c_d)], refs[len(c_d) :]
    hidden_out, up_out, gate_out, rest, diag, keep = refs[:6]
    held, held_c, held_ug, held_d, store, ug, gh, sems = refs[6:]
    load, r = Loader(sems), pl.program_id(0)
    w1 = load.weight(wug, c_ug, held_ug, coord)
    chips = load.tokens(acts, held)
    w2 = load.weight(wd, c_d, held_d, coord)
    chips_c = load.tokens(cots, held_c)
    sends = send_copies(load, store, rest, diag)

    @pl.when(r == 0)
    def _():
        start(*w2, *chips_c[0], *w1, *chips[0])
        for i in range(1, 4):
            start(*chips_c[i], *chips[i])
        wait(*w2)

    at_chip(r, chips_c)
    gh[...] = dot(rows_of(held_c, r), flat(held_d), NN)

    @pl.when(r == 0)
    def _():
        wait(*w1)

    at_chip(r, chips)
    ug[...] = dot(rows_of(held, r), flat(held_ug), NN)
    rows, n = gh.shape
    step = 16

    def chunk(i, carry):
        at = pl.ds(pl.multiple_of(i * step, step), step)
        up, g, e = ug[at, :n], ug[at, n:], gh[at, :]
        c = 0.7978845608028654
        square = g * g
        t = jnp.tanh(c * g * (1.0 + 0.044715 * square))
        half = 0.5 * (1.0 + t)
        gelu = g * half
        slope = half + (0.5 * c) * g * (1.0 - t * t) * (1.0 + (3 * 0.044715) * square)
        hidden_out[0, at, :] = (gelu * up).astype(bf16)
        up_out[0, at, :] = (e * gelu).astype(bf16)
        gate_out[0, at, :] = (e * up * slope).astype(bf16)
        return carry

    lax.fori_loop(0, rows // step, chunk, 0)
    grads = jnp.concatenate([up_out[0], gate_out[0]], 1)
    partial_rows(grads, held_ug, r, keep, store)
    at_chip_start(r, sends)


def feed_forward(coord, acts, cots, wug, wd):
    rows, model = acts[0].shape
    n = wd[1]
    outs, out_specs = partial_outs(rows, model)
    outs = [struct((4, 2 * rows, n), bf16)] * 3 + outs
    return chip_kernel(
        functools.partial(feed_body, columns_of(wug), columns_of(wd)),
        [coord, *acts, *cots, *arrays(wug, wd)],
        [SMEM] + [ANY] * (20 + len(arrays(wug, wd))),
        outs,
        [by_chip((2 * rows, n))] * 3 + out_specs,
        [
            held_tokens(acts),
            held_tokens(cots),
            held_weight(wug),
            held_weight(wd),
            pltpu.VMEM((4, rows, model), bf16),
            pltpu.VMEM((2 * rows, 2 * n), f32),
            pltpu.VMEM((2 * rows, n), f32),
        ],
        50,
        80 * rows * model * n,
    )


def back_body(columns, coord, *refs):
    count = len(columns)
    weights = []
    grads, refs = refs[:count], refs[count:]
    for c in columns:
        weights.append(refs[: len(c)])
        refs = refs[len(c) :]
    rest, diag, keep, refs = refs[0], refs[1], refs[2], refs[3:]
    helds, store, sems = refs[:count], refs[-2], refs[-1]
    load, r = Loader(sems), pl.program_id(0)
    copies = [load.weight(w, c, h, coord) for w, c, h in zip(weights, columns, helds)]
    sends = send_copies(load, store, rest, diag)

    @pl.when(r == 0)
    def _():
        for c in copies:
            start(*c)
        for c in copies:
            wait(*c)

    if count == 1:
        partial_rows(grads[0][0], helds[0], r, keep, store)
    else:
        rows = keep.shape[1]
        blocks = 4
        for j in range(0, 16, blocks):
            size = helds[0].shape[1] * blocks
            parts = [
                dot(g[0], h[j : j + blocks].reshape(size, h.shape[2]), NT) for g, h in zip(grads, helds)
            ]
            out = sum(parts[1:], parts[0]).astype(bf16)
            c = j * helds[0].shape[1]
            keep[0, :, c : c + size] = out[:rows]
            store[r, :, c : c + size] = out[rows:]
    at_chip_start(r, sends)


def back(coord, grads, weights):
    length = grads[0].shape[1]
    rows = length // 2
    model = sum(p.shape[0] * p.shape[1] for p in arrays(weights[0]))
    outs, out_specs = partial_outs(rows, model)
    return chip_kernel(
        functools.partial(back_body, tuple(columns_of(w) for w in weights)),
        [coord, *grads, *arrays(*weights)],
        [SMEM] + [by_chip(g.shape[1:]) for g in grads] + [ANY] * len(arrays(*weights)),
        outs,
        out_specs,
        [held_weight(w) for w in weights]
        + [pltpu.VMEM((4, rows, model), bf16)],
        40,
        8 * length * model * sum(g.shape[2] for g in grads),
    )


def attend_back_body(c_o, coord, mask, s, hat, scale, scores, q, k, v, *refs):
    acts, refs = refs[:10], refs[10:]
    wo, refs = refs[: len(c_o)], refs[len(c_o) :]
    gqk_out, gv_out, gs_out, held, held_o, dg, gr, sems = refs
    load, r = Loader(sems), pl.program_id(0)
    w1 = load.weight(wo, c_o, held_o, coord)
    chips = load.tokens(acts, held)

    @pl.when(r == 0)
    def _():
        start(*w1, *chips[0], *chips[1], *chips[2], *chips[3])
        wait(*w1)

    at_chip(r, chips)
    dg[...] = dot(rows_of(held, r), flat(held_o), NN)
    rows, step = dg.shape[0], 16

    def chunk(i, carry):
        at = pl.ds(pl.multiple_of(i * step, step), step)
        e, x, v_s = dg[at, :], hat[0, at, :], s[0, at, :]
        gate = 1.0 / (1.0 + jnp.exp(-v_s))
        silu = v_s * gate
        gs_out[0, at, :] = (e * x * (gate + silu * (1.0 - gate))).astype(bf16)
        f = e * silu
        f = f - jnp.mean(f, axis=-1, keepdims=True) - x * jnp.mean(f * x, axis=-1, keepdims=True)
        gr[at, :] = (f * scale[0, at, :1]).astype(bf16)
        return carry

    lax.fori_loop(0, rows // step, chunk, 0)
    grad_retained = gr[...]
    gv_out[0] = dot(scores[0], grad_retained, TN).astype(bf16)
    raw = (dot(grad_retained, v[0], NT) * mask[0]).astype(bf16)
    size = q.shape[2]
    gqk_out[0, :, :size] = dot(raw, k[0], NN).astype(bf16)
    gqk_out[0, :, size:] = dot(raw, q[0], TN).astype(bf16)


def attend_back(coord, mask, s, hat, scale, scores, q, k, v, acts, wo):
    length, n = s.shape[1:]
    model = acts[0].shape[1]
    blocks = [mask, s, hat, scale, scores, q, k, v]
    outs = [struct((4, length, 2 * q.shape[2]), bf16)] + [struct((4, length, n), bf16)] * 2
    return chip_kernel(
        functools.partial(attend_back_body, columns_of(wo)),
        [coord, *blocks, *acts, *arrays(wo)],
        [SMEM] + [by_chip(b.shape[1:]) for b in blocks] + [ANY] * (10 + len(arrays(wo))),
        outs,
        [by_chip(o.shape[1:]) for o in outs],
        [
            held_tokens(acts),
            held_weight(wo),
            pltpu.VMEM((length, n), f32),
            pltpu.VMEM((length, n), bf16),
        ],
        20,
        12 * length * model * n,
    )


def weight_grad_body(count, coord, *refs):
    grads, acts, refs = refs[:count], refs[count : count + 10], refs[count + 10 :]
    outs, held, sems = refs[: 2 * count], refs[2 * count], refs[-1]
    load, i = Loader(sems), pl.program_id(0)
    chips = load.tokens(acts, held)

    @pl.when(i == 0)
    def _():
        for c in chips:
            start(*c)
        for c in chips:
            wait(*c)

    width = held.shape[2] // 8
    y = coord[1] ^ jnp.where(i < 4, 1, 0)
    j = i % 4
    zh = coord[0] ^ jnp.where(j < 2, 1, 0)
    column = ((zh * 2 + j % 2) * 2 + y) * width
    x = held[:, :, pl.ds(pl.multiple_of(column, width), width)]
    x = x.reshape(x.shape[0] * x.shape[1], width).T
    for n in range(count):
        g = grads[n][...]
        out = dot(x, g.reshape(g.shape[0] * g.shape[1], g.shape[2]), NN).astype(bf16)
        pl.when(i < 4)(functools.partial(store_block, outs[2 * n], out))
        pl.when(i >= 4)(functools.partial(store_block, outs[2 * n + 1], out))


def store_block(ref, value):
    ref[0] = value


def weight_grads(coord, acts, grads):
    rows, model = acts[0].shape
    outs, out_specs = [], []
    for g in grads:
        shape = (4, model // 8, g.shape[2])
        outs += [struct(shape, bf16)] * 2
        out_specs += [
            pl.BlockSpec((1,) + shape[1:], lambda i: (jnp.minimum(i, 3), 0, 0)),
            pl.BlockSpec((1,) + shape[1:], lambda i: (jnp.maximum(i - 4, 0), 0, 0)),
        ]
    width = sum(g.shape[2] for g in grads)
    moved = sum(a.size * 2 for a in acts) + sum(g.size * 2 for g in grads) + 2 * model * width
    got = pl.pallas_call(
        functools.partial(weight_grad_body, len(grads)),
        grid=(8,),
        in_specs=[SMEM] + [pl.BlockSpec(memory_space=pltpu.VMEM)] * len(grads) + [ANY] * 10,
        out_specs=out_specs,
        out_shape=outs,
        scratch_shapes=[held_tokens(acts), pltpu.SemaphoreType.DMA((10,))],
        compiler_params=pltpu.CompilerParams(
            dimension_semantics=("arbitrary",), vmem_limit_bytes=VMEM_LIMIT
        ),
        cost_estimate=pl.CostEstimate(
            flops=16 * rows * model * width, bytes_accessed=moved, transcendentals=0
        ),
    )(coord, *grads, *acts)
    return [(got[2 * i], got[2 * i + 1]) for i in range(len(grads))]


def sum_everywhere(a):
    for axis in ("tensor",) + SPREAD:
        if lax.axis_size(axis) == 2:
            a = a + swap(a, axis)
        else:
            a = lax.psum(a, axis)
    return a


def local(
    tokens,
    segments,
    decay,
    norm1_gain,
    w_query,
    w_key,
    w_value,
    w_swish,
    w_out,
    norm2_gain,
    w_up,
    w_gate,
    w_down,
    cotangent,
):
    quarter = 2 * lax.axis_index("zl") + lax.axis_index("x")
    core = lax.axis_index("tensor")
    length = segments.shape[0]
    rows_each = tokens.shape[0]
    key_size = w_query.shape[1] // 4
    value_size = w_value.shape[1] // 4
    rate = take(decay, quarter, 0)

    rows_q, width = w_query.shape[0], value_size
    if lax.axis_size("zh") == 2:
        coord = jnp.stack([lax.axis_index("zh"), lax.axis_index("y")]).astype(jnp.int32)
    else:
        coord = jnp.zeros((2,), jnp.int32)

    clock = Clock()
    at = clock.at
    rows_local = tokens.astype(f32)
    normed_local = layer_norm(rows_local, norm1_gain).astype(bf16)

    piece_qk = group_exchange(jnp.concatenate([by_quarter(w_query), by_quarter(w_key)], 2))
    parts = jnp.concatenate([by_quarter(w_value), by_quarter(w_swish), by_quarter(w_out.T)], 2)
    clock.done(piece_qk)
    far_qk, near_qk = far_half(piece_qk, "zh_qk"), swap(piece_qk, "y", "ny_qk")
    piece_r = group_exchange(at(parts))

    def third(piece, k, count=1):
        return piece[:, :, k * width : (k + count) * width]

    clock.done(far_qk, near_qk, piece_r)
    far_y_qk = swap(at(far_qk), "y", "fy_qk")
    far_value = far_half(at(third(piece_r, 0)), "zh_value")
    near_r = swap(at(piece_r), "y", "ny_r")
    gather = Gather(clock, normed_local, "normed")
    segments = at(segments)
    seg_x = jnp.stack([segments, swap(segments, "x")])
    segs = jnp.concatenate([seg_x, swap(seg_x, "zl")])
    segs = jnp.where(core == 0, segs, jnp.roll(segs, length // 2, 1))
    position = (jnp.arange(length, dtype=jnp.int32) + core * rows_each) % length
    offset = position[:, None] - position[None, :]
    allowed = (offset >= 0)[None] & (segs[:, :, None] == segs[:, None, :])
    distance = jnp.maximum(offset, 0).astype(f32)
    decay_mask = jnp.where(allowed, jnp.exp(-rate * distance)[None], 0.0)

    clock.done(far_value, far_y_qk, *gather.first)
    far_swish = far_half(at(third(piece_r, 1)), "zh_swish")
    far_y_value = swap(at(far_value), "y", "fy_value")
    normed = gather.finish(clock)
    parts = jnp.concatenate([by_quarter(w_up), by_quarter(w_gate), by_quarter(w_down.T)], 2)
    piece_f = group_exchange(at(parts))

    clock.done(far_swish, far_y_value, piece_f, near_r, *normed)
    far_out = far_half(at(third(piece_r, 2)), "zh_out")
    far_y_swish = swap(at(far_swish), "y", "fy_swish")
    gather = Gather(clock, cotangent, "cot")
    near_f = swap(at(piece_f), "y", "ny_f")
    full_qk = whole_weight(piece_qk, near_qk, far_qk, far_y_qk, 0, width)
    full_value = whole_weight(piece_r, near_r, far_value, far_y_value, 0, width)
    query, key, values, scores, hat, scale = attend(
        at(coord), decay_mask, normed, full_qk, full_value, key_size
    )

    clock.done(query, far_out, far_y_swish, *gather.first)
    far_upgate = far_half(at(third(piece_f, 0, 2)), "zh_upgate")
    far_y_out = swap(at(far_out), "y", "fy_out")
    grad_rows = gather.finish(clock)
    full_swish = whole_weight(piece_r, near_r, far_swish, far_y_swish, width, width)
    full_out = whole_weight(piece_r, near_r, far_out, far_y_out, 2 * width, width)
    clock.done(far_y_out, *grad_rows)
    swish_in, gated, *partial = branch(at(coord), hat, normed, full_swish, full_out)
    scatter = Scatter(*partial, "branch")
    scatter.relay(clock)
    clock.done(scatter.diag)
    scatter.send(clock)
    middle = rows_local + scatter.finish()

    clock.done(far_upgate, near_f, *scatter.last)
    far_down = far_half(at(third(piece_f, 2)), "zh_down")
    far_y_upgate = swap(at(far_upgate), "y", "fy_upgate")
    gather = Gather(clock, layer_norm(middle, norm2_gain).astype(bf16), "two")
    clock.done(far_down, *gather.first)
    far_y_down = swap(at(far_down), "y", "fy_down")
    normed_two = gather.finish(clock)
    full_upgate = whole_weight(piece_f, near_f, far_upgate, far_y_upgate, 0, 2 * width)
    full_down = whole_weight(piece_f, near_f, far_down, far_y_down, 2 * width, width)
    hidden, grad_up_rows, grad_gate_rows, *partial = feed_forward(
        coord, normed_two, grad_rows, full_upgate, full_down
    )

    scatter = Scatter(*partial, "back_two")
    clock.done(scatter.diag)
    scatter.relay(clock)
    g_up, g_gate = weight_grads(at(coord), normed_two, [grad_up_rows, grad_gate_rows])
    clock.done(*scatter.second, g_up[0])
    scatter.send(clock)
    y_up = send_y(at(g_up[0]))
    (g_down,) = weight_grads(at(coord), grad_rows, [hidden])
    back_two_local = scatter.finish()
    _, norm_two_pull = jax.vjp(layer_norm, middle, norm2_gain)
    grad_mid_norm, grad_norm2_local = norm_two_pull(back_two_local)
    grad_middle = cotangent.astype(f32) + grad_mid_norm
    grad_branch_local = grad_middle.astype(bf16)

    clock.done(y_up, g_down[0], grad_branch_local)
    gather = Gather(clock, grad_branch_local, "gb")
    y_gate = send_y(at(g_gate[0]))
    up = scatter_zh(*scatter_y(g_up[1], at(y_up)), "zh_gup")
    feed = Scatter(*back(at(coord), [hidden], [full_down]), "feed")
    clock.done(y_gate, up, feed.diag, feed.rest, *gather.first)
    grad_branch = gather.finish(clock)
    y_down = send_y(at(g_down[0]))
    gate = scatter_zh(*scatter_y(g_gate[1], at(y_gate)), "zh_ggate")

    clock.done(*grad_branch)
    feed.relay(clock)
    (g_out,) = weight_grads(at(coord), grad_branch, [gated])
    clock.done(g_out[0], gate, y_down, *feed.second)
    feed.send(clock)
    y_out = send_y(at(g_out[0]))
    down = scatter_zh(*scatter_y(g_down[1], at(y_down)), "zh_gdown")
    grad_qk, grad_values, grad_swish_in = attend_back(
        at(coord),
        decay_mask,
        swish_in,
        hat,
        scale,
        scores,
        query,
        key,
        values,
        grad_branch,
        full_out,
    )
    clock.done(grad_qk, down, y_out, *feed.last)
    mixed = (middle + feed.finish()).astype(bf16)
    out = scatter_zh(*scatter_y(g_out[1], at(y_out)), "zh_gout")
    grad_ff = group_exchange(at(jnp.concatenate([up, gate, down], 2)))
    (g_swish,) = weight_grads(at(coord), normed, [grad_swish_in])
    clock.done(g_swish[0])
    y_swish = send_y(at(g_swish[0]))
    g_value, g_qk = weight_grads(at(coord), normed, [grad_values, grad_qk])
    clock.done(g_value[0], out, y_swish, grad_ff)
    y_value = send_y(at(g_value[0]))
    swish = scatter_zh(*scatter_y(g_swish[1], at(y_swish)), "zh_gswish")
    partial = back(
        at(coord), [grad_qk, grad_values, grad_swish_in], [full_qk, full_value, full_swish]
    )
    scatter = Scatter(*partial, "back_one")
    scatter.relay(clock)
    clock.done(y_value, swish, *scatter.second)
    y_qk = send_y(at(g_qk[0]))
    value = scatter_zh(*scatter_y(g_value[1], at(y_value)), "zh_gvalue")
    scatter.send(clock)
    back_one_local = scatter.finish()
    clock.done(y_qk, value, *scatter.last)
    grad_qk = scatter_zh(*scatter_y(g_qk[1], at(y_qk)), "zh_gqk")
    grad_r = group_exchange(at(jnp.concatenate([out, swish, value], 2)))
    grad_qk = group_exchange(after(grad_qk, grad_r))

    def columns(g):
        return g.transpose(1, 0, 2).reshape(rows_q, -1).astype(f32)

    def rows(g):
        return g.transpose(0, 2, 1).reshape(-1, rows_q).astype(f32)

    grad_up, grad_gate = columns(grad_ff[:, :, :width]), columns(grad_ff[:, :, width : 2 * width])
    grad_down = rows(grad_ff[:, :, 2 * width :])
    grad_query, grad_key = columns(grad_qk[:, :, :key_size]), columns(grad_qk[:, :, key_size:])
    grad_out, grad_swish = rows(grad_r[:, :, :width]), columns(grad_r[:, :, width : 2 * width])
    grad_value = columns(grad_r[:, :, 2 * width :])

    _, norm_one_pull = jax.vjp(layer_norm, rows_local, norm1_gain)
    grad_tok_norm, grad_norm1_local = norm_one_pull(back_one_local)
    grad_tokens = grad_middle + grad_tok_norm
    grad_norm1, grad_norm2 = sum_everywhere(jnp.stack([grad_norm1_local, grad_norm2_local]))
    return (
        mixed,
        grad_tokens,
        grad_norm1,
        grad_query,
        grad_key,
        grad_value,
        grad_swish,
        grad_out,
        grad_norm2,
        grad_up,
        grad_gate,
        grad_down,
    )


def solution(mesh):
    dp, tensor = mesh.shape["dp"], mesh.shape["tensor"]
    grid = Mesh(mesh.devices.reshape(dp // 8, 2, 2, 2, tensor), SPREAD + ("tensor",))
    rows = P(SPREAD + ("tensor",), None)
    rows_split = P(SPREAD, "tensor")
    columns_split = P("tensor", SPREAD)
    return jax.shard_map(
        local,
        mesh=grid,
        in_specs=(
            rows,
            P(SPREAD),
            P("tensor"),
            P(),
            rows_split,
            rows_split,
            rows_split,
            rows_split,
            columns_split,
            P(),
            rows_split,
            rows_split,
            columns_split,
            rows,
        ),
        out_specs=(
            rows,
            rows,
            P(),
            rows_split,
            rows_split,
            rows_split,
            rows_split,
            columns_split,
            P(),
            rows_split,
            rows_split,
            columns_split,
        ),
        check_vma=False,
    )
```

time: 956 us -> 759 us (0.79)
  Pallas kernels: 0 us -> 182 us
  matrix products: 125 us -> 0 us
  other arithmetic: 140 us -> 68.2 us
  waiting for transfers between devices: 413 us -> 343 us
  local copies, waits for them, and re-layouts: 107 us -> 45.2 us
  starting transfers between devices: 158 us -> 111 us
    pallas_call x0 -> x11, Pallas kernels: none -> 182 us  [the longest x6 117 us: chip_kernel(): pl.pallas_call(body, grid=(4,), in_specs=specs, out_specs=out_specs, out_...]
    dot_general x27 -> x0, matrix products: 125 us -> none  [the longest x7 47.3 us: right_product(): lax.dot_general(left, right, (((1,), (1,)), ((), ())), preferred_element_...]
    another operation x49 -> x10, other arithmetic: 54.1 us -> 2.26 us  [the longest x22 29.9 us: gather_tokens(): return jnp.stack([jnp.stack([p, swap(p, 'tensor')]) for p in pieces])]
    all_to_all x14 -> x6, waiting for transfers between devices: 51.6 us -> 8.25 us  [group_exchange(): return lax.all_to_all(parts, GROUP, 0, 0, tiled=True)]
    all_to_all x14 -> x6, starting transfers between devices: 58.7 us -> 26.4 us  [group_exchange(): return lax.all_to_all(parts, GROUP, 0, 0, tiled=True)]
    ppermute x111 -> x96, waiting for transfers between devices: 361 us -> 335 us  [swap(): return lax.ppermute(a, axis, [(0, 1), (1, 0)])]
    reshape x13 -> x8, local copies, waits for them, and re-layouts: 27.3 us -> 3.41 us  [by_quarter(): return w.reshape(rows, 4, cols // 4).transpose(1, 0, 2)]
    squeeze x18 -> x0, local copies, waits for them, and re-layouts: 19.4 us -> none  [the longest x14 13.9 us: take(): return lax.dynamic_index_in_dim(a, index, dim, keepdims=False)]
  transfers between devices with their start and end apart: 125 -> 102, of which waited for: 46 -> 45; matrix products, arithmetic and copies ran while one was open for 33% -> 11% of each run, Pallas kernels for 0% -> 15%
where the time goes in v2:
time: 759 us; the launch traced here: 753 us
  waiting for transfers between devices  343 us (45%)
  Pallas kernels  182 us (24%)
  starting transfers between devices  111 us (15%)
  other arithmetic  68.2 us (9%)
  local copies, waits for them, and re-layouts  45.2 us (6%)
    ppermute x96, waiting for transfers between devices, swap(): return lax.ppermute(a, axis, [(0, 1), (1, 0)])  335 us
    pallas_call x6, Pallas kernels, chip_kernel(): pl.pallas_call(body, grid=(4,), in_specs=specs, out_specs=out_specs, out_...  117 us
    ppermute x96, starting transfers between devices, swap(): return lax.ppermute(a, axis, [(0, 1), (1, 0)])  85 us
    pallas_call x5, Pallas kernels, weight_grads(): pl.pallas_call(functools.partial(weight_grad_body, len(grads)), grid=(8,)...  65 us
    all_to_all x6, starting transfers between devices, group_exchange(): return lax.all_to_all(parts, GROUP, 0, 0, tiled=True)  26.4 us
    convert_element_type x18, other arithmetic, add(): return (a.astype(f32) + b.astype(f32)).astype(bf16)  21.3 us
    unnamed x160, local copies, waits for them, and re-layouts  19.7 us
  transfers between devices with their start and end apart: 102, of which 45 were waited for; matrix products, arithmetic and copies ran while one was open for 11% of the time, Pallas kernels for 15%

profile of v2, /device:TPU:0, one launch (start us, length us, event | category | flops | bytes accessed | tf_op | source)
XLA Modules:
  0.0 752.8 jit_solution(6513045215260931841)
XLA Ops:
  4.1 5.4 all-to-all-start
  12.3 5.2 all-to-all-done.refs_10_.refs_3_
  17.5 3.6 all-to-all-start.1
  27.1 7.2 collective-permute-done.1.refs_11_.refs_4_
  35.2 13.5 %collective-permute-done.refs_12_.refs_5_ = bf16[4,128,512]{2,1,0:T(8,128)(2,1)} collective-permute-done((bf16[4,128,512]{2,1,0:T(8,128)(2,1)S(1)}, bf16[4,128,512]{2,1,0:T(8,128)(2,1)}, u32[]{:S(2)}, u32[]{:S(2)}) %collective-permute-start) | collective-permute-done | bytes 524320 | tf_op jit(solution)/shard_map/zh_qk/ppermute | solution.py:37
  67.1 14.6 %collective-permute-done.2.refs_16_.refs_9_ = bf16[4,128,512]{2,1,0:T(8,128)(2,1)} collective-permute-done((bf16[4,128,512]{2,1,0:T(8,128)(2,1)}, bf16[4,128,512]{2,1,0:T(8,128)(2,1)}, u32[]{:S(2)}, u32[]{:S(2)}) %collective-permute-start.2) | collective-permute-done | bytes 524320 | tf_op jit(solution)/shard_map/zh_value/ppermute | solution.py:37
  82.5 4.5 all-to-all-start.2
  90.7 13.8 %collective-permute-done.17 = s32[384]{0:T(512)S(1)} collective-permute-done((s32[384]{0:T(512)S(1)}, s32[384]{0:T(512)S(1)}, u32[]{:S(2)}, u32[]{:S(2)}) %collective-permute-start.17) | collective-permute-done | bytes 1568 | tf_op jit(solution)/shard_map/move/ppermute | solution.py:37
  111.6 7.5 %collective-permute-done.18 = s32[2,384]{1,0:T(2,128)S(1)} collective-permute-done((s32[2,384]{1,0:T(2,128)S(1)}, s32[2,384]{1,0:T(2,128)S(1)}, u32[]{:S(2)}, u32[]{:S(2)}) %collective-permute-start.18) | collective-permute-done | bytes 3104 | tf_op jit(solution)/shard_map/move/ppermute | solution.py:37
  125.4 18.6 %collective-permute-done.6.refs_12_.refs_13_ = bf16[4,128,512]{2,1,0:T(8,128)(2,1)} collective-permute-done((bf16[4,128,512]{2,1,0:T(8,128)(2,1)}, bf16[4,128,512]{2,1,0:T(8,128)(2,1)}, u32[]{:S(2)}, u32[]{:S(2)}) %collective-permute-start.6) | collective-permute-done | bytes 524320 | tf_op jit(solution)/shard_map/zh_swish/ppermute | solution.py:37
  151.9 3.4 collective-permute-start.16
  156.8 23.4 %shard_map.229 = (bf16[4,384,256]{2,1,0:T(8,128)(2,1)}, bf16[4,384,256]{2,1,0:T(8,128)(2,1)}, bf16[4,384,512]{2,1,0:T(8,128)(2,1)}, bf16[4,384,384]{2,1,0:T(8,12...) custom-call(s32[2]{0:T(128)} %pad_add_fusion.2.coord, f32[4,384,384]{2,1,0:T(8,128)} %and_select_fusion.mask, ...), custom_call_target="tpu_custom_call" | custom-call | flops 6442450944 | bytes 23199752 | tf_op jit(solution)/shard_map/pallas_call | solution.py:237
  185.7 6.7 collective-permute-done.26.refs_16_.refs_7_
  193.6 4.4 collective-permute-done.22.refs_17_.refs_13_
  200.0 15.7 %shard_map.230 = (f32[4,384,512]{2,1,0:T(8,128)}, bf16[4,384,512]{2,1,0:T(8,128)(2,1)}, bf16[3,192,2048]{2,1,0:T(8,128)(2,1)}, bf16[192,2048]{1,0:T(8,128)(2,1)}, bf16[4,192,2048]{2,1,0:T(8,128)(2,1)}) custom-call(s32[2]{0:T(128)} %pad_add_fusion.2.coord, f32[4,384,512]{2,1,0:T(8,128)} %get-tuple-element.143.hat, ...), custom_call_target="tpu_custom_call" | custom-call | flops 6442450944 | bytes 28835848 | tf_op jit(solution)/shard_map/pallas_call | solution.py:237
  216.3 5.4 collective-permute-done.31
  226.1 8.2 %collective-permute-done.32 = bf16[96,2048]{1,0:T(8,128)(2,1)S(1)} collective-permute-done((bf16[96,2048]{1,0:T(8,128)(2,1)S(1)}, bf16[96,2048]{1,0:T(8,128)(2,1)S(1)}, u32[]{:S(2)}, u32[]{:S(2)}) %collective-permute-start.32) | collective-permute-done | bytes 393248 | tf_op jit(solution)/shard_map/branch_dz/ppermute | solution.py:37
  243.5 24.8 %collective-permute-done.35 = bf16[192,2048]{1,0:T(8,128)(2,1)S(1)} collective-permute-done((bf16[192,2048]{1,0:T(8,128)(2,1)S(1)}, bf16[192,2048]{1,0:T(8,128)(2,1)S(1)}, u32[]{:S(2)}, u32[]{:S(2)}) %collective-permute-start.35) | collective-permute-done | bytes 786464 | tf_op jit(solution)/shard_map/branch_z/ppermute | solution.py:37
  270.0 4.3 collective-permute-done.37.refs_21_.refs_25_.refs_2_
  274.3 13.7 %collective-permute-done.36.refs_22_ = bf16[4,128,1024]{2,1,0:T(8,128)(2,1)S(1)} collective-permute-done((bf16[4,128,1024]{2,1,0:T(8,128)(2,1)S(1)}, bf16[4,128,1024]{2,1,0:T(8,128)(2,1)S(1)}, u32[]{:S(2)}, u32[]{:S(2)}) %collective-permute-start.36) | collective-permute-done | bytes 1048608 | tf_op jit(solution)/shard_map/zh_upgate/ppermute | solution.py:37
  293.4 24.2 %collective-permute-done.40.refs_26_.refs_3_ = bf16[4,128,512]{2,1,0:T(8,128)(2,1)S(1)} collective-permute-done((bf16[4,128,512]{2,1,0:T(8,128)(2,1)S(1)}, bf16[4,128,512]{2,1,0:T(8,128)(2,1)S(1)}, u32[]{:S(2)}, u32[]{:S(2)}) %collective-permute-start.40) | collective-permute-done | bytes 524320 | tf_op jit(solution)/shard_map/zh_down/ppermute | solution.py:37
  320.6 7.9 %collective-permute-done.44.refs_6_.refs_8_ = bf16[96,2048]{1,0:T(8,128)(2,1)S(1)} collective-permute-done((bf16[96,2048]{1,0:T(8,128)(2,1)S(1)}, bf16[96,2048]{1,0:T(8,128)(2,1)S(1)}, u32[]{:S(2)}, u32[]{:S(2)}) %collective-permute-start.44) | collective-permute-done | bytes 393248 | tf_op jit(solution)/shard_map/two_dx/ppermute | solution.py:37
  329.9 4.0 collective-permute-done.49.refs_27_.refs_4_
  335.9 28.1 %shard_map.231 = (bf16[4,384,512]{2,1,0:T(8,128)(2,1)}, bf16[4,384,512]{2,1,0:T(8,128)(2,1)}, bf16[4,384,512]{2,1,0:T(8,128)(2,1)}, bf16[3,192,2048]{2,1,0:T(8,1...) custom-call(s32[2]{0:T(128)} %pad_add_fusion.2.coord, bf16[192,2048]{1,0:T(8,128)(2,1)} %copy-done.25, ...), custom_call_target="tpu_custom_call" | custom-call | flops 16106127360 | bytes 33030152 | tf_op jit(solution)/shard_map/pallas_call | solution.py:237
  370.9 16.2 %shard_map.232 = (bf16[4,256,512]{2,1,0:T(8,128)(2,1)}, bf16[4,256,512]{2,1,0:T(8,128)(2,1)}, bf16[4,256,512]{2,1,0:T(8,128)(2,1)}, bf16[4,256,512]{2,1,0:T(8,128)(2,1)}) custom-call(s32[2]{0:T(128)} %pad_add_fusion.2.coord, bf16[4,384,512]{2,1,0:T(8,128)(2,1)} %get-tuple-element.162.refs_0_, bf16[4,384,512]{2,1,0:T(8,128)(2,1)} %get-tuple-element.163.refs_1_, ...), custom_call_target="tpu_custom_call" | custom-call | flops 6442450944 | bytes 13631488 | tf_op jit(solution)/shard_map/pallas_call | solution.py:666
  395.6 10.8 %shard_map.233 = (bf16[4,256,512]{2,1,0:T(8,128)(2,1)}, bf16[4,256,512]{2,1,0:T(8,128)(2,1)}) custom-call(s32[2]{0:T(128)} %pad_add_fusion.2.coord, bf16[4,384,512]{2,1,0:T(8,128)(2,1)} %get-tuple-element.169.refs_0_, bf16[192,2048]{1,0:T(8,128)(2,1)} %refs_1_, bf16[192,2048]{1,0:T(8,128)(2,1)} %collective-permute-done.23.refs_11_.refs_2_, ...), custom_call_target="tpu_custom_call" | custom-call | flops 3221225472 | bytes 9961472 | tf_op jit(solution)/shard_map/pallas_call | solution.py:666
  406.4 5.0 collective-permute-done.56
  419.6 9.2 %shard_map.234 = (bf16[3,192,2048]{2,1,0:T(8,128)(2,1)}, bf16[192,2048]{1,0:T(8,128)(2,1)}, bf16[4,192,2048]{2,1,0:T(8,128)(2,1)}) custom-call(s32[2]{0:T(128)} %pad_add_fusion.2.coord, bf16[4,384,512]{2,1,0:T(8,128)(2,1)} %get-tuple-element.169.refs_0_, bf16[4,128,1536]{2,1,0:T(8,128)(2,1)} %all-to-all-done.2.refs_20_.refs_24_.refs_1_, ...), custom_call_target="tpu_custom_call" | custom-call | flops 3221225472 | bytes 12058632 | tf_op jit(solution)/shard_map/pallas_call | solution.py:237
  433.9 23.0 %collective-permute-done.61 = bf16[2,256,512]{2,1,0:T(8,128)(2,1)S(1)} collective-permute-done((bf16[2,256,512]{2,1,0:T(8,128)(2,1)S(1)}, bf16[2,256,512]{2,1,0:T(8,128)(2,1)S(1)}, u32[]{:S(2)}, u32[]{:S(2)}) %collective-permute-start.61) | collective-permute-done | bytes 524320 | tf_op jit(solution)/shard_map/zh_gup/ppermute | solution.py:37
  463.0 12.9 %collective-permute-done.59.refs_3_.refs_2_ = bf16[192,2048]{1,0:T(8,128)(2,1)S(1)} collective-permute-done((bf16[192,2048]{1,0:T(8,128)(2,1)S(1)}, bf16[192,2048]{1,0:T(8,128)(2,1)S(1)}, u32[]{:S(2)}, u32[]{:S(2)}) %collective-permute-start.59) | collective-permute-done | bytes 786464 | tf_op jit(solution)/shard_map/gb_x/ppermute | solution.py:37
  477.3 8.5 %collective-permute-done.66.refs_7_.refs_6_ = bf16[96,2048]{1,0:T(8,128)(2,1)S(1)} collective-permute-done((bf16[96,2048]{1,0:T(8,128)(2,1)S(1)}, bf16[96,2048]{1,0:T(8,128)(2,1)S(1)}, u32[]{:S(2)}, u32[]{:S(2)}) %collective-permute-start.66) | collective-permute-done | bytes 393248 | tf_op jit(solution)/shard_map/gb_dx/ppermute | solution.py:37
  492.3 20.3 %collective-permute-done.70 = bf16[2,256,512]{2,1,0:T(8,128)(2,1)S(1)} collective-permute-done((bf16[2,256,512]{2,1,0:T(8,128)(2,1)S(1)}, bf16[2,256,512]{2,1,0:T(8,128)(2,1)S(1)}, u32[]{:S(2)}, u32[]{:S(2)}) %collective-permute-start.70) | collective-permute-done | bytes 524320 | tf_op jit(solution)/shard_map/zh_ggate/ppermute | solution.py:37
  512.8 10.9 %shard_map.235 = (bf16[4,256,512]{2,1,0:T(8,128)(2,1)}, bf16[4,256,512]{2,1,0:T(8,128)(2,1)}) custom-call(s32[2]{0:T(128)} %pad_add_fusion.2.coord, bf16[4,384,512]{2,1,0:T(8,128)(2,1)} %get-tuple-element.186.refs_0_, bf16[192,2048]{1,0:T(8,128)(2,1)} %copy-done.14, bf16[192,2048]{1,0:T(8,128)(2,1)} %copy-done.26, bf16[192,2048]{1,0:T(8,128)(2,1)} %copy-done.17, ...), custom_call_target="tpu_custom_call" | custom-call | flops 3221225472 | bytes 9961472 | tf_op jit(solution)/shard_map/pallas_call | solution.py:666
  538.3 23.6 %shard_map.236 = (bf16[4,384,512]{2,1,0:T(8,128)(2,1)}, bf16[4,384,512]{2,1,0:T(8,128)(2,1)}, bf16[4,384,512]{2,1,0:T(8,128)(2,1)}) custom-call(s32[2]{0:T(128)} %pad_add_fusion.2.coord, f32[4,384,384]{2,1,0:T(8,128)} %and_select_fusion.mask, f32[4,384,512]{2,1,0:T(8,128)} %get-tuple-element.196.s, f32[4,384,512]{2,1,0:T(8,128)} %get-tuple-element.143.hat, ...), custom_call_target="tpu_custom_call" | custom-call | flops 4831838208 | bytes 28966920 | tf_op jit(solution)/shard_map/pallas_call | solution.py:237
  565.0 4.5 all-to-all-start.3
  569.5 10.9 %shard_map.237 = (bf16[4,256,512]{2,1,0:T(8,128)(2,1)}, bf16[4,256,512]{2,1,0:T(8,128)(2,1)}) custom-call(s32[2]{0:T(128)} %pad_add_fusion.2.coord, bf16[4,384,512]{2,1,0:T(8,128)(2,1)} %get-tuple-element.206.refs_0_.refs_2_, bf16[192,2048]{1,0:T(8,128)(2,1)} %fusion.6.refs_0_.refs_1_.refs_2_, ...), custom_call_target="tpu_custom_call" | custom-call | flops 3221225472 | bytes 9961472 | tf_op jit(solution)/shard_map/pallas_call | solution.py:666
  583.1 16.2 %shard_map.238 = (bf16[4,256,512]{2,1,0:T(8,128)(2,1)}, bf16[4,256,512]{2,1,0:T(8,128)(2,1)}, bf16[4,256,512]{2,1,0:T(8,128)(2,1)}, bf16[4,256,512]{2,1,0:T(8,128)(2,1)}) custom-call(s32[2]{0:T(128)} %pad_add_fusion.2.coord, bf16[4,384,512]{2,1,0:T(8,128)(2,1)} %get-tuple-element.209.refs_0_.refs_1_, ...), custom_call_target="tpu_custom_call" | custom-call | flops 6442450944 | bytes 13631488 | tf_op jit(solution)/shard_map/pallas_call | solution.py:666
  599.3 7.9 %collective-permute-done.78 = bf16[2,256,512]{2,1,0:T(8,128)(2,1)S(1)} collective-permute-done((bf16[2,256,512]{2,1,0:T(8,128)(2,1)S(1)}, bf16[2,256,512]{2,1,0:T(8,128)(2,1)S(1)}, u32[]{:S(2)}, u32[]{:S(2)}) %collective-permute-start.78) | collective-permute-done | bytes 524320 | tf_op jit(solution)/shard_map/zh_gout/ppermute | solution.py:37
  608.6 16.9 %shard_map.239 = (bf16[3,192,2048]{2,1,0:T(8,128)(2,1)}, bf16[192,2048]{1,0:T(8,128)(2,1)}, bf16[4,192,2048]{2,1,0:T(8,128)(2,1)}) custom-call(s32[2]{0:T(128)} %pad_add_fusion.2.coord, bf16[4,384,512]{2,1,0:T(8,128)(2,1)} %get-tuple-element.201.refs_1_.refs_0_, bf16[4,384,512]{2,1,0:T(8,128)(2,1)} %get-tuple-element.209.refs_0_.refs_1_, ...), custom_call_target="tpu_custom_call" | custom-call | flops 9663676416 | bytes 21495816 | tf_op jit(solution)/shard_map/pallas_call | solution.py:237
  634.8 18.2 %collective-permute-done.82 = bf16[2,256,512]{2,1,0:T(8,128)(2,1)S(1)} collective-permute-done((bf16[2,256,512]{2,1,0:T(8,128)(2,1)S(1)}, bf16[2,256,512]{2,1,0:T(8,128)(2,1)S(1)}, u32[]{:S(2)}, u32[]{:S(2)}) %collective-permute-start.82) | collective-permute-done | bytes 524320 | tf_op jit(solution)/shard_map/zh_gswish/ppermute | solution.py:37
  662.2 18.3 %collective-permute-done.94 = bf16[2,256,512]{2,1,0:T(8,128)(2,1)S(1)} collective-permute-done((bf16[2,256,512]{2,1,0:T(8,128)(2,1)S(1)}, bf16[2,256,512]{2,1,0:T(8,128)(2,1)S(1)}, u32[]{:S(2)}, u32[]{:S(2)}) %collective-permute-start.94) | collective-permute-done | bytes 524320 | tf_op jit(solution)/shard_map/zh_gvalue/ppermute | solution.py:37
  681.9 6.5 collective-permute-done.87
  691.2 4.4 all-to-all-start.4
  695.5 3.6 fusion.17
  704.1 9.9 %collective-permute-done.89 = f32[2,2048]{1,0:T(2,128)S(1)} collective-permute-done((f32[2,2048]{1,0:T(2,128)S(1)}, f32[2,2048]{1,0:T(2,128)S(1)}, u32[]{:S(2)}, u32[]{:S(2)}) %collective-permute-start.89) | collective-permute-done | bytes 16416 | tf_op jit(solution)/shard_map/move/ppermute | solution.py:37
  714.1 3.3 collective-permute-start.90
  734.4 4.1 all-to-all-start.5
  738.5 3.3 add_add_fusion.2
  (456 shorter events, 213.2 us)
Async XLA Ops:
  17.5 34.2 %all-to-all-start.1 = ((bf16[4,128,1536]{2,1,0:T(8,128)(2,1)}), bf16[4,128,1536]{2,1,0:T(8,128)(2,1)S(1)}, u32[]{:S(2)}, u32[]{:S(2)}) async-start(bf16[4,128,1536]{2,1,0:T(8,128)(2,1)} %pad_maximum_fusion), calls=%async_computation.1 | async-start | bytes 3145728 | tf_op jit(solution)/shard_map/all_to_all | solution.py:55
  23.2 25.4 %collective-permute-start = (bf16[4,128,512]{2,1,0:T(8,128)(2,1)S(1)}, bf16[4,128,512]{2,1,0:T(8,128)(2,1)}, u32[]{:S(2)}, u32[]{:S(2)}) collective-permute-start(bf16[4,128,512]{2,1,0:T(8,128)(2,1)S(1)} %all-to-all-done.refs_10_.refs_3_), channel_id=1, source_target_pairs={{0,16},{16,0},{1,17},{17,1},{2,18},{18,2},{3,19},{19,3},{4,20},{20... | collective-permute-start | bytes 1572872 | tf_op jit(solution)/shard_map/zh_qk/ppermute | solution.py:37
  51.7 30.8 %collective-permute-start.5 = (bf16[192,2048]{1,0:T(8,128)(2,1)}, bf16[192,2048]{1,0:T(8,128)(2,1)}, u32[]{:S(2)}, u32[]{:S(2)}) collective-permute-start(bf16[192,2048]{1,0:T(8,128)(2,1)} %fusion.6.refs_0_.refs_1_.refs_2_), channel_id=1, source_target_pairs={{0,8},{8,0},{1,9},{9,1},{2,10},{10,2},{3,11},{11,3},{4,12},{12,4},... | collective-permute-start | bytes 2359304 | tf_op jit(solution)/shard_map/normed_z/ppermute | solution.py:37
  54.8 27.6 %collective-permute-start.4 = (bf16[192,2048]{1,0:T(8,128)(2,1)}, bf16[192,2048]{1,0:T(8,128)(2,1)}, u32[]{:S(2)}, u32[]{:S(2)}) collective-permute-start(bf16[192,2048]{1,0:T(8,128)(2,1)} %fusion.6.refs_0_.refs_1_.refs_2_), channel_id=1, source_target_pairs={{0,2},{2,0},{1,3},{3,1},{4,6},{6,4},{5,7},{7,5},{8,10},{10,8},{9,1... | collective-permute-start | bytes 2359304 | tf_op jit(solution)/shard_map/normed_x/ppermute | solution.py:37
  82.5 64.3 %all-to-all-start.2 = ((bf16[4,128,1536]{2,1,0:T(8,128)(2,1)}), bf16[4,128,1536]{2,1,0:T(8,128)(2,1)}, u32[]{:S(2)}, u32[]{:S(2)}) async-start(bf16[4,128,1536]{2,1,0:T(8,128)(2,1)} %pad_maximum_fusion.1), calls=%async_computation.2 | async-start | bytes 3145728 | tf_op jit(solution)/shard_map/all_to_all | solution.py:55
  87.0 34.5 %collective-permute-start.9 = (bf16[192,2048]{1,0:T(8,128)(2,1)}, bf16[192,2048]{1,0:T(8,128)(2,1)}, u32[]{:S(2)}, u32[]{:S(2)}) collective-permute-start(bf16[192,2048]{1,0:T(8,128)(2,1)} %fusion.6.refs_0_.refs_1_.refs_2_), channel_id=1, source_target_pairs={{0,1},{1,0},{2,3},{3,2},{4,5},{5,4},{6,7},{7,6},{8,9},{9,8},{10,11... | collective-permute-start | bytes 2359304 | tf_op jit(solution)/shard_map/normed_c/ppermute | solution.py:37
  87.1 57.6 %collective-permute-start.8 = (bf16[4,128,1536]{2,1,0:T(8,128)(2,1)S(1)}, bf16[4,128,1536]{2,1,0:T(8,128)(2,1)}, u32[]{:S(2)}, u32[]{:S(2)}) collective-permute-start(bf16[4,128,1536]{2,1,0:T(8,128)(2,1)S(1)} %all-to-all-done.1.refs_14_.refs_10_.refs_7_.refs_11_), channel_id=1, source_target_pairs={{0,4},{4,0},{1,5},{5,1},{2,6},{6,2},{3,7},{7,3},{8,12},{12,8},{9,1... | collective-permute-start | bytes 4718600 | tf_op jit(solution)/shard_map/ny_r/ppermute | solution.py:37
  119.1 24.9 %collective-permute-start.6 = (bf16[4,128,512]{2,1,0:T(8,128)(2,1)}, bf16[4,128,512]{2,1,0:T(8,128)(2,1)}, u32[]{:S(2)}, u32[]{:S(2)}) collective-permute-start(bf16[4,128,512]{2,1,0:T(8,128)(2,1)} %get-tuple-element.127), channel_id=1, source_target_pairs={{0,16},{16,0},{1,17},{17,1},{2,18},{18,2},{3,19},{19,3},{4,20},{20... | collective-permute-start | bytes 1572872 | tf_op jit(solution)/shard_map/zh_swish/ppermute | solution.py:37
  146.7 33.5 %collective-permute-start.21 = (bf16[192,2048]{1,0:T(8,128)(2,1)S(1)}, bf16[192,2048]{1,0:T(8,128)(2,1)S(1)}, u32[]{:S(2)}, u32[]{:S(2)}) collective-permute-start(bf16[192,2048]{1,0:T(8,128)(2,1)S(1)} %copy-done.7), channel_id=1, source_target_pairs={{0,8},{8,0},{1,9},{9,1},{2,10},{10,2},{3,11},{11,3},{4,12},{12,4},... | collective-permute-start | bytes 2359304 | tf_op jit(solution)/shard_map/cot_z/ppermute | solution.py:37
  147.3 33.0 %collective-permute-start.20 = (bf16[192,2048]{1,0:T(8,128)(2,1)S(1)}, bf16[192,2048]{1,0:T(8,128)(2,1)S(1)}, u32[]{:S(2)}, u32[]{:S(2)}) collective-permute-start(bf16[192,2048]{1,0:T(8,128)(2,1)S(1)} %copy-done.7), channel_id=1, source_target_pairs={{0,2},{2,0},{1,3},{3,1},{4,6},{6,4},{5,7},{7,5},{8,10},{10,8},{9,1... | collective-permute-start | bytes 2359304 | tf_op jit(solution)/shard_map/cot_x/ppermute | solution.py:37
  151.9 32.3 %collective-permute-start.23 = (bf16[192,2048]{1,0:T(8,128)(2,1)S(1)}, bf16[192,2048]{1,0:T(8,128)(2,1)}, u32[]{:S(2)}, u32[]{:S(2)}) collective-permute-start(bf16[192,2048]{1,0:T(8,128)(2,1)S(1)} %copy-done.7), channel_id=1, source_target_pairs={{0,1},{1,0},{2,3},{3,2},{4,5},{5,4},{6,7},{7,6},{8,9},{9,8},{10,11... | collective-permute-start | bytes 2359304 | tf_op jit(solution)/shard_map/cot_c/ppermute | solution.py:37
  151.9 28.4 %collective-permute-start.16 = (bf16[4,128,512]{2,1,0:T(8,128)(2,1)}, bf16[4,128,512]{2,1,0:T(8,128)(2,1)S(1)}, u32[]{:S(2)}, u32[]{:S(2)}) collective-permute-start(bf16[4,128,512]{2,1,0:T(8,128)(2,1)} %get-tuple-element.133), channel_id=1, source_target_pairs={{0,16},{16,0},{1,17},{17,1},{2,18},{18,2},{3,19},{19,3},{4,20},{20... | collective-permute-start | bytes 1572872 | tf_op jit(solution)/shard_map/zh_out/ppermute | solution.py:37
  155.3 25.0 %collective-permute-start.19 = (bf16[4,128,512]{2,1,0:T(8,128)(2,1)}, bf16[4,128,512]{2,1,0:T(8,128)(2,1)}, u32[]{:S(2)}, u32[]{:S(2)}) collective-permute-start(bf16[4,128,512]{2,1,0:T(8,128)(2,1)} %collective-permute-done.6.refs_12_.refs_13_), channel_id=1, source_target_pairs={{0,4},{4,0},{1,5},{5,1},{2,6},{6,2},{3,7},{7,3},{8,12},{12,8},{9,1... | collective-permute-start | bytes 1572872 | tf_op jit(solution)/shard_map/fy_swish/ppermute | solution.py:37
  236.9 31.4 %collective-permute-start.35 = (bf16[192,2048]{1,0:T(8,128)(2,1)S(1)}, bf16[192,2048]{1,0:T(8,128)(2,1)S(1)}, u32[]{:S(2)}, u32[]{:S(2)}) collective-permute-start(bf16[192,2048]{1,0:T(8,128)(2,1)S(1)} %pad_maximum_fusion.5), channel_id=1, source_target_pairs={{0,8},{8,0},{1,9},{9,1},{2,10},{10,2},{3,11},{11,3},{4,12},{12,4},... | collective-permute-start | bytes 2359304 | tf_op jit(solution)/shard_map/branch_z/ppermute | solution.py:37
  237.8 30.5 %collective-permute-start.33 = (bf16[192,2048]{1,0:T(8,128)(2,1)S(1)}, bf16[192,2048]{1,0:T(8,128)(2,1)S(1)}, u32[]{:S(2)}, u32[]{:S(2)}) collective-permute-start(bf16[192,2048]{1,0:T(8,128)(2,1)S(1)} %pad_maximum_fusion.4), channel_id=1, source_target_pairs={{0,2},{2,0},{1,3},{3,1},{4,6},{6,4},{5,7},{7,5},{8,10},{10,8},{9,1... | collective-permute-start | bytes 2359304 | tf_op jit(solution)/shard_map/branch_x/ppermute | solution.py:37
  239.2 35.2 %collective-permute-start.37 = (bf16[4,128,1536]{2,1,0:T(8,128)(2,1)}, bf16[4,128,1536]{2,1,0:T(8,128)(2,1)S(1)}, u32[]{:S(2)}, u32[]{:S(2)}) collective-permute-start(bf16[4,128,1536]{2,1,0:T(8,128)(2,1)} %all-to-all-done.2.refs_20_.refs_24_.refs_1_), channel_id=1, source_target_pairs={{0,4},{4,0},{1,5},{5,1},{2,6},{6,2},{3,7},{7,3},{8,12},{12,8},{9,1... | collective-permute-start | bytes 4718600 | tf_op jit(solution)/shard_map/ny_f/ppermute | solution.py:37
  241.2 46.8 %collective-permute-start.36 = (bf16[4,128,1024]{2,1,0:T(8,128)(2,1)S(1)}, bf16[4,128,1024]{2,1,0:T(8,128)(2,1)S(1)}, u32[]{:S(2)}, u32[]{:S(2)}) collective-permute-start(bf16[4,128,1024]{2,1,0:T(8,128)(2,1)S(1)} %slice.498), channel_id=1, source_target_pairs={{0,16},{16,0},{1,17},{17,1},{2,18},{18,2},{3,19},{19,3},{4,20},{20... | collective-permute-start | bytes 3145736 | tf_op jit(solution)/shard_map/zh_upgate/ppermute | solution.py:37
  288.0 29.6 %collective-permute-start.41 = (bf16[192,2048]{1,0:T(8,128)(2,1)S(1)}, bf16[192,2048]{1,0:T(8,128)(2,1)S(1)}, u32[]{:S(2)}, u32[]{:S(2)}) collective-permute-start(bf16[192,2048]{1,0:T(8,128)(2,1)S(1)} %multiply_convert_fusion.refs_0_.refs_2_), channel_id=1, source_target_pairs={{0,8},{8,0},{1,9},{9,1},{2,10},{10,2},{3,11},{11,3},{4,12},{12,4},... | collective-permute-start | bytes 2359304 | tf_op jit(solution)/shard_map/two_z/ppermute | solution.py:37
  288.0 29.6 %collective-permute-start.39 = (bf16[192,2048]{1,0:T(8,128)(2,1)S(1)}, bf16[192,2048]{1,0:T(8,128)(2,1)S(1)}, u32[]{:S(2)}, u32[]{:S(2)}) collective-permute-start(bf16[192,2048]{1,0:T(8,128)(2,1)S(1)} %multiply_convert_fusion.refs_0_.refs_2_), channel_id=1, source_target_pairs={{0,2},{2,0},{1,3},{3,1},{4,6},{6,4},{5,7},{7,5},{8,10},{10,8},{9,1... | collective-permute-start | bytes 2359304 | tf_op jit(solution)/shard_map/two_x/ppermute | solution.py:37
  289.5 30.5 %collective-permute-start.48 = (bf16[4,128,1024]{2,1,0:T(8,128)(2,1)S(1)}, bf16[4,128,1024]{2,1,0:T(8,128)(2,1)S(1)}, u32[]{:S(2)}, u32[]{:S(2)}) collective-permute-start(bf16[4,128,1024]{2,1,0:T(8,128)(2,1)S(1)} %collective-permute-done.36.refs_22_), channel_id=1, source_target_pairs={{0,4},{4,0},{1,5},{5,1},{2,6},{6,2},{3,7},{7,3},{8,12},{12,8},{9,1... | collective-permute-start | bytes 3145736 | tf_op jit(solution)/shard_map/fy_upgate/ppermute | solution.py:37
  290.0 29.5 %collective-permute-start.38 = (bf16[192,2048]{1,0:T(8,128)(2,1)S(1)}, bf16[192,2048]{1,0:T(8,128)(2,1)S(1)}, u32[]{:S(2)}, u32[]{:S(2)}) collective-permute-start(bf16[192,2048]{1,0:T(8,128)(2,1)S(1)} %multiply_convert_fusion.refs_0_.refs_2_), channel_id=1, source_target_pairs={{0,1},{1,0},{2,3},{3,2},{4,5},{5,4},{6,7},{7,6},{8,9},{9,8},{10,11... | collective-permute-start | bytes 2359304 | tf_op jit(solution)/shard_map/two_c/ppermute | solution.py:37
  291.1 26.6 %collective-permute-start.40 = (bf16[4,128,512]{2,1,0:T(8,128)(2,1)S(1)}, bf16[4,128,512]{2,1,0:T(8,128)(2,1)S(1)}, u32[]{:S(2)}, u32[]{:S(2)}) collective-permute-start(bf16[4,128,512]{2,1,0:T(8,128)(2,1)S(1)} %slice.499), channel_id=1, source_target_pairs={{0,16},{16,0},{1,17},{17,1},{2,18},{18,2},{3,19},{19,3},{4,20},{20... | collective-permute-start | bytes 1572872 | tf_op jit(solution)/shard_map/zh_down/ppermute | solution.py:37
  428.8 47.1 %collective-permute-start.57 = (bf16[3,192,2048]{2,1,0:T(8,128)(2,1)}, bf16[3,192,2048]{2,1,0:T(8,128)(2,1)S(1)}, u32[]{:S(2)}, u32[]{:S(2)}) collective-permute-start(bf16[3,192,2048]{2,1,0:T(8,128)(2,1)} %get-tuple-element.176), channel_id=1, source_target_pairs={{0,1},{1,0},{2,3},{3,2},{4,5},{5,4},{6,7},{7,6},{8,9},{9,8},{10,11... | collective-permute-start | bytes 7077896 | tf_op jit(solution)/shard_map/feed_cr/ppermute | solution.py:37
  430.3 26.6 %collective-permute-start.61 = (bf16[2,256,512]{2,1,0:T(8,128)(2,1)S(1)}, bf16[2,256,512]{2,1,0:T(8,128)(2,1)S(1)}, u32[]{:S(2)}, u32[]{:S(2)}) collective-permute-start(bf16[2,256,512]{2,1,0:T(8,128)(2,1)S(1)} %add_convert_fusion.19), channel_id=1, source_target_pairs={{0,16},{16,0},{1,17},{17,1},{2,18},{18,2},{3,19},{19,3},{4,20},{20... | collective-permute-start | bytes 1572872 | tf_op jit(solution)/shard_map/zh_gup/ppermute | solution.py:37
  432.3 26.4 %collective-permute-start.62 = (bf16[192,2048]{1,0:T(8,128)(2,1)}, bf16[192,2048]{1,0:T(8,128)(2,1)S(1)}, u32[]{:S(2)}, u32[]{:S(2)}) collective-permute-start(bf16[192,2048]{1,0:T(8,128)(2,1)} %get-tuple-element.182), channel_id=1, source_target_pairs={{0,1},{1,0},{2,3},{3,2},{4,5},{5,4},{6,7},{7,6},{8,9},{9,8},{10,11... | collective-permute-start | bytes 2359304 | tf_op jit(solution)/shard_map/feed_cd/ppermute | solution.py:37
  432.5 43.5 %collective-permute-start.60 = (bf16[4,256,512]{2,1,0:T(8,128)(2,1)}, bf16[4,256,512]{2,1,0:T(8,128)(2,1)S(1)}, u32[]{:S(2)}, u32[]{:S(2)}) collective-permute-start(bf16[4,256,512]{2,1,0:T(8,128)(2,1)} %get-tuple-element.179), channel_id=1, source_target_pairs={{0,4},{4,0},{1,5},{5,1},{2,6},{6,2},{3,7},{7,3},{8,12},{12,8},{9,1... | collective-permute-start | bytes 3145736 | tf_op jit(solution)/shard_map/y_grad/ppermute | solution.py:37
  433.5 29.5 %collective-permute-start.63 = (bf16[192,2048]{1,0:T(8,128)(2,1)S(1)}, bf16[192,2048]{1,0:T(8,128)(2,1)S(1)}, u32[]{:S(2)}, u32[]{:S(2)}) collective-permute-start(bf16[192,2048]{1,0:T(8,128)(2,1)S(1)} %fusion.28.refs_1_.refs_0_), channel_id=1, source_target_pairs={{0,8},{8,0},{1,9},{9,1},{2,10},{10,2},{3,11},{11,3},{4,12},{12,4},... | collective-permute-start | bytes 2359304 | tf_op jit(solution)/shard_map/gb_z/ppermute | solution.py:37
  458.7 27.7 %collective-permute-start.58 = (bf16[192,2048]{1,0:T(8,128)(2,1)S(1)}, bf16[192,2048]{1,0:T(8,128)(2,1)S(1)}, u32[]{:S(2)}, u32[]{:S(2)}) collective-permute-start(bf16[192,2048]{1,0:T(8,128)(2,1)S(1)} %fusion.28.refs_1_.refs_0_), channel_id=1, source_target_pairs={{0,1},{1,0},{2,3},{3,2},{4,5},{5,4},{6,7},{7,6},{8,9},{9,8},{10,11... | collective-permute-start | bytes 2359304 | tf_op jit(solution)/shard_map/gb_c/ppermute | solution.py:37
  486.4 26.1 %collective-permute-start.70 = (bf16[2,256,512]{2,1,0:T(8,128)(2,1)S(1)}, bf16[2,256,512]{2,1,0:T(8,128)(2,1)S(1)}, u32[]{:S(2)}, u32[]{:S(2)}) collective-permute-start(bf16[2,256,512]{2,1,0:T(8,128)(2,1)S(1)} %add_convert_fusion.16), channel_id=1, source_target_pairs={{0,16},{16,0},{1,17},{17,1},{2,18},{18,2},{3,19},{19,3},{4,20},{20... | collective-permute-start | bytes 1572872 | tf_op jit(solution)/shard_map/zh_ggate/ppermute | solution.py:37
  487.5 36.2 %collective-permute-start.71 = (bf16[4,256,512]{2,1,0:T(8,128)(2,1)}, bf16[4,256,512]{2,1,0:T(8,128)(2,1)}, u32[]{:S(2)}, u32[]{:S(2)}) collective-permute-start(bf16[4,256,512]{2,1,0:T(8,128)(2,1)} %get-tuple-element.190), channel_id=1, source_target_pairs={{0,4},{4,0},{1,5},{5,1},{2,6},{6,2},{3,7},{7,3},{8,12},{12,8},{9,1... | collective-permute-start | bytes 3145736 | tf_op jit(solution)/shard_map/y_grad/ppermute | solution.py:37
  489.5 34.2 %collective-permute-start.73 = (bf16[96,2048]{1,0:T(8,128)(2,1)}, bf16[96,2048]{1,0:T(8,128)(2,1)S(1)}, u32[]{:S(2)}, u32[]{:S(2)}) collective-permute-start(bf16[96,2048]{1,0:T(8,128)(2,1)} %get-tuple-element.264), channel_id=1, source_target_pairs={{0,8},{8,0},{1,9},{9,1},{2,10},{10,2},{3,11},{11,3},{4,12},{12,4},... | collective-permute-start | bytes 1179656 | tf_op jit(solution)/shard_map/feed_dz/ppermute | solution.py:37
  491.2 32.5 %collective-permute-start.72 = (bf16[96,2048]{1,0:T(8,128)(2,1)}, bf16[96,2048]{1,0:T(8,128)(2,1)}, u32[]{:S(2)}, u32[]{:S(2)}) collective-permute-start(bf16[96,2048]{1,0:T(8,128)(2,1)} %get-tuple-element.265), channel_id=1, source_target_pairs={{0,2},{2,0},{1,3},{3,1},{4,6},{6,4},{5,7},{7,5},{8,10},{10,8},{9,1... | collective-permute-start | bytes 1179656 | tf_op jit(solution)/shard_map/feed_dx/ppermute | solution.py:37
  525.8 36.1 %collective-permute-start.76 = (bf16[2,256,512]{2,1,0:T(8,128)(2,1)S(1)}, bf16[2,256,512]{2,1,0:T(8,128)(2,1)}, u32[]{:S(2)}, u32[]{:S(2)}) collective-permute-start(bf16[2,256,512]{2,1,0:T(8,128)(2,1)S(1)} %add_convert_fusion.13), channel_id=1, source_target_pairs={{0,16},{16,0},{1,17},{17,1},{2,18},{18,2},{3,19},{19,3},{4,20},{20... | collective-permute-start | bytes 1572872 | tf_op jit(solution)/shard_map/zh_gdown/ppermute | solution.py:37
  525.9 39.1 %collective-permute-start.77 = (bf16[4,256,512]{2,1,0:T(8,128)(2,1)}, bf16[4,256,512]{2,1,0:T(8,128)(2,1)}, u32[]{:S(2)}, u32[]{:S(2)}) collective-permute-start(bf16[4,256,512]{2,1,0:T(8,128)(2,1)} %get-tuple-element.204), channel_id=1, source_target_pairs={{0,4},{4,0},{1,5},{5,1},{2,6},{6,2},{3,7},{7,3},{8,12},{12,8},{9,1... | collective-permute-start | bytes 3145736 | tf_op jit(solution)/shard_map/y_grad/ppermute | solution.py:37
  534.1 30.9 %collective-permute-start.75 = (bf16[192,2048]{1,0:T(8,128)(2,1)}, bf16[192,2048]{1,0:T(8,128)(2,1)}, u32[]{:S(2)}, u32[]{:S(2)}) collective-permute-start(bf16[192,2048]{1,0:T(8,128)(2,1)} %pad_maximum_fusion.9), channel_id=1, source_target_pairs={{0,8},{8,0},{1,9},{9,1},{2,10},{10,2},{3,11},{11,3},{4,12},{12,4},... | collective-permute-start | bytes 2359304 | tf_op jit(solution)/shard_map/feed_z/ppermute | solution.py:37
  537.3 27.7 %collective-permute-start.74 = (bf16[192,2048]{1,0:T(8,128)(2,1)}, bf16[192,2048]{1,0:T(8,128)(2,1)}, u32[]{:S(2)}, u32[]{:S(2)}) collective-permute-start(bf16[192,2048]{1,0:T(8,128)(2,1)} %pad_maximum_fusion.8), channel_id=1, source_target_pairs={{0,2},{2,0},{1,3},{3,1},{4,6},{6,4},{5,7},{7,5},{8,10},{10,8},{9,1... | collective-permute-start | bytes 2359304 | tf_op jit(solution)/shard_map/feed_x/ppermute | solution.py:37
  565.0 43.6 %all-to-all-start.3 = ((bf16[4,128,1536]{2,1,0:T(8,128)(2,1)}), bf16[4,128,1536]{2,1,0:T(8,128)(2,1)}, u32[]{:S(2)}, u32[]{:S(2)}) async-start(bf16[4,128,1536]{2,1,0:T(8,128)(2,1)} %pad_maximum_fusion.2), calls=%async_computation.3 | async-start | bytes 3145728 | tf_op jit(solution)/shard_map/all_to_all | solution.py:55
  580.5 28.1 %collective-permute-start.79 = (bf16[4,256,512]{2,1,0:T(8,128)(2,1)}, bf16[4,256,512]{2,1,0:T(8,128)(2,1)}, u32[]{:S(2)}, u32[]{:S(2)}) collective-permute-start(bf16[4,256,512]{2,1,0:T(8,128)(2,1)} %get-tuple-element.213), channel_id=1, source_target_pairs={{0,4},{4,0},{1,5},{5,1},{2,6},{6,2},{3,7},{7,3},{8,12},{12,8},{9,1... | collective-permute-start | bytes 3145736 | tf_op jit(solution)/shard_map/y_grad/ppermute | solution.py:37
  582.4 24.8 %collective-permute-start.78 = (bf16[2,256,512]{2,1,0:T(8,128)(2,1)S(1)}, bf16[2,256,512]{2,1,0:T(8,128)(2,1)S(1)}, u32[]{:S(2)}, u32[]{:S(2)}) collective-permute-start(bf16[2,256,512]{2,1,0:T(8,128)(2,1)S(1)} %add_convert_fusion.10), channel_id=1, source_target_pairs={{0,16},{16,0},{1,17},{17,1},{2,18},{18,2},{3,19},{19,3},{4,20},{20... | collective-permute-start | bytes 1572872 | tf_op jit(solution)/shard_map/zh_gout/ppermute | solution.py:37
  625.5 29.9 %collective-permute-start.80 = (bf16[3,192,2048]{2,1,0:T(8,128)(2,1)}, bf16[3,192,2048]{2,1,0:T(8,128)(2,1)S(1)}, u32[]{:S(2)}, u32[]{:S(2)}) collective-permute-start(bf16[3,192,2048]{2,1,0:T(8,128)(2,1)} %get-tuple-element.217), channel_id=1, source_target_pairs={{0,1},{1,0},{2,3},{3,2},{4,5},{5,4},{6,7},{7,6},{8,9},{9,8},{10,11... | collective-permute-start | bytes 7077896 | tf_op jit(solution)/shard_map/back_one_cr/ppermute | solution.py:37
  627.4 25.7 %collective-permute-start.82 = (bf16[2,256,512]{2,1,0:T(8,128)(2,1)S(1)}, bf16[2,256,512]{2,1,0:T(8,128)(2,1)S(1)}, u32[]{:S(2)}, u32[]{:S(2)}) collective-permute-start(bf16[2,256,512]{2,1,0:T(8,128)(2,1)S(1)} %add_convert_fusion.7), channel_id=1, source_target_pairs={{0,16},{16,0},{1,17},{17,1},{2,18},{18,2},{3,19},{19,3},{4,20},{20... | collective-permute-start | bytes 1572872 | tf_op jit(solution)/shard_map/zh_gswish/ppermute | solution.py:37
  627.5 26.8 %collective-permute-start.81 = (bf16[4,256,512]{2,1,0:T(8,128)(2,1)S(1)}, bf16[4,256,512]{2,1,0:T(8,128)(2,1)S(1)}, u32[]{:S(2)}, u32[]{:S(2)}) collective-permute-start(bf16[4,256,512]{2,1,0:T(8,128)(2,1)S(1)} %copy-done.55), channel_id=1, source_target_pairs={{0,4},{4,0},{1,5},{5,1},{2,6},{6,2},{3,7},{7,3},{8,12},{12,8},{9,1... | collective-permute-start | bytes 3145736 | tf_op jit(solution)/shard_map/y_grad/ppermute | solution.py:37
  655.6 24.9 %collective-permute-start.94 = (bf16[2,256,512]{2,1,0:T(8,128)(2,1)S(1)}, bf16[2,256,512]{2,1,0:T(8,128)(2,1)S(1)}, u32[]{:S(2)}, u32[]{:S(2)}) collective-permute-start(bf16[2,256,512]{2,1,0:T(8,128)(2,1)S(1)} %add_convert_fusion.4), channel_id=1, source_target_pairs={{0,16},{16,0},{1,17},{17,1},{2,18},{18,2},{3,19},{19,3},{4,20},{20... | collective-permute-start | bytes 1572872 | tf_op jit(solution)/shard_map/zh_gvalue/ppermute | solution.py:37
  658.4 30.0 %collective-permute-start.87 = (bf16[192,2048]{1,0:T(8,128)(2,1)S(1)}, bf16[192,2048]{1,0:T(8,128)(2,1)S(1)}, u32[]{:S(2)}, u32[]{:S(2)}) collective-permute-start(bf16[192,2048]{1,0:T(8,128)(2,1)S(1)} %pad_maximum_fusion.11), channel_id=1, source_target_pairs={{0,8},{8,0},{1,9},{9,1},{2,10},{10,2},{3,11},{11,3},{4,12},{12,4},... | collective-permute-start | bytes 2359304 | tf_op jit(solution)/shard_map/back_one_z/ppermute | solution.py:37
  660.0 28.4 %collective-permute-start.86 = (bf16[192,2048]{1,0:T(8,128)(2,1)S(1)}, bf16[192,2048]{1,0:T(8,128)(2,1)S(1)}, u32[]{:S(2)}, u32[]{:S(2)}) collective-permute-start(bf16[192,2048]{1,0:T(8,128)(2,1)S(1)} %pad_maximum_fusion.10), channel_id=1, source_target_pairs={{0,2},{2,0},{1,3},{3,1},{4,6},{6,4},{5,7},{7,5},{8,10},{10,8},{9,1... | collective-permute-start | bytes 2359304 | tf_op jit(solution)/shard_map/back_one_x/ppermute | solution.py:37
  661.5 29.7 %collective-permute-start.93 = (bf16[4,256,512]{2,1,0:T(8,128)(2,1)S(1)}, bf16[4,256,512]{2,1,0:T(8,128)(2,1)}, u32[]{:S(2)}, u32[]{:S(2)}) collective-permute-start(bf16[4,256,512]{2,1,0:T(8,128)(2,1)S(1)} %copy-done.53), channel_id=1, source_target_pairs={{0,4},{4,0},{1,5},{5,1},{2,6},{6,2},{3,7},{7,3},{8,12},{12,8},{9,1... | collective-permute-start | bytes 3145736 | tf_op jit(solution)/shard_map/y_grad/ppermute | solution.py:37
  691.2 43.2 %all-to-all-start.4 = ((bf16[4,128,1536]{2,1,0:T(8,128)(2,1)}), bf16[4,128,1536]{2,1,0:T(8,128)(2,1)}, u32[]{:S(2)}, u32[]{:S(2)}) async-start(bf16[4,128,1536]{2,1,0:T(8,128)(2,1)} %pad_maximum_fusion.3), calls=%async_computation.4 | async-start | bytes 3145728 | tf_op jit(solution)/shard_map/all_to_all | solution.py:55
  701.6 30.6 %collective-permute-start.95 = (bf16[2,256,512]{2,1,0:T(8,128)(2,1)}, bf16[2,256,512]{2,1,0:T(8,128)(2,1)}, u32[]{:S(2)}, u32[]{:S(2)}) collective-permute-start(bf16[2,256,512]{2,1,0:T(8,128)(2,1)} %add_convert_fusion.1), channel_id=1, source_target_pairs={{0,16},{16,0},{1,17},{17,1},{2,18},{18,2},{3,19},{19,3},{4,20},{20... | collective-permute-start | bytes 1572872 | tf_op jit(solution)/shard_map/zh_gqk/ppermute | solution.py:37
  (131 other events, 1692.7 us)

commit v3 on v2

v3 whole, which is shorter than its diff:
```python
import functools
import jax
import jax.numpy as jnp
from jax import lax
from jax.experimental import pallas as pl
from jax.experimental.pallas import tpu as pltpu
from jax.sharding import Mesh, PartitionSpec as P

epsilon = 1e-05
bf16 = jnp.bfloat16
f32 = jnp.float32
SPREAD = ("zh", "zl", "y", "x")
GROUP = ("zl", "x")


def normalize(values):
    centred = values - jnp.mean(values, axis=-1, keepdims=True)
    variance = jnp.mean(centred * centred, axis=-1, keepdims=True)
    return centred * lax.rsqrt(variance + epsilon)


def layer_norm(rows, gain):
    return normalize(rows) * gain


def dot(left, right, dims):
    return lax.dot_general(left, right, (dims, ((), ())), preferred_element_type=f32)


NN = ((1,), (0,))
NT = ((1,), (1,))
TN = ((0,), (0,))


def swap(a, axis, label="move"):
    with jax.named_scope(label):
        return lax.ppermute(a, axis, [(0, 1), (1, 0)])


def after(value, *others):
    return lax.optimization_barrier((value,) + others)[0]


def ordered(own, other, axis, dim):
    first = lax.axis_index(axis) == 0
    return jnp.stack([jnp.where(first, own, other), jnp.where(first, other, own)], dim)


def by_quarter(w):
    rows, cols = w.shape
    return w.reshape(rows, 4, cols // 4).transpose(1, 0, 2)


def beside(*parts):
    return jnp.concatenate(parts, 2)


def group_exchange(parts):
    return lax.all_to_all(parts, GROUP, 0, 0, tiled=True)


def take(a, index, dim):
    return lax.dynamic_index_in_dim(a, index, dim, keepdims=False)


def add(a, b):
    return (a.astype(f32) + b.astype(f32)).astype(bf16)


def scatter_y(keep, got):
    n = got.shape[-1]
    if lax.axis_size("zh") == 2:
        return add(keep[:2], got[:2]), add(keep[2:], got[2:])
    flip = lambda g: jnp.flip(g.reshape(2, 2, 1, -1, n), 0)
    g = jnp.concatenate([flip(keep), flip(got)], 2).reshape(lax.axis_size("zh"), 2, 2, 2, -1, n)
    y = lax.axis_index("y")
    return add(take(g, y, 2), swap(take(g, 1 - y, 2), "y")), None


def send_y(send, label):
    return swap(send, "y", label) if lax.axis_size("zh") == 2 else send


def send_zh(send, label):
    return swap(send, "zh", label) if lax.axis_size("zh") == 2 else send


def scatter_zh(keep, got):
    if lax.axis_size("zh") == 2:
        g = add(keep, got)
    else:
        g = lax.psum_scatter(got, "zh", scatter_dimension=0)
    return g.reshape(4, -1, g.shape[-1])


class WeightGrad:
    def __init__(self, pair, label):
        self.send, self.keep, self.label = *pair, label

    def to_y(self, clock):
        self.y = send_y(clock.at(self.send), "y_" + self.label)

    def to_zh(self, clock):
        send, self.keep = scatter_y(self.keep, clock.at(self.y))
        self.zh = send_zh(send, "zh_g" + self.label)

    def sum(self, clock):
        return scatter_zh(self.keep, clock.at(self.zh))


class Clock:
    def __init__(self):
        self.now = ()

    def done(self, *values):
        self.now = values

    def at(self, value):
        return after(value, *self.now)

    def at_all(self, values):
        return lax.optimization_barrier(tuple(values) + self.now)[: len(values)]


class Plan:
    def __init__(self, count, rows, width, column):
        self.count, self.rows, self.width, self.column = count, rows, width, column


class Weight:
    def __init__(self, arrays, plan):
        self.arrays, self.plan = arrays, plan


class Unit:
    def __init__(self, arrays, rows):
        self.arrays, self.rows = arrays, rows

    def weight(self, column, width):
        return Weight(self.arrays, Plan(len(self.arrays), self.rows, width, column))


class WeightPipe:
    def __init__(self):
        self.last = None

    def step(self, clock, piece, label):
        piece = clock.at(piece)
        if lax.axis_size("zh") != 2:
            whole = gather_weight(piece)
            self.moved = (whole,)
            return Unit([whole], piece.shape[1])
        far, near = swap(piece, "zh", "zh_" + label), swap(piece, "y", "ny_" + label)
        self.moved = (far, near)
        self.carry(clock)
        self.last = Unit([piece, near, far], piece.shape[1])
        self.label = label
        return self.last

    def carry(self, clock):
        if self.last is not None:
            far_y = swap(clock.at(self.last.arrays[2]), "y", "fy_" + self.label)
            self.last.arrays.append(far_y)
            self.moved += (far_y,)

    def finish(self, clock):
        self.moved = ()
        self.carry(clock)
        return self.moved


def gather_weight(piece):
    return lax.all_gather(piece, ("zh", "y"), axis=0)


class Gather:
    def __init__(self, clock, a, label, halves=False):
        self.a, self.label, self.halves = clock.at(a), label, halves
        self.x = swap(self.a, "x", label + "_x")
        self.z = swap(self.a, "zl", label + "_z")
        self.c = swap(self.a, "tensor", label + "_c")
        self.first = (self.x, self.z, self.c)

    def second(self, clock):
        half, label = self.a.shape[0] // 2, self.label
        ax, az = clock.at_all((self.x, self.z))
        if self.halves:
            self.diag = (swap(az[:half], "x", label + "_dx"), swap(ax[half:], "zl", label + "_dz"))
        else:
            self.diag = (swap(az, "x", label + "_dx"),)
        self.pieces = [self.a, self.c]
        self.pieces += [ax, swap(ax, "tensor", label + "_c"), az, swap(az, "tensor", label + "_c")]
        self.held = (*self.pieces, *self.diag)

    def finish(self, clock):
        diag = clock.at_all(self.diag)
        return [*self.pieces, *diag, *(swap(d, "tensor", self.label + "_c") for d in diag)]


class Scatter:
    def __init__(self, send_rest, send_diag, keep, label, clock):
        self.label, self.keep = label, keep
        send_rest, send_diag = clock.at_all((send_rest, send_diag))
        self.diag = add(keep[3], swap(send_diag, "tensor", label + "_cd"))
        self.rest = swap(send_rest, "tensor", label + "_cr")

    def relay(self, clock):
        half = self.diag.shape[0] // 2
        diag = clock.at(self.diag)
        self.through_x = swap(diag[:half], "x", self.label + "_dx")
        self.through_z = swap(diag[half:], "zl", self.label + "_dz")
        self.second = (self.through_x, self.through_z, self.rest)

    def send(self, clock):
        through_x, through_z, rest = (v.astype(f32) for v in clock.at_all(self.second))
        half = through_x.shape[0]
        self.own, xmate, zmate = (self.keep[r].astype(f32) + rest[r] for r in range(3))
        zmate = jnp.concatenate([zmate[:half] + through_x, zmate[half:]]).astype(bf16)
        xmate = jnp.concatenate([xmate[:half], xmate[half:] + through_z]).astype(bf16)
        self.x = swap(xmate, "x", self.label + "_x")
        self.z = swap(zmate, "zl", self.label + "_z")
        self.last = (self.x, self.z)

    def finish(self, clock):
        x, z = clock.at_all(self.last)
        return self.own + x.astype(f32) + z.astype(f32)


VMEM_LIMIT = 60 * 2**20
WHOLE = tuple((i // 2, i, 0, 1) for i in range(8))
HALVES = WHOLE[:6] + tuple((3, slot, part, 2) for slot in (6, 7) for part in (0, 1))
ANY = pl.BlockSpec(memory_space=pl.ANY)
SMEM = pl.BlockSpec(memory_space=pltpu.SMEM)


class Loader:
    def __init__(self, sems):
        self.sems, self.used = sems, 0

    def copy(self, src, dst):
        self.used += 1
        return pltpu.make_async_copy(src, dst, self.sems.at[self.used - 1])

    def tokens(self, refs, held, coord):
        rows = held.shape[1]
        chips = [[], [], [], []]
        if len(refs) == 1:
            for slot in range(8):
                other = 2 * ((slot // 2) ^ coord[2]) + ((slot % 2) ^ coord[3])
                chips[slot // 2].append(self.copy(refs[0].at[other], held.at[slot]))
            return chips
        for ref, (chip, slot, part, parts) in zip(refs, HALVES if len(refs) == 10 else WHOLE):
            size = rows // parts
            chips[chip].append(self.copy(ref, held.at[slot, pl.ds(part * size, size)]))
        return chips

    def weight(self, refs, plan, held, coord):
        copies = []
        columns = pl.ds(plan.column, plan.width)
        if len(refs) == 4:
            for i, ref in enumerate(refs):
                zh, y = coord[0] ^ (i // 2), coord[1] ^ (i % 2)
                for zl in range(2):
                    block = ref.at[pl.ds(2 * zl, 2), :, columns]
                    row = ((zh * 2 + zl) * 2 + y) * 2
                    copies.append(self.copy(block, held.at[pl.ds(row, 2)]))
            return copies
        for i in range(refs[0].shape[0]):
            for zl in range(2):
                block = refs[0].at[i, pl.ds(2 * zl, 2), :, columns]
                row = ((i // 2 * 2 + zl) * 2 + i % 2) * 2
                copies.append(self.copy(block, held.at[pl.ds(row, 2)]))
        return copies


def start(*copies):
    for c in copies:
        c.start()


def wait(*copies):
    for c in copies:
        c.wait()


def at_chip(r, chips):
    for i, copies in enumerate(chips):
        pl.when(r == i)(functools.partial(wait, *copies))


def rows_of(held, r):
    pair = held[pl.ds(2 * r, 2)]
    return pair.reshape(2 * pair.shape[1], pair.shape[2])


def flat(w):
    value = w[...]
    return value.reshape(value.shape[0] * value.shape[1], value.shape[2])


def by_chip(shape):
    return pl.BlockSpec((1,) + shape, lambda r: (r,) + (0,) * len(shape))


def chip_kernel(body, operands, specs, outs, out_specs, scratch, copies, flops):
    moved = sum(a.size * a.dtype.itemsize for a in operands) + sum(
        o.size * jnp.dtype(o.dtype).itemsize for o in outs
    )
    return pl.pallas_call(
        body,
        grid=(4,),
        in_specs=specs,
        out_specs=out_specs,
        out_shape=outs,
        scratch_shapes=scratch + [pltpu.SemaphoreType.DMA((copies,))],
        compiler_params=pltpu.CompilerParams(
            dimension_semantics=("arbitrary",), vmem_limit_bytes=VMEM_LIMIT
        ),
        cost_estimate=pl.CostEstimate(flops=flops, bytes_accessed=moved, transcendentals=0),
    )(*operands)


def held_tokens(pieces):
    return pltpu.VMEM((8,) + pieces[0].shape[-2:], bf16)


def held_weight(w):
    devices = 16 if w.plan.count == 4 else 4 * w.arrays[0].shape[0]
    return pltpu.VMEM((devices, w.plan.rows, w.plan.width), bf16)


def arrays(*weights):
    return [a for w in weights for a in w.arrays]


def copies_of(*weights):
    return sum(8 if w.plan.count == 4 else 2 * w.arrays[0].shape[0] for w in weights)


def struct(shape, dtype):
    return jax.ShapeDtypeStruct(shape, dtype)


def partial_rows(grads, helds, r, keep, store):
    rows, blocks = keep.shape[1], helds[0].shape[0] // 4
    size = blocks * helds[0].shape[1]
    for j in range(4):
        parts = [
            dot(g, h[j * blocks : (j + 1) * blocks].reshape(size, h.shape[2]), NT)
            for g, h in zip(grads, helds)
        ]
        out = sum(parts[1:], parts[0]).astype(bf16)
        keep[0, :, j * size : (j + 1) * size] = out[:rows]
        store[r, :, j * size : (j + 1) * size] = out[rows:]


def send_copies(load, store, rest, diag):
    return [load.copy(store.at[i], rest.at[i]) for i in range(3)] + [load.copy(store.at[3], diag)]


def at_chip_start(r, copies):
    for i, c in enumerate(copies):
        pl.when(r == i)(c.start)

    @pl.when(r == 3)
    def _():
        wait(*copies)


def partial_outs(rows, model):
    outs = [
        struct((3, rows, model), bf16),
        struct((rows, model), bf16),
        struct((4, rows, model), bf16),
    ]
    return outs, [ANY, ANY, by_chip((rows, model))]


def attend_body(tokens, f_qk, f_v, coord, mask, *refs):
    acts, refs = refs[:tokens], refs[tokens:]
    wqk, refs = refs[: f_qk.count], refs[f_qk.count :]
    wv, refs = refs[: f_v.count], refs[f_v.count :]
    q_out, k_out, v_out, score_out, hat_out, scale_out, held, held_qk, held_v, sems = refs
    load, r = Loader(sems), pl.program_id(0)
    w1 = load.weight(wqk, f_qk, held_qk, coord)
    chips = load.tokens(acts, held, coord)
    w2 = load.weight(wv, f_v, held_v, coord)

    @pl.when(r == 0)
    def _():
        start(*w1, *chips[0], *w2, *chips[1], *chips[2], *chips[3])
        wait(*w1)

    at_chip(r, chips)
    x = rows_of(held, r)
    qk = dot(x, flat(held_qk), NN).astype(bf16)
    size = qk.shape[1] // 2
    q, k = qk[:, :size], qk[:, size:]
    q_out[0], k_out[0] = q, k
    scores = (dot(q, k, NT) * mask[0]).astype(bf16)
    score_out[0] = scores

    @pl.when(r == 0)
    def _():
        wait(*w2)

    v = dot(x, flat(held_v), NN).astype(bf16)
    v_out[0] = v
    hat_out[0] = dot(scores, v, NN)
    rows, step = hat_out.shape[1], 32

    def chunk(i, carry):
        at = pl.ds(pl.multiple_of(i * step, step), step)
        part = hat_out[0, at, :]
        part = part - jnp.mean(part, axis=-1, keepdims=True)
        scale = lax.rsqrt(jnp.mean(part * part, axis=-1, keepdims=True) + epsilon)
        hat_out[0, at, :] = part * scale
        scale_out[0, at, :] = jnp.broadcast_to(scale, (step, 128))
        return carry

    lax.fori_loop(0, rows // step, chunk, 0)


def attend(coord, mask, acts, wqk, wv, key_size):
    length, n = mask.shape[1], wv.plan.width
    model = acts[0].shape[-1]
    outs = [
        struct((4, length, key_size), bf16),
        struct((4, length, key_size), bf16),
        struct((4, length, n), bf16),
        struct((4, length, length), bf16),
        struct((4, length, n), f32),
        struct((4, length, 128), f32),
    ]
    return chip_kernel(
        functools.partial(attend_body, len(acts), wqk.plan, wv.plan),
        [coord, mask, *acts, *arrays(wqk, wv)],
        [SMEM, by_chip((length, length))] + [ANY] * (len(acts) + len(arrays(wqk, wv))),
        outs,
        [by_chip(o.shape[1:]) for o in outs],
        [held_tokens(acts), held_weight(wqk), held_weight(wv)],
        10 + copies_of(wqk, wv),
        16 * length * model * n,
    )


def branch_body(tokens, f_s, f_o, coord, hat, *refs):
    acts, refs = refs[:tokens], refs[tokens:]
    ws, refs = refs[: f_s.count], refs[f_s.count :]
    wo, refs = refs[: f_o.count], refs[f_o.count :]
    s_out, gated_out, rest, diag, keep, held, held_s, held_o, store, sems = refs
    load, r = Loader(sems), pl.program_id(0)
    w1 = load.weight(ws, f_s, held_s, coord)
    chips = load.tokens(acts, held, coord)
    w2 = load.weight(wo, f_o, held_o, coord)
    sends = send_copies(load, store, rest, diag)

    @pl.when(r == 0)
    def _():
        start(*w1, *chips[0], *w2, *chips[1], *chips[2], *chips[3])
        wait(*w1)

    at_chip(r, chips)
    s_out[0] = dot(rows_of(held, r), flat(held_s), NN)
    rows, step = s_out.shape[1], 32

    def chunk(i, carry):
        at = pl.ds(pl.multiple_of(i * step, step), step)
        s = s_out[0, at, :]
        gated_out[0, at, :] = (s / (1.0 + jnp.exp(-s)) * hat[0, at, :]).astype(bf16)
        return carry

    lax.fori_loop(0, rows // step, chunk, 0)

    @pl.when(r == 0)
    def _():
        wait(*w2)

    partial_rows([gated_out[0]], [held_o], r, keep, store)
    at_chip_start(r, sends)


def branch(coord, hat, acts, ws, wo):
    length, n = hat.shape[1:]
    rows, model = acts[0].shape[-2:]
    outs, out_specs = partial_outs(rows, model)
    outs = [struct((4, length, n), f32), struct((4, length, n), bf16)] + outs
    return chip_kernel(
        functools.partial(branch_body, len(acts), ws.plan, wo.plan),
        [coord, hat, *acts, *arrays(ws, wo)],
        [SMEM, by_chip((length, n))] + [ANY] * (len(acts) + len(arrays(ws, wo))),
        outs,
        [by_chip((length, n)), by_chip((length, n))] + out_specs,
        [held_tokens(acts), held_weight(ws), held_weight(wo), pltpu.VMEM((4, rows, model), bf16)],
        14 + copies_of(ws, wo),
        16 * length * model * n,
    )


def feed_body(tokens, others, f_u, f_g, f_d, coord, *refs):
    acts, cots, refs = refs[:tokens], refs[tokens : tokens + others], refs[tokens + others :]
    wu, refs = refs[: f_u.count], refs[f_u.count :]
    wg, refs = refs[: f_g.count], refs[f_g.count :]
    wd, refs = refs[: f_d.count], refs[f_d.count :]
    hidden_out, up_out, gate_out, rest, diag, keep = refs[:6]
    held, held_c, held_u, held_g, held_d, store, up, gate, gh, sems = refs[6:]
    load, r = Loader(sems), pl.program_id(0)
    w1 = load.weight(wu, f_u, held_u, coord)
    w2 = load.weight(wg, f_g, held_g, coord)
    w3 = load.weight(wd, f_d, held_d, coord)
    chips = load.tokens(acts, held, coord)
    chips_c = load.tokens(cots, held_c, coord)
    sends = send_copies(load, store, rest, diag)

    @pl.when(r == 0)
    def _():
        start(*w3, *chips_c[0], *w1, *chips[0], *w2)
        for i in range(1, 4):
            start(*chips_c[i], *chips[i])
        wait(*w3)

    at_chip(r, chips_c)
    gh[...] = dot(rows_of(held_c, r), flat(held_d), NN)

    @pl.when(r == 0)
    def _():
        wait(*w1)

    at_chip(r, chips)
    x = rows_of(held, r)
    up[...] = dot(x, flat(held_u), NN)

    @pl.when(r == 0)
    def _():
        wait(*w2)

    gate[...] = dot(x, flat(held_g), NN)
    step = 16

    def chunk(i, carry):
        at = pl.ds(pl.multiple_of(i * step, step), step)
        u, g, e = up[at, :], gate[at, :], gh[at, :]
        c = 0.7978845608028654
        square = g * g
        t = jnp.tanh(c * g * (1.0 + 0.044715 * square))
        half = 0.5 * (1.0 + t)
        gelu = g * half
        slope = half + (0.5 * c) * g * (1.0 - t * t) * (1.0 + (3 * 0.044715) * square)
        hidden_out[0, at, :] = (gelu * u).astype(bf16)
        up_out[0, at, :] = (e * gelu).astype(bf16)
        gate_out[0, at, :] = (e * u * slope).astype(bf16)
        return carry

    lax.fori_loop(0, gh.shape[0] // step, chunk, 0)
    partial_rows([up_out[0], gate_out[0]], [held_u, held_g], r, keep, store)
    at_chip_start(r, sends)


def feed_forward(coord, acts, cots, wu, wg, wd):
    rows, model = acts[0].shape[-2:]
    n = wd.plan.width
    outs, out_specs = partial_outs(rows, model)
    outs = [struct((4, 2 * rows, n), bf16)] * 3 + outs
    return chip_kernel(
        functools.partial(feed_body, len(acts), len(cots), wu.plan, wg.plan, wd.plan),
        [coord, *acts, *cots, *arrays(wu, wg, wd)],
        [SMEM] + [ANY] * (len(acts) + len(cots) + len(arrays(wu, wg, wd))),
        outs,
        [by_chip((2 * rows, n))] * 3 + out_specs,
        [
            held_tokens(acts),
            held_tokens(cots),
            held_weight(wu),
            held_weight(wg),
            held_weight(wd),
            pltpu.VMEM((4, rows, model), bf16),
        ]
        + [pltpu.VMEM((2 * rows, n), f32)] * 3,
        24 + copies_of(wu, wg, wd),
        80 * rows * model * n,
    )


def back_body(plans, whole, coord, *refs):
    count = len(plans)
    weights = []
    grads, refs = refs[:count], refs[count:]
    for plan in plans:
        weights.append(refs[: plan.count])
        refs = refs[plan.count :]
    load, r = Loader(refs[-1]), pl.program_id(0)
    if whole:
        result, helds, keep, store = refs[0], refs[1 : 1 + count], refs[-3], refs[-2]
    else:
        rest, diag, keep, helds, store = *refs[:3], refs[3 : 3 + count], refs[-2]
    copies = [load.weight(w, p, h, coord) for w, p, h in zip(weights, plans, helds)]

    @pl.when(r == 0)
    def _():
        for c in copies:
            start(*c)
        for c in copies:
            wait(*c)

    if not whole:
        sends = send_copies(load, store, rest, diag)
        partial_rows([g[0] for g in grads], helds, r, keep, store)
        at_chip_start(r, sends)
        return
    sends = []
    for i in range(4):
        at = 2 * (i ^ coord[2])
        sends.append(
            (
                load.copy(keep.at[i], result.at[at + coord[3]]),
                load.copy(store.at[i], result.at[at + (1 ^ coord[3])]),
            )
        )
    partial_rows([g[0] for g in grads], helds, r, keep.at[pl.ds(r, 1)], store)
    for i in range(4):
        pl.when(r == i)(functools.partial(start, *sends[i]))

    @pl.when(r == 3)
    def _():
        for c in sends:
            wait(*c)


def back(coord, grads, weights, whole=False):
    length = grads[0].shape[1]
    rows = length // 2
    held = held_weight(weights[0])
    model = held.shape[0] * held.shape[1]
    outs, out_specs = partial_outs(rows, model)
    store = pltpu.VMEM((4, rows, model), bf16)
    if whole:
        outs, out_specs = [struct((8, rows, model), bf16)], [ANY]
    return chip_kernel(
        functools.partial(back_body, tuple(w.plan for w in weights), whole),
        [coord, *grads, *arrays(*weights)],
        [SMEM] + [by_chip(g.shape[1:]) for g in grads] + [ANY] * len(arrays(*weights)),
        outs,
        out_specs,
        [held_weight(w) for w in weights] + [store] * (2 if whole else 1),
        8 + copies_of(*weights),
        8 * length * model * sum(g.shape[2] for g in grads),
    )


def attend_back_body(tokens, f_o, coord, mask, s, hat, scale, scores, q, k, v, *refs):
    acts, refs = refs[:tokens], refs[tokens:]
    wo, refs = refs[: f_o.count], refs[f_o.count :]
    gqk_out, gv_out, gs_out, held, held_o, dg, gr, sems = refs
    load, r = Loader(sems), pl.program_id(0)
    w1 = load.weight(wo, f_o, held_o, coord)
    chips = load.tokens(acts, held, coord)

    @pl.when(r == 0)
    def _():
        start(*w1, *chips[0], *chips[1], *chips[2], *chips[3])
        wait(*w1)

    at_chip(r, chips)
    dg[...] = dot(rows_of(held, r), flat(held_o), NN)
    rows, step = dg.shape[0], 16

    def chunk(i, carry):
        at = pl.ds(pl.multiple_of(i * step, step), step)
        e, x, v_s = dg[at, :], hat[0, at, :], s[0, at, :]
        gate = 1.0 / (1.0 + jnp.exp(-v_s))
        silu = v_s * gate
        gs_out[0, at, :] = (e * x * (gate + silu * (1.0 - gate))).astype(bf16)
        f = e * silu
        f = f - jnp.mean(f, axis=-1, keepdims=True) - x * jnp.mean(f * x, axis=-1, keepdims=True)
        gr[at, :] = (f * scale[0, at, :1]).astype(bf16)
        return carry

    lax.fori_loop(0, rows // step, chunk, 0)
    grad_retained = gr[...]
    gv_out[0] = dot(scores[0], grad_retained, TN).astype(bf16)
    raw = (dot(grad_retained, v[0], NT) * mask[0]).astype(bf16)
    size = q.shape[2]
    gqk_out[0, :, :size] = dot(raw, k[0], NN).astype(bf16)
    gqk_out[0, :, size:] = dot(raw, q[0], TN).astype(bf16)


def attend_back(coord, mask, s, hat, scale, scores, q, k, v, acts, wo):
    length, n = s.shape[1:]
    model = acts[0].shape[-1]
    blocks = [mask, s, hat, scale, scores, q, k, v]
    outs = [struct((4, length, 2 * q.shape[2]), bf16)] + [struct((4, length, n), bf16)] * 2
    return chip_kernel(
        functools.partial(attend_back_body, len(acts), wo.plan),
        [coord, *blocks, *acts, *arrays(wo)],
        [SMEM] + [by_chip(b.shape[1:]) for b in blocks] + [ANY] * (len(acts) + len(arrays(wo))),
        outs,
        [by_chip(o.shape[1:]) for o in outs],
        [
            held_tokens(acts),
            held_weight(wo),
            pltpu.VMEM((length, n), f32),
            pltpu.VMEM((length, n), bf16),
        ],
        10 + copies_of(wo),
        12 * length * model * n,
    )


def weight_grad_body(count, tokens, whole, coord, *refs):
    grads, refs = refs[:count], refs[count:]
    acts, refs = refs[:tokens], refs[tokens:]
    outs, held, sems = refs[:-2], refs[-2], refs[-1]
    load, i = Loader(sems), pl.program_id(0)
    chips = load.tokens(acts, held, coord)

    @pl.when(i == 0)
    def _():
        for c in chips:
            start(*c)
        for c in chips:
            wait(*c)

    width = held.shape[2] // 8
    j = i % 4
    if whole:
        column = ((i // 4 * 2 + i % 2) * 2 + i // 2 % 2) * width
    else:
        y = coord[1] ^ jnp.where(i < 4, 1, 0)
        zh = coord[0] ^ jnp.where(j < 2, 1, 0)
        column = ((zh * 2 + j % 2) * 2 + y) * width
    x = held[:, :, pl.ds(pl.multiple_of(column, width), width)]
    x = x.reshape(x.shape[0] * x.shape[1], width).T
    for n in range(count):
        g = grads[n][...]
        size = g.shape[2]
        out = dot(x, g.reshape(g.shape[0] * g.shape[1], size), NN).astype(bf16)
        if whole:
            outs[0][0, :, n * size : (n + 1) * size] = out
            continue
        pl.when(i < 4)(functools.partial(store_block, outs[2 * n], out))
        pl.when(i >= 4)(functools.partial(store_block, outs[2 * n + 1], out))


def store_block(ref, value):
    ref[0] = value


def weight_grads(coord, acts, grads, whole=False):
    rows, model = acts[0].shape[-2:]
    outs, out_specs = [], []
    width = sum(g.shape[2] for g in grads)
    for g in grads:
        shape = (4, model // 8, g.shape[2])
        outs += [struct(shape, bf16)] * 2
        out_specs += [
            pl.BlockSpec((1,) + shape[1:], lambda i: (jnp.minimum(i, 3), 0, 0)),
            pl.BlockSpec((1,) + shape[1:], lambda i: (jnp.maximum(i - 4, 0), 0, 0)),
        ]
    if whole:
        outs = [struct((8, model // 8, width), bf16)]
        out_specs = [pl.BlockSpec((1, model // 8, width), lambda i: (i, 0, 0))]
    moved = sum(a.size * 2 for a in acts) + sum(g.size * 2 for g in grads) + 2 * model * width
    got = pl.pallas_call(
        functools.partial(weight_grad_body, len(grads), len(acts), whole),
        grid=(8,),
        in_specs=[SMEM] + [pl.BlockSpec(memory_space=pltpu.VMEM)] * len(grads) + [ANY] * len(acts),
        out_specs=out_specs,
        out_shape=outs,
        scratch_shapes=[held_tokens(acts), pltpu.SemaphoreType.DMA((10,))],
        compiler_params=pltpu.CompilerParams(
            dimension_semantics=("arbitrary",), vmem_limit_bytes=VMEM_LIMIT
        ),
        cost_estimate=pl.CostEstimate(
            flops=16 * rows * model * width, bytes_accessed=moved, transcendentals=0
        ),
    )(coord, *grads, *acts)
    if whole:
        return got[0]
    return [(got[2 * i], got[2 * i + 1]) for i in range(len(grads))]


def scatter_whole(g):
    zh, n = lax.axis_size("zh"), g.shape[2]
    if zh == 2:
        g = g.reshape(4, 4, -1, n)
    else:
        g = g.reshape(2, 2, 2, -1, n).transpose(0, 2, 1, 3, 4).reshape(zh, 2, 2, 2, -1, n)
        g = g.transpose(0, 2, 1, 3, 4, 5).reshape(2 * zh, 4, -1, n)
    g = lax.psum_scatter(g, ("zh", "y"), scatter_dimension=0, tiled=True)
    return g.reshape(4, -1, n)


def sum_everywhere(a):
    for axis in ("tensor",) + SPREAD:
        if lax.axis_size(axis) == 2:
            a = a + swap(a, axis)
        else:
            a = lax.psum(a, axis)
    return a


def local(
    tokens,
    segments,
    decay,
    norm1_gain,
    w_query,
    w_key,
    w_value,
    w_swish,
    w_out,
    norm2_gain,
    w_up,
    w_gate,
    w_down,
    cotangent,
):
    rows_q, width = w_query.shape[0], w_value.shape[1] // 4
    quarter = 2 * lax.axis_index("zl") + lax.axis_index("x")
    core = lax.axis_index("tensor")
    length = segments.shape[0]
    rows_each = tokens.shape[0]
    key_size = w_query.shape[1] // 4
    value_size = w_value.shape[1] // 4
    rate = take(decay, quarter, 0)

    ids = [jnp.zeros((), jnp.int32)] * 2
    if lax.axis_size("zh") == 2:
        ids = [lax.axis_index("zh"), lax.axis_index("y")]
    coord = jnp.stack(ids + [quarter, core]).astype(jnp.int32)
    clock, free = Clock(), Clock()
    at = clock.at
    rows_local = tokens.astype(f32)
    everyone = ("zl", "x", "tensor")

    pipe = WeightPipe()
    seg_x, seg_z = swap(segments, "x", "seg"), swap(segments, "zl", "seg")
    with jax.named_scope("seg"):
        seg_d = lax.ppermute(segments, GROUP, [(i, 3 - i) for i in range(4)])
    parts = (by_quarter(w) for w in (w_query, w_key, w_value))
    piece = group_exchange(beside(*parts))
    parts = beside(by_quarter(w_swish), by_quarter(w_out.T))

    clock.done(piece, seg_x, seg_z, seg_d, parts)
    unit_qkv = pipe.step(clock, piece, "qkv")
    piece = group_exchange(at(parts))
    normed_local = layer_norm(rows_local, norm1_gain).astype(bf16)
    normed = [lax.all_gather(at(normed_local), everyone, axis=0)]
    segs = jnp.stack([segments, seg_x, seg_z, seg_d])
    segs = jnp.where(core == 0, segs, jnp.roll(segs, length // 2, 1))
    position = (jnp.arange(length, dtype=jnp.int32) + core * rows_each) % length
    offset = position[:, None] - position[None, :]
    allowed = (offset >= 0)[None] & (segs[:, :, None] == segs[:, None, :])
    distance = jnp.maximum(offset, 0).astype(f32)
    decay_mask = jnp.where(allowed, jnp.exp(-rate * distance)[None], 0.0)
    parts = beside(by_quarter(at(w_up)), by_quarter(at(w_gate)))

    clock.done(piece, parts, decay_mask, *pipe.moved)
    unit_so = pipe.step(clock, piece, "so")
    piece = group_exchange(at(parts))
    parts = by_quarter(at(w_down).T)
    full_qk, full_value = unit_qkv.weight(0, width), unit_qkv.weight(width, width)
    query, key, values, scores, hat, scale = attend(
        at(coord), decay_mask, normed, full_qk, full_value, key_size
    )

    clock.done(query, piece, parts, *pipe.moved)
    unit_ug = pipe.step(clock, piece, "ug")
    piece = group_exchange(at(parts))
    grad_rows = [lax.all_gather(at(cotangent), everyone, axis=0)]
    full_swish, full_out = unit_so.weight(0, width), unit_so.weight(width, width)
    swish_in, gated, *partial = branch(at(coord), hat, normed, full_swish, full_out)
    clock.done(piece, *pipe.moved, *partial)
    unit_d = pipe.step(clock, piece, "d")
    scatter = Scatter(*partial, "branch", clock)
    scatter.relay(free)
    clock.done(*scatter.second)
    scatter.send(clock)
    clock.done(*scatter.last, *pipe.moved)
    middle = rows_local + scatter.finish(clock)
    normed_two_local = layer_norm(middle, norm2_gain).astype(bf16)
    gather = Gather(clock, normed_two_local, "two", True)
    far_y = pipe.finish(clock)
    clock.done(*far_y, *gather.first)
    gather.second(clock)
    clock.done(*gather.held)
    normed_two = gather.finish(clock)
    full_up, full_gate = unit_ug.weight(0, width), unit_ug.weight(width, width)
    full_down = unit_d.weight(0, width)
    hidden, grad_up_rows, grad_gate_rows, *partial = feed_forward(
        at(coord), normed_two, grad_rows, full_up, full_gate, full_down
    )

    scatter = Scatter(*partial, "back_two", free)
    clock.done(scatter.diag)
    scatter.relay(clock)
    g_up, g_gate = weight_grads(at(coord), normed_two, [grad_up_rows, grad_gate_rows])
    g_up, g_gate = WeightGrad(g_up, "up"), WeightGrad(g_gate, "gate")
    clock.done(g_up.send, *scatter.second)
    scatter.send(clock)
    g_up.to_y(clock)
    (g_down,) = weight_grads(at(coord), grad_rows, [hidden])
    g_down = WeightGrad(g_down, "down")
    clock.done(g_down.send, g_up.y, *scatter.last)
    back_two_local = scatter.finish(clock)
    _, norm_two_pull = jax.vjp(layer_norm, middle, norm2_gain)
    grad_mid_norm, grad_norm2_local = norm_two_pull(back_two_local)
    grad_middle = cotangent.astype(f32) + grad_mid_norm
    grad_branch_local = grad_middle.astype(bf16)

    clock.done(grad_branch_local)
    gather = Gather(clock, grad_branch_local, "gb", True)
    g_gate.to_y(clock)
    clock.done(g_gate.y, *gather.first)
    gather.second(clock)
    g_down.to_y(clock)
    (feed,) = back(at(coord), [hidden], [full_down], True)
    clock.done(feed, *gather.held)
    grad_branch = gather.finish(clock)
    feed = lax.psum_scatter(at(feed), everyone, scatter_dimension=0, tiled=True)
    g_up.to_zh(clock)
    grad_qk, grad_values, grad_swish_in = attend_back(
        at(coord),
        decay_mask,
        swish_in,
        hat,
        scale,
        scores,
        query,
        key,
        values,
        grad_branch,
        full_out,
    )
    clock.done(grad_qk, g_up.zh, g_down.y)
    g_gate.to_zh(clock)
    (g_out,) = weight_grads(at(coord), grad_branch, [gated])
    g_out = WeightGrad(g_out, "out")
    clock.done(g_out.send)
    g_out.to_y(clock)
    (g_swish,) = weight_grads(at(coord), normed, [grad_swish_in])
    g_swish = WeightGrad(g_swish, "swish")
    clock.done(g_swish.send, g_gate.zh)
    g_down.to_zh(clock)
    g_swish.to_y(clock)
    g_value, g_qk = weight_grads(at(coord), normed, [grad_values, grad_qk])
    g_value, g_qk = WeightGrad(g_value, "value"), WeightGrad(g_qk, "qk")
    clock.done(g_value.send, g_down.zh, g_out.y)
    g_out.to_zh(clock)
    g_value.to_y(clock)
    partial = back(
        at(coord), [grad_qk, grad_values, grad_swish_in], [full_qk, full_value, full_swish]
    )
    clock.done(g_out.zh, g_swish.y, *partial)
    g_swish.to_zh(clock)
    scatter = Scatter(*partial, "back_one", clock)
    clock.done(scatter.diag)
    scatter.relay(clock)
    grad_ff = group_exchange(beside(g_up.sum(clock), g_gate.sum(clock), g_down.sum(clock)))
    clock.done(g_value.y, *scatter.second)
    g_qk.to_y(clock)
    scatter.send(clock)
    clock.done(g_swish.zh)
    g_value.to_zh(clock)
    clock.done(grad_ff, *scatter.last)
    back_one_local = scatter.finish(clock)
    grad_os = group_exchange(beside(g_out.sum(clock), g_swish.sum(clock)))
    clock.done(g_qk.y, g_value.zh)
    g_qk.to_zh(clock)
    mixed = (middle + feed.reshape(middle.shape).astype(f32)).astype(bf16)
    clock.done(g_qk.zh, grad_os)
    grad_qkv = group_exchange(beside(g_qk.sum(clock), g_value.sum(clock)))

    def columns(g):
        return g.transpose(1, 0, 2).reshape(rows_q, -1).astype(f32)

    def rows(g):
        return g.transpose(0, 2, 1).reshape(-1, rows_q).astype(f32)

    grad_up, grad_gate = columns(grad_ff[:, :, :width]), columns(grad_ff[:, :, width : 2 * width])
    grad_down = rows(grad_ff[:, :, 2 * width :])
    grad_query = columns(grad_qkv[:, :, :key_size])
    grad_key, grad_value = columns(grad_qkv[:, :, key_size:width]), columns(grad_qkv[:, :, width:])
    grad_out, grad_swish = rows(grad_os[:, :, :width]), columns(grad_os[:, :, width:])

    _, norm_one_pull = jax.vjp(layer_norm, rows_local, norm1_gain)
    grad_tok_norm, grad_norm1_local = norm_one_pull(back_one_local)
    grad_tokens = grad_middle + grad_tok_norm
    grad_norm1, grad_norm2 = sum_everywhere(jnp.stack([grad_norm1_local, grad_norm2_local]))
    return (
        mixed,
        grad_tokens,
        grad_norm1,
        grad_query,
        grad_key,
        grad_value,
        grad_swish,
        grad_out,
        grad_norm2,
        grad_up,
        grad_gate,
        grad_down,
    )


def solution(mesh):
    dp, tensor = mesh.shape["dp"], mesh.shape["tensor"]
    grid = Mesh(mesh.devices.reshape(dp // 8, 2, 2, 2, tensor), SPREAD + ("tensor",))
    rows = P(SPREAD + ("tensor",), None)
    rows_split = P(SPREAD, "tensor")
    columns_split = P("tensor", SPREAD)
    return jax.shard_map(
        local,
        mesh=grid,
        in_specs=(
            rows,
            P(SPREAD),
            P("tensor"),
            P(),
            rows_split,
            rows_split,
            rows_split,
            rows_split,
            columns_split,
            P(),
            rows_split,
            rows_split,
            columns_split,
            rows,
        ),
        out_specs=(
            rows,
            rows,
            P(),
            rows_split,
            rows_split,
            rows_split,
            rows_split,
            columns_split,
            P(),
            rows_split,
            rows_split,
            columns_split,
        ),
        check_vma=False,
    )
```

time: 759 us -> 702 us (0.925)
  waiting for transfers between devices: 343 us -> 272 us
  between operations: 3.16 us -> 16.1 us
  local copies, waits for them, and re-layouts: 45.2 us -> 36 us
    ppermute x96 -> x69, waiting for transfers between devices: 335 us -> 242 us  [swap(): return lax.ppermute(a, axis, [(0, 1), (1, 0)])]
    all_to_all x6 -> x7, starting transfers between devices: 26.4 us -> 54.7 us  [group_exchange(): return lax.all_to_all(parts, GROUP, 0, 0, tiled=True)]
    ppermute x96 -> x69, starting transfers between devices: 85 us -> 60 us  [swap(): return lax.ppermute(a, axis, [(0, 1), (1, 0)])]
    all_to_all x6 -> x7, waiting for transfers between devices: 8.25 us -> 28.8 us  [group_exchange(): return lax.all_to_all(parts, GROUP, 0, 0, tiled=True)]
    unnamed x160 -> x124, local copies, waits for them, and re-layouts: 19.7 us -> 14.6 us
    convert_element_type x18 -> x16, other arithmetic: 21.3 us -> 25 us  [add(): return (a.astype(f32) + b.astype(f32)).astype(bf16)]
  transfers between devices with their start and end apart: 102 -> 80, of which waited for: 45 -> 38; matrix products, arithmetic and copies ran while one was open for 11% -> 13% of each run, Pallas kernels for 15% -> 22%
where the time goes in v3:
time: 702 us; the launch traced here: 694 us
  waiting for transfers between devices  272 us (39%)
  Pallas kernels  181 us (26%)
  starting transfers between devices  115 us (16%)
  other arithmetic  74.1 us (11%)
  local copies, waits for them, and re-layouts  36 us (5%)
  between operations  16.1 us (2%)
    ppermute x69, waiting for transfers between devices, swap(): return lax.ppermute(a, axis, [(0, 1), (1, 0)])  242 us
    pallas_call x6, Pallas kernels, chip_kernel(): pl.pallas_call(body, grid=(4,), in_specs=specs, out_specs=out_specs, out_...  116 us
    pallas_call x5, Pallas kernels, weight_grads(): pl.pallas_call(functools.partial(weight_grad_body, len(grads), len(acts),...  65.6 us
    ppermute x69, starting transfers between devices, swap(): return lax.ppermute(a, axis, [(0, 1), (1, 0)])  60 us
    all_to_all x7, starting transfers between devices, group_exchange(): return lax.all_to_all(parts, GROUP, 0, 0, tiled=True)  54.7 us
    all_to_all x7, waiting for transfers between devices, group_exchange(): return lax.all_to_all(parts, GROUP, 0, 0, tiled=True)  28.8 us
    convert_element_type x16, other arithmetic, add(): return (a.astype(f32) + b.astype(f32)).astype(bf16)  25 us
    unnamed x124, local copies, waits for them, and re-layouts  14.6 us
  transfers between devices with their start and end apart: 80, of which 38 were waited for; matrix products, arithmetic and copies ran while one was open for 13% of the time, Pallas kernels for 22%

profile of v3, /device:TPU:0, one launch (start us, length us, event | category | flops | bytes accessed | tf_op | source)
XLA Modules:
  0.0 694.2 jit_solution(18223312900768856137)
XLA Ops:
  11.5 5.2 all-to-all-start
  24.2 6.8 collective-permute-done.1
  31.9 3.5 all-to-all-start.1
  38.7 2.6 collective-permute-start.3
  46.2 15.2 %collective-permute-done.4.refs_2_.refs_6_.refs_4_.refs_8_ = bf16[4,128,1024]{2,1,0:T(8,128)(2,1)} collective-permute-done((bf16[4,128,1024]{2,1,0:T(8,128)(2,1)}, bf16[4,128,1024]{2,1,0:T(8,128)(2,1)}, u32[]{:S(2)}, u32[]{:S(2)}) %collective-permute-start.4) | collective-permute-done | bytes 1048608 | tf_op jit(solution)/shard_map/ny_qkv/ppermute | solution.py:37
  61.4 26.2 %collective-permute-done.3.refs_3_.refs_7_.refs_5_.refs_9_ = bf16[4,128,1024]{2,1,0:T(8,128)(2,1)} collective-permute-done((bf16[4,128,1024]{2,1,0:T(8,128)(2,1)}, bf16[4,128,1024]{2,1,0:T(8,128)(2,1)}, u32[]{:S(2)}, u32[]{:S(2)}) %collective-permute-start.3) | collective-permute-done | bytes 1048608 | tf_op jit(solution)/shard_map/zh_qkv/ppermute | solution.py:37
  89.9 11.9 %all-to-all-start.2 = ((bf16[4,128,1024]{2,1,0:T(8,128)(2,1)}), bf16[4,128,1024]{2,1,0:T(8,128)(2,1)S(1)}, u32[]{:S(2)}, u32[]{:S(2)}) async-start(bf16[4,128,1024]{2,1,0:T(8,128)(2,1)} %pad_maximum_fusion.3), calls=%async_computation.2 | async-start | bytes 2097152 | tf_op jit(solution)/shard_map/all_to_all | solution.py:59
  104.2 9.4 %collective-permute-done.5.refs_4_.refs_8_.refs_6_.refs_10_ = bf16[4,128,1024]{2,1,0:T(8,128)(2,1)} collective-permute-done((bf16[4,128,1024]{2,1,0:T(8,128)(2,1)}, bf16[4,128,1024]{2,1,0:T(8,128)(2,1)}, u32[]{:S(2)}, u32[]{:S(2)}) %collective-permute-start.5) | collective-permute-done | bytes 1048608 | tf_op jit(solution)/shard_map/fy_qkv/ppermute | solution.py:37
  113.6 23.2 %shard_map.229 = (bf16[4,384,256]{2,1,0:T(8,128)(2,1)}, bf16[4,384,256]{2,1,0:T(8,128)(2,1)}, bf16[4,384,512]{2,1,0:T(8,128)(2,1)}, bf16[4,384,384]{2,1,0:T(8,12...) custom-call(s32[4]{0:T(128)} %pad_add_fusion.1.coord, f32[4,384,384]{2,1,0:T(8,128)} %and_select_fusion.mask, ...), custom_call_target="tpu_custom_call" | custom-call | flops 6442450944 | bytes 25296912 | tf_op jit(solution)/shard_map/pallas_call | solution.py:309
  136.8 11.2 %collective-permute-done.6.refs_3_.refs_7_.refs_12_.refs_13_ = bf16[4,128,1024]{2,1,0:T(8,128)(2,1)} collective-permute-done((bf16[4,128,1024]{2,1,0:T(8,128)(2,1)S(1)}, bf16[4,128,1024]{2,1,0:T(8,128)(2,1)}, u32[]{:S(2)}, u32[]{:S(2)}) %collective-permute-start.6) | collective-permute-done | bytes 1048608 | tf_op jit(solution)/shard_map/zh_so/ppermute | solution.py:37
  150.1 20.8 %all-to-all-start.3 = ((bf16[4,128,512]{2,1,0:T(8,128)(2,1)}), bf16[4,128,512]{2,1,0:T(8,128)(2,1)S(1)}, u32[]{:S(2)}, u32[]{:S(2)}) async-start(bf16[4,128,512]{2,1,0:T(8,128)(2,1)} %bitcast.23), calls=%async_computation.3 | async-start | bytes 1048576 | tf_op jit(solution)/shard_map/all_to_all | solution.py:59
  171.1 3.3 collective-permute-done.8.refs_4_.refs_8_.refs_13_.refs_14_
  175.3 15.5 %shard_map.230 = (f32[4,384,512]{2,1,0:T(8,128)}, bf16[4,384,512]{2,1,0:T(8,128)(2,1)}, bf16[3,192,2048]{2,1,0:T(8,128)(2,1)}, bf16[192,2048]{1,0:T(8,128)(2,1)}, bf16[4,192,2048]{2,1,0:T(8,128)(2,1)}) custom-call(s32[4]{0:T(128)} %pad_add_fusion.1.coord, f32[4,384,512]{2,1,0:T(8,128)} %get-tuple-element.143.hat, bf16[8,192,2048]{2,1,0:T(8,128)(2,1)} %bitcast.190, ...), custom_call_target="tpu_custom_call" | custom-call | flops 6442450944 | bytes 28835856 | tf_op jit(solution)/shard_map/pallas_call | solution.py:309
  190.8 10.9 %all-to-all-done.3.refs_19_.refs_1_ = bf16[4,128,512]{2,1,0:T(8,128)(2,1)S(1)} async-done(((bf16[4,128,512]{2,1,0:T(8,128)(2,1)}), bf16[4,128,512]{2,1,0:T(8,128)(2,1)S(1)}, u32[]{:S(2)}, u32[]{:S(2)}) %all-to-all-start.3) | async-done | bytes 524320 | tf_op jit(solution)/shard_map/all_to_all | solution.py:59
  203.0 5.9 collective-permute-done.11
  213.2 17.3 %collective-permute-done.13 = bf16[96,2048]{1,0:T(8,128)(2,1)S(1)} collective-permute-done((bf16[96,2048]{1,0:T(8,128)(2,1)S(1)}, bf16[96,2048]{1,0:T(8,128)(2,1)S(1)}, u32[]{:S(2)}, u32[]{:S(2)}) %collective-permute-start.13) | collective-permute-done | bytes 393248 | tf_op jit(solution)/shard_map/branch_dz/ppermute | solution.py:37
  235.7 12.3 %collective-permute-done.18.refs_20_.refs_2_ = bf16[4,128,512]{2,1,0:T(8,128)(2,1)S(1)} collective-permute-done((bf16[4,128,512]{2,1,0:T(8,128)(2,1)S(1)}, bf16[4,128,512]{2,1,0:T(8,128)(2,1)S(1)}, u32[]{:S(2)}, u32[]{:S(2)}) %collective-permute-start.18) | collective-permute-done | bytes 524320 | tf_op jit(solution)/shard_map/ny_d/ppermute | solution.py:37
  248.0 12.9 %collective-permute-done.17.refs_21_.refs_3_ = bf16[4,128,512]{2,1,0:T(8,128)(2,1)S(1)} collective-permute-done((bf16[4,128,512]{2,1,0:T(8,128)(2,1)S(1)}, bf16[4,128,512]{2,1,0:T(8,128)(2,1)S(1)}, u32[]{:S(2)}, u32[]{:S(2)}) %collective-permute-start.17) | collective-permute-done | bytes 524320 | tf_op jit(solution)/shard_map/zh_d/ppermute | solution.py:37
  268.5 12.8 %collective-permute-done.23.refs_22_.refs_4_ = bf16[4,128,512]{2,1,0:T(8,128)(2,1)S(1)} collective-permute-done((bf16[4,128,512]{2,1,0:T(8,128)(2,1)S(1)}, bf16[4,128,512]{2,1,0:T(8,128)(2,1)S(1)}, u32[]{:S(2)}, u32[]{:S(2)}) %collective-permute-start.23) | collective-permute-done | bytes 524320 | tf_op jit(solution)/shard_map/fy_d/ppermute | solution.py:37
  286.7 9.7 %collective-permute-done.26.refs_6_.refs_8_ = bf16[96,2048]{1,0:T(8,128)(2,1)S(1)} collective-permute-done((bf16[96,2048]{1,0:T(8,128)(2,1)S(1)}, bf16[96,2048]{1,0:T(8,128)(2,1)S(1)}, u32[]{:S(2)}, u32[]{:S(2)}) %collective-permute-start.26) | collective-permute-done | bytes 393248 | tf_op jit(solution)/shard_map/two_dx/ppermute | solution.py:37
  300.3 27.6 %shard_map.231 = (bf16[4,384,512]{2,1,0:T(8,128)(2,1)}, bf16[4,384,512]{2,1,0:T(8,128)(2,1)}, bf16[4,384,512]{2,1,0:T(8,128)(2,1)}, bf16[3,192,2048]{2,1,0:T(8,1...) custom-call(s32[4]{0:T(128)} %pad_add_fusion.1.coord, bf16[192,2048]{1,0:T(8,128)(2,1)} %copy-done.22, ...), custom_call_target="tpu_custom_call" | custom-call | flops 16106127360 | bytes 34078736 | tf_op jit(solution)/shard_map/pallas_call | solution.py:309
  334.4 16.2 %shard_map.232 = (bf16[4,256,512]{2,1,0:T(8,128)(2,1)}, bf16[4,256,512]{2,1,0:T(8,128)(2,1)}, bf16[4,256,512]{2,1,0:T(8,128)(2,1)}, bf16[4,256,512]{2,1,0:T(8,128)(2,1)}) custom-call(s32[4]{0:T(128)} %pad_add_fusion.1.coord, bf16[4,384,512]{2,1,0:T(8,128)(2,1)} %get-tuple-element.172.refs_0_, bf16[4,384,512]{2,1,0:T(8,128)(2,1)} %get-tuple-element.173.refs_1_, ...), custom_call_target="tpu_custom_call" | custom-call | flops 6442450944 | bytes 13631488 | tf_op jit(solution)/shard_map/pallas_call | solution.py:763
  361.9 11.1 %shard_map.233 = (bf16[4,256,512]{2,1,0:T(8,128)(2,1)}, bf16[4,256,512]{2,1,0:T(8,128)(2,1)}) custom-call(s32[4]{0:T(128)} %pad_add_fusion.1.coord, bf16[4,384,512]{2,1,0:T(8,128)(2,1)} %get-tuple-element.182.refs_0_, bf16[8,192,2048]{2,1,0:T(8,128)(2,1)} %bitcast.194), custom_call_target="tpu_custom_call" | custom-call | flops 3221225472 | bytes 9961472 | tf_op jit(solution)/shard_map/pallas_call | solution.py:763
  373.0 4.6 collective-permute-done.34
  379.0 3.2 multiply_reduce_fusion
  387.6 17.8 %collective-permute-done.39.refs_4_.refs_5_ = bf16[192,2048]{1,0:T(8,128)(2,1)} collective-permute-done((bf16[192,2048]{1,0:T(8,128)(2,1)S(1)}, bf16[192,2048]{1,0:T(8,128)(2,1)}, u32[]{:S(2)}, u32[]{:S(2)}) %collective-permute-start.39) | collective-permute-done | bytes 786464 | tf_op jit(solution)/shard_map/gb_z/ppermute | solution.py:37
  414.1 8.3 %shard_map.234 = bf16[8,192,2048]{2,1,0:T(8,128)(2,1)} custom-call(s32[4]{0:T(128)} %pad_add_fusion.1.coord, bf16[4,384,512]{2,1,0:T(8,128)(2,1)} %get-tuple-element.182.refs_0_, bf16[4,128,512]{2,1,0:T(8,128)(2,1)} %copy-done.30, bf16[4,128,512]{2,1,0:T(8,128)(2,1)} %copy-done.53, bf16[4,128,512]{2,1,0:T(8,128)(2,1)} %copy-done.54, ...), custom_call_target="tpu_custom_call" | custom-call | flops 3221225472 | bytes 9961488 | tf_op jit(solution)/shard_map/pallas_call | solution.py:309
  428.6 24.1 %shard_map.235 = (bf16[4,384,512]{2,1,0:T(8,128)(2,1)}, bf16[4,384,512]{2,1,0:T(8,128)(2,1)}, bf16[4,384,512]{2,1,0:T(8,128)(2,1)}) custom-call(s32[4]{0:T(128)} %pad_add_fusion.1.coord, f32[4,384,384]{2,1,0:T(8,128)} %and_select_fusion.mask, f32[4,384,512]{2,1,0:T(8,128)} %get-tuple-element.194.s, f32[4,384,512]{2,1,0:T(8,128)} %get-tuple-element.143.hat, ...), custom_call_target="tpu_custom_call" | custom-call | flops 4831838208 | bytes 28966928 | tf_op jit(solution)/shard_map/pallas_call | solution.py:309
  454.6 11.0 %shard_map.236 = (bf16[4,256,512]{2,1,0:T(8,128)(2,1)}, bf16[4,256,512]{2,1,0:T(8,128)(2,1)}) custom-call(s32[4]{0:T(128)} %pad_add_fusion.1.coord, bf16[4,384,512]{2,1,0:T(8,128)(2,1)} %get-tuple-element.206.refs_0_, bf16[192,2048]{1,0:T(8,128)(2,1)} %copy-done.9, bf16[192,2048]{1,0:T(8,128)(2,1)} %copy-done.23, ...), custom_call_target="tpu_custom_call" | custom-call | flops 3221225472 | bytes 9961472 | tf_op jit(solution)/shard_map/pallas_call | solution.py:763
  466.2 10.9 %shard_map.237 = (bf16[4,256,512]{2,1,0:T(8,128)(2,1)}, bf16[4,256,512]{2,1,0:T(8,128)(2,1)}) custom-call(s32[4]{0:T(128)} %pad_add_fusion.1.coord, bf16[4,384,512]{2,1,0:T(8,128)(2,1)} %get-tuple-element.209.refs_0_.refs_2_, bf16[8,192,2048]{2,1,0:T(8,128)(2,1)} %bitcast.191), custom_call_target="tpu_custom_call" | custom-call | flops 3221225472 | bytes 9961472 | tf_op jit(solution)/shard_map/pallas_call | solution.py:763
  482.4 16.4 %shard_map.238 = (bf16[4,256,512]{2,1,0:T(8,128)(2,1)}, bf16[4,256,512]{2,1,0:T(8,128)(2,1)}, bf16[4,256,512]{2,1,0:T(8,128)(2,1)}, bf16[4,256,512]{2,1,0:T(8,128)(2,1)}) custom-call(s32[4]{0:T(128)} %pad_add_fusion.1.coord, bf16[4,384,512]{2,1,0:T(8,128)(2,1)} %get-tuple-element.214.refs_0_.refs_1_, ...), custom_call_target="tpu_custom_call" | custom-call | flops 6442450944 | bytes 13631488 | tf_op jit(solution)/shard_map/pallas_call | solution.py:763
  498.8 6.3 collective-permute-done.50
  506.6 16.8 %shard_map.239 = (bf16[3,192,2048]{2,1,0:T(8,128)(2,1)}, bf16[192,2048]{1,0:T(8,128)(2,1)}, bf16[4,192,2048]{2,1,0:T(8,128)(2,1)}) custom-call(s32[4]{0:T(128)} %pad_add_fusion.1.coord, bf16[4,384,512]{2,1,0:T(8,128)(2,1)} %get-tuple-element.201.refs_1_.refs_0_, bf16[4,384,512]{2,1,0:T(8,128)(2,1)} %get-tuple-element.214.refs_0_.refs_1_, ...), custom_call_target="tpu_custom_call" | custom-call | flops 9663676416 | bytes 23592976 | tf_op jit(solution)/shard_map/pallas_call | solution.py:309
  523.4 8.8 %collective-permute-done.52 = bf16[2,256,512]{2,1,0:T(8,128)(2,1)} collective-permute-done((bf16[2,256,512]{2,1,0:T(8,128)(2,1)S(1)}, bf16[2,256,512]{2,1,0:T(8,128)(2,1)}, u32[]{:S(2)}, u32[]{:S(2)}) %collective-permute-start.52) | collective-permute-done | bytes 524320 | tf_op jit(solution)/shard_map/zh_gout/ppermute | solution.py:37
  545.5 4.6 all-to-all-start.4
  550.1 8.0 %collective-permute-done.58 = bf16[4,256,512]{2,1,0:T(8,128)(2,1)} collective-permute-done((bf16[4,256,512]{2,1,0:T(8,128)(2,1)}, bf16[4,256,512]{2,1,0:T(8,128)(2,1)}, u32[]{:S(2)}, u32[]{:S(2)}) %collective-permute-start.58) | collective-permute-done | bytes 1048608 | tf_op jit(solution)/shard_map/y_value/ppermute | solution.py:37
  571.5 17.9 %all-to-all-done.4 = bf16[4,128,1536]{2,1,0:T(8,128)(2,1)} async-done(((bf16[4,128,1536]{2,1,0:T(8,128)(2,1)}), bf16[4,128,1536]{2,1,0:T(8,128)(2,1)}, u32[]{:S(2)}, u32[]{:S(2)}) %all-to-all-start.4) | async-done | bytes 1572896 | tf_op jit(solution)/shard_map/all_to_all | solution.py:59
  589.4 16.8 %collective-permute-done.60 = bf16[192,2048]{1,0:T(8,128)(2,1)} collective-permute-done((bf16[192,2048]{1,0:T(8,128)(2,1)}, bf16[192,2048]{1,0:T(8,128)(2,1)}, u32[]{:S(2)}, u32[]{:S(2)}) %collective-permute-start.60) | collective-permute-done | bytes 786464 | tf_op jit(solution)/shard_map/back_one_z/ppermute | solution.py:37
  606.2 3.8 fusion.9
  614.0 4.4 all-to-all-start.5
  623.2 3.0 collective-permute-start.69
  626.2 5.0 collective-permute-done.62
  631.3 2.8 collective-permute-start.63
  634.0 8.2 %collective-permute-done.63 = f32[2,2048]{1,0:T(2,128)S(1)} collective-permute-done((f32[2,2048]{1,0:T(2,128)S(1)}, f32[2,2048]{1,0:T(2,128)S(1)}, u32[]{:S(2)}, u32[]{:S(2)}) %collective-permute-start.63) | collective-permute-done | bytes 16416 | tf_op jit(solution)/shard_map/move/ppermute | solution.py:37
  642.9 6.9 collective-permute-done.69
  654.1 4.4 all-to-all-start.6
  658.5 3.7 add_add_fusion.2
  664.3 3.1 convert_bitcast_fusion
  (366 shorter events, 166.0 us)
Async XLA Ops:
  11.5 20.4 %all-to-all-start = ((bf16[4,128,1024]{2,1,0:T(8,128)(2,1)}), bf16[4,128,1024]{2,1,0:T(8,128)(2,1)}, u32[]{:S(2)}, u32[]{:S(2)}) async-start(bf16[4,128,1024]{2,1,0:T(8,128)(2,1)} %pad_maximum_fusion.2), calls=%async_computation | async-start | bytes 2097152 | tf_op jit(solution)/shard_map/all_to_all | solution.py:59
  16.7 96.9 %all-gather.5.cloned.1.call-start = ((), (), s32[]{:S(2)}) async-start(), calls=%async_computation.9 | async-start | bytes 7077888 | tf_op jit(solution)/shard_map/all_gather | solution.py:848
  31.9 55.7 %all-to-all-start.1 = ((bf16[4,128,1024]{2,1,0:T(8,128)(2,1)}), bf16[4,128,1024]{2,1,0:T(8,128)(2,1)S(1)}, u32[]{:S(2)}, u32[]{:S(2)}) async-start(bf16[4,128,1024]{2,1,0:T(8,128)(2,1)} %pad_maximum_fusion.1), calls=%async_computation.1 | async-start | bytes 2097152 | tf_op jit(solution)/shard_map/all_to_all | solution.py:59
  37.0 24.4 %collective-permute-start.4 = (bf16[4,128,1024]{2,1,0:T(8,128)(2,1)}, bf16[4,128,1024]{2,1,0:T(8,128)(2,1)}, u32[]{:S(2)}, u32[]{:S(2)}) collective-permute-start(bf16[4,128,1024]{2,1,0:T(8,128)(2,1)} %all-to-all-done.refs_1_.refs_5_.refs_3_.refs_7_), channel_id=1, source_target_pairs={{0,4},{4,0},{1,5},{5,1},{2,6},{6,2},{3,7},{7,3},{8,12},{12,8},{9,1... | collective-permute-start | bytes 3145736 | tf_op jit(solution)/shard_map/ny_qkv/ppermute | solution.py:37
  38.7 48.9 %collective-permute-start.3 = (bf16[4,128,1024]{2,1,0:T(8,128)(2,1)}, bf16[4,128,1024]{2,1,0:T(8,128)(2,1)}, u32[]{:S(2)}, u32[]{:S(2)}) collective-permute-start(bf16[4,128,1024]{2,1,0:T(8,128)(2,1)} %all-to-all-done.refs_1_.refs_5_.refs_3_.refs_7_), channel_id=1, source_target_pairs={{0,16},{16,0},{1,17},{17,1},{2,18},{18,2},{3,19},{19,3},{4,20},{20... | collective-permute-start | bytes 3145736 | tf_op jit(solution)/shard_map/zh_qkv/ppermute | solution.py:37
  87.6 26.0 %collective-permute-start.5 = (bf16[4,128,1024]{2,1,0:T(8,128)(2,1)}, bf16[4,128,1024]{2,1,0:T(8,128)(2,1)}, u32[]{:S(2)}, u32[]{:S(2)}) collective-permute-start(bf16[4,128,1024]{2,1,0:T(8,128)(2,1)} %collective-permute-done.3.refs_3_.refs_7_.refs_5_.refs_9_), channel_id=1, source_target_pairs={{0,4},{4,0},{1,5},{5,1},{2,6},{6,2},{3,7},{7,3},{8,12},{12,8},{9,1... | collective-permute-start | bytes 3145736 | tf_op jit(solution)/shard_map/fy_qkv/ppermute | solution.py:37
  89.9 58.1 %all-to-all-start.2 = ((bf16[4,128,1024]{2,1,0:T(8,128)(2,1)}), bf16[4,128,1024]{2,1,0:T(8,128)(2,1)S(1)}, u32[]{:S(2)}, u32[]{:S(2)}) async-start(bf16[4,128,1024]{2,1,0:T(8,128)(2,1)} %pad_maximum_fusion.3), calls=%async_computation.2 | async-start | bytes 2097152 | tf_op jit(solution)/shard_map/all_to_all | solution.py:59
  101.7 198.6 %all-gather.7.cloned.1.call-start = ((), (), s32[]{:S(2)}) async-start(), calls=%async_computation.10 | async-start | bytes 7077888 | tf_op jit(solution)/shard_map/all_gather | solution.py:870
  101.7 35.1 %collective-permute-start.7 = (bf16[4,128,1024]{2,1,0:T(8,128)(2,1)S(1)}, bf16[4,128,1024]{2,1,0:T(8,128)(2,1)}, u32[]{:S(2)}, u32[]{:S(2)}) collective-permute-start(bf16[4,128,1024]{2,1,0:T(8,128)(2,1)S(1)} %all-to-all-done.1.refs_1_.refs_5_.refs_10_.refs_11_), channel_id=1, source_target_pairs={{0,4},{4,0},{1,5},{5,1},{2,6},{6,2},{3,7},{7,3},{8,12},{12,8},{9,1... | collective-permute-start | bytes 3145736 | tf_op jit(solution)/shard_map/ny_so/ppermute | solution.py:37
  102.3 45.7 %collective-permute-start.6 = (bf16[4,128,1024]{2,1,0:T(8,128)(2,1)S(1)}, bf16[4,128,1024]{2,1,0:T(8,128)(2,1)}, u32[]{:S(2)}, u32[]{:S(2)}) collective-permute-start(bf16[4,128,1024]{2,1,0:T(8,128)(2,1)S(1)} %all-to-all-done.1.refs_1_.refs_5_.refs_10_.refs_11_), channel_id=1, source_target_pairs={{0,16},{16,0},{1,17},{17,1},{2,18},{18,2},{3,19},{19,3},{4,20},{20... | collective-permute-start | bytes 3145736 | tf_op jit(solution)/shard_map/zh_so/ppermute | solution.py:37
  148.0 26.3 %collective-permute-start.8 = (bf16[4,128,1024]{2,1,0:T(8,128)(2,1)}, bf16[4,128,1024]{2,1,0:T(8,128)(2,1)S(1)}, u32[]{:S(2)}, u32[]{:S(2)}) collective-permute-start(bf16[4,128,1024]{2,1,0:T(8,128)(2,1)} %collective-permute-done.6.refs_3_.refs_7_.refs_12_.refs_13_), channel_id=1, source_target_pairs={{0,4},{4,0},{1,5},{5,1},{2,6},{6,2},{3,7},{7,3},{8,12},{12,8},{9,1... | collective-permute-start | bytes 3145736 | tf_op jit(solution)/shard_map/fy_so/ppermute | solution.py:37
  149.5 52.1 %collective-permute-start.10 = (bf16[4,128,1024]{2,1,0:T(8,128)(2,1)S(1)}, bf16[4,128,1024]{2,1,0:T(8,128)(2,1)}, u32[]{:S(2)}, u32[]{:S(2)}) collective-permute-start(bf16[4,128,1024]{2,1,0:T(8,128)(2,1)S(1)} %all-to-all-done.2.refs_11_.refs_15_), channel_id=1, source_target_pairs={{0,4},{4,0},{1,5},{5,1},{2,6},{6,2},{3,7},{7,3},{8,12},{12,8},{9,1... | collective-permute-start | bytes 3145736 | tf_op jit(solution)/shard_map/ny_ug/ppermute | solution.py:37
  150.1 51.5 %collective-permute-start.9 = (bf16[4,128,1024]{2,1,0:T(8,128)(2,1)S(1)}, bf16[4,128,1024]{2,1,0:T(8,128)(2,1)}, u32[]{:S(2)}, u32[]{:S(2)}) collective-permute-start(bf16[4,128,1024]{2,1,0:T(8,128)(2,1)S(1)} %all-to-all-done.2.refs_11_.refs_15_), channel_id=1, source_target_pairs={{0,16},{16,0},{1,17},{17,1},{2,18},{18,2},{3,19},{19,3},{4,20},{20... | collective-permute-start | bytes 3145736 | tf_op jit(solution)/shard_map/zh_ug/ppermute | solution.py:37
  150.1 51.5 %all-to-all-start.3 = ((bf16[4,128,512]{2,1,0:T(8,128)(2,1)}), bf16[4,128,512]{2,1,0:T(8,128)(2,1)S(1)}, u32[]{:S(2)}, u32[]{:S(2)}) async-start(bf16[4,128,512]{2,1,0:T(8,128)(2,1)} %bitcast.23), calls=%async_computation.3 | async-start | bytes 1048576 | tf_op jit(solution)/shard_map/all_to_all | solution.py:59
  170.9 514.1 %reduce-scatter.2.cloned.1.call-start = ((), (), s32[]{:S(2)}) async-start(), calls=%async_computation.8 | async-start | bytes 7077888 | tf_op jit(solution)/shard_map/reduce_scatter | solution.py:920
  202.4 28.1 %collective-permute-start.14 = (bf16[3,192,2048]{2,1,0:T(8,128)(2,1)}, bf16[3,192,2048]{2,1,0:T(8,128)(2,1)S(1)}, u32[]{:S(2)}, u32[]{:S(2)}) collective-permute-start(bf16[3,192,2048]{2,1,0:T(8,128)(2,1)} %get-tuple-element.151), channel_id=1, source_target_pairs={{0,1},{1,0},{2,3},{3,2},{4,5},{5,4},{6,7},{7,6},{8,9},{9,8},{10,11... | collective-permute-start | bytes 7077896 | tf_op jit(solution)/shard_map/branch_cr/ppermute | solution.py:37
  210.4 20.1 %collective-permute-start.13 = (bf16[96,2048]{1,0:T(8,128)(2,1)S(1)}, bf16[96,2048]{1,0:T(8,128)(2,1)S(1)}, u32[]{:S(2)}, u32[]{:S(2)}) collective-permute-start(bf16[96,2048]{1,0:T(8,128)(2,1)S(1)} %get-tuple-element.278), channel_id=1, source_target_pairs={{0,8},{8,0},{1,9},{9,1},{2,10},{10,2},{3,11},{11,3},{4,12},{12,4},... | collective-permute-start | bytes 1179656 | tf_op jit(solution)/shard_map/branch_dz/ppermute | solution.py:37
  210.4 20.1 %collective-permute-start.12 = (bf16[96,2048]{1,0:T(8,128)(2,1)S(1)}, bf16[96,2048]{1,0:T(8,128)(2,1)S(1)}, u32[]{:S(2)}, u32[]{:S(2)}) collective-permute-start(bf16[96,2048]{1,0:T(8,128)(2,1)S(1)} %get-tuple-element.279), channel_id=1, source_target_pairs={{0,2},{2,0},{1,3},{3,1},{4,6},{6,4},{5,7},{7,5},{8,10},{10,8},{9,1... | collective-permute-start | bytes 1179656 | tf_op jit(solution)/shard_map/branch_dx/ppermute | solution.py:37
  211.7 49.2 %collective-permute-start.19 = (bf16[4,128,1024]{2,1,0:T(8,128)(2,1)}, bf16[4,128,1024]{2,1,0:T(8,128)(2,1)S(1)}, u32[]{:S(2)}, u32[]{:S(2)}) collective-permute-start(bf16[4,128,1024]{2,1,0:T(8,128)(2,1)} %collective-permute-done.9.refs_13_.refs_17_), channel_id=1, source_target_pairs={{0,4},{4,0},{1,5},{5,1},{2,6},{6,2},{3,7},{7,3},{8,12},{12,8},{9,1... | collective-permute-start | bytes 3145736 | tf_op jit(solution)/shard_map/fy_ug/ppermute | solution.py:37
  232.0 28.9 %collective-permute-start.15 = (bf16[192,2048]{1,0:T(8,128)(2,1)S(1)}, bf16[192,2048]{1,0:T(8,128)(2,1)S(1)}, u32[]{:S(2)}, u32[]{:S(2)}) collective-permute-start(bf16[192,2048]{1,0:T(8,128)(2,1)S(1)} %pad_maximum_fusion.6), channel_id=1, source_target_pairs={{0,2},{2,0},{1,3},{3,1},{4,6},{6,4},{5,7},{7,5},{8,10},{10,8},{9,1... | collective-permute-start | bytes 2359304 | tf_op jit(solution)/shard_map/branch_x/ppermute | solution.py:37
  232.7 30.4 %collective-permute-start.16 = (bf16[192,2048]{1,0:T(8,128)(2,1)S(1)}, bf16[192,2048]{1,0:T(8,128)(2,1)S(1)}, u32[]{:S(2)}, u32[]{:S(2)}) collective-permute-start(bf16[192,2048]{1,0:T(8,128)(2,1)S(1)} %pad_maximum_fusion.7), channel_id=1, source_target_pairs={{0,8},{8,0},{1,9},{9,1},{2,10},{10,2},{3,11},{11,3},{4,12},{12,4},... | collective-permute-start | bytes 2359304 | tf_op jit(solution)/shard_map/branch_z/ppermute | solution.py:37
  234.4 26.5 %collective-permute-start.17 = (bf16[4,128,512]{2,1,0:T(8,128)(2,1)S(1)}, bf16[4,128,512]{2,1,0:T(8,128)(2,1)S(1)}, u32[]{:S(2)}, u32[]{:S(2)}) collective-permute-start(bf16[4,128,512]{2,1,0:T(8,128)(2,1)S(1)} %copy-done.31), channel_id=1, source_target_pairs={{0,16},{16,0},{1,17},{17,1},{2,18},{18,2},{3,19},{19,3},{4,20},{20... | collective-permute-start | bytes 1572872 | tf_op jit(solution)/shard_map/zh_d/ppermute | solution.py:37
  328.2 22.5 %collective-permute-start.33 = (bf16[3,192,2048]{2,1,0:T(8,128)(2,1)}, bf16[3,192,2048]{2,1,0:T(8,128)(2,1)}, u32[]{:S(2)}, u32[]{:S(2)}) collective-permute-start(bf16[3,192,2048]{2,1,0:T(8,128)(2,1)} %get-tuple-element.176), channel_id=1, source_target_pairs={{0,1},{1,0},{2,3},{3,2},{4,5},{5,4},{6,7},{7,6},{8,9},{9,8},{10,11... | collective-permute-start | bytes 7077896 | tf_op jit(solution)/shard_map/back_two_cr/ppermute | solution.py:37
  351.4 27.6 %collective-permute-start.36 = (bf16[4,256,512]{2,1,0:T(8,128)(2,1)}, bf16[4,256,512]{2,1,0:T(8,128)(2,1)S(1)}, u32[]{:S(2)}, u32[]{:S(2)}) collective-permute-start(bf16[4,256,512]{2,1,0:T(8,128)(2,1)} %get-tuple-element.184), channel_id=1, source_target_pairs={{0,4},{4,0},{1,5},{5,1},{2,6},{6,2},{3,7},{7,3},{8,12},{12,8},{9,1... | collective-permute-start | bytes 3145736 | tf_op jit(solution)/shard_map/y_up/ppermute | solution.py:37
  358.5 19.0 %collective-permute-start.34 = (bf16[192,2048]{1,0:T(8,128)(2,1)}, bf16[192,2048]{1,0:T(8,128)(2,1)}, u32[]{:S(2)}, u32[]{:S(2)}) collective-permute-start(bf16[192,2048]{1,0:T(8,128)(2,1)} %pad_maximum_fusion.8), channel_id=1, source_target_pairs={{0,2},{2,0},{1,3},{3,1},{4,6},{6,4},{5,7},{7,5},{8,10},{10,8},{9,1... | collective-permute-start | bytes 2359304 | tf_op jit(solution)/shard_map/back_two_x/ppermute | solution.py:37
  384.6 23.2 %collective-permute-start.37 = (bf16[4,256,512]{2,1,0:T(8,128)(2,1)S(1)}, bf16[4,256,512]{2,1,0:T(8,128)(2,1)}, u32[]{:S(2)}, u32[]{:S(2)}) collective-permute-start(bf16[4,256,512]{2,1,0:T(8,128)(2,1)S(1)} %copy-done.49), channel_id=1, source_target_pairs={{0,4},{4,0},{1,5},{5,1},{2,6},{6,2},{3,7},{7,3},{8,12},{12,8},{9,1... | collective-permute-start | bytes 3145736 | tf_op jit(solution)/shard_map/y_gate/ppermute | solution.py:37
  385.3 20.1 %collective-permute-start.39 = (bf16[192,2048]{1,0:T(8,128)(2,1)S(1)}, bf16[192,2048]{1,0:T(8,128)(2,1)}, u32[]{:S(2)}, u32[]{:S(2)}) collective-permute-start(bf16[192,2048]{1,0:T(8,128)(2,1)S(1)} %fusion.23.refs_0_.refs_1_), channel_id=1, source_target_pairs={{0,8},{8,0},{1,9},{9,1},{2,10},{10,2},{3,11},{11,3},{4,12},{12,4},... | collective-permute-start | bytes 2359304 | tf_op jit(solution)/shard_map/gb_z/ppermute | solution.py:37
  386.9 19.8 %collective-permute-start.38 = (bf16[192,2048]{1,0:T(8,128)(2,1)S(1)}, bf16[192,2048]{1,0:T(8,128)(2,1)}, u32[]{:S(2)}, u32[]{:S(2)}) collective-permute-start(bf16[192,2048]{1,0:T(8,128)(2,1)S(1)} %fusion.23.refs_0_.refs_1_), channel_id=1, source_target_pairs={{0,2},{2,0},{1,3},{3,1},{4,6},{6,4},{5,7},{7,5},{8,10},{10,8},{9,1... | collective-permute-start | bytes 2359304 | tf_op jit(solution)/shard_map/gb_x/ppermute | solution.py:37
  413.4 39.3 %collective-permute-start.48 = (bf16[4,256,512]{2,1,0:T(8,128)(2,1)}, bf16[4,256,512]{2,1,0:T(8,128)(2,1)}, u32[]{:S(2)}, u32[]{:S(2)}) collective-permute-start(bf16[4,256,512]{2,1,0:T(8,128)(2,1)} %get-tuple-element.204), channel_id=1, source_target_pairs={{0,4},{4,0},{1,5},{5,1},{2,6},{6,2},{3,7},{7,3},{8,12},{12,8},{9,1... | collective-permute-start | bytes 3145736 | tf_op jit(solution)/shard_map/y_down/ppermute | solution.py:37
  425.9 26.7 %collective-permute-start.47 = (bf16[2,256,512]{2,1,0:T(8,128)(2,1)}, bf16[2,256,512]{2,1,0:T(8,128)(2,1)}, u32[]{:S(2)}, u32[]{:S(2)}) collective-permute-start(bf16[2,256,512]{2,1,0:T(8,128)(2,1)} %add_convert_fusion.20), channel_id=1, source_target_pairs={{0,16},{16,0},{1,17},{17,1},{2,18},{18,2},{3,19},{19,3},{4,20},{20... | collective-permute-start | bytes 1572872 | tf_op jit(solution)/shard_map/zh_gup/ppermute | solution.py:37
  454.0 25.2 %collective-permute-start.49 = (bf16[2,256,512]{2,1,0:T(8,128)(2,1)S(1)}, bf16[2,256,512]{2,1,0:T(8,128)(2,1)}, u32[]{:S(2)}, u32[]{:S(2)}) collective-permute-start(bf16[2,256,512]{2,1,0:T(8,128)(2,1)S(1)} %add_convert_fusion.19), channel_id=1, source_target_pairs={{0,16},{16,0},{1,17},{17,1},{2,18},{18,2},{3,19},{19,3},{4,20},{20... | collective-permute-start | bytes 1572872 | tf_op jit(solution)/shard_map/zh_ggate/ppermute | solution.py:37
  465.6 33.2 %collective-permute-start.51 = (bf16[4,256,512]{2,1,0:T(8,128)(2,1)}, bf16[4,256,512]{2,1,0:T(8,128)(2,1)}, u32[]{:S(2)}, u32[]{:S(2)}) collective-permute-start(bf16[4,256,512]{2,1,0:T(8,128)(2,1)} %get-tuple-element.218), channel_id=1, source_target_pairs={{0,4},{4,0},{1,5},{5,1},{2,6},{6,2},{3,7},{7,3},{8,12},{12,8},{9,1... | collective-permute-start | bytes 3145736 | tf_op jit(solution)/shard_map/y_out/ppermute | solution.py:37
  480.6 24.6 %collective-permute-start.50 = (bf16[2,256,512]{2,1,0:T(8,128)(2,1)S(1)}, bf16[2,256,512]{2,1,0:T(8,128)(2,1)}, u32[]{:S(2)}, u32[]{:S(2)}) collective-permute-start(bf16[2,256,512]{2,1,0:T(8,128)(2,1)S(1)} %add_convert_fusion.18), channel_id=1, source_target_pairs={{0,16},{16,0},{1,17},{17,1},{2,18},{18,2},{3,19},{19,3},{4,20},{20... | collective-permute-start | bytes 1572872 | tf_op jit(solution)/shard_map/zh_gdown/ppermute | solution.py:37
  480.7 51.5 %collective-permute-start.53 = (bf16[4,256,512]{2,1,0:T(8,128)(2,1)}, bf16[4,256,512]{2,1,0:T(8,128)(2,1)}, u32[]{:S(2)}, u32[]{:S(2)}) collective-permute-start(bf16[4,256,512]{2,1,0:T(8,128)(2,1)} %get-tuple-element.225), channel_id=1, source_target_pairs={{0,4},{4,0},{1,5},{5,1},{2,6},{6,2},{3,7},{7,3},{8,12},{12,8},{9,1... | collective-permute-start | bytes 3145736 | tf_op jit(solution)/shard_map/y_swish/ppermute | solution.py:37
  506.5 25.7 %collective-permute-start.52 = (bf16[2,256,512]{2,1,0:T(8,128)(2,1)S(1)}, bf16[2,256,512]{2,1,0:T(8,128)(2,1)}, u32[]{:S(2)}, u32[]{:S(2)}) collective-permute-start(bf16[2,256,512]{2,1,0:T(8,128)(2,1)S(1)} %add_convert_fusion.17), channel_id=1, source_target_pairs={{0,16},{16,0},{1,17},{17,1},{2,18},{18,2},{3,19},{19,3},{4,20},{20... | collective-permute-start | bytes 1572872 | tf_op jit(solution)/shard_map/zh_gout/ppermute | solution.py:37
  532.2 25.9 %collective-permute-start.57 = (bf16[3,192,2048]{2,1,0:T(8,128)(2,1)}, bf16[3,192,2048]{2,1,0:T(8,128)(2,1)}, u32[]{:S(2)}, u32[]{:S(2)}) collective-permute-start(bf16[3,192,2048]{2,1,0:T(8,128)(2,1)} %get-tuple-element.228), channel_id=1, source_target_pairs={{0,1},{1,0},{2,3},{3,2},{4,5},{5,4},{6,7},{7,6},{8,9},{9,8},{10,11... | collective-permute-start | bytes 7077896 | tf_op jit(solution)/shard_map/back_one_cr/ppermute | solution.py:37
  532.7 25.4 %collective-permute-start.58 = (bf16[4,256,512]{2,1,0:T(8,128)(2,1)}, bf16[4,256,512]{2,1,0:T(8,128)(2,1)}, u32[]{:S(2)}, u32[]{:S(2)}) collective-permute-start(bf16[4,256,512]{2,1,0:T(8,128)(2,1)} %get-tuple-element.229), channel_id=1, source_target_pairs={{0,4},{4,0},{1,5},{5,1},{2,6},{6,2},{3,7},{7,3},{8,12},{12,8},{9,1... | collective-permute-start | bytes 3145736 | tf_op jit(solution)/shard_map/y_value/ppermute | solution.py:37
  535.6 31.9 %collective-permute-start.67 = (bf16[2,256,512]{2,1,0:T(8,128)(2,1)}, bf16[2,256,512]{2,1,0:T(8,128)(2,1)}, u32[]{:S(2)}, u32[]{:S(2)}) collective-permute-start(bf16[2,256,512]{2,1,0:T(8,128)(2,1)} %add_convert_fusion.10), channel_id=1, source_target_pairs={{0,16},{16,0},{1,17},{17,1},{2,18},{18,2},{3,19},{19,3},{4,20},{20... | collective-permute-start | bytes 1572872 | tf_op jit(solution)/shard_map/zh_gswish/ppermute | solution.py:37
  538.1 20.0 %collective-permute-start.56 = (bf16[96,2048]{1,0:T(8,128)(2,1)}, bf16[96,2048]{1,0:T(8,128)(2,1)}, u32[]{:S(2)}, u32[]{:S(2)}) collective-permute-start(bf16[96,2048]{1,0:T(8,128)(2,1)} %get-tuple-element.274), channel_id=1, source_target_pairs={{0,8},{8,0},{1,9},{9,1},{2,10},{10,2},{3,11},{11,3},{4,12},{12,4},... | collective-permute-start | bytes 1179656 | tf_op jit(solution)/shard_map/back_one_dz/ppermute | solution.py:37
  545.5 43.9 %all-to-all-start.4 = ((bf16[4,128,1536]{2,1,0:T(8,128)(2,1)}), bf16[4,128,1536]{2,1,0:T(8,128)(2,1)}, u32[]{:S(2)}, u32[]{:S(2)}) async-start(bf16[4,128,1536]{2,1,0:T(8,128)(2,1)} %pad_maximum_fusion), calls=%async_computation.5 | async-start | bytes 3145728 | tf_op jit(solution)/shard_map/all_to_all | solution.py:59
  564.7 24.7 %collective-permute-start.59 = (bf16[192,2048]{1,0:T(8,128)(2,1)}, bf16[192,2048]{1,0:T(8,128)(2,1)}, u32[]{:S(2)}, u32[]{:S(2)}) collective-permute-start(bf16[192,2048]{1,0:T(8,128)(2,1)} %pad_maximum_fusion.10), channel_id=1, source_target_pairs={{0,2},{2,0},{1,3},{3,1},{4,6},{6,4},{5,7},{7,5},{8,10},{10,8},{9,1... | collective-permute-start | bytes 2359304 | tf_op jit(solution)/shard_map/back_one_x/ppermute | solution.py:37
  566.1 40.1 %collective-permute-start.60 = (bf16[192,2048]{1,0:T(8,128)(2,1)}, bf16[192,2048]{1,0:T(8,128)(2,1)}, u32[]{:S(2)}, u32[]{:S(2)}) collective-permute-start(bf16[192,2048]{1,0:T(8,128)(2,1)} %pad_maximum_fusion.11), channel_id=1, source_target_pairs={{0,8},{8,0},{1,9},{9,1},{2,10},{10,2},{3,11},{11,3},{4,12},{12,4},... | collective-permute-start | bytes 2359304 | tf_op jit(solution)/shard_map/back_one_z/ppermute | solution.py:37
  569.5 52.5 %collective-permute-start.68 = (bf16[2,256,512]{2,1,0:T(8,128)(2,1)}, bf16[2,256,512]{2,1,0:T(8,128)(2,1)}, u32[]{:S(2)}, u32[]{:S(2)}) collective-permute-start(bf16[2,256,512]{2,1,0:T(8,128)(2,1)} %add_convert_fusion.9), channel_id=1, source_target_pairs={{0,16},{16,0},{1,17},{17,1},{2,18},{18,2},{3,19},{19,3},{4,20},{20... | collective-permute-start | bytes 1572872 | tf_op jit(solution)/shard_map/zh_gvalue/ppermute | solution.py:37
  570.7 51.4 %collective-permute-start.66 = (bf16[4,256,512]{2,1,0:T(8,128)(2,1)}, bf16[4,256,512]{2,1,0:T(8,128)(2,1)}, u32[]{:S(2)}, u32[]{:S(2)}) collective-permute-start(bf16[4,256,512]{2,1,0:T(8,128)(2,1)} %get-tuple-element.240), channel_id=1, source_target_pairs={{0,4},{4,0},{1,5},{5,1},{2,6},{6,2},{3,7},{7,3},{8,12},{12,8},{9,1... | collective-permute-start | bytes 3145736 | tf_op jit(solution)/shard_map/y_qk/ppermute | solution.py:37
  614.0 35.9 %all-to-all-start.5 = ((bf16[4,128,1024]{2,1,0:T(8,128)(2,1)}), bf16[4,128,1024]{2,1,0:T(8,128)(2,1)}, u32[]{:S(2)}, u32[]{:S(2)}) async-start(bf16[4,128,1024]{2,1,0:T(8,128)(2,1)} %pad_maximum_fusion.4), calls=%async_computation.6 | async-start | bytes 2097152 | tf_op jit(solution)/shard_map/all_to_all | solution.py:59
  623.2 26.6 %collective-permute-start.69 = (bf16[2,256,512]{2,1,0:T(8,128)(2,1)S(1)}, bf16[2,256,512]{2,1,0:T(8,128)(2,1)}, u32[]{:S(2)}, u32[]{:S(2)}) collective-permute-start(bf16[2,256,512]{2,1,0:T(8,128)(2,1)S(1)} %add_convert_fusion.7), channel_id=1, source_target_pairs={{0,16},{16,0},{1,17},{17,1},{2,18},{18,2},{3,19},{19,3},{4,20},{20... | collective-permute-start | bytes 1572872 | tf_op jit(solution)/shard_map/zh_gqk/ppermute | solution.py:37
  642.3 20.0 %collective-permute-start.64 = (f32[2,2048]{1,0:T(2,128)S(1)}, f32[2,2048]{1,0:T(2,128)S(1)}, u32[]{:S(2)}, u32[]{:S(2)}) collective-permute-start(f32[2,2048]{1,0:T(2,128)S(1)} %add.286), channel_id=1, source_target_pairs={{0,4},{4,0},{1,5},{5,1},{2,6},{6,2},{3,7},{7,3},{8,12},{12,8},{9,1... | collective-permute-start | bytes 49160 | tf_op jit(solution)/shard_map/move/ppermute | solution.py:37
  654.1 25.9 %all-to-all-start.6 = ((bf16[4,128,1024]{2,1,0:T(8,128)(2,1)}), bf16[4,128,1024]{2,1,0:T(8,128)(2,1)}, u32[]{:S(2)}, u32[]{:S(2)}) async-start(bf16[4,128,1024]{2,1,0:T(8,128)(2,1)} %pad_maximum_fusion.5), calls=%async_computation.7 | async-start | bytes 2097152 | tf_op jit(solution)/shard_map/all_to_all | solution.py:59
  (92 other events, 834.9 us)
Sparse Core Ops, SparseCore 0:
  32.0 65.9 all-gather.4
  149.7 82.5 all-gather.6
  428.0 71.4 reduce-scatter.1

commit v4 on v3

--- a/solution.py
+++ b/solution.py
@@ -418,7 +418,7 @@
         scale_out[0, at, :] = jnp.broadcast_to(scale, (step, 128))
         return carry
 
-    lax.fori_loop(0, rows // step, chunk, 0)
+    lax.fori_loop(0, rows // step, chunk, 0, unroll=4)
 
 
 def attend(coord, mask, acts, wqk, wv, key_size):
@@ -470,7 +470,7 @@
         gated_out[0, at, :] = (s / (1.0 + jnp.exp(-s)) * hat[0, at, :]).astype(bf16)
         return carry
 
-    lax.fori_loop(0, rows // step, chunk, 0)
+    lax.fori_loop(0, rows // step, chunk, 0, unroll=4)
 
     @pl.when(r == 0)
     def _():
@@ -551,7 +551,7 @@
         gate_out[0, at, :] = (e * u * slope).astype(bf16)
         return carry
 
-    lax.fori_loop(0, gh.shape[0] // step, chunk, 0)
+    lax.fori_loop(0, gh.shape[0] // step, chunk, 0, unroll=4)
     partial_rows([up_out[0], gate_out[0]], [held_u, held_g], r, keep, store)
     at_chip_start(r, sends)
 
@@ -675,7 +675,7 @@
         gr[at, :] = (f * scale[0, at, :1]).astype(bf16)
         return carry
 
-    lax.fori_loop(0, rows // step, chunk, 0)
+    lax.fori_loop(0, rows // step, chunk, 0, unroll=4)
     grad_retained = gr[...]
     gv_out[0] = dot(scores[0], grad_retained, TN).astype(bf16)
     raw = (dot(grad_retained, v[0], NT) * mask[0]).astype(bf16)
@@ -779,6 +779,35 @@
     return [(got[2 * i], got[2 * i + 1]) for i in range(len(grads))]
 
 
+def place_body(parts, g, *outs):
+    column = 0
+    for (width, way), out in zip(parts, outs):
+        value = g[0, :, column : column + width].astype(f32)
+        out[...] = value.T if way == "r" else value
+        column += width
+
+
+def place(g, parts):
+    rows = g.shape[1]
+    outs, specs = [], []
+    for width, way in parts:
+        if way == "r":
+            outs.append(struct((4 * width, rows), f32))
+            specs.append(pl.BlockSpec((width, rows), lambda q: (q, 0)))
+        else:
+            outs.append(struct((rows, 4 * width), f32))
+            specs.append(pl.BlockSpec((rows, width), lambda q: (0, q)))
+    return pl.pallas_call(
+        functools.partial(place_body, parts),
+        grid=(4,),
+        in_specs=[by_chip(g.shape[1:])],
+        out_specs=specs,
+        out_shape=outs,
+        compiler_params=pltpu.CompilerParams(dimension_semantics=("arbitrary",)),
+        cost_estimate=pl.CostEstimate(flops=0, bytes_accessed=6 * g.size, transcendentals=0),
+    )(g)
+
+
 def scatter_whole(g):
     zh, n = lax.axis_size("zh"), g.shape[2]
     if zh == 2:
@@ -839,9 +868,10 @@
         seg_d = lax.ppermute(segments, GROUP, [(i, 3 - i) for i in range(4)])
     parts = (by_quarter(w) for w in (w_query, w_key, w_value))
     piece = group_exchange(beside(*parts))
+    grad_rows = [lax.all_gather(cotangent, everyone, axis=0)]
     parts = beside(by_quarter(w_swish), by_quarter(w_out.T))
 
-    clock.done(piece, seg_x, seg_z, seg_d, parts)
+    clock.done(piece, parts)
     unit_qkv = pipe.step(clock, piece, "qkv")
     piece = group_exchange(at(parts))
     normed_local = layer_norm(rows_local, norm1_gain).astype(bf16)
@@ -853,25 +883,22 @@
     allowed = (offset >= 0)[None] & (segs[:, :, None] == segs[:, None, :])
     distance = jnp.maximum(offset, 0).astype(f32)
     decay_mask = jnp.where(allowed, jnp.exp(-rate * distance)[None], 0.0)
-    parts = beside(by_quarter(at(w_up)), by_quarter(at(w_gate)))
+    parts = beside(by_quarter(at(w_up)), by_quarter(at(w_gate)), by_quarter(at(w_down).T))
 
     clock.done(piece, parts, decay_mask, *pipe.moved)
     unit_so = pipe.step(clock, piece, "so")
     piece = group_exchange(at(parts))
-    parts = by_quarter(at(w_down).T)
     full_qk, full_value = unit_qkv.weight(0, width), unit_qkv.weight(width, width)
     query, key, values, scores, hat, scale = attend(
         at(coord), decay_mask, normed, full_qk, full_value, key_size
     )
 
-    clock.done(query, piece, parts, *pipe.moved)
-    unit_ug = pipe.step(clock, piece, "ug")
-    piece = group_exchange(at(parts))
-    grad_rows = [lax.all_gather(at(cotangent), everyone, axis=0)]
+    clock.done(query, piece, *pipe.moved)
+    unit_ug = pipe.step(clock, piece[:, :, : 2 * width], "ug")
     full_swish, full_out = unit_so.weight(0, width), unit_so.weight(width, width)
     swish_in, gated, *partial = branch(at(coord), hat, normed, full_swish, full_out)
-    clock.done(piece, *pipe.moved, *partial)
-    unit_d = pipe.step(clock, piece, "d")
+    clock.done(*pipe.moved, *partial)
+    unit_d = pipe.step(clock, piece[:, :, 2 * width :], "d")
     scatter = Scatter(*partial, "branch", clock)
     scatter.relay(free)
     clock.done(*scatter.second)
@@ -894,14 +921,14 @@
     scatter = Scatter(*partial, "back_two", free)
     clock.done(scatter.diag)
     scatter.relay(clock)
+    (g_down,) = weight_grads(at(coord), grad_rows, [hidden])
+    g_down = WeightGrad(g_down, "down")
+    clock.done(g_down.send, *scatter.second)
+    scatter.send(clock)
+    g_down.to_y(clock)
     g_up, g_gate = weight_grads(at(coord), normed_two, [grad_up_rows, grad_gate_rows])
     g_up, g_gate = WeightGrad(g_up, "up"), WeightGrad(g_gate, "gate")
-    clock.done(g_up.send, *scatter.second)
-    scatter.send(clock)
-    g_up.to_y(clock)
-    (g_down,) = weight_grads(at(coord), grad_rows, [hidden])
-    g_down = WeightGrad(g_down, "down")
-    clock.done(g_down.send, g_up.y, *scatter.last)
+    clock.done(g_up.send, g_down.y, *scatter.last)
     back_two_local = scatter.finish(clock)
     _, norm_two_pull = jax.vjp(layer_norm, middle, norm2_gain)
     grad_mid_norm, grad_norm2_local = norm_two_pull(back_two_local)
@@ -910,10 +937,11 @@
 
     clock.done(grad_branch_local)
     gather = Gather(clock, grad_branch_local, "gb", True)
+    g_down.to_zh(clock)
+    g_up.to_y(clock)
+    clock.done(g_down.zh, g_up.y, *gather.first)
+    gather.second(clock)
     g_gate.to_y(clock)
-    clock.done(g_gate.y, *gather.first)
-    gather.second(clock)
-    g_down.to_y(clock)
     (feed,) = back(at(coord), [hidden], [full_down], True)
     clock.done(feed, *gather.held)
     grad_branch = gather.finish(clock)
@@ -932,7 +960,7 @@
         grad_branch,
         full_out,
     )
-    clock.done(grad_qk, g_up.zh, g_down.y)
+    clock.done(grad_qk, g_up.zh, g_gate.y)
     g_gate.to_zh(clock)
     (g_out,) = weight_grads(at(coord), grad_branch, [gated])
     g_out = WeightGrad(g_out, "out")
@@ -941,52 +969,45 @@
     (g_swish,) = weight_grads(at(coord), normed, [grad_swish_in])
     g_swish = WeightGrad(g_swish, "swish")
     clock.done(g_swish.send, g_gate.zh)
-    g_down.to_zh(clock)
-    g_swish.to_y(clock)
     g_value, g_qk = weight_grads(at(coord), normed, [grad_values, grad_qk])
     g_value, g_qk = WeightGrad(g_value, "value"), WeightGrad(g_qk, "qk")
-    clock.done(g_value.send, g_down.zh, g_out.y)
+    clock.done(g_value.send, g_out.y)
     g_out.to_zh(clock)
-    g_value.to_y(clock)
+    g_swish.to_y(clock)
     partial = back(
         at(coord), [grad_qk, grad_values, grad_swish_in], [full_qk, full_value, full_swish]
     )
     clock.done(g_out.zh, g_swish.y, *partial)
     g_swish.to_zh(clock)
+    g_value.to_y(clock)
     scatter = Scatter(*partial, "back_one", clock)
     clock.done(scatter.diag)
     scatter.relay(clock)
+    clock.done(*scatter.second)
+    scatter.send(clock)
+    clock.done(g_swish.zh, g_value.y)
+    g_value.to_zh(clock)
+    g_qk.to_y(clock)
     grad_ff = group_exchange(beside(g_up.sum(clock), g_gate.sum(clock), g_down.sum(clock)))
-    clock.done(g_value.y, *scatter.second)
-    g_qk.to_y(clock)
-    scatter.send(clock)
-    clock.done(g_swish.zh)
-    g_value.to_zh(clock)
-    clock.done(grad_ff, *scatter.last)
+    clock.done(g_value.zh, g_qk.y)
+    g_qk.to_zh(clock)
+    clock.done(*scatter.last)
     back_one_local = scatter.finish(clock)
-    grad_os = group_exchange(beside(g_out.sum(clock), g_swish.sum(clock)))
-    clock.done(g_qk.y, g_value.zh)
-    g_qk.to_zh(clock)
+    grad_os = group_exchange(after(beside(g_out.sum(clock), g_swish.sum(clock)), grad_ff))
+    grad_up, grad_gate, grad_down = place(at(grad_ff), ((width, "c"), (width, "c"), (width, "r")))
     mixed = (middle + feed.reshape(middle.shape).astype(f32)).astype(bf16)
-    clock.done(g_qk.zh, grad_os)
-    grad_qkv = group_exchange(beside(g_qk.sum(clock), g_value.sum(clock)))
-
-    def columns(g):
-        return g.transpose(1, 0, 2).reshape(rows_q, -1).astype(f32)
-
-    def rows(g):
-        return g.transpose(0, 2, 1).reshape(-1, rows_q).astype(f32)
-
-    grad_up, grad_gate = columns(grad_ff[:, :, :width]), columns(grad_ff[:, :, width : 2 * width])
-    grad_down = rows(grad_ff[:, :, 2 * width :])
-    grad_query = columns(grad_qkv[:, :, :key_size])
-    grad_key, grad_value = columns(grad_qkv[:, :, key_size:width]), columns(grad_qkv[:, :, width:])
-    grad_out, grad_swish = rows(grad_os[:, :, :width]), columns(grad_os[:, :, width:])
-
     _, norm_one_pull = jax.vjp(layer_norm, rows_local, norm1_gain)
     grad_tok_norm, grad_norm1_local = norm_one_pull(back_one_local)
     grad_tokens = grad_middle + grad_tok_norm
-    grad_norm1, grad_norm2 = sum_everywhere(jnp.stack([grad_norm1_local, grad_norm2_local]))
+    grad_norm1, grad_norm2 = sum_everywhere(
+        after(jnp.stack([grad_norm1_local, grad_norm2_local]), g_qk.zh)
+    )
+    clock.done(g_qk.zh, grad_os, grad_up, mixed, grad_norm1, grad_tokens)
+    grad_qkv = group_exchange(beside(g_qk.sum(clock), g_value.sum(clock)))
+    grad_out, grad_swish = place(at(grad_os), ((width, "r"), (width, "c")))
+    parts = ((key_size, "c"), (key_size, "c"), (width, "c"))
+    grad_query, grad_key, grad_value = place(grad_qkv, parts)
+
     return (
         mixed,
         grad_tokens,

time: 702 us -> 681 us (0.970)
  waiting for transfers between devices: 272 us -> 292 us
  starting transfers between devices: 115 us -> 97.1 us
  other arithmetic: 74.1 us -> 57.4 us
  local copies, waits for them, and re-layouts: 36 us -> 25.7 us
    ppermute x69, waiting for transfers between devices: 242 us -> 273 us  [swap(): return lax.ppermute(a, axis, [(0, 1), (1, 0)])]
    all_to_all x7 -> x6, starting transfers between devices: 54.7 us -> 30.7 us  [group_exchange(): return lax.all_to_all(parts, GROUP, 0, 0, tiled=True)]
    convert_element_type x8 -> x0, local copies, waits for them, and re-layouts: 12.2 us -> none  [the longest x6 7.18 us: columns(): return g.transpose(1, 0, 2).reshape(rows_q, -1).astype(f32)]
    pallas_call x0 -> x3, Pallas kernels: none -> 11 us  [place(): pl.pallas_call(functools.partial(place_body, parts), grid=(4,), in_specs=...]
    all_to_all x7 -> x6, waiting for transfers between devices: 28.8 us -> 19.1 us  [group_exchange(): return lax.all_to_all(parts, GROUP, 0, 0, tiled=True)]
    pallas_call x6, Pallas kernels: 116 us -> 108 us  [chip_kernel(): pl.pallas_call(body, grid=(4,), in_specs=specs, out_specs=out_specs, out_...]
    unnamed x124 -> x130, local copies, waits for them, and re-layouts: 14.6 us -> 14.9 us
  transfers between devices with their start and end apart: 80 -> 79, of which waited for: 38 -> 35; matrix products, arithmetic and copies ran while one was open for 13% -> 9% of each run, Pallas kernels for 22% -> 23%
where the time goes in v4:
time: 681 us; the launch traced here: 673 us
  waiting for transfers between devices  292 us (43%)
  Pallas kernels  185 us (27%)
  starting transfers between devices  97.1 us (14%)
  other arithmetic  57.4 us (8%)
  local copies, waits for them, and re-layouts  25.7 us (4%)
  between operations  16.3 us (2%)
    ppermute x69, waiting for transfers between devices, swap(): return lax.ppermute(a, axis, [(0, 1), (1, 0)])  273 us
    pallas_call x6, Pallas kernels, chip_kernel(): pl.pallas_call(body, grid=(4,), in_specs=specs, out_specs=out_specs, out_...  108 us
    pallas_call x5, Pallas kernels, weight_grads(): pl.pallas_call(functools.partial(weight_grad_body, len(grads), len(acts),...  65.7 us
    ppermute x69, starting transfers between devices, swap(): return lax.ppermute(a, axis, [(0, 1), (1, 0)])  64.8 us
    all_to_all x6, starting transfers between devices, group_exchange(): return lax.all_to_all(parts, GROUP, 0, 0, tiled=True)  30.7 us
    convert_element_type x16, other arithmetic, add(): return (a.astype(f32) + b.astype(f32)).astype(bf16)  20.3 us
    all_to_all x6, waiting for transfers between devices, group_exchange(): return lax.all_to_all(parts, GROUP, 0, 0, tiled=True)  19.1 us
    unnamed x130, local copies, waits for them, and re-layouts  14.9 us
  transfers between devices with their start and end apart: 79, of which 35 were waited for; matrix products, arithmetic and copies ran while one was open for 9% of the time, Pallas kernels for 23%

profile of v4, /device:TPU:0, one launch (start us, length us, event | category | flops | bytes accessed | tf_op | source)
XLA Modules:
  0.0 672.9 jit_solution(5115681426406011831)
XLA Ops:
  11.4 5.2 all-to-all-start
  21.5 8.8 %all-to-all-done.refs_1_.refs_5_.refs_3_.refs_7_ = bf16[4,128,1024]{2,1,0:T(8,128)(2,1)S(1)} async-done(((bf16[4,128,1024]{2,1,0:T(8,128)(2,1)}), bf16[4,128,1024]{2,1,0:T(8,128)(2,1)S(1)}, u32[]{:S(2)}, u32[]{:S(2)}) %all-to-all-start) | async-done | bytes 1048608 | tf_op jit(solution)/shard_map/all_to_all | solution.py:59
  35.2 3.5 all-to-all-start.1
  50.1 13.1 %collective-permute-done.4.refs_2_.refs_6_.refs_4_.refs_8_ = bf16[4,128,1024]{2,1,0:T(8,128)(2,1)} collective-permute-done((bf16[4,128,1024]{2,1,0:T(8,128)(2,1)}, bf16[4,128,1024]{2,1,0:T(8,128)(2,1)}, u32[]{:S(2)}, u32[]{:S(2)}) %collective-permute-start.4) | collective-permute-done | bytes 1048608 | tf_op jit(solution)/shard_map/ny_qkv/ppermute | solution.py:37
  63.2 30.2 %collective-permute-done.3.refs_3_.refs_7_.refs_5_.refs_9_ = bf16[4,128,1024]{2,1,0:T(8,128)(2,1)} collective-permute-done((bf16[4,128,1024]{2,1,0:T(8,128)(2,1)}, bf16[4,128,1024]{2,1,0:T(8,128)(2,1)}, u32[]{:S(2)}, u32[]{:S(2)}) %collective-permute-start.3) | collective-permute-done | bytes 1048608 | tf_op jit(solution)/shard_map/zh_qkv/ppermute | solution.py:37
  93.4 9.8 %all-to-all-start.2 = ((bf16[4,128,1536]{2,1,0:T(8,128)(2,1)}), bf16[4,128,1536]{2,1,0:T(8,128)(2,1)S(1)}, u32[]{:S(2)}, u32[]{:S(2)}) async-start(bf16[4,128,1536]{2,1,0:T(8,128)(2,1)} %pad_maximum_fusion), calls=%async_computation.2 | async-start | bytes 3145728 | tf_op jit(solution)/shard_map/all_to_all | solution.py:59
  106.0 23.7 %collective-permute-done.5.refs_4_.refs_8_.refs_6_.refs_10_ = bf16[4,128,1024]{2,1,0:T(8,128)(2,1)} collective-permute-done((bf16[4,128,1024]{2,1,0:T(8,128)(2,1)}, bf16[4,128,1024]{2,1,0:T(8,128)(2,1)}, u32[]{:S(2)}, u32[]{:S(2)}) %collective-permute-start.5) | collective-permute-done | bytes 1048608 | tf_op jit(solution)/shard_map/fy_qkv/ppermute | solution.py:37
  129.7 23.2 %shard_map.229 = (bf16[4,384,256]{2,1,0:T(8,128)(2,1)}, bf16[4,384,256]{2,1,0:T(8,128)(2,1)}, bf16[4,384,512]{2,1,0:T(8,128)(2,1)}, bf16[4,384,384]{2,1,0:T(8,12...) custom-call(s32[4]{0:T(128)} %pad_add_fusion.1.coord, f32[4,384,384]{2,1,0:T(8,128)} %and_select_fusion.mask, ...), custom_call_target="tpu_custom_call" | custom-call | flops 6442450944 | bytes 25296912 | tf_op jit(solution)/shard_map/pallas_call | solution.py:309
  155.5 23.9 %collective-permute-done.8.refs_4_.refs_8_.refs_13_.refs_14_ = bf16[4,128,1024]{2,1,0:T(8,128)(2,1)} collective-permute-done((bf16[4,128,1024]{2,1,0:T(8,128)(2,1)}, bf16[4,128,1024]{2,1,0:T(8,128)(2,1)}, u32[]{:S(2)}, u32[]{:S(2)}) %collective-permute-start.8) | collective-permute-done | bytes 1048608 | tf_op jit(solution)/shard_map/fy_so/ppermute | solution.py:37
  179.4 15.0 %shard_map.230 = (f32[4,384,512]{2,1,0:T(8,128)}, bf16[4,384,512]{2,1,0:T(8,128)(2,1)}, bf16[3,192,2048]{2,1,0:T(8,128)(2,1)}, bf16[192,2048]{1,0:T(8,128)(2,1)}, bf16[4,192,2048]{2,1,0:T(8,128)(2,1)}) custom-call(s32[4]{0:T(128)} %pad_add_fusion.1.coord, f32[4,384,512]{2,1,0:T(8,128)} %get-tuple-element.152.hat, bf16[8,192,2048]{2,1,0:T(8,128)(2,1)} %bitcast.149, ...), custom_call_target="tpu_custom_call" | custom-call | flops 6442450944 | bytes 28835856 | tf_op jit(solution)/shard_map/pallas_call | solution.py:309
  194.5 2.6 collective-permute-done.10.refs_12_.refs_16_
  197.1 2.7 collective-permute-done.9.refs_13_.refs_17_
  200.2 5.9 collective-permute-done.11
  210.1 8.8 %collective-permute-done.13 = bf16[96,2048]{1,0:T(8,128)(2,1)S(1)} collective-permute-done((bf16[96,2048]{1,0:T(8,128)(2,1)S(1)}, bf16[96,2048]{1,0:T(8,128)(2,1)S(1)}, u32[]{:S(2)}, u32[]{:S(2)}) %collective-permute-start.13) | collective-permute-done | bytes 393248 | tf_op jit(solution)/shard_map/branch_dz/ppermute | solution.py:37
  220.6 3.2 collective-permute-start.15
  228.0 17.6 %collective-permute-done.18.refs_20_.refs_2_ = bf16[4,128,512]{2,1,0:T(8,128)(2,1)S(1)} collective-permute-done((bf16[4,128,512]{2,1,0:T(8,128)(2,1)S(1)}, bf16[4,128,512]{2,1,0:T(8,128)(2,1)S(1)}, u32[]{:S(2)}, u32[]{:S(2)}) %collective-permute-start.18) | collective-permute-done | bytes 524320 | tf_op jit(solution)/shard_map/ny_d/ppermute | solution.py:37
  245.6 6.3 collective-permute-done.17.refs_21_.refs_3_
  259.5 12.9 %collective-permute-done.23.refs_22_.refs_4_ = bf16[4,128,512]{2,1,0:T(8,128)(2,1)S(1)} collective-permute-done((bf16[4,128,512]{2,1,0:T(8,128)(2,1)S(1)}, bf16[4,128,512]{2,1,0:T(8,128)(2,1)S(1)}, u32[]{:S(2)}, u32[]{:S(2)}) %collective-permute-start.23) | collective-permute-done | bytes 524320 | tf_op jit(solution)/shard_map/fy_d/ppermute | solution.py:37
  277.6 10.2 %collective-permute-done.26.refs_6_.refs_8_ = bf16[96,2048]{1,0:T(8,128)(2,1)} collective-permute-done((bf16[96,2048]{1,0:T(8,128)(2,1)S(1)}, bf16[96,2048]{1,0:T(8,128)(2,1)}, u32[]{:S(2)}, u32[]{:S(2)}) %collective-permute-start.26) | collective-permute-done | bytes 393248 | tf_op jit(solution)/shard_map/two_dx/ppermute | solution.py:37
  291.8 27.2 %shard_map.231 = (bf16[4,384,512]{2,1,0:T(8,128)(2,1)}, bf16[4,384,512]{2,1,0:T(8,128)(2,1)}, bf16[4,384,512]{2,1,0:T(8,128)(2,1)}, bf16[3,192,2048]{2,1,0:T(8,1...) custom-call(s32[4]{0:T(128)} %pad_add_fusion.1.coord, bf16[192,2048]{1,0:T(8,128)(2,1)} %copy-done.29, ...), custom_call_target="tpu_custom_call" | custom-call | flops 16106127360 | bytes 34078736 | tf_op jit(solution)/shard_map/pallas_call | solution.py:309
  319.6 5.1 collective-permute-done.30
  328.5 10.8 %shard_map.232 = (bf16[4,256,512]{2,1,0:T(8,128)(2,1)}, bf16[4,256,512]{2,1,0:T(8,128)(2,1)}) custom-call(s32[4]{0:T(128)} %pad_add_fusion.1.coord, bf16[4,384,512]{2,1,0:T(8,128)(2,1)} %get-tuple-element.179.refs_0_, bf16[8,192,2048]{2,1,0:T(8,128)(2,1)} %bitcast.153), custom_call_target="tpu_custom_call" | custom-call | flops 3221225472 | bytes 9961472 | tf_op jit(solution)/shard_map/pallas_call | solution.py:763
  350.7 16.5 %shard_map.233 = (bf16[4,256,512]{2,1,0:T(8,128)(2,1)}, bf16[4,256,512]{2,1,0:T(8,128)(2,1)}, bf16[4,256,512]{2,1,0:T(8,128)(2,1)}, bf16[4,256,512]{2,1,0:T(8,128)(2,1)}) custom-call(s32[4]{0:T(128)} %pad_add_fusion.1.coord, bf16[4,384,512]{2,1,0:T(8,128)(2,1)} %get-tuple-element.189.refs_0_, bf16[4,384,512]{2,1,0:T(8,128)(2,1)} %get-tuple-element.190.refs_1_, ...), custom_call_target="tpu_custom_call" | custom-call | flops 6442450944 | bytes 13631488 | tf_op jit(solution)/shard_map/pallas_call | solution.py:763
  368.1 3.8 multiply_reduce_fusion
  378.9 26.4 %collective-permute-done.37 = bf16[2,256,512]{2,1,0:T(8,128)(2,1)S(1)} collective-permute-done((bf16[2,256,512]{2,1,0:T(8,128)(2,1)S(1)}, bf16[2,256,512]{2,1,0:T(8,128)(2,1)S(1)}, u32[]{:S(2)}, u32[]{:S(2)}) %collective-permute-start.37) | collective-permute-done | bytes 524320 | tf_op jit(solution)/shard_map/zh_gdown/ppermute | solution.py:37
  414.2 8.3 %shard_map.234 = bf16[8,192,2048]{2,1,0:T(8,128)(2,1)} custom-call(s32[4]{0:T(128)} %pad_add_fusion.1.coord, bf16[4,384,512]{2,1,0:T(8,128)(2,1)} %get-tuple-element.179.refs_0_, bf16[4,128,512]{2,1,0:T(8,128)(2,1)} %copy-done.34, bf16[4,128,512]{2,1,0:T(8,128)(2,1)} %copy-done.59, bf16[4,128,512]{2,1,0:T(8,128)(2,1)} %copy-done.60, ...), custom_call_target="tpu_custom_call" | custom-call | flops 3221225472 | bytes 9961488 | tf_op jit(solution)/shard_map/pallas_call | solution.py:309
  427.6 17.3 %shard_map.235 = (bf16[4,384,512]{2,1,0:T(8,128)(2,1)}, bf16[4,384,512]{2,1,0:T(8,128)(2,1)}, bf16[4,384,512]{2,1,0:T(8,128)(2,1)}) custom-call(s32[4]{0:T(128)} %pad_add_fusion.1.coord, f32[4,384,384]{2,1,0:T(8,128)} %and_select_fusion.mask, f32[4,384,512]{2,1,0:T(8,128)} %get-tuple-element.202.s, f32[4,384,512]{2,1,0:T(8,128)} %get-tuple-element.152.hat, ...), custom_call_target="tpu_custom_call" | custom-call | flops 4831838208 | bytes 28966928 | tf_op jit(solution)/shard_map/pallas_call | solution.py:309
  444.9 6.8 %collective-permute-done.48 = bf16[2,256,512]{2,1,0:T(8,128)(2,1)} collective-permute-done((bf16[2,256,512]{2,1,0:T(8,128)(2,1)}, bf16[2,256,512]{2,1,0:T(8,128)(2,1)}, u32[]{:S(2)}, u32[]{:S(2)}) %collective-permute-start.48) | collective-permute-done | bytes 524320 | tf_op jit(solution)/shard_map/zh_gup/ppermute | solution.py:37
  453.1 11.0 %shard_map.236 = (bf16[4,256,512]{2,1,0:T(8,128)(2,1)}, bf16[4,256,512]{2,1,0:T(8,128)(2,1)}) custom-call(s32[4]{0:T(128)} %pad_add_fusion.1.coord, bf16[4,384,512]{2,1,0:T(8,128)(2,1)} %get-tuple-element.215.refs_0_, bf16[192,2048]{1,0:T(8,128)(2,1)} %copy-done.11, bf16[192,2048]{1,0:T(8,128)(2,1)} %copy-done.30, ...), custom_call_target="tpu_custom_call" | custom-call | flops 3221225472 | bytes 9961472 | tf_op jit(solution)/shard_map/pallas_call | solution.py:763
  464.9 10.9 %shard_map.237 = (bf16[4,256,512]{2,1,0:T(8,128)(2,1)}, bf16[4,256,512]{2,1,0:T(8,128)(2,1)}) custom-call(s32[4]{0:T(128)} %pad_add_fusion.1.coord, bf16[4,384,512]{2,1,0:T(8,128)(2,1)} %get-tuple-element.218.refs_0_.refs_2_, bf16[8,192,2048]{2,1,0:T(8,128)(2,1)} %bitcast.150), custom_call_target="tpu_custom_call" | custom-call | flops 3221225472 | bytes 9961472 | tf_op jit(solution)/shard_map/pallas_call | solution.py:763
  478.2 16.4 %shard_map.238 = (bf16[4,256,512]{2,1,0:T(8,128)(2,1)}, bf16[4,256,512]{2,1,0:T(8,128)(2,1)}, bf16[4,256,512]{2,1,0:T(8,128)(2,1)}, bf16[4,256,512]{2,1,0:T(8,128)(2,1)}) custom-call(s32[4]{0:T(128)} %pad_add_fusion.1.coord, bf16[4,384,512]{2,1,0:T(8,128)(2,1)} %get-tuple-element.223.refs_0_.refs_1_, ...), custom_call_target="tpu_custom_call" | custom-call | flops 6442450944 | bytes 13631488 | tf_op jit(solution)/shard_map/pallas_call | solution.py:763
  498.0 17.0 %shard_map.239 = (bf16[3,192,2048]{2,1,0:T(8,128)(2,1)}, bf16[192,2048]{1,0:T(8,128)(2,1)}, bf16[4,192,2048]{2,1,0:T(8,128)(2,1)}) custom-call(s32[4]{0:T(128)} %pad_add_fusion.1.coord, bf16[4,384,512]{2,1,0:T(8,128)(2,1)} %get-tuple-element.209.refs_1_.refs_0_, bf16[4,384,512]{2,1,0:T(8,128)(2,1)} %get-tuple-element.223.refs_0_.refs_1_, ...), custom_call_target="tpu_custom_call" | custom-call | flops 9663676416 | bytes 23592976 | tf_op jit(solution)/shard_map/pallas_call | solution.py:309
  515.0 6.8 %collective-permute-done.52 = bf16[2,256,512]{2,1,0:T(8,128)(2,1)} collective-permute-done((bf16[2,256,512]{2,1,0:T(8,128)(2,1)S(1)}, bf16[2,256,512]{2,1,0:T(8,128)(2,1)}, u32[]{:S(2)}, u32[]{:S(2)}) %collective-permute-start.52) | collective-permute-done | bytes 524320 | tf_op jit(solution)/shard_map/zh_gout/ppermute | solution.py:37
  526.1 2.6 collective-permute-start.56
  529.7 19.9 %collective-permute-done.60 = bf16[2,256,512]{2,1,0:T(8,128)(2,1)S(1)} collective-permute-done((bf16[2,256,512]{2,1,0:T(8,128)(2,1)S(1)}, bf16[2,256,512]{2,1,0:T(8,128)(2,1)S(1)}, u32[]{:S(2)}, u32[]{:S(2)}) %collective-permute-start.60) | collective-permute-done | bytes 524320 | tf_op jit(solution)/shard_map/zh_gswish/ppermute | solution.py:37
  564.8 4.3 all-to-all-start.3
  569.2 7.1 %collective-permute-done.63 = bf16[2,256,512]{2,1,0:T(8,128)(2,1)} collective-permute-done((bf16[2,256,512]{2,1,0:T(8,128)(2,1)}, bf16[2,256,512]{2,1,0:T(8,128)(2,1)}, u32[]{:S(2)}, u32[]{:S(2)}) %collective-permute-start.63) | collective-permute-done | bytes 524320 | tf_op jit(solution)/shard_map/zh_gvalue/ppermute | solution.py:37
  577.6 2.6 collective-permute-start.64
  580.2 24.2 %collective-permute-done.59 = bf16[192,2048]{1,0:T(8,128)(2,1)} collective-permute-done((bf16[192,2048]{1,0:T(8,128)(2,1)}, bf16[192,2048]{1,0:T(8,128)(2,1)}, u32[]{:S(2)}, u32[]{:S(2)}) %collective-permute-start.59) | collective-permute-done | bytes 786464 | tf_op jit(solution)/shard_map/back_one_z/ppermute | solution.py:37
  604.4 2.7 fusion.9
  616.9 3.4 collective-permute-done.67
  625.4 4.3 all-to-all-start.4
  629.6 3.7 add_add_fusion.2
  634.0 3.8 shard_map.240
  644.9 3.5 all-to-all-start.5
  648.4 3.6 shard_map.242
  652.0 9.5 %all-to-all-done.5.g = bf16[4,128,1024]{2,1,0:T(8,128)(2,1)S(1)} async-done(((bf16[4,128,1024]{2,1,0:T(8,128)(2,1)}), bf16[4,128,1024]{2,1,0:T(8,128)(2,1)S(1)}, u32[]{:S(2)}, u32[]{:S(2)}) %all-to-all-start.5) | async-done | bytes 1048608 | tf_op jit(solution)/shard_map/all_to_all | solution.py:59
  662.4 3.5 shard_map.241
  (363 shorter events, 146.6 us)
Async XLA Ops:
  11.4 18.9 %all-to-all-start = ((bf16[4,128,1024]{2,1,0:T(8,128)(2,1)}), bf16[4,128,1024]{2,1,0:T(8,128)(2,1)S(1)}, u32[]{:S(2)}, u32[]{:S(2)}) async-start(bf16[4,128,1024]{2,1,0:T(8,128)(2,1)} %pad_maximum_fusion.3), calls=%async_computation | async-start | bytes 2097152 | tf_op jit(solution)/shard_map/all_to_all | solution.py:59
  16.7 113.0 %all-gather.5.cloned.1.call-start = ((), (), s32[]{:S(2)}) async-start(), calls=%async_computation.8 | async-start | bytes 7077888 | tf_op jit(solution)/shard_map/all_gather | solution.py:878
  35.2 58.3 %all-to-all-start.1 = ((bf16[4,128,1024]{2,1,0:T(8,128)(2,1)}), bf16[4,128,1024]{2,1,0:T(8,128)(2,1)S(1)}, u32[]{:S(2)}, u32[]{:S(2)}) async-start(bf16[4,128,1024]{2,1,0:T(8,128)(2,1)} %pad_maximum_fusion.2), calls=%async_computation.1 | async-start | bytes 2097152 | tf_op jit(solution)/shard_map/all_to_all | solution.py:59
  38.9 24.3 %collective-permute-start.4 = (bf16[4,128,1024]{2,1,0:T(8,128)(2,1)}, bf16[4,128,1024]{2,1,0:T(8,128)(2,1)}, u32[]{:S(2)}, u32[]{:S(2)}) collective-permute-start(bf16[4,128,1024]{2,1,0:T(8,128)(2,1)} %copy-done.12), channel_id=1, source_target_pairs={{0,4},{4,0},{1,5},{5,1},{2,6},{6,2},{3,7},{7,3},{8,12},{12,8},{9,1... | collective-permute-start | bytes 3145736 | tf_op jit(solution)/shard_map/ny_qkv/ppermute | solution.py:37
  40.5 52.9 %collective-permute-start.3 = (bf16[4,128,1024]{2,1,0:T(8,128)(2,1)}, bf16[4,128,1024]{2,1,0:T(8,128)(2,1)}, u32[]{:S(2)}, u32[]{:S(2)}) collective-permute-start(bf16[4,128,1024]{2,1,0:T(8,128)(2,1)} %copy-done.12), channel_id=1, source_target_pairs={{0,16},{16,0},{1,17},{17,1},{2,18},{18,2},{3,19},{19,3},{4,20},{20... | collective-permute-start | bytes 3145736 | tf_op jit(solution)/shard_map/zh_qkv/ppermute | solution.py:37
  93.4 59.5 %all-to-all-start.2 = ((bf16[4,128,1536]{2,1,0:T(8,128)(2,1)}), bf16[4,128,1536]{2,1,0:T(8,128)(2,1)S(1)}, u32[]{:S(2)}, u32[]{:S(2)}) async-start(bf16[4,128,1536]{2,1,0:T(8,128)(2,1)} %pad_maximum_fusion), calls=%async_computation.2 | async-start | bytes 3145728 | tf_op jit(solution)/shard_map/all_to_all | solution.py:59
  103.3 186.5 %all-gather.7.cloned.1.call-start = ((), (), s32[]{:S(2)}) async-start(), calls=%async_computation.9 | async-start | bytes 7077888 | tf_op jit(solution)/shard_map/all_gather | solution.py:871
  103.3 26.4 %collective-permute-start.5 = (bf16[4,128,1024]{2,1,0:T(8,128)(2,1)}, bf16[4,128,1024]{2,1,0:T(8,128)(2,1)}, u32[]{:S(2)}, u32[]{:S(2)}) collective-permute-start(bf16[4,128,1024]{2,1,0:T(8,128)(2,1)} %collective-permute-done.3.refs_3_.refs_7_.refs_5_.refs_9_), channel_id=1, source_target_pairs={{0,4},{4,0},{1,5},{5,1},{2,6},{6,2},{3,7},{7,3},{8,12},{12,8},{9,1... | collective-permute-start | bytes 3145736 | tf_op jit(solution)/shard_map/fy_qkv/ppermute | solution.py:37
  104.8 48.1 %collective-permute-start.7 = (bf16[4,128,1024]{2,1,0:T(8,128)(2,1)S(1)}, bf16[4,128,1024]{2,1,0:T(8,128)(2,1)}, u32[]{:S(2)}, u32[]{:S(2)}) collective-permute-start(bf16[4,128,1024]{2,1,0:T(8,128)(2,1)S(1)} %all-to-all-done.1.refs_1_.refs_5_.refs_10_.refs_11_), channel_id=1, source_target_pairs={{0,4},{4,0},{1,5},{5,1},{2,6},{6,2},{3,7},{7,3},{8,12},{12,8},{9,1... | collective-permute-start | bytes 3145736 | tf_op jit(solution)/shard_map/ny_so/ppermute | solution.py:37
  105.3 47.6 %collective-permute-start.6 = (bf16[4,128,1024]{2,1,0:T(8,128)(2,1)S(1)}, bf16[4,128,1024]{2,1,0:T(8,128)(2,1)}, u32[]{:S(2)}, u32[]{:S(2)}) collective-permute-start(bf16[4,128,1024]{2,1,0:T(8,128)(2,1)S(1)} %all-to-all-done.1.refs_1_.refs_5_.refs_10_.refs_11_), channel_id=1, source_target_pairs={{0,16},{16,0},{1,17},{17,1},{2,18},{18,2},{3,19},{19,3},{4,20},{20... | collective-permute-start | bytes 3145736 | tf_op jit(solution)/shard_map/zh_so/ppermute | solution.py:37
  152.9 26.5 %collective-permute-start.8 = (bf16[4,128,1024]{2,1,0:T(8,128)(2,1)}, bf16[4,128,1024]{2,1,0:T(8,128)(2,1)}, u32[]{:S(2)}, u32[]{:S(2)}) collective-permute-start(bf16[4,128,1024]{2,1,0:T(8,128)(2,1)} %collective-permute-done.6.refs_3_.refs_7_.refs_12_.refs_13_), channel_id=1, source_target_pairs={{0,4},{4,0},{1,5},{5,1},{2,6},{6,2},{3,7},{7,3},{8,12},{12,8},{9,1... | collective-permute-start | bytes 3145736 | tf_op jit(solution)/shard_map/fy_so/ppermute | solution.py:37
  154.6 483.3 %reduce-scatter.2.cloned.1.call-start = ((), (), s32[]{:S(2)}) async-start(), calls=%async_computation.7 | async-start | bytes 7077888 | tf_op jit(solution)/shard_map/reduce_scatter | solution.py:948
  155.0 42.1 %collective-permute-start.10 = (bf16[4,128,1024]{2,1,0:T(8,128)(2,1)S(1)}, bf16[4,128,1024]{2,1,0:T(8,128)(2,1)}, u32[]{:S(2)}, u32[]{:S(2)}) collective-permute-start(bf16[4,128,1024]{2,1,0:T(8,128)(2,1)S(1)} %slice.358.refs_11_.refs_15_), channel_id=1, source_target_pairs={{0,4},{4,0},{1,5},{5,1},{2,6},{6,2},{3,7},{7,3},{8,12},{12,8},{9,1... | collective-permute-start | bytes 3145736 | tf_op jit(solution)/shard_map/ny_ug/ppermute | solution.py:37
  155.5 44.2 %collective-permute-start.9 = (bf16[4,128,1024]{2,1,0:T(8,128)(2,1)S(1)}, bf16[4,128,1024]{2,1,0:T(8,128)(2,1)}, u32[]{:S(2)}, u32[]{:S(2)}) collective-permute-start(bf16[4,128,1024]{2,1,0:T(8,128)(2,1)S(1)} %slice.358.refs_11_.refs_15_), channel_id=1, source_target_pairs={{0,16},{16,0},{1,17},{17,1},{2,18},{18,2},{3,19},{19,3},{4,20},{20... | collective-permute-start | bytes 3145736 | tf_op jit(solution)/shard_map/zh_ug/ppermute | solution.py:37
  199.7 19.3 %collective-permute-start.14 = (bf16[3,192,2048]{2,1,0:T(8,128)(2,1)}, bf16[3,192,2048]{2,1,0:T(8,128)(2,1)S(1)}, u32[]{:S(2)}, u32[]{:S(2)}) collective-permute-start(bf16[3,192,2048]{2,1,0:T(8,128)(2,1)} %get-tuple-element.159), channel_id=1, source_target_pairs={{0,1},{1,0},{2,3},{3,2},{4,5},{5,4},{6,7},{7,6},{8,9},{9,8},{10,11... | collective-permute-start | bytes 7077896 | tf_op jit(solution)/shard_map/branch_cr/ppermute | solution.py:37
  209.2 42.7 %collective-permute-start.19 = (bf16[4,128,1024]{2,1,0:T(8,128)(2,1)}, bf16[4,128,1024]{2,1,0:T(8,128)(2,1)S(1)}, u32[]{:S(2)}, u32[]{:S(2)}) collective-permute-start(bf16[4,128,1024]{2,1,0:T(8,128)(2,1)} %collective-permute-done.9.refs_13_.refs_17_), channel_id=1, source_target_pairs={{0,4},{4,0},{1,5},{5,1},{2,6},{6,2},{3,7},{7,3},{8,12},{12,8},{9,1... | collective-permute-start | bytes 3145736 | tf_op jit(solution)/shard_map/fy_ug/ppermute | solution.py:37
  220.6 31.3 %collective-permute-start.15 = (bf16[192,2048]{1,0:T(8,128)(2,1)S(1)}, bf16[192,2048]{1,0:T(8,128)(2,1)S(1)}, u32[]{:S(2)}, u32[]{:S(2)}) collective-permute-start(bf16[192,2048]{1,0:T(8,128)(2,1)S(1)} %pad_maximum_fusion.6), channel_id=1, source_target_pairs={{0,2},{2,0},{1,3},{3,1},{4,6},{6,4},{5,7},{7,5},{8,10},{10,8},{9,1... | collective-permute-start | bytes 2359304 | tf_op jit(solution)/shard_map/branch_x/ppermute | solution.py:37
  223.8 30.3 %collective-permute-start.16 = (bf16[192,2048]{1,0:T(8,128)(2,1)S(1)}, bf16[192,2048]{1,0:T(8,128)(2,1)S(1)}, u32[]{:S(2)}, u32[]{:S(2)}) collective-permute-start(bf16[192,2048]{1,0:T(8,128)(2,1)S(1)} %pad_maximum_fusion.7), channel_id=1, source_target_pairs={{0,8},{8,0},{1,9},{9,1},{2,10},{10,2},{3,11},{11,3},{4,12},{12,4},... | collective-permute-start | bytes 2359304 | tf_op jit(solution)/shard_map/branch_z/ppermute | solution.py:37
  223.9 21.7 %collective-permute-start.18 = (bf16[4,128,512]{2,1,0:T(8,128)(2,1)S(1)}, bf16[4,128,512]{2,1,0:T(8,128)(2,1)S(1)}, u32[]{:S(2)}, u32[]{:S(2)}) collective-permute-start(bf16[4,128,512]{2,1,0:T(8,128)(2,1)S(1)} %slice.368.refs_19_.refs_1_), channel_id=1, source_target_pairs={{0,4},{4,0},{1,5},{5,1},{2,6},{6,2},{3,7},{7,3},{8,12},{12,8},{9,1... | collective-permute-start | bytes 1572872 | tf_op jit(solution)/shard_map/ny_d/ppermute | solution.py:37
  225.5 26.4 %collective-permute-start.17 = (bf16[4,128,512]{2,1,0:T(8,128)(2,1)S(1)}, bf16[4,128,512]{2,1,0:T(8,128)(2,1)S(1)}, u32[]{:S(2)}, u32[]{:S(2)}) collective-permute-start(bf16[4,128,512]{2,1,0:T(8,128)(2,1)S(1)} %slice.368.refs_19_.refs_1_), channel_id=1, source_target_pairs={{0,16},{16,0},{1,17},{17,1},{2,18},{18,2},{3,19},{19,3},{4,20},{20... | collective-permute-start | bytes 1572872 | tf_op jit(solution)/shard_map/zh_d/ppermute | solution.py:37
  255.8 18.2 %collective-permute-start.22 = (bf16[192,2048]{1,0:T(8,128)(2,1)S(1)}, bf16[192,2048]{1,0:T(8,128)(2,1)S(1)}, u32[]{:S(2)}, u32[]{:S(2)}) collective-permute-start(bf16[192,2048]{1,0:T(8,128)(2,1)S(1)} %multiply_convert_fusion.refs_0_.refs_2_), channel_id=1, source_target_pairs={{0,8},{8,0},{1,9},{9,1},{2,10},{10,2},{3,11},{11,3},{4,12},{12,4},... | collective-permute-start | bytes 2359304 | tf_op jit(solution)/shard_map/two_z/ppermute | solution.py:37
  257.0 18.1 %collective-permute-start.21 = (bf16[192,2048]{1,0:T(8,128)(2,1)S(1)}, bf16[192,2048]{1,0:T(8,128)(2,1)S(1)}, u32[]{:S(2)}, u32[]{:S(2)}) collective-permute-start(bf16[192,2048]{1,0:T(8,128)(2,1)S(1)} %multiply_convert_fusion.refs_0_.refs_2_), channel_id=1, source_target_pairs={{0,2},{2,0},{1,3},{3,1},{4,6},{6,4},{5,7},{7,5},{8,10},{10,8},{9,1... | collective-permute-start | bytes 2359304 | tf_op jit(solution)/shard_map/two_x/ppermute | solution.py:37
  319.0 20.4 %collective-permute-start.33 = (bf16[3,192,2048]{2,1,0:T(8,128)(2,1)}, bf16[3,192,2048]{2,1,0:T(8,128)(2,1)}, u32[]{:S(2)}, u32[]{:S(2)}) collective-permute-start(bf16[3,192,2048]{2,1,0:T(8,128)(2,1)} %get-tuple-element.183), channel_id=1, source_target_pairs={{0,1},{1,0},{2,3},{3,2},{4,5},{5,4},{6,7},{7,6},{8,9},{9,8},{10,11... | collective-permute-start | bytes 7077896 | tf_op jit(solution)/shard_map/back_two_cr/ppermute | solution.py:37
  340.1 28.0 %collective-permute-start.34 = (bf16[4,256,512]{2,1,0:T(8,128)(2,1)}, bf16[4,256,512]{2,1,0:T(8,128)(2,1)S(1)}, u32[]{:S(2)}, u32[]{:S(2)}) collective-permute-start(bf16[4,256,512]{2,1,0:T(8,128)(2,1)} %get-tuple-element.184), channel_id=1, source_target_pairs={{0,4},{4,0},{1,5},{5,1},{2,6},{6,2},{3,7},{7,3},{8,12},{12,8},{9,1... | collective-permute-start | bytes 3145736 | tf_op jit(solution)/shard_map/y_down/ppermute | solution.py:37
  347.3 19.9 %collective-permute-start.35 = (bf16[192,2048]{1,0:T(8,128)(2,1)}, bf16[192,2048]{1,0:T(8,128)(2,1)}, u32[]{:S(2)}, u32[]{:S(2)}) collective-permute-start(bf16[192,2048]{1,0:T(8,128)(2,1)} %pad_maximum_fusion.8), channel_id=1, source_target_pairs={{0,2},{2,0},{1,3},{3,1},{4,6},{6,4},{5,7},{7,5},{8,10},{10,8},{9,1... | collective-permute-start | bytes 2359304 | tf_op jit(solution)/shard_map/back_two_x/ppermute | solution.py:37
  349.1 19.0 %collective-permute-start.36 = (bf16[192,2048]{1,0:T(8,128)(2,1)}, bf16[192,2048]{1,0:T(8,128)(2,1)}, u32[]{:S(2)}, u32[]{:S(2)}) collective-permute-start(bf16[192,2048]{1,0:T(8,128)(2,1)} %pad_maximum_fusion.9), channel_id=1, source_target_pairs={{0,8},{8,0},{1,9},{9,1},{2,10},{10,2},{3,11},{11,3},{4,12},{12,4},... | collective-permute-start | bytes 2359304 | tf_op jit(solution)/shard_map/back_two_z/ppermute | solution.py:37
  374.3 32.0 %collective-permute-start.38 = (bf16[4,256,512]{2,1,0:T(8,128)(2,1)S(1)}, bf16[4,256,512]{2,1,0:T(8,128)(2,1)S(1)}, u32[]{:S(2)}, u32[]{:S(2)}) collective-permute-start(bf16[4,256,512]{2,1,0:T(8,128)(2,1)S(1)} %copy-done.55), channel_id=1, source_target_pairs={{0,4},{4,0},{1,5},{5,1},{2,6},{6,2},{3,7},{7,3},{8,12},{12,8},{9,1... | collective-permute-start | bytes 3145736 | tf_op jit(solution)/shard_map/y_up/ppermute | solution.py:37
  375.1 30.3 %collective-permute-start.41 = (bf16[192,2048]{1,0:T(8,128)(2,1)S(1)}, bf16[192,2048]{1,0:T(8,128)(2,1)S(1)}, u32[]{:S(2)}, u32[]{:S(2)}) collective-permute-start(bf16[192,2048]{1,0:T(8,128)(2,1)S(1)} %fusion.23.refs_0_.refs_1_), channel_id=1, source_target_pairs={{0,1},{1,0},{2,3},{3,2},{4,5},{5,4},{6,7},{7,6},{8,9},{9,8},{10,11... | collective-permute-start | bytes 2359304 | tf_op jit(solution)/shard_map/gb_c/ppermute | solution.py:37
  375.1 31.3 %collective-permute-start.40 = (bf16[192,2048]{1,0:T(8,128)(2,1)S(1)}, bf16[192,2048]{1,0:T(8,128)(2,1)}, u32[]{:S(2)}, u32[]{:S(2)}) collective-permute-start(bf16[192,2048]{1,0:T(8,128)(2,1)S(1)} %fusion.23.refs_0_.refs_1_), channel_id=1, source_target_pairs={{0,8},{8,0},{1,9},{9,1},{2,10},{10,2},{3,11},{11,3},{4,12},{12,4},... | collective-permute-start | bytes 2359304 | tf_op jit(solution)/shard_map/gb_z/ppermute | solution.py:37
  376.7 29.7 %collective-permute-start.39 = (bf16[192,2048]{1,0:T(8,128)(2,1)S(1)}, bf16[192,2048]{1,0:T(8,128)(2,1)}, u32[]{:S(2)}, u32[]{:S(2)}) collective-permute-start(bf16[192,2048]{1,0:T(8,128)(2,1)S(1)} %fusion.23.refs_0_.refs_1_), channel_id=1, source_target_pairs={{0,2},{2,0},{1,3},{3,1},{4,6},{6,4},{5,7},{7,5},{8,10},{10,8},{9,1... | collective-permute-start | bytes 2359304 | tf_op jit(solution)/shard_map/gb_x/ppermute | solution.py:37
  377.8 27.6 %collective-permute-start.37 = (bf16[2,256,512]{2,1,0:T(8,128)(2,1)S(1)}, bf16[2,256,512]{2,1,0:T(8,128)(2,1)S(1)}, u32[]{:S(2)}, u32[]{:S(2)}) collective-permute-start(bf16[2,256,512]{2,1,0:T(8,128)(2,1)S(1)} %add_convert_fusion.20), channel_id=1, source_target_pairs={{0,16},{16,0},{1,17},{17,1},{2,18},{18,2},{3,19},{19,3},{4,20},{20... | collective-permute-start | bytes 1572872 | tf_op jit(solution)/shard_map/zh_gdown/ppermute | solution.py:37
  412.9 32.0 %collective-permute-start.49 = (bf16[4,256,512]{2,1,0:T(8,128)(2,1)}, bf16[4,256,512]{2,1,0:T(8,128)(2,1)}, u32[]{:S(2)}, u32[]{:S(2)}) collective-permute-start(bf16[4,256,512]{2,1,0:T(8,128)(2,1)} %get-tuple-element.213), channel_id=1, source_target_pairs={{0,4},{4,0},{1,5},{5,1},{2,6},{6,2},{3,7},{7,3},{8,12},{12,8},{9,1... | collective-permute-start | bytes 3145736 | tf_op jit(solution)/shard_map/y_gate/ppermute | solution.py:37
  425.3 26.5 %collective-permute-start.48 = (bf16[2,256,512]{2,1,0:T(8,128)(2,1)}, bf16[2,256,512]{2,1,0:T(8,128)(2,1)}, u32[]{:S(2)}, u32[]{:S(2)}) collective-permute-start(bf16[2,256,512]{2,1,0:T(8,128)(2,1)} %add_convert_fusion.19), channel_id=1, source_target_pairs={{0,16},{16,0},{1,17},{17,1},{2,18},{18,2},{3,19},{19,3},{4,20},{20... | collective-permute-start | bytes 1572872 | tf_op jit(solution)/shard_map/zh_gup/ppermute | solution.py:37
  453.1 25.1 %collective-permute-start.50 = (bf16[2,256,512]{2,1,0:T(8,128)(2,1)S(1)}, bf16[2,256,512]{2,1,0:T(8,128)(2,1)}, u32[]{:S(2)}, u32[]{:S(2)}) collective-permute-start(bf16[2,256,512]{2,1,0:T(8,128)(2,1)S(1)} %add_convert_fusion.18), channel_id=1, source_target_pairs={{0,16},{16,0},{1,17},{17,1},{2,18},{18,2},{3,19},{19,3},{4,20},{20... | collective-permute-start | bytes 1572872 | tf_op jit(solution)/shard_map/zh_ggate/ppermute | solution.py:37
  464.2 30.4 %collective-permute-start.51 = (bf16[4,256,512]{2,1,0:T(8,128)(2,1)}, bf16[4,256,512]{2,1,0:T(8,128)(2,1)}, u32[]{:S(2)}, u32[]{:S(2)}) collective-permute-start(bf16[4,256,512]{2,1,0:T(8,128)(2,1)} %get-tuple-element.225), channel_id=1, source_target_pairs={{0,4},{4,0},{1,5},{5,1},{2,6},{6,2},{3,7},{7,3},{8,12},{12,8},{9,1... | collective-permute-start | bytes 3145736 | tf_op jit(solution)/shard_map/y_out/ppermute | solution.py:37
  494.6 27.2 %collective-permute-start.53 = (bf16[4,256,512]{2,1,0:T(8,128)(2,1)}, bf16[4,256,512]{2,1,0:T(8,128)(2,1)}, u32[]{:S(2)}, u32[]{:S(2)}) collective-permute-start(bf16[4,256,512]{2,1,0:T(8,128)(2,1)} %get-tuple-element.232), channel_id=1, source_target_pairs={{0,4},{4,0},{1,5},{5,1},{2,6},{6,2},{3,7},{7,3},{8,12},{12,8},{9,1... | collective-permute-start | bytes 3145736 | tf_op jit(solution)/shard_map/y_swish/ppermute | solution.py:37
  496.3 25.5 %collective-permute-start.52 = (bf16[2,256,512]{2,1,0:T(8,128)(2,1)S(1)}, bf16[2,256,512]{2,1,0:T(8,128)(2,1)}, u32[]{:S(2)}, u32[]{:S(2)}) collective-permute-start(bf16[2,256,512]{2,1,0:T(8,128)(2,1)S(1)} %add_convert_fusion.17), channel_id=1, source_target_pairs={{0,16},{16,0},{1,17},{17,1},{2,18},{18,2},{3,19},{19,3},{4,20},{20... | collective-permute-start | bytes 1572872 | tf_op jit(solution)/shard_map/zh_gout/ppermute | solution.py:37
  521.8 31.7 %collective-permute-start.57 = (bf16[3,192,2048]{2,1,0:T(8,128)(2,1)}, bf16[3,192,2048]{2,1,0:T(8,128)(2,1)S(1)}, u32[]{:S(2)}, u32[]{:S(2)}) collective-permute-start(bf16[3,192,2048]{2,1,0:T(8,128)(2,1)} %get-tuple-element.234), channel_id=1, source_target_pairs={{0,1},{1,0},{2,3},{3,2},{4,5},{5,4},{6,7},{7,6},{8,9},{9,8},{10,11... | collective-permute-start | bytes 7077896 | tf_op jit(solution)/shard_map/back_one_cr/ppermute | solution.py:37
  522.3 27.3 %collective-permute-start.61 = (bf16[4,256,512]{2,1,0:T(8,128)(2,1)}, bf16[4,256,512]{2,1,0:T(8,128)(2,1)S(1)}, u32[]{:S(2)}, u32[]{:S(2)}) collective-permute-start(bf16[4,256,512]{2,1,0:T(8,128)(2,1)} %get-tuple-element.244), channel_id=1, source_target_pairs={{0,4},{4,0},{1,5},{5,1},{2,6},{6,2},{3,7},{7,3},{8,12},{12,8},{9,1... | collective-permute-start | bytes 3145736 | tf_op jit(solution)/shard_map/y_value/ppermute | solution.py:37
  524.4 25.2 %collective-permute-start.60 = (bf16[2,256,512]{2,1,0:T(8,128)(2,1)S(1)}, bf16[2,256,512]{2,1,0:T(8,128)(2,1)S(1)}, u32[]{:S(2)}, u32[]{:S(2)}) collective-permute-start(bf16[2,256,512]{2,1,0:T(8,128)(2,1)S(1)} %add_convert_fusion.16), channel_id=1, source_target_pairs={{0,16},{16,0},{1,17},{17,1},{2,18},{18,2},{3,19},{19,3},{4,20},{20... | collective-permute-start | bytes 1572872 | tf_op jit(solution)/shard_map/zh_gswish/ppermute | solution.py:37
  526.1 27.4 %collective-permute-start.56 = (bf16[96,2048]{1,0:T(8,128)(2,1)S(1)}, bf16[96,2048]{1,0:T(8,128)(2,1)S(1)}, u32[]{:S(2)}, u32[]{:S(2)}) collective-permute-start(bf16[96,2048]{1,0:T(8,128)(2,1)S(1)} %get-tuple-element.285), channel_id=1, source_target_pairs={{0,8},{8,0},{1,9},{9,1},{2,10},{10,2},{3,11},{11,3},{4,12},{12,4},... | collective-permute-start | bytes 1179656 | tf_op jit(solution)/shard_map/back_one_dz/ppermute | solution.py:37
  528.7 24.8 %collective-permute-start.55 = (bf16[96,2048]{1,0:T(8,128)(2,1)S(1)}, bf16[96,2048]{1,0:T(8,128)(2,1)S(1)}, u32[]{:S(2)}, u32[]{:S(2)}) collective-permute-start(bf16[96,2048]{1,0:T(8,128)(2,1)S(1)} %get-tuple-element.286), channel_id=1, source_target_pairs={{0,2},{2,0},{1,3},{3,1},{4,6},{6,4},{5,7},{7,5},{8,10},{10,8},{9,1... | collective-permute-start | bytes 1179656 | tf_op jit(solution)/shard_map/back_one_dx/ppermute | solution.py:37
  550.7 25.5 %collective-permute-start.63 = (bf16[2,256,512]{2,1,0:T(8,128)(2,1)}, bf16[2,256,512]{2,1,0:T(8,128)(2,1)}, u32[]{:S(2)}, u32[]{:S(2)}) collective-permute-start(bf16[2,256,512]{2,1,0:T(8,128)(2,1)} %add_convert_fusion.15), channel_id=1, source_target_pairs={{0,16},{16,0},{1,17},{17,1},{2,18},{18,2},{3,19},{19,3},{4,20},{20... | collective-permute-start | bytes 1572872 | tf_op jit(solution)/shard_map/zh_gvalue/ppermute | solution.py:37
  550.8 25.4 %collective-permute-start.62 = (bf16[4,256,512]{2,1,0:T(8,128)(2,1)}, bf16[4,256,512]{2,1,0:T(8,128)(2,1)}, u32[]{:S(2)}, u32[]{:S(2)}) collective-permute-start(bf16[4,256,512]{2,1,0:T(8,128)(2,1)} %get-tuple-element.245), channel_id=1, source_target_pairs={{0,4},{4,0},{1,5},{5,1},{2,6},{6,2},{3,7},{7,3},{8,12},{12,8},{9,1... | collective-permute-start | bytes 3145736 | tf_op jit(solution)/shard_map/y_qk/ppermute | solution.py:37
  558.9 21.3 %collective-permute-start.58 = (bf16[192,2048]{1,0:T(8,128)(2,1)}, bf16[192,2048]{1,0:T(8,128)(2,1)}, u32[]{:S(2)}, u32[]{:S(2)}) collective-permute-start(bf16[192,2048]{1,0:T(8,128)(2,1)} %pad_maximum_fusion.10), channel_id=1, source_target_pairs={{0,2},{2,0},{1,3},{3,1},{4,6},{6,4},{5,7},{7,5},{8,10},{10,8},{9,1... | collective-permute-start | bytes 2359304 | tf_op jit(solution)/shard_map/back_one_x/ppermute | solution.py:37
  560.8 43.5 %collective-permute-start.59 = (bf16[192,2048]{1,0:T(8,128)(2,1)}, bf16[192,2048]{1,0:T(8,128)(2,1)}, u32[]{:S(2)}, u32[]{:S(2)}) collective-permute-start(bf16[192,2048]{1,0:T(8,128)(2,1)} %pad_maximum_fusion.11), channel_id=1, source_target_pairs={{0,8},{8,0},{1,9},{9,1},{2,10},{10,2},{3,11},{11,3},{4,12},{12,4},... | collective-permute-start | bytes 2359304 | tf_op jit(solution)/shard_map/back_one_z/ppermute | solution.py:37
  564.8 60.6 %all-to-all-start.3 = ((bf16[4,128,1536]{2,1,0:T(8,128)(2,1)}), bf16[4,128,1536]{2,1,0:T(8,128)(2,1)}, u32[]{:S(2)}, u32[]{:S(2)}) async-start(bf16[4,128,1536]{2,1,0:T(8,128)(2,1)} %pad_maximum_fusion.1), calls=%async_computation.4 | async-start | bytes 3145728 | tf_op jit(solution)/shard_map/all_to_all | solution.py:59
  577.6 30.4 %collective-permute-start.64 = (bf16[2,256,512]{2,1,0:T(8,128)(2,1)S(1)}, bf16[2,256,512]{2,1,0:T(8,128)(2,1)S(1)}, u32[]{:S(2)}, u32[]{:S(2)}) collective-permute-start(bf16[2,256,512]{2,1,0:T(8,128)(2,1)S(1)} %add_convert_fusion.14), channel_id=1, source_target_pairs={{0,16},{16,0},{1,17},{17,1},{2,18},{18,2},{3,19},{19,3},{4,20},{20... | collective-permute-start | bytes 1572872 | tf_op jit(solution)/shard_map/zh_gqk/ppermute | solution.py:37
  (94 other events, 820.1 us)
Sparse Core Ops, SparseCore 0:
  30.4 70.6 all-gather.4
  154.7 57.2 all-gather.6
  426.9 64.5 reduce-scatter.1

commit v5 on v4

--- a/solution.py
+++ b/solution.py
@@ -204,17 +204,28 @@
         self.diag = add(keep[3], swap(send_diag, "tensor", label + "_cd"))
         self.rest = swap(send_rest, "tensor", label + "_cr")
 
-    def relay(self, clock):
+    def relay(self, clock, whole=False):
         half = self.diag.shape[0] // 2
         diag = clock.at(self.diag)
+        self.whole = whole
+        if whole:
+            self.through_x = swap(diag, "x", self.label + "_dx")
+            self.second = (self.through_x, self.rest)
+            return
         self.through_x = swap(diag[:half], "x", self.label + "_dx")
         self.through_z = swap(diag[half:], "zl", self.label + "_dz")
         self.second = (self.through_x, self.through_z, self.rest)
 
     def send(self, clock):
-        through_x, through_z, rest = (v.astype(f32) for v in clock.at_all(self.second))
+        *through, rest = (v.astype(f32) for v in clock.at_all(self.second))
+        self.own, xmate, zmate = (self.keep[r].astype(f32) + rest[r] for r in range(3))
+        if self.whole:
+            self.x = swap(xmate.astype(bf16), "x", self.label + "_x")
+            self.z = swap((zmate + through[0]).astype(bf16), "zl", self.label + "_z")
+            self.last = (self.x, self.z)
+            return
+        through_x, through_z = through
         half = through_x.shape[0]
-        self.own, xmate, zmate = (self.keep[r].astype(f32) + rest[r] for r in range(3))
         zmate = jnp.concatenate([zmate[:half] + through_x, zmate[half:]]).astype(bf16)
         xmate = jnp.concatenate([xmate[:half], xmate[half:] + through_z]).astype(bf16)
         self.x = swap(xmate, "x", self.label + "_x")
@@ -497,33 +508,55 @@
     )
 
 
-def feed_body(tokens, others, f_u, f_g, f_d, coord, *refs):
-    acts, cots, refs = refs[:tokens], refs[tokens : tokens + others], refs[tokens + others :]
+def project_body(tokens, f_d, coord, *refs):
+    acts, refs = refs[:tokens], refs[tokens:]
+    wd, refs = refs[: f_d.count], refs[f_d.count :]
+    out, held, held_d, sems = refs
+    load, r = Loader(sems), pl.program_id(0)
+    w1 = load.weight(wd, f_d, held_d, coord)
+    chips = load.tokens(acts, held, coord)
+
+    @pl.when(r == 0)
+    def _():
+        start(*w1, *chips[0], *chips[1], *chips[2], *chips[3])
+        wait(*w1)
+
+    at_chip(r, chips)
+    out[0] = dot(rows_of(held, r), flat(held_d), NN)
+
+
+def project(coord, acts, wd):
+    rows, model = acts[0].shape[-2:]
+    shape = (2 * rows, wd.plan.width)
+    return chip_kernel(
+        functools.partial(project_body, len(acts), wd.plan),
+        [coord, *acts, *arrays(wd)],
+        [SMEM] + [ANY] * (len(acts) + len(arrays(wd))),
+        [struct((4,) + shape, f32)],
+        [by_chip(shape)],
+        [held_tokens(acts), held_weight(wd)],
+        10 + copies_of(wd),
+        16 * rows * model * wd.plan.width,
+    )[0]
+
+
+def feed_body(tokens, f_u, f_g, coord, gh, *refs):
+    acts, refs = refs[:tokens], refs[tokens:]
     wu, refs = refs[: f_u.count], refs[f_u.count :]
     wg, refs = refs[: f_g.count], refs[f_g.count :]
-    wd, refs = refs[: f_d.count], refs[f_d.count :]
     hidden_out, up_out, gate_out, rest, diag, keep = refs[:6]
-    held, held_c, held_u, held_g, held_d, store, up, gate, gh, sems = refs[6:]
+    held, held_u, held_g, store, up, gate, sems = refs[6:]
     load, r = Loader(sems), pl.program_id(0)
     w1 = load.weight(wu, f_u, held_u, coord)
     w2 = load.weight(wg, f_g, held_g, coord)
-    w3 = load.weight(wd, f_d, held_d, coord)
     chips = load.tokens(acts, held, coord)
-    chips_c = load.tokens(cots, held_c, coord)
     sends = send_copies(load, store, rest, diag)
 
     @pl.when(r == 0)
     def _():
-        start(*w3, *chips_c[0], *w1, *chips[0], *w2)
+        start(*w1, *chips[0], *w2)
         for i in range(1, 4):
-            start(*chips_c[i], *chips[i])
-        wait(*w3)
-
-    at_chip(r, chips_c)
-    gh[...] = dot(rows_of(held_c, r), flat(held_d), NN)
-
-    @pl.when(r == 0)
-    def _():
+            start(*chips[i])
         wait(*w1)
 
     at_chip(r, chips)
@@ -539,7 +572,7 @@
 
     def chunk(i, carry):
         at = pl.ds(pl.multiple_of(i * step, step), step)
-        u, g, e = up[at, :], gate[at, :], gh[at, :]
+        u, g, e = up[at, :], gate[at, :], gh[0, at, :]
         c = 0.7978845608028654
         square = g * g
         t = jnp.tanh(c * g * (1.0 + 0.044715 * square))
@@ -551,33 +584,31 @@
         gate_out[0, at, :] = (e * u * slope).astype(bf16)
         return carry
 
-    lax.fori_loop(0, gh.shape[0] // step, chunk, 0, unroll=4)
+    lax.fori_loop(0, up.shape[0] // step, chunk, 0, unroll=4)
     partial_rows([up_out[0], gate_out[0]], [held_u, held_g], r, keep, store)
     at_chip_start(r, sends)
 
 
-def feed_forward(coord, acts, cots, wu, wg, wd):
+def feed_forward(coord, gh, acts, wu, wg):
     rows, model = acts[0].shape[-2:]
-    n = wd.plan.width
+    n = wu.plan.width
     outs, out_specs = partial_outs(rows, model)
     outs = [struct((4, 2 * rows, n), bf16)] * 3 + outs
     return chip_kernel(
-        functools.partial(feed_body, len(acts), len(cots), wu.plan, wg.plan, wd.plan),
-        [coord, *acts, *cots, *arrays(wu, wg, wd)],
-        [SMEM] + [ANY] * (len(acts) + len(cots) + len(arrays(wu, wg, wd))),
+        functools.partial(feed_body, len(acts), wu.plan, wg.plan),
+        [coord, gh, *acts, *arrays(wu, wg)],
+        [SMEM, by_chip((2 * rows, n))] + [ANY] * (len(acts) + len(arrays(wu, wg))),
         outs,
         [by_chip((2 * rows, n))] * 3 + out_specs,
         [
             held_tokens(acts),
-            held_tokens(cots),
             held_weight(wu),
             held_weight(wg),
-            held_weight(wd),
             pltpu.VMEM((4, rows, model), bf16),
         ]
-        + [pltpu.VMEM((2 * rows, n), f32)] * 3,
-        24 + copies_of(wu, wg, wd),
-        80 * rows * model * n,
+        + [pltpu.VMEM((2 * rows, n), f32)] * 2,
+        14 + copies_of(wu, wg),
+        64 * rows * model * n,
     )
 
 
@@ -868,7 +899,6 @@
         seg_d = lax.ppermute(segments, GROUP, [(i, 3 - i) for i in range(4)])
     parts = (by_quarter(w) for w in (w_query, w_key, w_value))
     piece = group_exchange(beside(*parts))
-    grad_rows = [lax.all_gather(cotangent, everyone, axis=0)]
     parts = beside(by_quarter(w_swish), by_quarter(w_out.T))
 
     clock.done(piece, parts)
@@ -894,6 +924,7 @@
     )
 
     clock.done(query, piece, *pipe.moved)
+    grad_rows = [lax.all_gather(at(cotangent), everyone, axis=0)]
     unit_ug = pipe.step(clock, piece[:, :, : 2 * width], "ug")
     full_swish, full_out = unit_so.weight(0, width), unit_so.weight(width, width)
     swish_in, gated, *partial = branch(at(coord), hat, normed, full_swish, full_out)
@@ -910,12 +941,13 @@
     far_y = pipe.finish(clock)
     clock.done(*far_y, *gather.first)
     gather.second(clock)
-    clock.done(*gather.held)
-    normed_two = gather.finish(clock)
     full_up, full_gate = unit_ug.weight(0, width), unit_ug.weight(width, width)
     full_down = unit_d.weight(0, width)
+    grad_hidden = project(at(coord), grad_rows, full_down)
+    clock.done(grad_hidden, *gather.held)
+    normed_two = gather.finish(clock)
     hidden, grad_up_rows, grad_gate_rows, *partial = feed_forward(
-        at(coord), normed_two, grad_rows, full_up, full_gate, full_down
+        at(coord), grad_hidden, normed_two, full_up, full_gate
     )
 
     scatter = Scatter(*partial, "back_two", free)
@@ -982,7 +1014,7 @@
     g_value.to_y(clock)
     scatter = Scatter(*partial, "back_one", clock)
     clock.done(scatter.diag)
-    scatter.relay(clock)
+    scatter.relay(clock, True)
     clock.done(*scatter.second)
     scatter.send(clock)
     clock.done(g_swish.zh, g_value.y)

time: 681 us -> 679 us (level)
    ppermute x69 -> x68, waiting for transfers between devices: 273 us -> 267 us  [swap(): return lax.ppermute(a, axis, [(0, 1), (1, 0)])]
    pallas_call x6 -> x7, Pallas kernels: 108 us -> 112 us  [chip_kernel(): pl.pallas_call(body, grid=(4,), in_specs=specs, out_specs=out_specs, out_...]
    unnamed x130 -> x142, local copies, waits for them, and re-layouts: 14.9 us -> 12 us
    ppermute x69 -> x68, starting transfers between devices: 64.8 us -> 65.4 us  [swap(): return lax.ppermute(a, axis, [(0, 1), (1, 0)])]
  transfers between devices with their start and end apart: 79 -> 78, of which waited for: 35 -> 39; matrix products, arithmetic and copies ran while one was open for 9% -> 9% of each run, Pallas kernels for 23% -> 24%
where the time goes in v5:
time: 679 us; the launch traced here: 671 us
  waiting for transfers between devices  287 us (42%)
  Pallas kernels  189 us (28%)
  starting transfers between devices  97.7 us (14%)
  other arithmetic  56.6 us (8%)
  local copies, waits for them, and re-layouts  25.4 us (4%)
  between operations  16.2 us (2%)
    ppermute x68, waiting for transfers between devices, swap(): return lax.ppermute(a, axis, [(0, 1), (1, 0)])  267 us
    pallas_call x7, Pallas kernels, chip_kernel(): pl.pallas_call(body, grid=(4,), in_specs=specs, out_specs=out_specs, out_...  112 us
    pallas_call x5, Pallas kernels, weight_grads(): pl.pallas_call(functools.partial(weight_grad_body, len(grads), len(acts),...  65.7 us
    ppermute x68, starting transfers between devices, swap(): return lax.ppermute(a, axis, [(0, 1), (1, 0)])  65.4 us
    all_to_all x6, starting transfers between devices, group_exchange(): return lax.all_to_all(parts, GROUP, 0, 0, tiled=True)  30.7 us
    convert_element_type x16, other arithmetic, add(): return (a.astype(f32) + b.astype(f32)).astype(bf16)  19.7 us
    all_to_all x6, waiting for transfers between devices, group_exchange(): return lax.all_to_all(parts, GROUP, 0, 0, tiled=True)  19.5 us
  transfers between devices with their start and end apart: 78, of which 39 were waited for; matrix products, arithmetic and copies ran while one was open for 9% of the time, Pallas kernels for 24%

profile of v5, /device:TPU:0, one launch (start us, length us, event | category | flops | bytes accessed | tf_op | source)
XLA Modules:
  0.0 671.1 jit_solution(4210667828138760990)
XLA Ops:
  11.4 5.2 all-to-all-start
  21.6 8.7 %all-to-all-done.refs_1_.refs_5_.refs_3_.refs_7_ = bf16[4,128,1024]{2,1,0:T(8,128)(2,1)S(1)} async-done(((bf16[4,128,1024]{2,1,0:T(8,128)(2,1)}), bf16[4,128,1024]{2,1,0:T(8,128)(2,1)S(1)}, u32[]{:S(2)}, u32[]{:S(2)}) %all-to-all-start) | async-done | bytes 1048608 | tf_op jit(solution)/shard_map/all_to_all | solution.py:59
  35.2 3.5 all-to-all-start.1
  40.6 2.6 collective-permute-start.3
  50.1 13.2 %collective-permute-done.4.refs_2_.refs_6_.refs_4_.refs_8_ = bf16[4,128,1024]{2,1,0:T(8,128)(2,1)} collective-permute-done((bf16[4,128,1024]{2,1,0:T(8,128)(2,1)}, bf16[4,128,1024]{2,1,0:T(8,128)(2,1)}, u32[]{:S(2)}, u32[]{:S(2)}) %collective-permute-start.4) | collective-permute-done | bytes 1048608 | tf_op jit(solution)/shard_map/ny_qkv/ppermute | solution.py:37
  63.2 30.2 %collective-permute-done.3.refs_3_.refs_7_.refs_5_.refs_9_ = bf16[4,128,1024]{2,1,0:T(8,128)(2,1)} collective-permute-done((bf16[4,128,1024]{2,1,0:T(8,128)(2,1)}, bf16[4,128,1024]{2,1,0:T(8,128)(2,1)}, u32[]{:S(2)}, u32[]{:S(2)}) %collective-permute-start.3) | collective-permute-done | bytes 1048608 | tf_op jit(solution)/shard_map/zh_qkv/ppermute | solution.py:37
  93.5 9.8 %all-to-all-start.2 = ((bf16[4,128,1536]{2,1,0:T(8,128)(2,1)}), bf16[4,128,1536]{2,1,0:T(8,128)(2,1)S(1)}, u32[]{:S(2)}, u32[]{:S(2)}) async-start(bf16[4,128,1536]{2,1,0:T(8,128)(2,1)} %pad_maximum_fusion), calls=%async_computation.2 | async-start | bytes 3145728 | tf_op jit(solution)/shard_map/all_to_all | solution.py:59
  105.9 23.8 %collective-permute-done.5.refs_4_.refs_8_.refs_6_.refs_10_ = bf16[4,128,1024]{2,1,0:T(8,128)(2,1)} collective-permute-done((bf16[4,128,1024]{2,1,0:T(8,128)(2,1)}, bf16[4,128,1024]{2,1,0:T(8,128)(2,1)}, u32[]{:S(2)}, u32[]{:S(2)}) %collective-permute-start.5) | collective-permute-done | bytes 1048608 | tf_op jit(solution)/shard_map/fy_qkv/ppermute | solution.py:37
  129.7 23.2 %shard_map.229 = (bf16[4,384,256]{2,1,0:T(8,128)(2,1)}, bf16[4,384,256]{2,1,0:T(8,128)(2,1)}, bf16[4,384,512]{2,1,0:T(8,128)(2,1)}, bf16[4,384,384]{2,1,0:T(8,12...) custom-call(s32[4]{0:T(128)} %pad_add_fusion.1.coord, f32[4,384,384]{2,1,0:T(8,128)} %and_select_fusion.mask, ...), custom_call_target="tpu_custom_call" | custom-call | flops 6442450944 | bytes 25296912 | tf_op jit(solution)/shard_map/pallas_call | solution.py:320
  155.5 24.2 %collective-permute-done.8.refs_4_.refs_8_.refs_13_.refs_14_ = bf16[4,128,1024]{2,1,0:T(8,128)(2,1)} collective-permute-done((bf16[4,128,1024]{2,1,0:T(8,128)(2,1)}, bf16[4,128,1024]{2,1,0:T(8,128)(2,1)}, u32[]{:S(2)}, u32[]{:S(2)}) %collective-permute-start.8) | collective-permute-done | bytes 1048608 | tf_op jit(solution)/shard_map/fy_so/ppermute | solution.py:37
  179.7 15.0 %shard_map.230 = (f32[4,384,512]{2,1,0:T(8,128)}, bf16[4,384,512]{2,1,0:T(8,128)(2,1)}, bf16[3,192,2048]{2,1,0:T(8,128)(2,1)}, bf16[192,2048]{1,0:T(8,128)(2,1)}, bf16[4,192,2048]{2,1,0:T(8,128)(2,1)}) custom-call(s32[4]{0:T(128)} %pad_add_fusion.1.coord, f32[4,384,512]{2,1,0:T(8,128)} %get-tuple-element.153.hat, bf16[8,192,2048]{2,1,0:T(8,128)(2,1)} %bitcast.141, ...), custom_call_target="tpu_custom_call" | custom-call | flops 6442450944 | bytes 28835856 | tf_op jit(solution)/shard_map/pallas_call | solution.py:320
  194.7 2.7 collective-permute-done.10.refs_11_.refs_15_
  200.4 5.9 collective-permute-done.11
  210.2 8.8 %collective-permute-done.13 = bf16[96,2048]{1,0:T(8,128)(2,1)S(1)} collective-permute-done((bf16[96,2048]{1,0:T(8,128)(2,1)S(1)}, bf16[96,2048]{1,0:T(8,128)(2,1)S(1)}, u32[]{:S(2)}, u32[]{:S(2)}) %collective-permute-start.13) | collective-permute-done | bytes 393248 | tf_op jit(solution)/shard_map/branch_dz/ppermute | solution.py:37
  227.4 18.3 %collective-permute-done.18.refs_2_ = bf16[4,128,512]{2,1,0:T(8,128)(2,1)S(1)} collective-permute-done((bf16[4,128,512]{2,1,0:T(8,128)(2,1)S(1)}, bf16[4,128,512]{2,1,0:T(8,128)(2,1)S(1)}, u32[]{:S(2)}, u32[]{:S(2)}) %collective-permute-start.18) | collective-permute-done | bytes 524320 | tf_op jit(solution)/shard_map/ny_d/ppermute | solution.py:37
  245.7 5.6 collective-permute-done.17.refs_3_
  259.0 12.2 %collective-permute-done.20.refs_4_ = bf16[4,128,512]{2,1,0:T(8,128)(2,1)S(1)} collective-permute-done((bf16[4,128,512]{2,1,0:T(8,128)(2,1)S(1)}, bf16[4,128,512]{2,1,0:T(8,128)(2,1)S(1)}, u32[]{:S(2)}, u32[]{:S(2)}) %collective-permute-start.20) | collective-permute-done | bytes 524320 | tf_op jit(solution)/shard_map/fy_d/ppermute | solution.py:37
  271.2 4.1 collective-permute-done.22.refs_4_.refs_6_
  280.9 7.8 %shard_map.231.gh = f32[4,384,512]{2,1,0:T(8,128)} custom-call(s32[4]{0:T(128)} %pad_add_fusion.1.coord, bf16[8,192,2048]{2,1,0:T(8,128)(2,1)} %bitcast.144, bf16[4,128,512]{2,1,0:T(8,128)(2,1)} %copy-done.34, bf16[4,128,512]{2,1,0:T(8,128)(2,1)} %copy-done.63, bf16[4,128,512]{2,1,0:T(8,128)(2,1)} %copy-done.64, bf16[4,128,512]{2,1,0:T(8,128)(2,1)} %copy-done.65), custom_call_target="tpu_custom_call" | custom-call | flops 3221225472 | bytes 11534352 | tf_op jit(solution)/shard_map/pallas_call | solution.py:320
  294.9 23.6 %shard_map.232 = (bf16[4,384,512]{2,1,0:T(8,128)(2,1)}, bf16[4,384,512]{2,1,0:T(8,128)(2,1)}, bf16[4,384,512]{2,1,0:T(8,128)(2,1)}, bf16[3,192,2048]{2,1,0:T(8,1...) custom-call(s32[4]{0:T(128)} %pad_add_fusion.1.coord, f32[4,384,512]{2,1,0:T(8,128)} %shard_map.231.gh, ...), custom_call_target="tpu_custom_call" | custom-call | flops 12884901888 | bytes 28835856 | tf_op jit(solution)/shard_map/pallas_call | solution.py:320
  319.1 5.1 collective-permute-done.30
  328.4 10.9 %shard_map.233 = (bf16[4,256,512]{2,1,0:T(8,128)(2,1)}, bf16[4,256,512]{2,1,0:T(8,128)(2,1)}) custom-call(s32[4]{0:T(128)} %pad_add_fusion.1.coord, bf16[4,384,512]{2,1,0:T(8,128)(2,1)} %get-tuple-element.182.refs_0_, bf16[8,192,2048]{2,1,0:T(8,128)(2,1)} %bitcast.145), custom_call_target="tpu_custom_call" | custom-call | flops 3221225472 | bytes 9961472 | tf_op jit(solution)/shard_map/pallas_call | solution.py:794
  350.4 16.5 %shard_map.234 = (bf16[4,256,512]{2,1,0:T(8,128)(2,1)}, bf16[4,256,512]{2,1,0:T(8,128)(2,1)}, bf16[4,256,512]{2,1,0:T(8,128)(2,1)}, bf16[4,256,512]{2,1,0:T(8,128)(2,1)}) custom-call(s32[4]{0:T(128)} %pad_add_fusion.1.coord, bf16[4,384,512]{2,1,0:T(8,128)(2,1)} %get-tuple-element.192.refs_0_, bf16[4,384,512]{2,1,0:T(8,128)(2,1)} %get-tuple-element.193.refs_1_, ...), custom_call_target="tpu_custom_call" | custom-call | flops 6442450944 | bytes 13631488 | tf_op jit(solution)/shard_map/pallas_call | solution.py:794
  367.9 3.9 multiply_reduce_fusion
  379.0 26.1 %collective-permute-done.37 = bf16[2,256,512]{2,1,0:T(8,128)(2,1)S(1)} collective-permute-done((bf16[2,256,512]{2,1,0:T(8,128)(2,1)S(1)}, bf16[2,256,512]{2,1,0:T(8,128)(2,1)S(1)}, u32[]{:S(2)}, u32[]{:S(2)}) %collective-permute-start.37) | collective-permute-done | bytes 524320 | tf_op jit(solution)/shard_map/zh_gdown/ppermute | solution.py:37
  412.7 8.3 %shard_map.235 = bf16[8,192,2048]{2,1,0:T(8,128)(2,1)} custom-call(s32[4]{0:T(128)} %pad_add_fusion.1.coord, bf16[4,384,512]{2,1,0:T(8,128)(2,1)} %get-tuple-element.182.refs_0_, bf16[4,128,512]{2,1,0:T(8,128)(2,1)} %copy-done.34, bf16[4,128,512]{2,1,0:T(8,128)(2,1)} %copy-done.63, bf16[4,128,512]{2,1,0:T(8,128)(2,1)} %copy-done.64, ...), custom_call_target="tpu_custom_call" | custom-call | flops 3221225472 | bytes 9961488 | tf_op jit(solution)/shard_map/pallas_call | solution.py:320
  428.0 17.0 %shard_map.236 = (bf16[4,384,512]{2,1,0:T(8,128)(2,1)}, bf16[4,384,512]{2,1,0:T(8,128)(2,1)}, bf16[4,384,512]{2,1,0:T(8,128)(2,1)}) custom-call(s32[4]{0:T(128)} %pad_add_fusion.1.coord, f32[4,384,384]{2,1,0:T(8,128)} %and_select_fusion.mask, f32[4,384,512]{2,1,0:T(8,128)} %get-tuple-element.205.s, f32[4,384,512]{2,1,0:T(8,128)} %get-tuple-element.153.hat, ...), custom_call_target="tpu_custom_call" | custom-call | flops 4831838208 | bytes 28966928 | tf_op jit(solution)/shard_map/pallas_call | solution.py:320
  446.4 5.1 collective-permute-done.48
  452.9 11.0 %shard_map.237 = (bf16[4,256,512]{2,1,0:T(8,128)(2,1)}, bf16[4,256,512]{2,1,0:T(8,128)(2,1)}) custom-call(s32[4]{0:T(128)} %pad_add_fusion.1.coord, bf16[4,384,512]{2,1,0:T(8,128)(2,1)} %get-tuple-element.218.refs_0_, bf16[192,2048]{1,0:T(8,128)(2,1)} %copy-done.11, bf16[192,2048]{1,0:T(8,128)(2,1)} %copy-done.30, ...), custom_call_target="tpu_custom_call" | custom-call | flops 3221225472 | bytes 9961472 | tf_op jit(solution)/shard_map/pallas_call | solution.py:794
  464.7 10.9 %shard_map.238 = (bf16[4,256,512]{2,1,0:T(8,128)(2,1)}, bf16[4,256,512]{2,1,0:T(8,128)(2,1)}) custom-call(s32[4]{0:T(128)} %pad_add_fusion.1.coord, bf16[4,384,512]{2,1,0:T(8,128)(2,1)} %get-tuple-element.221.refs_0_.refs_2_, bf16[8,192,2048]{2,1,0:T(8,128)(2,1)} %bitcast.142), custom_call_target="tpu_custom_call" | custom-call | flops 3221225472 | bytes 9961472 | tf_op jit(solution)/shard_map/pallas_call | solution.py:794
  477.5 16.4 %shard_map.239 = (bf16[4,256,512]{2,1,0:T(8,128)(2,1)}, bf16[4,256,512]{2,1,0:T(8,128)(2,1)}, bf16[4,256,512]{2,1,0:T(8,128)(2,1)}, bf16[4,256,512]{2,1,0:T(8,128)(2,1)}) custom-call(s32[4]{0:T(128)} %pad_add_fusion.1.coord, bf16[4,384,512]{2,1,0:T(8,128)(2,1)} %get-tuple-element.226.refs_0_.refs_1_, ...), custom_call_target="tpu_custom_call" | custom-call | flops 6442450944 | bytes 13631488 | tf_op jit(solution)/shard_map/pallas_call | solution.py:794
  497.7 17.0 %shard_map.240 = (bf16[3,192,2048]{2,1,0:T(8,128)(2,1)}, bf16[192,2048]{1,0:T(8,128)(2,1)}, bf16[4,192,2048]{2,1,0:T(8,128)(2,1)}) custom-call(s32[4]{0:T(128)} %pad_add_fusion.1.coord, bf16[4,384,512]{2,1,0:T(8,128)(2,1)} %get-tuple-element.212.refs_1_.refs_0_, bf16[4,384,512]{2,1,0:T(8,128)(2,1)} %get-tuple-element.226.refs_0_.refs_1_, ...), custom_call_target="tpu_custom_call" | custom-call | flops 9663676416 | bytes 23592976 | tf_op jit(solution)/shard_map/pallas_call | solution.py:320
  514.7 6.3 collective-permute-done.52
  524.1 2.8 collective-permute-done.54
  529.4 19.5 %collective-permute-done.59 = bf16[2,256,512]{2,1,0:T(8,128)(2,1)S(1)} collective-permute-done((bf16[2,256,512]{2,1,0:T(8,128)(2,1)S(1)}, bf16[2,256,512]{2,1,0:T(8,128)(2,1)S(1)}, u32[]{:S(2)}, u32[]{:S(2)}) %collective-permute-start.59) | collective-permute-done | bytes 524320 | tf_op jit(solution)/shard_map/zh_gswish/ppermute | solution.py:37
  562.4 4.3 all-to-all-start.3
  566.8 9.1 %collective-permute-done.62 = bf16[2,256,512]{2,1,0:T(8,128)(2,1)} collective-permute-done((bf16[2,256,512]{2,1,0:T(8,128)(2,1)}, bf16[2,256,512]{2,1,0:T(8,128)(2,1)}, u32[]{:S(2)}, u32[]{:S(2)}) %collective-permute-start.62) | collective-permute-done | bytes 524320 | tf_op jit(solution)/shard_map/zh_gvalue/ppermute | solution.py:37
  579.5 22.5 %collective-permute-done.58 = bf16[192,2048]{1,0:T(8,128)(2,1)} collective-permute-done((bf16[192,2048]{1,0:T(8,128)(2,1)}, bf16[192,2048]{1,0:T(8,128)(2,1)}, u32[]{:S(2)}, u32[]{:S(2)}) %collective-permute-start.58) | collective-permute-done | bytes 786464 | tf_op jit(solution)/shard_map/back_one_z/ppermute | solution.py:37
  602.1 2.7 fusion.9
  608.4 3.5 collective-permute-start.65
  613.6 2.6 collective-permute-start.66
  623.2 4.3 all-to-all-start.4
  627.5 3.7 add_add_fusion.2
  631.8 3.8 shard_map.241
  643.0 3.5 all-to-all-start.5
  646.5 3.6 shard_map.243
  650.1 9.5 %all-to-all-done.5.g = bf16[4,128,1024]{2,1,0:T(8,128)(2,1)S(1)} async-done(((bf16[4,128,1024]{2,1,0:T(8,128)(2,1)}), bf16[4,128,1024]{2,1,0:T(8,128)(2,1)S(1)}, u32[]{:S(2)}, u32[]{:S(2)}) %all-to-all-start.5) | async-done | bytes 1048608 | tf_op jit(solution)/shard_map/all_to_all | solution.py:59
  660.6 3.5 shard_map.242
  (368 shorter events, 152.8 us)
Async XLA Ops:
  11.4 18.9 %all-to-all-start = ((bf16[4,128,1024]{2,1,0:T(8,128)(2,1)}), bf16[4,128,1024]{2,1,0:T(8,128)(2,1)S(1)}, u32[]{:S(2)}, u32[]{:S(2)}) async-start(bf16[4,128,1024]{2,1,0:T(8,128)(2,1)} %pad_maximum_fusion.3), calls=%async_computation | async-start | bytes 2097152 | tf_op jit(solution)/shard_map/all_to_all | solution.py:59
  16.7 113.0 %all-gather.5.cloned.1.call-start = ((), (), s32[]{:S(2)}) async-start(), calls=%async_computation.8 | async-start | bytes 7077888 | tf_op jit(solution)/shard_map/all_gather | solution.py:908
  35.2 58.3 %all-to-all-start.1 = ((bf16[4,128,1024]{2,1,0:T(8,128)(2,1)}), bf16[4,128,1024]{2,1,0:T(8,128)(2,1)S(1)}, u32[]{:S(2)}, u32[]{:S(2)}) async-start(bf16[4,128,1024]{2,1,0:T(8,128)(2,1)} %pad_maximum_fusion.2), calls=%async_computation.1 | async-start | bytes 2097152 | tf_op jit(solution)/shard_map/all_to_all | solution.py:59
  39.0 24.3 %collective-permute-start.4 = (bf16[4,128,1024]{2,1,0:T(8,128)(2,1)}, bf16[4,128,1024]{2,1,0:T(8,128)(2,1)}, u32[]{:S(2)}, u32[]{:S(2)}) collective-permute-start(bf16[4,128,1024]{2,1,0:T(8,128)(2,1)} %copy-done.12), channel_id=1, source_target_pairs={{0,4},{4,0},{1,5},{5,1},{2,6},{6,2},{3,7},{7,3},{8,12},{12,8},{9,1... | collective-permute-start | bytes 3145736 | tf_op jit(solution)/shard_map/ny_qkv/ppermute | solution.py:37
  40.6 52.9 %collective-permute-start.3 = (bf16[4,128,1024]{2,1,0:T(8,128)(2,1)}, bf16[4,128,1024]{2,1,0:T(8,128)(2,1)}, u32[]{:S(2)}, u32[]{:S(2)}) collective-permute-start(bf16[4,128,1024]{2,1,0:T(8,128)(2,1)} %copy-done.12), channel_id=1, source_target_pairs={{0,16},{16,0},{1,17},{17,1},{2,18},{18,2},{3,19},{19,3},{4,20},{20... | collective-permute-start | bytes 3145736 | tf_op jit(solution)/shard_map/zh_qkv/ppermute | solution.py:37
  93.5 59.5 %all-to-all-start.2 = ((bf16[4,128,1536]{2,1,0:T(8,128)(2,1)}), bf16[4,128,1536]{2,1,0:T(8,128)(2,1)S(1)}, u32[]{:S(2)}, u32[]{:S(2)}) async-start(bf16[4,128,1536]{2,1,0:T(8,128)(2,1)} %pad_maximum_fusion), calls=%async_computation.2 | async-start | bytes 3145728 | tf_op jit(solution)/shard_map/all_to_all | solution.py:59
  103.3 177.6 %all-gather.7.cloned.1.call-start = ((), (), s32[]{:S(2)}) async-start(), calls=%async_computation.9 | async-start | bytes 7077888 | tf_op jit(solution)/shard_map/all_gather | solution.py:927
  103.3 26.4 %collective-permute-start.5 = (bf16[4,128,1024]{2,1,0:T(8,128)(2,1)}, bf16[4,128,1024]{2,1,0:T(8,128)(2,1)}, u32[]{:S(2)}, u32[]{:S(2)}) collective-permute-start(bf16[4,128,1024]{2,1,0:T(8,128)(2,1)} %collective-permute-done.3.refs_3_.refs_7_.refs_5_.refs_9_), channel_id=1, source_target_pairs={{0,4},{4,0},{1,5},{5,1},{2,6},{6,2},{3,7},{7,3},{8,12},{12,8},{9,1... | collective-permute-start | bytes 3145736 | tf_op jit(solution)/shard_map/fy_qkv/ppermute | solution.py:37
  104.9 48.1 %collective-permute-start.7 = (bf16[4,128,1024]{2,1,0:T(8,128)(2,1)S(1)}, bf16[4,128,1024]{2,1,0:T(8,128)(2,1)}, u32[]{:S(2)}, u32[]{:S(2)}) collective-permute-start(bf16[4,128,1024]{2,1,0:T(8,128)(2,1)S(1)} %all-to-all-done.1.refs_1_.refs_5_.refs_10_.refs_11_), channel_id=1, source_target_pairs={{0,4},{4,0},{1,5},{5,1},{2,6},{6,2},{3,7},{7,3},{8,12},{12,8},{9,1... | collective-permute-start | bytes 3145736 | tf_op jit(solution)/shard_map/ny_so/ppermute | solution.py:37
  105.3 47.6 %collective-permute-start.6 = (bf16[4,128,1024]{2,1,0:T(8,128)(2,1)S(1)}, bf16[4,128,1024]{2,1,0:T(8,128)(2,1)}, u32[]{:S(2)}, u32[]{:S(2)}) collective-permute-start(bf16[4,128,1024]{2,1,0:T(8,128)(2,1)S(1)} %all-to-all-done.1.refs_1_.refs_5_.refs_10_.refs_11_), channel_id=1, source_target_pairs={{0,16},{16,0},{1,17},{17,1},{2,18},{18,2},{3,19},{19,3},{4,20},{20... | collective-permute-start | bytes 3145736 | tf_op jit(solution)/shard_map/zh_so/ppermute | solution.py:37
  153.0 482.7 %reduce-scatter.2.cloned.1.call-start = ((), (), s32[]{:S(2)}) async-start(), calls=%async_computation.7 | async-start | bytes 7077888 | tf_op jit(solution)/shard_map/reduce_scatter | solution.py:980
  153.2 26.5 %collective-permute-start.8 = (bf16[4,128,1024]{2,1,0:T(8,128)(2,1)}, bf16[4,128,1024]{2,1,0:T(8,128)(2,1)}, u32[]{:S(2)}, u32[]{:S(2)}) collective-permute-start(bf16[4,128,1024]{2,1,0:T(8,128)(2,1)} %collective-permute-done.6.refs_3_.refs_7_.refs_12_.refs_13_), channel_id=1, source_target_pairs={{0,4},{4,0},{1,5},{5,1},{2,6},{6,2},{3,7},{7,3},{8,12},{12,8},{9,1... | collective-permute-start | bytes 3145736 | tf_op jit(solution)/shard_map/fy_so/ppermute | solution.py:37
  155.0 42.4 %collective-permute-start.10 = (bf16[4,128,1024]{2,1,0:T(8,128)(2,1)S(1)}, bf16[4,128,1024]{2,1,0:T(8,128)(2,1)}, u32[]{:S(2)}, u32[]{:S(2)}) collective-permute-start(bf16[4,128,1024]{2,1,0:T(8,128)(2,1)S(1)} %slice.316.refs_10_.refs_14_), channel_id=1, source_target_pairs={{0,4},{4,0},{1,5},{5,1},{2,6},{6,2},{3,7},{7,3},{8,12},{12,8},{9,1... | collective-permute-start | bytes 3145736 | tf_op jit(solution)/shard_map/ny_ug/ppermute | solution.py:37
  155.5 44.3 %collective-permute-start.9 = (bf16[4,128,1024]{2,1,0:T(8,128)(2,1)S(1)}, bf16[4,128,1024]{2,1,0:T(8,128)(2,1)}, u32[]{:S(2)}, u32[]{:S(2)}) collective-permute-start(bf16[4,128,1024]{2,1,0:T(8,128)(2,1)S(1)} %slice.316.refs_10_.refs_14_), channel_id=1, source_target_pairs={{0,16},{16,0},{1,17},{17,1},{2,18},{18,2},{3,19},{19,3},{4,20},{20... | collective-permute-start | bytes 3145736 | tf_op jit(solution)/shard_map/zh_ug/ppermute | solution.py:37
  199.8 19.2 %collective-permute-start.14 = (bf16[3,192,2048]{2,1,0:T(8,128)(2,1)}, bf16[3,192,2048]{2,1,0:T(8,128)(2,1)S(1)}, u32[]{:S(2)}, u32[]{:S(2)}) collective-permute-start(bf16[3,192,2048]{2,1,0:T(8,128)(2,1)} %get-tuple-element.160), channel_id=1, source_target_pairs={{0,1},{1,0},{2,3},{3,2},{4,5},{5,4},{6,7},{7,6},{8,9},{9,8},{10,11... | collective-permute-start | bytes 7077896 | tf_op jit(solution)/shard_map/branch_cr/ppermute | solution.py:37
  209.3 42.0 %collective-permute-start.19 = (bf16[4,128,1024]{2,1,0:T(8,128)(2,1)}, bf16[4,128,1024]{2,1,0:T(8,128)(2,1)S(1)}, u32[]{:S(2)}, u32[]{:S(2)}) collective-permute-start(bf16[4,128,1024]{2,1,0:T(8,128)(2,1)} %collective-permute-done.9.refs_12_.refs_16_), channel_id=1, source_target_pairs={{0,4},{4,0},{1,5},{5,1},{2,6},{6,2},{3,7},{7,3},{8,12},{12,8},{9,1... | collective-permute-start | bytes 3145736 | tf_op jit(solution)/shard_map/fy_ug/ppermute | solution.py:37
  220.6 30.7 %collective-permute-start.15 = (bf16[192,2048]{1,0:T(8,128)(2,1)S(1)}, bf16[192,2048]{1,0:T(8,128)(2,1)S(1)}, u32[]{:S(2)}, u32[]{:S(2)}) collective-permute-start(bf16[192,2048]{1,0:T(8,128)(2,1)S(1)} %pad_maximum_fusion.6), channel_id=1, source_target_pairs={{0,2},{2,0},{1,3},{3,1},{4,6},{6,4},{5,7},{7,5},{8,10},{10,8},{9,1... | collective-permute-start | bytes 2359304 | tf_op jit(solution)/shard_map/branch_x/ppermute | solution.py:37
  223.2 30.3 %collective-permute-start.16 = (bf16[192,2048]{1,0:T(8,128)(2,1)S(1)}, bf16[192,2048]{1,0:T(8,128)(2,1)S(1)}, u32[]{:S(2)}, u32[]{:S(2)}) collective-permute-start(bf16[192,2048]{1,0:T(8,128)(2,1)S(1)} %pad_maximum_fusion.7), channel_id=1, source_target_pairs={{0,8},{8,0},{1,9},{9,1},{2,10},{10,2},{3,11},{11,3},{4,12},{12,4},... | collective-permute-start | bytes 2359304 | tf_op jit(solution)/shard_map/branch_z/ppermute | solution.py:37
  224.0 21.7 %collective-permute-start.18 = (bf16[4,128,512]{2,1,0:T(8,128)(2,1)S(1)}, bf16[4,128,512]{2,1,0:T(8,128)(2,1)S(1)}, u32[]{:S(2)}, u32[]{:S(2)}) collective-permute-start(bf16[4,128,512]{2,1,0:T(8,128)(2,1)S(1)} %slice.326.refs_1_), channel_id=1, source_target_pairs={{0,4},{4,0},{1,5},{5,1},{2,6},{6,2},{3,7},{7,3},{8,12},{12,8},{9,1... | collective-permute-start | bytes 1572872 | tf_op jit(solution)/shard_map/ny_d/ppermute | solution.py:37
  224.9 26.4 %collective-permute-start.17 = (bf16[4,128,512]{2,1,0:T(8,128)(2,1)S(1)}, bf16[4,128,512]{2,1,0:T(8,128)(2,1)S(1)}, u32[]{:S(2)}, u32[]{:S(2)}) collective-permute-start(bf16[4,128,512]{2,1,0:T(8,128)(2,1)S(1)} %slice.326.refs_1_), channel_id=1, source_target_pairs={{0,16},{16,0},{1,17},{17,1},{2,18},{18,2},{3,19},{19,3},{4,20},{20... | collective-permute-start | bytes 1572872 | tf_op jit(solution)/shard_map/zh_d/ppermute | solution.py:37
  255.3 20.1 %collective-permute-start.22 = (bf16[192,2048]{1,0:T(8,128)(2,1)S(1)}, bf16[192,2048]{1,0:T(8,128)(2,1)}, u32[]{:S(2)}, u32[]{:S(2)}) collective-permute-start(bf16[192,2048]{1,0:T(8,128)(2,1)S(1)} %multiply_convert_fusion.refs_0_.refs_2_), channel_id=1, source_target_pairs={{0,8},{8,0},{1,9},{9,1},{2,10},{10,2},{3,11},{11,3},{4,12},{12,4},... | collective-permute-start | bytes 2359304 | tf_op jit(solution)/shard_map/two_z/ppermute | solution.py:37
  256.5 19.7 %collective-permute-start.21 = (bf16[192,2048]{1,0:T(8,128)(2,1)S(1)}, bf16[192,2048]{1,0:T(8,128)(2,1)}, u32[]{:S(2)}, u32[]{:S(2)}) collective-permute-start(bf16[192,2048]{1,0:T(8,128)(2,1)S(1)} %multiply_convert_fusion.refs_0_.refs_2_), channel_id=1, source_target_pairs={{0,2},{2,0},{1,3},{3,1},{4,6},{6,4},{5,7},{7,5},{8,10},{10,8},{9,1... | collective-permute-start | bytes 2359304 | tf_op jit(solution)/shard_map/two_x/ppermute | solution.py:37
  318.6 20.7 %collective-permute-start.33 = (bf16[3,192,2048]{2,1,0:T(8,128)(2,1)}, bf16[3,192,2048]{2,1,0:T(8,128)(2,1)}, u32[]{:S(2)}, u32[]{:S(2)}) collective-permute-start(bf16[3,192,2048]{2,1,0:T(8,128)(2,1)} %get-tuple-element.186), channel_id=1, source_target_pairs={{0,1},{1,0},{2,3},{3,2},{4,5},{5,4},{6,7},{7,6},{8,9},{9,8},{10,11... | collective-permute-start | bytes 7077896 | tf_op jit(solution)/shard_map/back_two_cr/ppermute | solution.py:37
  340.0 27.8 %collective-permute-start.34 = (bf16[4,256,512]{2,1,0:T(8,128)(2,1)}, bf16[4,256,512]{2,1,0:T(8,128)(2,1)S(1)}, u32[]{:S(2)}, u32[]{:S(2)}) collective-permute-start(bf16[4,256,512]{2,1,0:T(8,128)(2,1)} %get-tuple-element.187), channel_id=1, source_target_pairs={{0,4},{4,0},{1,5},{5,1},{2,6},{6,2},{3,7},{7,3},{8,12},{12,8},{9,1... | collective-permute-start | bytes 3145736 | tf_op jit(solution)/shard_map/y_down/ppermute | solution.py:37
  347.3 19.6 %collective-permute-start.35 = (bf16[192,2048]{1,0:T(8,128)(2,1)}, bf16[192,2048]{1,0:T(8,128)(2,1)}, u32[]{:S(2)}, u32[]{:S(2)}) collective-permute-start(bf16[192,2048]{1,0:T(8,128)(2,1)} %pad_maximum_fusion.8), channel_id=1, source_target_pairs={{0,2},{2,0},{1,3},{3,1},{4,6},{6,4},{5,7},{7,5},{8,10},{10,8},{9,1... | collective-permute-start | bytes 2359304 | tf_op jit(solution)/shard_map/back_two_x/ppermute | solution.py:37
  348.8 19.0 %collective-permute-start.36 = (bf16[192,2048]{1,0:T(8,128)(2,1)}, bf16[192,2048]{1,0:T(8,128)(2,1)}, u32[]{:S(2)}, u32[]{:S(2)}) collective-permute-start(bf16[192,2048]{1,0:T(8,128)(2,1)} %pad_maximum_fusion.9), channel_id=1, source_target_pairs={{0,8},{8,0},{1,9},{9,1},{2,10},{10,2},{3,11},{11,3},{4,12},{12,4},... | collective-permute-start | bytes 2359304 | tf_op jit(solution)/shard_map/back_two_z/ppermute | solution.py:37
  374.1 32.0 %collective-permute-start.38 = (bf16[4,256,512]{2,1,0:T(8,128)(2,1)S(1)}, bf16[4,256,512]{2,1,0:T(8,128)(2,1)S(1)}, u32[]{:S(2)}, u32[]{:S(2)}) collective-permute-start(bf16[4,256,512]{2,1,0:T(8,128)(2,1)S(1)} %copy-done.61), channel_id=1, source_target_pairs={{0,4},{4,0},{1,5},{5,1},{2,6},{6,2},{3,7},{7,3},{8,12},{12,8},{9,1... | collective-permute-start | bytes 3145736 | tf_op jit(solution)/shard_map/y_up/ppermute | solution.py:37
  374.8 30.3 %collective-permute-start.41 = (bf16[192,2048]{1,0:T(8,128)(2,1)S(1)}, bf16[192,2048]{1,0:T(8,128)(2,1)S(1)}, u32[]{:S(2)}, u32[]{:S(2)}) collective-permute-start(bf16[192,2048]{1,0:T(8,128)(2,1)S(1)} %fusion.27.refs_0_.refs_1_), channel_id=1, source_target_pairs={{0,1},{1,0},{2,3},{3,2},{4,5},{5,4},{6,7},{7,6},{8,9},{9,8},{10,11... | collective-permute-start | bytes 2359304 | tf_op jit(solution)/shard_map/gb_c/ppermute | solution.py:37
  374.8 31.3 %collective-permute-start.40 = (bf16[192,2048]{1,0:T(8,128)(2,1)S(1)}, bf16[192,2048]{1,0:T(8,128)(2,1)}, u32[]{:S(2)}, u32[]{:S(2)}) collective-permute-start(bf16[192,2048]{1,0:T(8,128)(2,1)S(1)} %fusion.27.refs_0_.refs_1_), channel_id=1, source_target_pairs={{0,8},{8,0},{1,9},{9,1},{2,10},{10,2},{3,11},{11,3},{4,12},{12,4},... | collective-permute-start | bytes 2359304 | tf_op jit(solution)/shard_map/gb_z/ppermute | solution.py:37
  376.4 29.7 %collective-permute-start.39 = (bf16[192,2048]{1,0:T(8,128)(2,1)S(1)}, bf16[192,2048]{1,0:T(8,128)(2,1)}, u32[]{:S(2)}, u32[]{:S(2)}) collective-permute-start(bf16[192,2048]{1,0:T(8,128)(2,1)S(1)} %fusion.27.refs_0_.refs_1_), channel_id=1, source_target_pairs={{0,2},{2,0},{1,3},{3,1},{4,6},{6,4},{5,7},{7,5},{8,10},{10,8},{9,1... | collective-permute-start | bytes 2359304 | tf_op jit(solution)/shard_map/gb_x/ppermute | solution.py:37
  377.6 27.5 %collective-permute-start.37 = (bf16[2,256,512]{2,1,0:T(8,128)(2,1)S(1)}, bf16[2,256,512]{2,1,0:T(8,128)(2,1)S(1)}, u32[]{:S(2)}, u32[]{:S(2)}) collective-permute-start(bf16[2,256,512]{2,1,0:T(8,128)(2,1)S(1)} %add_convert_fusion.20), channel_id=1, source_target_pairs={{0,16},{16,0},{1,17},{17,1},{2,18},{18,2},{3,19},{19,3},{4,20},{20... | collective-permute-start | bytes 1572872 | tf_op jit(solution)/shard_map/zh_gdown/ppermute | solution.py:37
  422.0 24.4 %collective-permute-start.49 = (bf16[4,256,512]{2,1,0:T(8,128)(2,1)}, bf16[4,256,512]{2,1,0:T(8,128)(2,1)}, u32[]{:S(2)}, u32[]{:S(2)}) collective-permute-start(bf16[4,256,512]{2,1,0:T(8,128)(2,1)} %get-tuple-element.216), channel_id=1, source_target_pairs={{0,4},{4,0},{1,5},{5,1},{2,6},{6,2},{3,7},{7,3},{8,12},{12,8},{9,1... | collective-permute-start | bytes 3145736 | tf_op jit(solution)/shard_map/y_gate/ppermute | solution.py:37
  425.3 26.2 %collective-permute-start.48 = (bf16[2,256,512]{2,1,0:T(8,128)(2,1)S(1)}, bf16[2,256,512]{2,1,0:T(8,128)(2,1)}, u32[]{:S(2)}, u32[]{:S(2)}) collective-permute-start(bf16[2,256,512]{2,1,0:T(8,128)(2,1)S(1)} %add_convert_fusion.19), channel_id=1, source_target_pairs={{0,16},{16,0},{1,17},{17,1},{2,18},{18,2},{3,19},{19,3},{4,20},{20... | collective-permute-start | bytes 1572872 | tf_op jit(solution)/shard_map/zh_gup/ppermute | solution.py:37
  452.8 24.6 %collective-permute-start.50 = (bf16[2,256,512]{2,1,0:T(8,128)(2,1)S(1)}, bf16[2,256,512]{2,1,0:T(8,128)(2,1)}, u32[]{:S(2)}, u32[]{:S(2)}) collective-permute-start(bf16[2,256,512]{2,1,0:T(8,128)(2,1)S(1)} %add_convert_fusion.18), channel_id=1, source_target_pairs={{0,16},{16,0},{1,17},{17,1},{2,18},{18,2},{3,19},{19,3},{4,20},{20... | collective-permute-start | bytes 1572872 | tf_op jit(solution)/shard_map/zh_ggate/ppermute | solution.py:37
  463.9 29.9 %collective-permute-start.51 = (bf16[4,256,512]{2,1,0:T(8,128)(2,1)}, bf16[4,256,512]{2,1,0:T(8,128)(2,1)}, u32[]{:S(2)}, u32[]{:S(2)}) collective-permute-start(bf16[4,256,512]{2,1,0:T(8,128)(2,1)} %get-tuple-element.228), channel_id=1, source_target_pairs={{0,4},{4,0},{1,5},{5,1},{2,6},{6,2},{3,7},{7,3},{8,12},{12,8},{9,1... | collective-permute-start | bytes 3145736 | tf_op jit(solution)/shard_map/y_out/ppermute | solution.py:37
  493.9 27.1 %collective-permute-start.53 = (bf16[4,256,512]{2,1,0:T(8,128)(2,1)}, bf16[4,256,512]{2,1,0:T(8,128)(2,1)}, u32[]{:S(2)}, u32[]{:S(2)}) collective-permute-start(bf16[4,256,512]{2,1,0:T(8,128)(2,1)} %get-tuple-element.235), channel_id=1, source_target_pairs={{0,4},{4,0},{1,5},{5,1},{2,6},{6,2},{3,7},{7,3},{8,12},{12,8},{9,1... | collective-permute-start | bytes 3145736 | tf_op jit(solution)/shard_map/y_swish/ppermute | solution.py:37
  496.0 25.0 %collective-permute-start.52 = (bf16[2,256,512]{2,1,0:T(8,128)(2,1)S(1)}, bf16[2,256,512]{2,1,0:T(8,128)(2,1)}, u32[]{:S(2)}, u32[]{:S(2)}) collective-permute-start(bf16[2,256,512]{2,1,0:T(8,128)(2,1)S(1)} %add_convert_fusion.17), channel_id=1, source_target_pairs={{0,16},{16,0},{1,17},{17,1},{2,18},{18,2},{3,19},{19,3},{4,20},{20... | collective-permute-start | bytes 1572872 | tf_op jit(solution)/shard_map/zh_gout/ppermute | solution.py:37
  521.0 32.2 %collective-permute-start.56 = (bf16[3,192,2048]{2,1,0:T(8,128)(2,1)}, bf16[3,192,2048]{2,1,0:T(8,128)(2,1)S(1)}, u32[]{:S(2)}, u32[]{:S(2)}) collective-permute-start(bf16[3,192,2048]{2,1,0:T(8,128)(2,1)} %get-tuple-element.237), channel_id=1, source_target_pairs={{0,1},{1,0},{2,3},{3,2},{4,5},{5,4},{6,7},{7,6},{8,9},{9,8},{10,11... | collective-permute-start | bytes 7077896 | tf_op jit(solution)/shard_map/back_one_cr/ppermute | solution.py:37
  521.5 27.4 %collective-permute-start.60 = (bf16[4,256,512]{2,1,0:T(8,128)(2,1)}, bf16[4,256,512]{2,1,0:T(8,128)(2,1)S(1)}, u32[]{:S(2)}, u32[]{:S(2)}) collective-permute-start(bf16[4,256,512]{2,1,0:T(8,128)(2,1)} %get-tuple-element.246), channel_id=1, source_target_pairs={{0,4},{4,0},{1,5},{5,1},{2,6},{6,2},{3,7},{7,3},{8,12},{12,8},{9,1... | collective-permute-start | bytes 3145736 | tf_op jit(solution)/shard_map/y_value/ppermute | solution.py:37
  524.0 24.9 %collective-permute-start.59 = (bf16[2,256,512]{2,1,0:T(8,128)(2,1)S(1)}, bf16[2,256,512]{2,1,0:T(8,128)(2,1)S(1)}, u32[]{:S(2)}, u32[]{:S(2)}) collective-permute-start(bf16[2,256,512]{2,1,0:T(8,128)(2,1)S(1)} %add_convert_fusion.16), channel_id=1, source_target_pairs={{0,16},{16,0},{1,17},{17,1},{2,18},{18,2},{3,19},{19,3},{4,20},{20... | collective-permute-start | bytes 1572872 | tf_op jit(solution)/shard_map/zh_gswish/ppermute | solution.py:37
  528.3 25.0 %collective-permute-start.55 = (bf16[192,2048]{1,0:T(8,128)(2,1)S(1)}, bf16[192,2048]{1,0:T(8,128)(2,1)S(1)}, u32[]{:S(2)}, u32[]{:S(2)}) collective-permute-start(bf16[192,2048]{1,0:T(8,128)(2,1)S(1)} %fusion.23), channel_id=1, source_target_pairs={{0,2},{2,0},{1,3},{3,1},{4,6},{6,4},{5,7},{7,5},{8,10},{10,8},{9,1... | collective-permute-start | bytes 2359304 | tf_op jit(solution)/shard_map/back_one_dx/ppermute | solution.py:37
  550.0 25.8 %collective-permute-start.62 = (bf16[2,256,512]{2,1,0:T(8,128)(2,1)}, bf16[2,256,512]{2,1,0:T(8,128)(2,1)}, u32[]{:S(2)}, u32[]{:S(2)}) collective-permute-start(bf16[2,256,512]{2,1,0:T(8,128)(2,1)} %add_convert_fusion.15), channel_id=1, source_target_pairs={{0,16},{16,0},{1,17},{17,1},{2,18},{18,2},{3,19},{19,3},{4,20},{20... | collective-permute-start | bytes 1572872 | tf_op jit(solution)/shard_map/zh_gvalue/ppermute | solution.py:37
  550.3 25.6 %collective-permute-start.61 = (bf16[4,256,512]{2,1,0:T(8,128)(2,1)}, bf16[4,256,512]{2,1,0:T(8,128)(2,1)}, u32[]{:S(2)}, u32[]{:S(2)}) collective-permute-start(bf16[4,256,512]{2,1,0:T(8,128)(2,1)} %get-tuple-element.247), channel_id=1, source_target_pairs={{0,4},{4,0},{1,5},{5,1},{2,6},{6,2},{3,7},{7,3},{8,12},{12,8},{9,1... | collective-permute-start | bytes 3145736 | tf_op jit(solution)/shard_map/y_qk/ppermute | solution.py:37
  556.4 23.1 %collective-permute-start.57 = (bf16[192,2048]{1,0:T(8,128)(2,1)}, bf16[192,2048]{1,0:T(8,128)(2,1)}, u32[]{:S(2)}, u32[]{:S(2)}) collective-permute-start(bf16[192,2048]{1,0:T(8,128)(2,1)} %fusion.28), channel_id=1, source_target_pairs={{0,2},{2,0},{1,3},{3,1},{4,6},{6,4},{5,7},{7,5},{8,10},{10,8},{9,1... | collective-permute-start | bytes 2359304 | tf_op jit(solution)/shard_map/back_one_x/ppermute | solution.py:37
  558.7 43.3 %collective-permute-start.58 = (bf16[192,2048]{1,0:T(8,128)(2,1)}, bf16[192,2048]{1,0:T(8,128)(2,1)}, u32[]{:S(2)}, u32[]{:S(2)}) collective-permute-start(bf16[192,2048]{1,0:T(8,128)(2,1)} %fusion.12), channel_id=1, source_target_pairs={{0,8},{8,0},{1,9},{9,1},{2,10},{10,2},{3,11},{11,3},{4,12},{12,4},... | collective-permute-start | bytes 2359304 | tf_op jit(solution)/shard_map/back_one_z/ppermute | solution.py:37
  562.4 60.8 %all-to-all-start.3 = ((bf16[4,128,1536]{2,1,0:T(8,128)(2,1)}), bf16[4,128,1536]{2,1,0:T(8,128)(2,1)}, u32[]{:S(2)}, u32[]{:S(2)}) async-start(bf16[4,128,1536]{2,1,0:T(8,128)(2,1)} %pad_maximum_fusion.1), calls=%async_computation.4 | async-start | bytes 3145728 | tf_op jit(solution)/shard_map/all_to_all | solution.py:59
  577.2 29.7 %collective-permute-start.63 = (bf16[2,256,512]{2,1,0:T(8,128)(2,1)S(1)}, bf16[2,256,512]{2,1,0:T(8,128)(2,1)S(1)}, u32[]{:S(2)}, u32[]{:S(2)}) collective-permute-start(bf16[2,256,512]{2,1,0:T(8,128)(2,1)S(1)} %add_convert_fusion.14), channel_id=1, source_target_pairs={{0,16},{16,0},{1,17},{17,1},{2,18},{18,2},{3,19},{19,3},{4,20},{20... | collective-permute-start | bytes 1572872 | tf_op jit(solution)/shard_map/zh_gqk/ppermute | solution.py:37
  643.0 16.7 %all-to-all-start.5 = ((bf16[4,128,1024]{2,1,0:T(8,128)(2,1)}), bf16[4,128,1024]{2,1,0:T(8,128)(2,1)S(1)}, u32[]{:S(2)}, u32[]{:S(2)}) async-start(bf16[4,128,1024]{2,1,0:T(8,128)(2,1)} %pad_maximum_fusion.5), calls=%async_computation.6 | async-start | bytes 2097152 | tf_op jit(solution)/shard_map/all_to_all | solution.py:59
  (99 other events, 941.4 us)
Sparse Core Ops, SparseCore 0:
  30.4 70.6 all-gather.4
  153.1 58.3 all-gather.6
  422.1 65.6 reduce-scatter.1

commit v6 on v5

--- a/solution.py
+++ b/solution.py
@@ -218,7 +218,7 @@
 
     def send(self, clock):
         *through, rest = (v.astype(f32) for v in clock.at_all(self.second))
-        self.own, xmate, zmate = (self.keep[r].astype(f32) + rest[r] for r in range(3))
+        xmate, zmate = (self.keep[r].astype(f32) + rest[r] for r in (1, 2))
         if self.whole:
             self.x = swap(xmate.astype(bf16), "x", self.label + "_x")
             self.z = swap((zmate + through[0]).astype(bf16), "zl", self.label + "_z")
@@ -234,7 +234,8 @@
 
     def finish(self, clock):
         x, z = clock.at_all(self.last)
-        return self.own + x.astype(f32) + z.astype(f32)
+        own = self.keep[0].astype(f32) + self.rest[0].astype(f32)
+        return own + x.astype(f32) + z.astype(f32)
 
 
 VMEM_LIMIT = 60 * 2**20

time: 679 us -> 677 us (level)
  no operation moved by 1% of the time
where the time goes in v6:
time: 677 us; the launch traced here: 669 us
  waiting for transfers between devices  284 us (42%)
  Pallas kernels  189 us (28%)
  starting transfers between devices  97.7 us (14%)
  other arithmetic  59.7 us (9%)
  local copies, waits for them, and re-layouts  22.8 us (3%)
  between operations  16.2 us (2%)
    ppermute x68, waiting for transfers between devices, swap(): return lax.ppermute(a, axis, [(0, 1), (1, 0)])  265 us
    pallas_call x7, Pallas kernels, chip_kernel(): pl.pallas_call(body, grid=(4,), in_specs=specs, out_specs=out_specs, out_...  112 us
    pallas_call x5, Pallas kernels, weight_grads(): pl.pallas_call(functools.partial(weight_grad_body, len(grads), len(acts),...  65.7 us
    ppermute x68, starting transfers between devices, swap(): return lax.ppermute(a, axis, [(0, 1), (1, 0)])  65.3 us
    all_to_all x6, starting transfers between devices, group_exchange(): return lax.all_to_all(parts, GROUP, 0, 0, tiled=True)  30.7 us
    convert_element_type x16, other arithmetic, add(): return (a.astype(f32) + b.astype(f32)).astype(bf16)  21.6 us
    all_to_all x6, waiting for transfers between devices, group_exchange(): return lax.all_to_all(parts, GROUP, 0, 0, tiled=True)  19.1 us
  transfers between devices with their start and end apart: 78, of which 39 were waited for; matrix products, arithmetic and copies ran while one was open for 9% of the time, Pallas kernels for 24%

profile of v6, /device:TPU:0, one launch (start us, length us, event | category | flops | bytes accessed | tf_op | source)
XLA Modules:
  0.0 669.4 jit_solution(8884690874180799465)
XLA Ops:
  11.4 5.2 all-to-all-start
  21.6 8.7 %all-to-all-done.refs_1_.refs_5_.refs_3_.refs_7_ = bf16[4,128,1024]{2,1,0:T(8,128)(2,1)S(1)} async-done(((bf16[4,128,1024]{2,1,0:T(8,128)(2,1)}), bf16[4,128,1024]{2,1,0:T(8,128)(2,1)S(1)}, u32[]{:S(2)}, u32[]{:S(2)}) %all-to-all-start) | async-done | bytes 1048608 | tf_op jit(solution)/shard_map/all_to_all | solution.py:59
  35.2 3.5 all-to-all-start.1
  50.1 13.1 %collective-permute-done.4.refs_2_.refs_6_.refs_4_.refs_8_ = bf16[4,128,1024]{2,1,0:T(8,128)(2,1)} collective-permute-done((bf16[4,128,1024]{2,1,0:T(8,128)(2,1)}, bf16[4,128,1024]{2,1,0:T(8,128)(2,1)}, u32[]{:S(2)}, u32[]{:S(2)}) %collective-permute-start.4) | collective-permute-done | bytes 1048608 | tf_op jit(solution)/shard_map/ny_qkv/ppermute | solution.py:37
  63.2 30.2 %collective-permute-done.3.refs_3_.refs_7_.refs_5_.refs_9_ = bf16[4,128,1024]{2,1,0:T(8,128)(2,1)} collective-permute-done((bf16[4,128,1024]{2,1,0:T(8,128)(2,1)}, bf16[4,128,1024]{2,1,0:T(8,128)(2,1)}, u32[]{:S(2)}, u32[]{:S(2)}) %collective-permute-start.3) | collective-permute-done | bytes 1048608 | tf_op jit(solution)/shard_map/zh_qkv/ppermute | solution.py:37
  93.5 9.8 %all-to-all-start.2 = ((bf16[4,128,1536]{2,1,0:T(8,128)(2,1)}), bf16[4,128,1536]{2,1,0:T(8,128)(2,1)S(1)}, u32[]{:S(2)}, u32[]{:S(2)}) async-start(bf16[4,128,1536]{2,1,0:T(8,128)(2,1)} %pad_maximum_fusion), calls=%async_computation.2 | async-start | bytes 3145728 | tf_op jit(solution)/shard_map/all_to_all | solution.py:59
  106.0 23.7 %collective-permute-done.5.refs_4_.refs_8_.refs_6_.refs_10_ = bf16[4,128,1024]{2,1,0:T(8,128)(2,1)} collective-permute-done((bf16[4,128,1024]{2,1,0:T(8,128)(2,1)}, bf16[4,128,1024]{2,1,0:T(8,128)(2,1)}, u32[]{:S(2)}, u32[]{:S(2)}) %collective-permute-start.5) | collective-permute-done | bytes 1048608 | tf_op jit(solution)/shard_map/fy_qkv/ppermute | solution.py:37
  129.7 23.2 %shard_map.229 = (bf16[4,384,256]{2,1,0:T(8,128)(2,1)}, bf16[4,384,256]{2,1,0:T(8,128)(2,1)}, bf16[4,384,512]{2,1,0:T(8,128)(2,1)}, bf16[4,384,384]{2,1,0:T(8,12...) custom-call(s32[4]{0:T(128)} %pad_add_fusion.1.coord, f32[4,384,384]{2,1,0:T(8,128)} %and_select_fusion.mask, ...), custom_call_target="tpu_custom_call" | custom-call | flops 6442450944 | bytes 25296912 | tf_op jit(solution)/shard_map/pallas_call | solution.py:321
  155.5 24.2 %collective-permute-done.8.refs_4_.refs_8_.refs_13_.refs_14_ = bf16[4,128,1024]{2,1,0:T(8,128)(2,1)} collective-permute-done((bf16[4,128,1024]{2,1,0:T(8,128)(2,1)}, bf16[4,128,1024]{2,1,0:T(8,128)(2,1)}, u32[]{:S(2)}, u32[]{:S(2)}) %collective-permute-start.8) | collective-permute-done | bytes 1048608 | tf_op jit(solution)/shard_map/fy_so/ppermute | solution.py:37
  179.6 15.0 %shard_map.230 = (f32[4,384,512]{2,1,0:T(8,128)}, bf16[4,384,512]{2,1,0:T(8,128)(2,1)}, bf16[3,192,2048]{2,1,0:T(8,128)(2,1)}, bf16[192,2048]{1,0:T(8,128)(2,1)}, bf16[4,192,2048]{2,1,0:T(8,128)(2,1)}) custom-call(s32[4]{0:T(128)} %pad_add_fusion.1.coord, f32[4,384,512]{2,1,0:T(8,128)} %get-tuple-element.153.hat, bf16[8,192,2048]{2,1,0:T(8,128)(2,1)} %bitcast.141, ...), custom_call_target="tpu_custom_call" | custom-call | flops 6442450944 | bytes 28835856 | tf_op jit(solution)/shard_map/pallas_call | solution.py:321
  194.7 2.7 collective-permute-done.10.refs_11_.refs_15_
  200.4 5.9 collective-permute-done.12
  210.2 8.8 %collective-permute-done.14 = bf16[96,2048]{1,0:T(8,128)(2,1)S(1)} collective-permute-done((bf16[96,2048]{1,0:T(8,128)(2,1)S(1)}, bf16[96,2048]{1,0:T(8,128)(2,1)S(1)}, u32[]{:S(2)}, u32[]{:S(2)}) %collective-permute-start.14) | collective-permute-done | bytes 393248 | tf_op jit(solution)/shard_map/branch_dz/ppermute | solution.py:37
  227.4 18.3 %collective-permute-done.18.refs_2_ = bf16[4,128,512]{2,1,0:T(8,128)(2,1)S(1)} collective-permute-done((bf16[4,128,512]{2,1,0:T(8,128)(2,1)S(1)}, bf16[4,128,512]{2,1,0:T(8,128)(2,1)S(1)}, u32[]{:S(2)}, u32[]{:S(2)}) %collective-permute-start.18) | collective-permute-done | bytes 524320 | tf_op jit(solution)/shard_map/ny_d/ppermute | solution.py:37
  245.7 5.7 collective-permute-done.17.refs_3_
  259.0 12.2 %collective-permute-done.20.refs_4_ = bf16[4,128,512]{2,1,0:T(8,128)(2,1)S(1)} collective-permute-done((bf16[4,128,512]{2,1,0:T(8,128)(2,1)S(1)}, bf16[4,128,512]{2,1,0:T(8,128)(2,1)S(1)}, u32[]{:S(2)}, u32[]{:S(2)}) %collective-permute-start.20) | collective-permute-done | bytes 524320 | tf_op jit(solution)/shard_map/fy_d/ppermute | solution.py:37
  271.2 4.2 collective-permute-done.22.refs_4_.refs_6_
  280.9 7.8 %shard_map.231.gh = f32[4,384,512]{2,1,0:T(8,128)} custom-call(s32[4]{0:T(128)} %pad_add_fusion.1.coord, bf16[8,192,2048]{2,1,0:T(8,128)(2,1)} %bitcast.144, bf16[4,128,512]{2,1,0:T(8,128)(2,1)} %copy-done.32, bf16[4,128,512]{2,1,0:T(8,128)(2,1)} %copy-done.59, bf16[4,128,512]{2,1,0:T(8,128)(2,1)} %copy-done.60, bf16[4,128,512]{2,1,0:T(8,128)(2,1)} %copy-done.61), custom_call_target="tpu_custom_call" | custom-call | flops 3221225472 | bytes 11534352 | tf_op jit(solution)/shard_map/pallas_call | solution.py:321
  294.9 23.7 %shard_map.232 = (bf16[4,384,512]{2,1,0:T(8,128)(2,1)}, bf16[4,384,512]{2,1,0:T(8,128)(2,1)}, bf16[4,384,512]{2,1,0:T(8,128)(2,1)}, bf16[3,192,2048]{2,1,0:T(8,1...) custom-call(s32[4]{0:T(128)} %pad_add_fusion.1.coord, f32[4,384,512]{2,1,0:T(8,128)} %shard_map.231.gh, ...), custom_call_target="tpu_custom_call" | custom-call | flops 12884901888 | bytes 28835856 | tf_op jit(solution)/shard_map/pallas_call | solution.py:321
  319.2 5.1 collective-permute-done.30
  327.8 10.9 %shard_map.233 = (bf16[4,256,512]{2,1,0:T(8,128)(2,1)}, bf16[4,256,512]{2,1,0:T(8,128)(2,1)}) custom-call(s32[4]{0:T(128)} %pad_add_fusion.1.coord, bf16[4,384,512]{2,1,0:T(8,128)(2,1)} %get-tuple-element.182.refs_0_, bf16[8,192,2048]{2,1,0:T(8,128)(2,1)} %bitcast.145), custom_call_target="tpu_custom_call" | custom-call | flops 3221225472 | bytes 9961472 | tf_op jit(solution)/shard_map/pallas_call | solution.py:795
  347.5 16.5 %shard_map.234 = (bf16[4,256,512]{2,1,0:T(8,128)(2,1)}, bf16[4,256,512]{2,1,0:T(8,128)(2,1)}, bf16[4,256,512]{2,1,0:T(8,128)(2,1)}, bf16[4,256,512]{2,1,0:T(8,128)(2,1)}) custom-call(s32[4]{0:T(128)} %pad_add_fusion.1.coord, bf16[4,384,512]{2,1,0:T(8,128)(2,1)} %get-tuple-element.192.refs_0_, bf16[4,384,512]{2,1,0:T(8,128)(2,1)} %get-tuple-element.193.refs_1_, ...), custom_call_target="tpu_custom_call" | custom-call | flops 6442450944 | bytes 13631488 | tf_op jit(solution)/shard_map/pallas_call | solution.py:795
  364.8 3.1 multiply_reduce_fusion
  367.9 2.7 fusion.45
  378.4 25.1 %collective-permute-done.37 = bf16[2,256,512]{2,1,0:T(8,128)(2,1)S(1)} collective-permute-done((bf16[2,256,512]{2,1,0:T(8,128)(2,1)S(1)}, bf16[2,256,512]{2,1,0:T(8,128)(2,1)S(1)}, u32[]{:S(2)}, u32[]{:S(2)}) %collective-permute-start.37) | collective-permute-done | bytes 524320 | tf_op jit(solution)/shard_map/zh_gdown/ppermute | solution.py:37
  411.1 8.3 %shard_map.235 = bf16[8,192,2048]{2,1,0:T(8,128)(2,1)} custom-call(s32[4]{0:T(128)} %pad_add_fusion.1.coord, bf16[4,384,512]{2,1,0:T(8,128)(2,1)} %get-tuple-element.182.refs_0_, bf16[4,128,512]{2,1,0:T(8,128)(2,1)} %copy-done.32, bf16[4,128,512]{2,1,0:T(8,128)(2,1)} %copy-done.59, bf16[4,128,512]{2,1,0:T(8,128)(2,1)} %copy-done.60, ...), custom_call_target="tpu_custom_call" | custom-call | flops 3221225472 | bytes 9961488 | tf_op jit(solution)/shard_map/pallas_call | solution.py:321
  426.4 17.0 %shard_map.236 = (bf16[4,384,512]{2,1,0:T(8,128)(2,1)}, bf16[4,384,512]{2,1,0:T(8,128)(2,1)}, bf16[4,384,512]{2,1,0:T(8,128)(2,1)}) custom-call(s32[4]{0:T(128)} %pad_add_fusion.1.coord, f32[4,384,384]{2,1,0:T(8,128)} %and_select_fusion.mask, f32[4,384,512]{2,1,0:T(8,128)} %get-tuple-element.205.s, f32[4,384,512]{2,1,0:T(8,128)} %get-tuple-element.153.hat, ...), custom_call_target="tpu_custom_call" | custom-call | flops 4831838208 | bytes 28966928 | tf_op jit(solution)/shard_map/pallas_call | solution.py:321
  444.8 5.1 collective-permute-done.48
  451.3 11.0 %shard_map.237 = (bf16[4,256,512]{2,1,0:T(8,128)(2,1)}, bf16[4,256,512]{2,1,0:T(8,128)(2,1)}) custom-call(s32[4]{0:T(128)} %pad_add_fusion.1.coord, bf16[4,384,512]{2,1,0:T(8,128)(2,1)} %get-tuple-element.218.refs_0_, bf16[192,2048]{1,0:T(8,128)(2,1)} %copy-done.12, bf16[192,2048]{1,0:T(8,128)(2,1)} %copy-done.28, ...), custom_call_target="tpu_custom_call" | custom-call | flops 3221225472 | bytes 9961472 | tf_op jit(solution)/shard_map/pallas_call | solution.py:795
  463.1 10.9 %shard_map.238 = (bf16[4,256,512]{2,1,0:T(8,128)(2,1)}, bf16[4,256,512]{2,1,0:T(8,128)(2,1)}) custom-call(s32[4]{0:T(128)} %pad_add_fusion.1.coord, bf16[4,384,512]{2,1,0:T(8,128)(2,1)} %get-tuple-element.221.refs_0_.refs_2_, bf16[8,192,2048]{2,1,0:T(8,128)(2,1)} %bitcast.142), custom_call_target="tpu_custom_call" | custom-call | flops 3221225472 | bytes 9961472 | tf_op jit(solution)/shard_map/pallas_call | solution.py:795
  475.8 16.4 %shard_map.239 = (bf16[4,256,512]{2,1,0:T(8,128)(2,1)}, bf16[4,256,512]{2,1,0:T(8,128)(2,1)}, bf16[4,256,512]{2,1,0:T(8,128)(2,1)}, bf16[4,256,512]{2,1,0:T(8,128)(2,1)}) custom-call(s32[4]{0:T(128)} %pad_add_fusion.1.coord, bf16[4,384,512]{2,1,0:T(8,128)(2,1)} %get-tuple-element.226.refs_0_.refs_1_, ...), custom_call_target="tpu_custom_call" | custom-call | flops 6442450944 | bytes 13631488 | tf_op jit(solution)/shard_map/pallas_call | solution.py:795
  496.1 17.0 %shard_map.240 = (bf16[3,192,2048]{2,1,0:T(8,128)(2,1)}, bf16[192,2048]{1,0:T(8,128)(2,1)}, bf16[4,192,2048]{2,1,0:T(8,128)(2,1)}) custom-call(s32[4]{0:T(128)} %pad_add_fusion.1.coord, bf16[4,384,512]{2,1,0:T(8,128)(2,1)} %get-tuple-element.212.refs_1_.refs_0_, bf16[4,384,512]{2,1,0:T(8,128)(2,1)} %get-tuple-element.226.refs_0_.refs_1_, ...), custom_call_target="tpu_custom_call" | custom-call | flops 9663676416 | bytes 23592976 | tf_op jit(solution)/shard_map/pallas_call | solution.py:321
  513.1 6.3 collective-permute-done.52
  522.4 2.9 collective-permute-done.55
  527.8 19.5 %collective-permute-done.59 = bf16[2,256,512]{2,1,0:T(8,128)(2,1)S(1)} collective-permute-done((bf16[2,256,512]{2,1,0:T(8,128)(2,1)S(1)}, bf16[2,256,512]{2,1,0:T(8,128)(2,1)S(1)}, u32[]{:S(2)}, u32[]{:S(2)}) %collective-permute-start.59) | collective-permute-done | bytes 524320 | tf_op jit(solution)/shard_map/zh_gswish/ppermute | solution.py:37
  557.3 2.6 collective-permute-start.58
  562.4 4.3 all-to-all-start.3
  566.8 7.4 %collective-permute-done.62 = bf16[2,256,512]{2,1,0:T(8,128)(2,1)} collective-permute-done((bf16[2,256,512]{2,1,0:T(8,128)(2,1)}, bf16[2,256,512]{2,1,0:T(8,128)(2,1)}, u32[]{:S(2)}, u32[]{:S(2)}) %collective-permute-start.62) | collective-permute-done | bytes 524320 | tf_op jit(solution)/shard_map/zh_gvalue/ppermute | solution.py:37
  577.9 23.2 %collective-permute-done.58 = bf16[192,2048]{1,0:T(8,128)(2,1)} collective-permute-done((bf16[192,2048]{1,0:T(8,128)(2,1)}, bf16[192,2048]{1,0:T(8,128)(2,1)}, u32[]{:S(2)}, u32[]{:S(2)}) %collective-permute-start.58) | collective-permute-done | bytes 786464 | tf_op jit(solution)/shard_map/back_one_z/ppermute | solution.py:37
  606.8 3.4 collective-permute-start.65
  612.0 2.6 collective-permute-start.66
  621.8 4.3 all-to-all-start.4
  626.1 3.7 add_add_fusion.2
  630.5 3.8 shard_map.241
  641.4 3.5 all-to-all-start.5
  644.9 3.6 shard_map.243
  648.5 9.4 %all-to-all-done.5.g = bf16[4,128,1024]{2,1,0:T(8,128)(2,1)S(1)} async-done(((bf16[4,128,1024]{2,1,0:T(8,128)(2,1)}), bf16[4,128,1024]{2,1,0:T(8,128)(2,1)S(1)}, u32[]{:S(2)}, u32[]{:S(2)}) %all-to-all-start.5) | async-done | bytes 1048608 | tf_op jit(solution)/shard_map/all_to_all | solution.py:59
  658.9 3.5 shard_map.242
  (360 shorter events, 154.0 us)
Async XLA Ops:
  11.4 18.9 %all-to-all-start = ((bf16[4,128,1024]{2,1,0:T(8,128)(2,1)}), bf16[4,128,1024]{2,1,0:T(8,128)(2,1)S(1)}, u32[]{:S(2)}, u32[]{:S(2)}) async-start(bf16[4,128,1024]{2,1,0:T(8,128)(2,1)} %pad_maximum_fusion.3), calls=%async_computation | async-start | bytes 2097152 | tf_op jit(solution)/shard_map/all_to_all | solution.py:59
  16.7 113.0 %all-gather.5.cloned.1.call-start = ((), (), s32[]{:S(2)}) async-start(), calls=%async_computation.8 | async-start | bytes 7077888 | tf_op jit(solution)/shard_map/all_gather | solution.py:909
  35.2 58.3 %all-to-all-start.1 = ((bf16[4,128,1024]{2,1,0:T(8,128)(2,1)}), bf16[4,128,1024]{2,1,0:T(8,128)(2,1)S(1)}, u32[]{:S(2)}, u32[]{:S(2)}) async-start(bf16[4,128,1024]{2,1,0:T(8,128)(2,1)} %pad_maximum_fusion.2), calls=%async_computation.1 | async-start | bytes 2097152 | tf_op jit(solution)/shard_map/all_to_all | solution.py:59
  39.0 24.3 %collective-permute-start.4 = (bf16[4,128,1024]{2,1,0:T(8,128)(2,1)}, bf16[4,128,1024]{2,1,0:T(8,128)(2,1)}, u32[]{:S(2)}, u32[]{:S(2)}) collective-permute-start(bf16[4,128,1024]{2,1,0:T(8,128)(2,1)} %copy-done.13), channel_id=1, source_target_pairs={{0,4},{4,0},{1,5},{5,1},{2,6},{6,2},{3,7},{7,3},{8,12},{12,8},{9,1... | collective-permute-start | bytes 3145736 | tf_op jit(solution)/shard_map/ny_qkv/ppermute | solution.py:37
  40.6 52.9 %collective-permute-start.3 = (bf16[4,128,1024]{2,1,0:T(8,128)(2,1)}, bf16[4,128,1024]{2,1,0:T(8,128)(2,1)}, u32[]{:S(2)}, u32[]{:S(2)}) collective-permute-start(bf16[4,128,1024]{2,1,0:T(8,128)(2,1)} %copy-done.13), channel_id=1, source_target_pairs={{0,16},{16,0},{1,17},{17,1},{2,18},{18,2},{3,19},{19,3},{4,20},{20... | collective-permute-start | bytes 3145736 | tf_op jit(solution)/shard_map/zh_qkv/ppermute | solution.py:37
  93.5 59.4 %all-to-all-start.2 = ((bf16[4,128,1536]{2,1,0:T(8,128)(2,1)}), bf16[4,128,1536]{2,1,0:T(8,128)(2,1)S(1)}, u32[]{:S(2)}, u32[]{:S(2)}) async-start(bf16[4,128,1536]{2,1,0:T(8,128)(2,1)} %pad_maximum_fusion), calls=%async_computation.2 | async-start | bytes 3145728 | tf_op jit(solution)/shard_map/all_to_all | solution.py:59
  103.3 177.6 %all-gather.7.cloned.1.call-start = ((), (), s32[]{:S(2)}) async-start(), calls=%async_computation.9 | async-start | bytes 7077888 | tf_op jit(solution)/shard_map/all_gather | solution.py:928
  103.3 26.4 %collective-permute-start.5 = (bf16[4,128,1024]{2,1,0:T(8,128)(2,1)}, bf16[4,128,1024]{2,1,0:T(8,128)(2,1)}, u32[]{:S(2)}, u32[]{:S(2)}) collective-permute-start(bf16[4,128,1024]{2,1,0:T(8,128)(2,1)} %collective-permute-done.3.refs_3_.refs_7_.refs_5_.refs_9_), channel_id=1, source_target_pairs={{0,4},{4,0},{1,5},{5,1},{2,6},{6,2},{3,7},{7,3},{8,12},{12,8},{9,1... | collective-permute-start | bytes 3145736 | tf_op jit(solution)/shard_map/fy_qkv/ppermute | solution.py:37
  104.9 48.0 %collective-permute-start.7 = (bf16[4,128,1024]{2,1,0:T(8,128)(2,1)S(1)}, bf16[4,128,1024]{2,1,0:T(8,128)(2,1)}, u32[]{:S(2)}, u32[]{:S(2)}) collective-permute-start(bf16[4,128,1024]{2,1,0:T(8,128)(2,1)S(1)} %all-to-all-done.1.refs_1_.refs_5_.refs_10_.refs_11_), channel_id=1, source_target_pairs={{0,4},{4,0},{1,5},{5,1},{2,6},{6,2},{3,7},{7,3},{8,12},{12,8},{9,1... | collective-permute-start | bytes 3145736 | tf_op jit(solution)/shard_map/ny_so/ppermute | solution.py:37
  105.3 47.6 %collective-permute-start.6 = (bf16[4,128,1024]{2,1,0:T(8,128)(2,1)S(1)}, bf16[4,128,1024]{2,1,0:T(8,128)(2,1)}, u32[]{:S(2)}, u32[]{:S(2)}) collective-permute-start(bf16[4,128,1024]{2,1,0:T(8,128)(2,1)S(1)} %all-to-all-done.1.refs_1_.refs_5_.refs_10_.refs_11_), channel_id=1, source_target_pairs={{0,16},{16,0},{1,17},{17,1},{2,18},{18,2},{3,19},{19,3},{4,20},{20... | collective-permute-start | bytes 3145736 | tf_op jit(solution)/shard_map/zh_so/ppermute | solution.py:37
  152.9 481.4 %reduce-scatter.2.cloned.1.call-start = ((), (), s32[]{:S(2)}) async-start(), calls=%async_computation.7 | async-start | bytes 7077888 | tf_op jit(solution)/shard_map/reduce_scatter | solution.py:981
  153.2 26.5 %collective-permute-start.8 = (bf16[4,128,1024]{2,1,0:T(8,128)(2,1)}, bf16[4,128,1024]{2,1,0:T(8,128)(2,1)}, u32[]{:S(2)}, u32[]{:S(2)}) collective-permute-start(bf16[4,128,1024]{2,1,0:T(8,128)(2,1)} %collective-permute-done.6.refs_3_.refs_7_.refs_12_.refs_13_), channel_id=1, source_target_pairs={{0,4},{4,0},{1,5},{5,1},{2,6},{6,2},{3,7},{7,3},{8,12},{12,8},{9,1... | collective-permute-start | bytes 3145736 | tf_op jit(solution)/shard_map/fy_so/ppermute | solution.py:37
  155.0 42.5 %collective-permute-start.10 = (bf16[4,128,1024]{2,1,0:T(8,128)(2,1)S(1)}, bf16[4,128,1024]{2,1,0:T(8,128)(2,1)}, u32[]{:S(2)}, u32[]{:S(2)}) collective-permute-start(bf16[4,128,1024]{2,1,0:T(8,128)(2,1)S(1)} %slice.316.refs_10_.refs_14_), channel_id=1, source_target_pairs={{0,4},{4,0},{1,5},{5,1},{2,6},{6,2},{3,7},{7,3},{8,12},{12,8},{9,1... | collective-permute-start | bytes 3145736 | tf_op jit(solution)/shard_map/ny_ug/ppermute | solution.py:37
  155.5 44.4 %collective-permute-start.9 = (bf16[4,128,1024]{2,1,0:T(8,128)(2,1)S(1)}, bf16[4,128,1024]{2,1,0:T(8,128)(2,1)}, u32[]{:S(2)}, u32[]{:S(2)}) collective-permute-start(bf16[4,128,1024]{2,1,0:T(8,128)(2,1)S(1)} %slice.316.refs_10_.refs_14_), channel_id=1, source_target_pairs={{0,16},{16,0},{1,17},{17,1},{2,18},{18,2},{3,19},{19,3},{4,20},{20... | collective-permute-start | bytes 3145736 | tf_op jit(solution)/shard_map/zh_ug/ppermute | solution.py:37
  199.8 19.2 %collective-permute-start.11 = (bf16[3,192,2048]{2,1,0:T(8,128)(2,1)}, bf16[3,192,2048]{2,1,0:T(8,128)(2,1)S(1)}, u32[]{:S(2)}, u32[]{:S(2)}) collective-permute-start(bf16[3,192,2048]{2,1,0:T(8,128)(2,1)} %get-tuple-element.159), channel_id=1, source_target_pairs={{0,1},{1,0},{2,3},{3,2},{4,5},{5,4},{6,7},{7,6},{8,9},{9,8},{10,11... | collective-permute-start | bytes 7077896 | tf_op jit(solution)/shard_map/branch_cr/ppermute | solution.py:37
  209.3 42.0 %collective-permute-start.19 = (bf16[4,128,1024]{2,1,0:T(8,128)(2,1)}, bf16[4,128,1024]{2,1,0:T(8,128)(2,1)S(1)}, u32[]{:S(2)}, u32[]{:S(2)}) collective-permute-start(bf16[4,128,1024]{2,1,0:T(8,128)(2,1)} %collective-permute-done.9.refs_12_.refs_16_), channel_id=1, source_target_pairs={{0,4},{4,0},{1,5},{5,1},{2,6},{6,2},{3,7},{7,3},{8,12},{12,8},{9,1... | collective-permute-start | bytes 3145736 | tf_op jit(solution)/shard_map/fy_ug/ppermute | solution.py:37
  220.6 30.7 %collective-permute-start.15 = (bf16[192,2048]{1,0:T(8,128)(2,1)S(1)}, bf16[192,2048]{1,0:T(8,128)(2,1)S(1)}, u32[]{:S(2)}, u32[]{:S(2)}) collective-permute-start(bf16[192,2048]{1,0:T(8,128)(2,1)S(1)} %pad_maximum_fusion.6), channel_id=1, source_target_pairs={{0,2},{2,0},{1,3},{3,1},{4,6},{6,4},{5,7},{7,5},{8,10},{10,8},{9,1... | collective-permute-start | bytes 2359304 | tf_op jit(solution)/shard_map/branch_x/ppermute | solution.py:37
  223.2 30.3 %collective-permute-start.16 = (bf16[192,2048]{1,0:T(8,128)(2,1)S(1)}, bf16[192,2048]{1,0:T(8,128)(2,1)S(1)}, u32[]{:S(2)}, u32[]{:S(2)}) collective-permute-start(bf16[192,2048]{1,0:T(8,128)(2,1)S(1)} %pad_maximum_fusion.7), channel_id=1, source_target_pairs={{0,8},{8,0},{1,9},{9,1},{2,10},{10,2},{3,11},{11,3},{4,12},{12,4},... | collective-permute-start | bytes 2359304 | tf_op jit(solution)/shard_map/branch_z/ppermute | solution.py:37
  224.0 21.7 %collective-permute-start.18 = (bf16[4,128,512]{2,1,0:T(8,128)(2,1)S(1)}, bf16[4,128,512]{2,1,0:T(8,128)(2,1)S(1)}, u32[]{:S(2)}, u32[]{:S(2)}) collective-permute-start(bf16[4,128,512]{2,1,0:T(8,128)(2,1)S(1)} %slice.326.refs_1_), channel_id=1, source_target_pairs={{0,4},{4,0},{1,5},{5,1},{2,6},{6,2},{3,7},{7,3},{8,12},{12,8},{9,1... | collective-permute-start | bytes 1572872 | tf_op jit(solution)/shard_map/ny_d/ppermute | solution.py:37
  224.9 26.4 %collective-permute-start.17 = (bf16[4,128,512]{2,1,0:T(8,128)(2,1)S(1)}, bf16[4,128,512]{2,1,0:T(8,128)(2,1)S(1)}, u32[]{:S(2)}, u32[]{:S(2)}) collective-permute-start(bf16[4,128,512]{2,1,0:T(8,128)(2,1)S(1)} %slice.326.refs_1_), channel_id=1, source_target_pairs={{0,16},{16,0},{1,17},{17,1},{2,18},{18,2},{3,19},{19,3},{4,20},{20... | collective-permute-start | bytes 1572872 | tf_op jit(solution)/shard_map/zh_d/ppermute | solution.py:37
  255.3 20.1 %collective-permute-start.22 = (bf16[192,2048]{1,0:T(8,128)(2,1)S(1)}, bf16[192,2048]{1,0:T(8,128)(2,1)}, u32[]{:S(2)}, u32[]{:S(2)}) collective-permute-start(bf16[192,2048]{1,0:T(8,128)(2,1)S(1)} %multiply_convert_fusion.refs_0_.refs_2_), channel_id=1, source_target_pairs={{0,8},{8,0},{1,9},{9,1},{2,10},{10,2},{3,11},{11,3},{4,12},{12,4},... | collective-permute-start | bytes 2359304 | tf_op jit(solution)/shard_map/two_z/ppermute | solution.py:37
  256.5 19.7 %collective-permute-start.21 = (bf16[192,2048]{1,0:T(8,128)(2,1)S(1)}, bf16[192,2048]{1,0:T(8,128)(2,1)}, u32[]{:S(2)}, u32[]{:S(2)}) collective-permute-start(bf16[192,2048]{1,0:T(8,128)(2,1)S(1)} %multiply_convert_fusion.refs_0_.refs_2_), channel_id=1, source_target_pairs={{0,2},{2,0},{1,3},{3,1},{4,6},{6,4},{5,7},{7,5},{8,10},{10,8},{9,1... | collective-permute-start | bytes 2359304 | tf_op jit(solution)/shard_map/two_x/ppermute | solution.py:37
  318.6 20.1 %collective-permute-start.33 = (bf16[3,192,2048]{2,1,0:T(8,128)(2,1)}, bf16[3,192,2048]{2,1,0:T(8,128)(2,1)}, u32[]{:S(2)}, u32[]{:S(2)}) collective-permute-start(bf16[3,192,2048]{2,1,0:T(8,128)(2,1)} %get-tuple-element.186), channel_id=1, source_target_pairs={{0,1},{1,0},{2,3},{3,2},{4,5},{5,4},{6,7},{7,6},{8,9},{9,8},{10,11... | collective-permute-start | bytes 7077896 | tf_op jit(solution)/shard_map/back_two_cr/ppermute | solution.py:37
  338.7 26.1 %collective-permute-start.34 = (bf16[4,256,512]{2,1,0:T(8,128)(2,1)}, bf16[4,256,512]{2,1,0:T(8,128)(2,1)}, u32[]{:S(2)}, u32[]{:S(2)}) collective-permute-start(bf16[4,256,512]{2,1,0:T(8,128)(2,1)} %get-tuple-element.187), channel_id=1, source_target_pairs={{0,4},{4,0},{1,5},{5,1},{2,6},{6,2},{3,7},{7,3},{8,12},{12,8},{9,1... | collective-permute-start | bytes 3145736 | tf_op jit(solution)/shard_map/y_down/ppermute | solution.py:37
  344.4 19.6 %collective-permute-start.35 = (bf16[192,2048]{1,0:T(8,128)(2,1)}, bf16[192,2048]{1,0:T(8,128)(2,1)S(1)}, u32[]{:S(2)}, u32[]{:S(2)}) collective-permute-start(bf16[192,2048]{1,0:T(8,128)(2,1)} %pad_maximum_fusion.8), channel_id=1, source_target_pairs={{0,2},{2,0},{1,3},{3,1},{4,6},{6,4},{5,7},{7,5},{8,10},{10,8},{9,1... | collective-permute-start | bytes 2359304 | tf_op jit(solution)/shard_map/back_two_x/ppermute | solution.py:37
  345.9 18.9 %collective-permute-start.36 = (bf16[192,2048]{1,0:T(8,128)(2,1)}, bf16[192,2048]{1,0:T(8,128)(2,1)S(1)}, u32[]{:S(2)}, u32[]{:S(2)}) collective-permute-start(bf16[192,2048]{1,0:T(8,128)(2,1)} %pad_maximum_fusion.9), channel_id=1, source_target_pairs={{0,8},{8,0},{1,9},{9,1},{2,10},{10,2},{3,11},{11,3},{4,12},{12,4},... | collective-permute-start | bytes 2359304 | tf_op jit(solution)/shard_map/back_two_z/ppermute | solution.py:37
  372.5 32.0 %collective-permute-start.38 = (bf16[4,256,512]{2,1,0:T(8,128)(2,1)S(1)}, bf16[4,256,512]{2,1,0:T(8,128)(2,1)S(1)}, u32[]{:S(2)}, u32[]{:S(2)}) collective-permute-start(bf16[4,256,512]{2,1,0:T(8,128)(2,1)S(1)} %copy-done.57), channel_id=1, source_target_pairs={{0,4},{4,0},{1,5},{5,1},{2,6},{6,2},{3,7},{7,3},{8,12},{12,8},{9,1... | collective-permute-start | bytes 3145736 | tf_op jit(solution)/shard_map/y_up/ppermute | solution.py:37
  373.2 30.3 %collective-permute-start.41 = (bf16[192,2048]{1,0:T(8,128)(2,1)S(1)}, bf16[192,2048]{1,0:T(8,128)(2,1)S(1)}, u32[]{:S(2)}, u32[]{:S(2)}) collective-permute-start(bf16[192,2048]{1,0:T(8,128)(2,1)S(1)} %fusion.21.refs_0_.refs_1_), channel_id=1, source_target_pairs={{0,1},{1,0},{2,3},{3,2},{4,5},{5,4},{6,7},{7,6},{8,9},{9,8},{10,11... | collective-permute-start | bytes 2359304 | tf_op jit(solution)/shard_map/gb_c/ppermute | solution.py:37
  373.2 31.3 %collective-permute-start.40 = (bf16[192,2048]{1,0:T(8,128)(2,1)S(1)}, bf16[192,2048]{1,0:T(8,128)(2,1)}, u32[]{:S(2)}, u32[]{:S(2)}) collective-permute-start(bf16[192,2048]{1,0:T(8,128)(2,1)S(1)} %fusion.21.refs_0_.refs_1_), channel_id=1, source_target_pairs={{0,8},{8,0},{1,9},{9,1},{2,10},{10,2},{3,11},{11,3},{4,12},{12,4},... | collective-permute-start | bytes 2359304 | tf_op jit(solution)/shard_map/gb_z/ppermute | solution.py:37
  374.8 29.7 %collective-permute-start.39 = (bf16[192,2048]{1,0:T(8,128)(2,1)S(1)}, bf16[192,2048]{1,0:T(8,128)(2,1)}, u32[]{:S(2)}, u32[]{:S(2)}) collective-permute-start(bf16[192,2048]{1,0:T(8,128)(2,1)S(1)} %fusion.21.refs_0_.refs_1_), channel_id=1, source_target_pairs={{0,2},{2,0},{1,3},{3,1},{4,6},{6,4},{5,7},{7,5},{8,10},{10,8},{9,1... | collective-permute-start | bytes 2359304 | tf_op jit(solution)/shard_map/gb_x/ppermute | solution.py:37
  377.0 26.5 %collective-permute-start.37 = (bf16[2,256,512]{2,1,0:T(8,128)(2,1)S(1)}, bf16[2,256,512]{2,1,0:T(8,128)(2,1)S(1)}, u32[]{:S(2)}, u32[]{:S(2)}) collective-permute-start(bf16[2,256,512]{2,1,0:T(8,128)(2,1)S(1)} %add_convert_fusion.20), channel_id=1, source_target_pairs={{0,16},{16,0},{1,17},{17,1},{2,18},{18,2},{3,19},{19,3},{4,20},{20... | collective-permute-start | bytes 1572872 | tf_op jit(solution)/shard_map/zh_gdown/ppermute | solution.py:37
  420.4 24.4 %collective-permute-start.49 = (bf16[4,256,512]{2,1,0:T(8,128)(2,1)}, bf16[4,256,512]{2,1,0:T(8,128)(2,1)}, u32[]{:S(2)}, u32[]{:S(2)}) collective-permute-start(bf16[4,256,512]{2,1,0:T(8,128)(2,1)} %get-tuple-element.216), channel_id=1, source_target_pairs={{0,4},{4,0},{1,5},{5,1},{2,6},{6,2},{3,7},{7,3},{8,12},{12,8},{9,1... | collective-permute-start | bytes 3145736 | tf_op jit(solution)/shard_map/y_gate/ppermute | solution.py:37
  423.6 26.2 %collective-permute-start.48 = (bf16[2,256,512]{2,1,0:T(8,128)(2,1)S(1)}, bf16[2,256,512]{2,1,0:T(8,128)(2,1)}, u32[]{:S(2)}, u32[]{:S(2)}) collective-permute-start(bf16[2,256,512]{2,1,0:T(8,128)(2,1)S(1)} %add_convert_fusion.19), channel_id=1, source_target_pairs={{0,16},{16,0},{1,17},{17,1},{2,18},{18,2},{3,19},{19,3},{4,20},{20... | collective-permute-start | bytes 1572872 | tf_op jit(solution)/shard_map/zh_gup/ppermute | solution.py:37
  451.2 24.6 %collective-permute-start.50 = (bf16[2,256,512]{2,1,0:T(8,128)(2,1)S(1)}, bf16[2,256,512]{2,1,0:T(8,128)(2,1)}, u32[]{:S(2)}, u32[]{:S(2)}) collective-permute-start(bf16[2,256,512]{2,1,0:T(8,128)(2,1)S(1)} %add_convert_fusion.18), channel_id=1, source_target_pairs={{0,16},{16,0},{1,17},{17,1},{2,18},{18,2},{3,19},{19,3},{4,20},{20... | collective-permute-start | bytes 1572872 | tf_op jit(solution)/shard_map/zh_ggate/ppermute | solution.py:37
  462.3 29.9 %collective-permute-start.51 = (bf16[4,256,512]{2,1,0:T(8,128)(2,1)}, bf16[4,256,512]{2,1,0:T(8,128)(2,1)}, u32[]{:S(2)}, u32[]{:S(2)}) collective-permute-start(bf16[4,256,512]{2,1,0:T(8,128)(2,1)} %get-tuple-element.228), channel_id=1, source_target_pairs={{0,4},{4,0},{1,5},{5,1},{2,6},{6,2},{3,7},{7,3},{8,12},{12,8},{9,1... | collective-permute-start | bytes 3145736 | tf_op jit(solution)/shard_map/y_out/ppermute | solution.py:37
  492.3 27.2 %collective-permute-start.53 = (bf16[4,256,512]{2,1,0:T(8,128)(2,1)}, bf16[4,256,512]{2,1,0:T(8,128)(2,1)}, u32[]{:S(2)}, u32[]{:S(2)}) collective-permute-start(bf16[4,256,512]{2,1,0:T(8,128)(2,1)} %get-tuple-element.235), channel_id=1, source_target_pairs={{0,4},{4,0},{1,5},{5,1},{2,6},{6,2},{3,7},{7,3},{8,12},{12,8},{9,1... | collective-permute-start | bytes 3145736 | tf_op jit(solution)/shard_map/y_swish/ppermute | solution.py:37
  494.4 25.1 %collective-permute-start.52 = (bf16[2,256,512]{2,1,0:T(8,128)(2,1)S(1)}, bf16[2,256,512]{2,1,0:T(8,128)(2,1)}, u32[]{:S(2)}, u32[]{:S(2)}) collective-permute-start(bf16[2,256,512]{2,1,0:T(8,128)(2,1)S(1)} %add_convert_fusion.17), channel_id=1, source_target_pairs={{0,16},{16,0},{1,17},{17,1},{2,18},{18,2},{3,19},{19,3},{4,20},{20... | collective-permute-start | bytes 1572872 | tf_op jit(solution)/shard_map/zh_gout/ppermute | solution.py:37
  519.4 32.3 %collective-permute-start.54 = (bf16[3,192,2048]{2,1,0:T(8,128)(2,1)}, bf16[3,192,2048]{2,1,0:T(8,128)(2,1)S(1)}, u32[]{:S(2)}, u32[]{:S(2)}) collective-permute-start(bf16[3,192,2048]{2,1,0:T(8,128)(2,1)} %get-tuple-element.236), channel_id=1, source_target_pairs={{0,1},{1,0},{2,3},{3,2},{4,5},{5,4},{6,7},{7,6},{8,9},{9,8},{10,11... | collective-permute-start | bytes 7077896 | tf_op jit(solution)/shard_map/back_one_cr/ppermute | solution.py:37
  519.9 27.3 %collective-permute-start.60 = (bf16[4,256,512]{2,1,0:T(8,128)(2,1)}, bf16[4,256,512]{2,1,0:T(8,128)(2,1)S(1)}, u32[]{:S(2)}, u32[]{:S(2)}) collective-permute-start(bf16[4,256,512]{2,1,0:T(8,128)(2,1)} %get-tuple-element.246), channel_id=1, source_target_pairs={{0,4},{4,0},{1,5},{5,1},{2,6},{6,2},{3,7},{7,3},{8,12},{12,8},{9,1... | collective-permute-start | bytes 3145736 | tf_op jit(solution)/shard_map/y_value/ppermute | solution.py:37
  522.3 24.9 %collective-permute-start.59 = (bf16[2,256,512]{2,1,0:T(8,128)(2,1)S(1)}, bf16[2,256,512]{2,1,0:T(8,128)(2,1)S(1)}, u32[]{:S(2)}, u32[]{:S(2)}) collective-permute-start(bf16[2,256,512]{2,1,0:T(8,128)(2,1)S(1)} %add_convert_fusion.16), channel_id=1, source_target_pairs={{0,16},{16,0},{1,17},{17,1},{2,18},{18,2},{3,19},{19,3},{4,20},{20... | collective-permute-start | bytes 1572872 | tf_op jit(solution)/shard_map/zh_gswish/ppermute | solution.py:37
  526.7 25.0 %collective-permute-start.56 = (bf16[192,2048]{1,0:T(8,128)(2,1)S(1)}, bf16[192,2048]{1,0:T(8,128)(2,1)S(1)}, u32[]{:S(2)}, u32[]{:S(2)}) collective-permute-start(bf16[192,2048]{1,0:T(8,128)(2,1)S(1)} %fusion.14), channel_id=1, source_target_pairs={{0,2},{2,0},{1,3},{3,1},{4,6},{6,4},{5,7},{7,5},{8,10},{10,8},{9,1... | collective-permute-start | bytes 2359304 | tf_op jit(solution)/shard_map/back_one_dx/ppermute | solution.py:37
  548.4 25.8 %collective-permute-start.62 = (bf16[2,256,512]{2,1,0:T(8,128)(2,1)}, bf16[2,256,512]{2,1,0:T(8,128)(2,1)}, u32[]{:S(2)}, u32[]{:S(2)}) collective-permute-start(bf16[2,256,512]{2,1,0:T(8,128)(2,1)} %add_convert_fusion.15), channel_id=1, source_target_pairs={{0,16},{16,0},{1,17},{17,1},{2,18},{18,2},{3,19},{19,3},{4,20},{20... | collective-permute-start | bytes 1572872 | tf_op jit(solution)/shard_map/zh_gvalue/ppermute | solution.py:37
  548.7 25.5 %collective-permute-start.61 = (bf16[4,256,512]{2,1,0:T(8,128)(2,1)}, bf16[4,256,512]{2,1,0:T(8,128)(2,1)}, u32[]{:S(2)}, u32[]{:S(2)}) collective-permute-start(bf16[4,256,512]{2,1,0:T(8,128)(2,1)} %get-tuple-element.247), channel_id=1, source_target_pairs={{0,4},{4,0},{1,5},{5,1},{2,6},{6,2},{3,7},{7,3},{8,12},{12,8},{9,1... | collective-permute-start | bytes 3145736 | tf_op jit(solution)/shard_map/y_qk/ppermute | solution.py:37
  555.5 22.4 %collective-permute-start.57 = (bf16[192,2048]{1,0:T(8,128)(2,1)}, bf16[192,2048]{1,0:T(8,128)(2,1)}, u32[]{:S(2)}, u32[]{:S(2)}) collective-permute-start(bf16[192,2048]{1,0:T(8,128)(2,1)} %fusion.22), channel_id=1, source_target_pairs={{0,2},{2,0},{1,3},{3,1},{4,6},{6,4},{5,7},{7,5},{8,10},{10,8},{9,1... | collective-permute-start | bytes 2359304 | tf_op jit(solution)/shard_map/back_one_x/ppermute | solution.py:37
  557.3 43.8 %collective-permute-start.58 = (bf16[192,2048]{1,0:T(8,128)(2,1)}, bf16[192,2048]{1,0:T(8,128)(2,1)}, u32[]{:S(2)}, u32[]{:S(2)}) collective-permute-start(bf16[192,2048]{1,0:T(8,128)(2,1)} %fusion.12), channel_id=1, source_target_pairs={{0,8},{8,0},{1,9},{9,1},{2,10},{10,2},{3,11},{11,3},{4,12},{12,4},... | collective-permute-start | bytes 2359304 | tf_op jit(solution)/shard_map/back_one_z/ppermute | solution.py:37
  562.4 59.4 %all-to-all-start.3 = ((bf16[4,128,1536]{2,1,0:T(8,128)(2,1)}), bf16[4,128,1536]{2,1,0:T(8,128)(2,1)}, u32[]{:S(2)}, u32[]{:S(2)}) async-start(bf16[4,128,1536]{2,1,0:T(8,128)(2,1)} %pad_maximum_fusion.1), calls=%async_computation.4 | async-start | bytes 3145728 | tf_op jit(solution)/shard_map/all_to_all | solution.py:59
  575.5 29.8 %collective-permute-start.63 = (bf16[2,256,512]{2,1,0:T(8,128)(2,1)S(1)}, bf16[2,256,512]{2,1,0:T(8,128)(2,1)S(1)}, u32[]{:S(2)}, u32[]{:S(2)}) collective-permute-start(bf16[2,256,512]{2,1,0:T(8,128)(2,1)S(1)} %add_convert_fusion.14), channel_id=1, source_target_pairs={{0,16},{16,0},{1,17},{17,1},{2,18},{18,2},{3,19},{19,3},{4,20},{20... | collective-permute-start | bytes 1572872 | tf_op jit(solution)/shard_map/zh_gqk/ppermute | solution.py:37
  641.4 16.5 %all-to-all-start.5 = ((bf16[4,128,1024]{2,1,0:T(8,128)(2,1)}), bf16[4,128,1024]{2,1,0:T(8,128)(2,1)S(1)}, u32[]{:S(2)}, u32[]{:S(2)}) async-start(bf16[4,128,1024]{2,1,0:T(8,128)(2,1)} %pad_maximum_fusion.5), calls=%async_computation.6 | async-start | bytes 2097152 | tf_op jit(solution)/shard_map/all_to_all | solution.py:59
  (95 other events, 927.3 us)
Sparse Core Ops, SparseCore 0:
  30.4 70.6 all-gather.4
  153.1 58.3 all-gather.6
  420.5 65.6 reduce-scatter.1
